TPU v7x, 32 devices: a whole 2x2x4 slice. The times are simulated.
32 devices in a mesh: seq: 8 (over y, x, core), head: 4 (over z).
Axes of the slice: x: 2, y: 2, z: 4, core: 2. Of those that a mesh axis runs over, the one named last changes fastest.
Arguments:
- queries: bfloat16 [1024, 32, 576], P('seq', 'head'), may hold values from -0.06982422 to 0.06982422
- out_grad: bfloat16 [1024, 32, 512], P('seq', 'head'), may hold values from -12 to 12
- latents: bfloat16 [6144, 576], P('seq'), may hold values from -1.6953125 to 1.6953125
- log_norm: bfloat16 [1024, 32], P('seq', 'head'), may hold values from 0 to 12, as said below
- out_delta: bfloat16 [1024, 32], P('seq', 'head'), may hold values from -4 to 4
- plan: int32 [8, 2], P('seq'), may hold values from 0 to 1
Outputs:
- query_out: bfloat16 [1024, 32, 576], P('seq', 'head')
- latent_out: bfloat16 [6144, 576], P(('seq', 'head'))
Inputs may be any that keep to these rules, and one draw needn't show every extreme that they name: plan[k, t] names which of the 2 latent blocks of shard k the queries of shard k + t (modulo the shards) visit at step t. log_norm lies within one unit of the log of 768.
All inputs are finite; a program needn't handle non-finite values.
Results may differ from a plain program's by a relative error of at most 0.0049.
Values may be sent and summed in bfloat16 or wider, within the bound.
No kernel may reach another device: no remote copies, remote signals or barrier semaphores. Data moves between devices by JAX's collectives and lax.ppermute only.
A program may use at most 64 MiB of HBM per device.

v0:
```python
import functools

import jax
import jax.numpy as jnp
from jax import lax
from jax.experimental import pallas as pl
from jax.experimental.pallas import tpu as pltpu
from jax.sharding import PartitionSpec as P

LAT = 512
PACKET = 128
BLOCK = 384
SHARD = 768
WIDE = 256
VMEM_LIMIT = 24 * 2**20

F32 = jnp.float32
BF16 = jnp.bfloat16


def dot(a, b):
    return lax.dot_general(a, b, (((1,), (0,)), ((), ())), preferred_element_type=F32)


def dot_nt(a, b):
    return lax.dot_general(a, b, (((1,), (1,)), ((), ())), preferred_element_type=F32)


def block_of(lat_ref, block):
    return lat_ref[:, pl.ds(pl.multiple_of(block * BLOCK, 128), BLOCK)]


def send_block_kernel(plan_ref, lat_ref, out_ref):
    out_ref[...] = block_of(lat_ref, plan_ref[0, 1]).T


def heads_side_by_side(q_ref, first, count):
    return jnp.concatenate([q_ref[first + i] for i in range(count)], axis=1)


def visit(keys, q_ref, grad_ref, norm_ref, delta_ref, visible, ds_ref, p_ref, grad_out_ref):
    heads = q_ref.shape[0]
    per = WIDE // PACKET
    for first in range(0, heads, per):
        cols = slice(first * PACKET, (first + per) * PACKET)
        scores = dot(keys, heads_side_by_side(q_ref, first, per))
        prob_grad = dot_nt(keys[:, :LAT], grad_ref[cols, :])
        for i in range(per):
            lanes = slice(i * PACKET, (i + 1) * PACKET)
            norm = norm_ref[first + i : first + i + 1, :].astype(F32)
            delta = delta_ref[first + i : first + i + 1, :].astype(F32)
            prob = jnp.exp(scores[:, lanes] - norm)
            if visible is not None:
                prob = jnp.where(visible, prob, 0.0)
            here = slice((first + i) * PACKET, (first + i + 1) * PACKET)
            ds_ref[:, here] = (prob * (prob_grad[:, lanes] - delta)).astype(BF16)
            p_ref[:, here] = prob.astype(BF16)
    key_grad = dot_nt(ds_ref[...], heads_side_by_side(q_ref, 0, heads))
    value_grad = dot(p_ref[...], grad_ref[...])
    grad_out_ref[:, :LAT] = key_grad[:, :LAT] + value_grad
    grad_out_ref[:, LAT:] = key_grad[:, LAT:]


def pieces_out(total_ref, out_refs, low):
    rows = BLOCK // low
    r = lax.rem(lax.axis_index("head"), low)
    for d, out_ref in enumerate(out_refs):
        start = pl.multiple_of(lax.rem(r + d, low) * rows, 16)
        out_ref[...] = total_ref[pl.ds(start, rows), :].astype(out_ref.dtype)


def own_kernel(low, plan_ref, lat_ref, q_ref, grad_ref, norm_ref, delta_ref, *rest):
    rows_ref, ds_ref = rest[:2]
    out_refs = rest[2 : 2 + low]
    p_ref, total_ref = rest[2 + low :]
    heads = q_ref.shape[0]
    group = WIDE // heads
    at = lax.broadcasted_iota(jnp.int32, (WIDE, WIDE), 0)
    come = lax.broadcasted_iota(jnp.int32, (WIDE, WIDE), 1)
    order = (come == lax.rem(at, group) * heads + lax.div(at, group)).astype(F32).astype(BF16)
    for g in range(PACKET // group):
        moved = dot(order, grad_ref[g * WIDE : (g + 1) * WIDE, :]).astype(BF16)
        for h in range(heads):
            rows_ref[h * PACKET + g * group : h * PACKET + (g + 1) * group, :] = moved[h * group : (h + 1) * group, :]
    b0 = plan_ref[0, 0]
    keys = block_of(lat_ref, b0).T
    k_pos = b0 * BLOCK + lax.broadcasted_iota(jnp.int32, (BLOCK, PACKET), 0)
    q_pos = SHARD - PACKET + lax.broadcasted_iota(jnp.int32, (BLOCK, PACKET), 1)
    visit(keys, q_ref, rows_ref, norm_ref, delta_ref, k_pos <= q_pos, ds_ref, p_ref, total_ref)
    pieces_out(total_ref, out_refs, low)


def far_kernel(low, keys_ref, q_ref, grad_ref, norm_ref, delta_ref, *rest):
    ds_ref = rest[0]
    out_refs = rest[1 : 1 + low]
    p_ref, total_ref = rest[1 + low :]
    visit(keys_ref[...], q_ref, grad_ref, norm_ref, delta_ref, None, ds_ref, p_ref, total_ref)
    pieces_out(total_ref, out_refs, low)


def query_kernel(plan_ref, lat_ref, far_ref, own_ds_ref, far_ds_ref, out_ref):
    heads = out_ref.shape[0]
    per = WIDE // PACKET
    own = block_of(lat_ref, plan_ref[0, 0])
    far = far_ref[...].T
    for first in range(0, heads, per):
        cols = slice(first * PACKET, (first + per) * PACKET)
        total = dot(own, own_ds_ref[:, cols]) + dot(far, far_ds_ref[:, cols])
        for i in range(per):
            out_ref[first + i] = total[:, i * PACKET : (i + 1) * PACKET].astype(BF16)


def combine_kernel(low, plan_ref, *rest):
    own_refs = rest[:low]
    far_refs = rest[low : 2 * low]
    send_ref, mine_ref = rest[2 * low :]
    own = own_refs[0][...]
    for ref in own_refs[1:]:
        own = own + ref[...].astype(F32)
    far = far_refs[0][...].astype(F32)
    for ref in far_refs[1:]:
        far = far + ref[...].astype(F32)
    t = lax.div(lax.axis_index("head"), low)
    b0, b1 = plan_ref[0, 0], plan_ref[0, 1]

    def total(block):
        return jnp.where(b0 == block, own, 0.0) + jnp.where(b1 == block, far, 0.0)

    mine_ref[...] = total(t)
    send_ref[...] = total(1 - t).astype(BF16)


def last_kernel(mine_ref, got_ref, out_ref):
    out_ref[...] = (mine_ref[...] + got_ref[...].astype(F32)).astype(BF16)


def call(kernel, name, ins, outs, scratch=(), smem=0, flops=0, transcendentals=0):
    specs = [pl.BlockSpec(memory_space=pltpu.SMEM if i < smem else pltpu.VMEM) for i in range(len(ins))]
    size = sum(x.size * x.dtype.itemsize for x in ins)
    size += sum(functools.reduce(lambda a, b: a * b, s, jnp.dtype(d).itemsize) for s, d in outs)
    return pl.pallas_call(
        kernel,
        name=name,
        out_shape=[jax.ShapeDtypeStruct(s, d) for s, d in outs],
        in_specs=specs,
        out_specs=[pl.BlockSpec(memory_space=pltpu.VMEM) for _ in outs],
        scratch_shapes=scratch,
        compiler_params=pltpu.CompilerParams(vmem_limit_bytes=VMEM_LIMIT),
        cost_estimate=pl.CostEstimate(flops=flops, bytes_accessed=size, transcendentals=transcendentals),
    )(*ins)


def local(queries, out_grad, latents, log_norm, out_delta, plan):
    n_seq = lax.axis_size("seq")
    n_head = lax.axis_size("head")
    low = n_head // 2
    rows = BLOCK // low
    packet, heads, width = queries.shape
    columns = packet * heads

    lat_t = latents.T
    q_t = jnp.transpose(queries, (1, 2, 0))
    grad = out_grad.reshape(columns, LAT)
    norm_t = log_norm.T
    delta_t = out_delta.T
    visit_flops = 2 * columns * BLOCK * (2 * width + 2 * LAT)

    def route(d, back):
        pairs = []
        for i in range(back, n_seq):
            for j in range(n_head):
                to = j // low * low + (j + d) % low
                pairs.append((i * n_head + j, (i - back) * n_head + to))
        return pairs

    (sent,) = call(send_block_kernel, "send_block", (plan, lat_t), [((BLOCK, width), BF16)], smem=1)
    far_keys = lax.ppermute(sent, "seq", [(i, i + 1) for i in range(n_seq - 1)])

    scratch = [pltpu.VMEM((BLOCK, columns), BF16), pltpu.VMEM((BLOCK, width), F32)]
    grad_rows, own_ds, *own = call(
        functools.partial(own_kernel, low),
        "own_visit",
        (plan, lat_t, q_t, grad, norm_t, delta_t),
        [((columns, LAT), BF16), ((BLOCK, columns), BF16), ((rows, width), F32)] + [((rows, width), BF16)] * (low - 1),
        scratch,
        smem=1,
        flops=visit_flops,
        transcendentals=columns * BLOCK,
    )
    own_parts = [own[0]] + [lax.ppermute(own[d], ("seq", "head"), route(d, 0)) for d in range(1, low)]

    far_ds, *far = call(
        functools.partial(far_kernel, low),
        "far_visit",
        (far_keys, q_t, grad_rows, norm_t, delta_t),
        [((BLOCK, columns), BF16)] + [((rows, width), BF16)] * low,
        scratch,
        flops=visit_flops,
        transcendentals=columns * BLOCK,
    )
    far_parts = [lax.ppermute(far[d], ("seq", "head"), route(d, 1)) for d in reversed(range(low))]

    (query_t,) = call(
        query_kernel,
        "query_grad",
        (plan, lat_t, far_keys, own_ds, far_ds),
        [((heads, width, packet), BF16)],
        smem=1,
        flops=4 * columns * BLOCK * width,
    )
    send, mine = call(
        functools.partial(combine_kernel, low),
        "combine",
        (plan, *own_parts, *far_parts),
        [((rows, width), BF16), ((rows, width), F32)],
        smem=1,
    )
    got = lax.ppermute(send, "head", [(j, (j + low) % n_head) for j in range(n_head)])
    (latent_out,) = call(last_kernel, "last_sum", (mine, got), [((rows, width), BF16)])
    return jnp.transpose(query_t, (2, 0, 1)), latent_out


def solution(mesh):
    return jax.shard_map(
        local,
        mesh=mesh,
        in_specs=(
            P("seq", "head", None),
            P("seq", "head", None),
            P("seq", None),
            P("seq", "head"),
            P("seq", "head"),
            P("seq", None),
        ),
        out_specs=(P("seq", "head", None), P(("seq", "head"), None)),
        check_vma=False,
    )
```

profile of v0, /device:TPU:5, one launch (start us, length us, event | category | flops | bytes accessed | tf_op | source)
XLA Modules:
  0.0 44.2 jit_solution(14632868426817476946)
XLA Ops:
  0.6 0.0 copy-start
  0.6 1.2 %copy-done = bf16[768,576]{0,1:T(8,128)(2,1)S(1)} copy-done((bf16[768,576]{0,1:T(8,128)(2,1)S(1)}, bf16[768,576]{0,1:T(8,128)(2,1)}, u32[]{:S(2)}) %copy-start) | copy-done | bytes 884760
  1.8 0.0 copy-start.2
  1.8 0.7 %copy-done.2 = s32[1,2]{1,0:T(1,128)S(1)} copy-done((s32[1,2]{1,0:T(1,128)S(1)}, s32[1,2]{1,0:T(1,128)}, u32[]{:S(2)}) %copy-start.2) | copy-done | bytes 32
  2.5 0.0 copy-start.4
  2.5 0.0 copy-start.6
  2.5 0.0 copy-start.7
  2.5 0.7 %send_block.1 = bf16[384,576]{1,0:T(8,128)(2,1)S(1)} custom-call(s32[1,2]{1,0:T(1,128)S(1)} %copy-done.2, bf16[576,768]{1,0:T(8,128)(2,1)S(1)} %bitcast.6), custom_call_target="tpu_custom_call" | custom-call | bytes 1327112 | tf_op jit(solution)/shard_map/send_block/pallas_call | solution.py:141
  3.2 3.7 %collective-permute-start = (bf16[384,576]{1,0:T(8,128)(2,1)S(1)}, bf16[384,576]{1,0:T(8,128)(2,1)S(1)}, u32[]{:S(2)}, u32[]{:S(2)}) collective-permute-start(bf16[384,576]{1,0:T(8,128)(2,1)S(1)} %send_block.1), channel_id=1, source_target_pairs={{0,4},{4,8},{8,12},{12,16},{16,20},{20,24},{24,28},{1,5},{5,9},{9,... | collective-permute-start | bytes 1327112 | tf_op jit(solution)/shard_map/ppermute | solution.py:177
  6.9 0.0 copy-done.4
  6.9 0.0 copy-done.6
  6.9 0.0 copy-done.7
  6.9 0.0 copy-start.5
  6.9 1.2 %copy-done.5 = bf16[128,8,512]{2,1,0:T(8,128)(2,1)S(1)} copy-done((bf16[128,8,512]{2,1,0:T(8,128)(2,1)S(1)}, bf16[128,8,512]{2,1,0:T(8,128)(2,1)}, u32[]{:S(2)}) %copy-start.5) | copy-done | bytes 1048600
  8.1 3.4 %own_visit.1 = (bf16[1024,512]{1,0:T(8,128)(2,1)S(1)}, bf16[384,1024]{1,0:T(8,128)(2,1)S(1)}, f32[192,576]{1,0:T(8,128)S(1)}, bf16[192,576]{1,0:T(8,128)(2,1)S(1)}) custom-call(s32[1,2]{1,0:T(1,128)S(1)} %copy-done.2, bf16[576,768]{1,0:T(8,128)(2,1)S(1)} %bitcast.7, bf16[8,576,128]{2,1,0:T(8,128)(2,1)S(1)} %bitcast.9, bf16[1024,512]{1,0:T(8,128)(2,1)S(1)} %bitcast.11, ...), custom_call_target="tpu_custom_call" | custom-call | flops 1711276032 | bytes 5615624 | tf_op jit(solution)/shard_map/own_visit/pallas_call | solution.py:141
  11.5 1.4 %collective-permute-start.1 = (bf16[192,576]{1,0:T(8,128)(2,1)S(1)}, bf16[192,576]{1,0:T(8,128)(2,1)S(1)}, u32[]{:S(2)}, u32[]{:S(2)}) collective-permute-start(bf16[192,576]{1,0:T(8,128)(2,1)S(1)} %get-tuple-element.15), channel_id=1, source_target_pairs={{0,1},{1,0},{2,3},{3,2},{4,5},{5,4},{6,7},{7,6},{8,9},{9,8},{10,11... | collective-permute-start | bytes 663560 | tf_op jit(solution)/shard_map/ppermute | solution.py:190
  12.9 0.0 collective-permute-done.keys_ref.far_ref
  12.9 0.0 copy-start.3
  12.9 2.5 %far_visit.1 = (bf16[384,1024]{1,0:T(8,128)(2,1)S(1)}, bf16[192,576]{1,0:T(8,128)(2,1)S(1)}, bf16[192,576]{1,0:T(8,128)(2,1)S(1)}) custom-call(bf16[384,576]{1,0:T(8,128)(2,1)S(1)} %collective-permute-done.keys_ref.far_ref, bf16[8,576,128]{2,1,0:T(8,128)(2,1)S(1)} %bitcast.10, bf16[1024,512]{1,0:T(8,128)(2,1)S(1)} %get-tuple-element.12.grad_ref, ...), custom_call_target="tpu_custom_call" | custom-call | flops 1711276032 | bytes 3903488 | tf_op jit(solution)/shard_map/far_visit/pallas_call | solution.py:141
  15.5 0.0 copy-start.1
  15.5 5.2 %collective-permute-start.2 = (bf16[192,576]{1,0:T(8,128)(2,1)S(1)}, bf16[192,576]{1,0:T(8,128)(2,1)S(1)}, u32[]{:S(2)}, u32[]{:S(2)}) collective-permute-start(bf16[192,576]{1,0:T(8,128)(2,1)S(1)} %get-tuple-element.16), channel_id=1, source_target_pairs={{4,1},{5,0},{6,3},{7,2},{8,5},{9,4},{10,7},{11,6},{12,9},{13,8},{1... | collective-permute-start | bytes 663560 | tf_op jit(solution)/shard_map/ppermute | solution.py:201
  20.7 1.9 %collective-permute-start.3 = (bf16[192,576]{1,0:T(8,128)(2,1)S(1)}, bf16[192,576]{1,0:T(8,128)(2,1)S(1)}, u32[]{:S(2)}, u32[]{:S(2)}) collective-permute-start(bf16[192,576]{1,0:T(8,128)(2,1)S(1)} %get-tuple-element.17), channel_id=1, source_target_pairs={{4,0},{5,1},{6,2},{7,3},{8,4},{9,5},{10,6},{11,7},{12,8},{13,9},{1... | collective-permute-start | bytes 663560 | tf_op jit(solution)/shard_map/ppermute | solution.py:201
  22.7 0.0 collective-permute-done.1.rest_1_
  22.7 4.5 %collective-permute-done.2.rest_2_ = bf16[192,576]{1,0:T(8,128)(2,1)S(1)} collective-permute-done((bf16[192,576]{1,0:T(8,128)(2,1)S(1)}, bf16[192,576]{1,0:T(8,128)(2,1)S(1)}, u32[]{:S(2)}, u32[]{:S(2)}) %collective-permute-start.2) | collective-permute-done | bytes 221216 | tf_op jit(solution)/shard_map/ppermute | solution.py:201
  27.2 1.8 %collective-permute-done.3.rest_3_ = bf16[192,576]{1,0:T(8,128)(2,1)S(1)} collective-permute-done((bf16[192,576]{1,0:T(8,128)(2,1)S(1)}, bf16[192,576]{1,0:T(8,128)(2,1)S(1)}, u32[]{:S(2)}, u32[]{:S(2)}) %collective-permute-start.3) | collective-permute-done | bytes 221216 | tf_op jit(solution)/shard_map/ppermute | solution.py:201
  29.1 0.0 copy-done.3
  29.1 0.7 %combine.1 = (bf16[192,576]{1,0:T(8,128)(2,1)S(1)}, f32[192,576]{1,0:T(8,128)S(1)}) custom-call(s32[1,2]{1,0:T(1,128)S(1)} %copy-done.3, f32[192,576]{1,0:T(8,128)S(1)} %get-tuple-element.14.rest_0_, bf16[192,576]{1,0:T(8,128)(2,1)S(1)} %collective-permute-done.1.rest_1_, bf16[192,576]{1,0:T(8,128)(2,1)S(1)} %collective-permute-done.2.rest_2_, ...), custom_call_target="tpu_custom_call" | custom-call | bytes 1769480 | tf_op jit(solution)/shard_map/combine/pallas_call | solution.py:141
  29.8 2.4 %collective-permute-start.4 = (bf16[192,576]{1,0:T(8,128)(2,1)S(1)}, bf16[192,576]{1,0:T(8,128)(2,1)S(1)}, u32[]{:S(2)}, u32[]{:S(2)}) collective-permute-start(bf16[192,576]{1,0:T(8,128)(2,1)S(1)} %get-tuple-element.19), channel_id=1, source_target_pairs={{0,2},{1,3},{2,0},{3,1},{4,6},{5,7},{6,4},{7,5},{8,10},{9,11},{10,... | collective-permute-start | bytes 663560 | tf_op jit(solution)/shard_map/ppermute | solution.py:218
  32.2 0.0 copy-done.1
  32.2 3.0 %query_grad.1 = bf16[8,576,128]{2,1,0:T(8,128)(2,1)} custom-call(s32[1,2]{1,0:T(1,128)S(1)} %copy-done.3, bf16[576,768]{1,0:T(8,128)(2,1)S(1)} %bitcast.8, bf16[384,576]{1,0:T(8,128)(2,1)S(1)} %collective-permute-done.keys_ref.far_ref, bf16[384,1024]{1,0:T(8,128)(2,1)S(1)} %get-tuple-element.11.own_ds_ref, bf16[384,1024]{1,0:T(8,128)(2,1)S(1)} %get-tuple-element.13.far_ds_ref), custom_call_target="tpu_custom_call" | custom-call | flops 905969664 | bytes 4079624 | tf_op jit(solution)/shard_map/query_grad/pallas_call | solution.py:141
  35.2 8.3 %collective-permute-done.4.got_ref = bf16[192,576]{1,0:T(8,128)(2,1)S(1)} collective-permute-done((bf16[192,576]{1,0:T(8,128)(2,1)S(1)}, bf16[192,576]{1,0:T(8,128)(2,1)S(1)}, u32[]{:S(2)}, u32[]{:S(2)}) %collective-permute-start.4) | collective-permute-done | bytes 221216 | tf_op jit(solution)/shard_map/ppermute | solution.py:218
  43.5 0.7 %last_sum.1 = bf16[192,576]{1,0:T(8,128)(2,1)} custom-call(f32[192,576]{1,0:T(8,128)S(1)} %get-tuple-element.18.mine_ref, bf16[192,576]{1,0:T(8,128)(2,1)S(1)} %collective-permute-done.4.got_ref), custom_call_target="tpu_custom_call" | custom-call | bytes 884736 | tf_op jit(solution)/shard_map/last_sum/pallas_call | solution.py:141
Async XLA Ops:
  0.6 1.2 %copy-start = (bf16[768,576]{0,1:T(8,128)(2,1)S(1)}, bf16[768,576]{0,1:T(8,128)(2,1)}, u32[]{:S(2)}) copy-start(bf16[768,576]{0,1:T(8,128)(2,1)} %param.8) | copy-start | bytes 2654212
  1.8 0.7 %copy-start.2 = (s32[1,2]{1,0:T(1,128)S(1)}, s32[1,2]{1,0:T(1,128)}, u32[]{:S(2)}) copy-start(s32[1,2]{1,0:T(1,128)} %plan_ref.7) | copy-start | bytes 28
  2.5 4.4 %copy-start.4 = (bf16[128,8,576]{0,2,1:T(8,128)(2,1)S(1)}, bf16[128,8,576]{0,2,1:T(8,128)(2,1)}, u32[]{:S(2)}) copy-start(bf16[128,8,576]{0,2,1:T(8,128)(2,1)} %param.6) | copy-start | bytes 3538948
  2.5 4.4 %copy-start.6 = (bf16[128,8]{0,1:T(8,128)(2,1)S(1)}, bf16[128,8]{0,1:T(8,128)(2,1)}, u32[]{:S(2)}) copy-start(bf16[128,8]{0,1:T(8,128)(2,1)} %param.9) | copy-start | bytes 6148
  2.5 4.4 %copy-start.7 = (bf16[128,8]{0,1:T(8,128)(2,1)S(1)}, bf16[128,8]{0,1:T(8,128)(2,1)}, u32[]{:S(2)}) copy-start(bf16[128,8]{0,1:T(8,128)(2,1)} %param.10) | copy-start | bytes 6148
  3.2 9.7 %collective-permute-start = (bf16[384,576]{1,0:T(8,128)(2,1)S(1)}, bf16[384,576]{1,0:T(8,128)(2,1)S(1)}, u32[]{:S(2)}, u32[]{:S(2)}) collective-permute-start(bf16[384,576]{1,0:T(8,128)(2,1)S(1)} %send_block.1), channel_id=1, source_target_pairs={{0,4},{4,8},{8,12},{12,16},{16,20},{20,24},{24,28},{1,5},{5,9},{9,... | collective-permute-start | bytes 1327112 | tf_op jit(solution)/shard_map/ppermute | solution.py:177
  6.9 1.2 %copy-start.5 = (bf16[128,8,512]{2,1,0:T(8,128)(2,1)S(1)}, bf16[128,8,512]{2,1,0:T(8,128)(2,1)}, u32[]{:S(2)}) copy-start(bf16[128,8,512]{2,1,0:T(8,128)(2,1)} %param.7) | copy-start | bytes 3145732
  11.5 11.1 %collective-permute-start.1 = (bf16[192,576]{1,0:T(8,128)(2,1)S(1)}, bf16[192,576]{1,0:T(8,128)(2,1)S(1)}, u32[]{:S(2)}, u32[]{:S(2)}) collective-permute-start(bf16[192,576]{1,0:T(8,128)(2,1)S(1)} %get-tuple-element.15), channel_id=1, source_target_pairs={{0,1},{1,0},{2,3},{3,2},{4,5},{5,4},{6,7},{7,6},{8,9},{9,8},{10,11... | collective-permute-start | bytes 663560 | tf_op jit(solution)/shard_map/ppermute | solution.py:190
  12.9 16.2 %copy-start.3 = (s32[1,2]{1,0:T(1,128)S(1)}, s32[1,2]{1,0:T(1,128)}, u32[]{:S(2)}) copy-start(s32[1,2]{1,0:T(1,128)} %plan_ref.7) | copy-start | bytes 28
  15.5 16.7 %copy-start.1 = (bf16[768,576]{0,1:T(8,128)(2,1)S(1)}, bf16[768,576]{0,1:T(8,128)(2,1)}, u32[]{:S(2)}) copy-start(bf16[768,576]{0,1:T(8,128)(2,1)} %param.8) | copy-start | bytes 2654212
  15.5 11.7 %collective-permute-start.2 = (bf16[192,576]{1,0:T(8,128)(2,1)S(1)}, bf16[192,576]{1,0:T(8,128)(2,1)S(1)}, u32[]{:S(2)}, u32[]{:S(2)}) collective-permute-start(bf16[192,576]{1,0:T(8,128)(2,1)S(1)} %get-tuple-element.16), channel_id=1, source_target_pairs={{4,1},{5,0},{6,3},{7,2},{8,5},{9,4},{10,7},{11,6},{12,9},{13,8},{1... | collective-permute-start | bytes 663560 | tf_op jit(solution)/shard_map/ppermute | solution.py:201
  20.7 8.3 %collective-permute-start.3 = (bf16[192,576]{1,0:T(8,128)(2,1)S(1)}, bf16[192,576]{1,0:T(8,128)(2,1)S(1)}, u32[]{:S(2)}, u32[]{:S(2)}) collective-permute-start(bf16[192,576]{1,0:T(8,128)(2,1)S(1)} %get-tuple-element.17), channel_id=1, source_target_pairs={{4,0},{5,1},{6,2},{7,3},{8,4},{9,5},{10,6},{11,7},{12,8},{13,9},{1... | collective-permute-start | bytes 663560 | tf_op jit(solution)/shard_map/ppermute | solution.py:201
  29.8 13.6 %collective-permute-start.4 = (bf16[192,576]{1,0:T(8,128)(2,1)S(1)}, bf16[192,576]{1,0:T(8,128)(2,1)S(1)}, u32[]{:S(2)}, u32[]{:S(2)}) collective-permute-start(bf16[192,576]{1,0:T(8,128)(2,1)S(1)} %get-tuple-element.19), channel_id=1, source_target_pairs={{0,2},{1,3},{2,0},{3,1},{4,6},{5,7},{6,4},{7,5},{8,10},{9,11},{10,... | collective-permute-start | bytes 663560 | tf_op jit(solution)/shard_map/ppermute | solution.py:218
where the time goes:
time: 44.5 us; the launch traced here: 44.2 us
  waiting for transfers between devices  14.7 us (33%)
  starting transfers between devices  14.6 us (33%)
  Pallas kernels  11.1 us (25%)
  local copies, waits for them, and re-layouts  3.06 us (7%)
  between operations  0.74 us (2%)
    pallas_call x6, Pallas kernels, call(): pl.pallas_call(kernel, name=name, out_shape=[jax.ShapeDtypeStruct(s, d) f...  11.1 us
    ppermute x1, waiting for transfers between devices, local(): lax.ppermute(send, 'head', [(j, (j + low) % n_head) for j in range(n_head)])  8.29 us
    ppermute x2, starting transfers between devices, local(): lax.ppermute(far[d], ('seq', 'head'), route(d, 1))  7.17 us
    ppermute x2, waiting for transfers between devices, local(): lax.ppermute(far[d], ('seq', 'head'), route(d, 1))  6.4 us
    ppermute x1, starting transfers between devices, local(): far_keys = lax.ppermute(sent, 'seq', [(i, i + 1) for i in range(n_seq - 1)])  3.68 us
    unnamed x16, local copies, waits for them, and re-layouts  3.06 us
    ppermute x1, starting transfers between devices, local(): lax.ppermute(send, 'head', [(j, (j + low) % n_head) for j in range(n_head)])  2.37 us
    ppermute x1, starting transfers between devices, local(): lax.ppermute(own[d], ('seq', 'head'), route(d, 0))  1.37 us
  transfers between devices with their start and end apart: 5, of which 3 were waited for; matrix products, arithmetic and copies ran while one was open for 0% of the time, Pallas kernels for 20%

commit v1 on v0

--- a/solution.py
+++ b/solution.py
@@ -13,6 +13,7 @@
 SHARD = 768
 WIDE = 256
 VMEM_LIMIT = 24 * 2**20
+NEVER = 1e30
 
 F32 = jnp.float32
 BF16 = jnp.bfloat16
@@ -30,7 +31,13 @@
     return lat_ref[:, pl.ds(pl.multiple_of(block * BLOCK, 128), BLOCK)]
 
 
-def send_block_kernel(plan_ref, lat_ref, out_ref):
+def send_block_kernel(plan_hbm, lat_hbm, out_ref, plan_ref, lat_ref, sems):
+    plan_copy = pltpu.make_async_copy(plan_hbm, plan_ref, sems.at[0])
+    lat_copy = pltpu.make_async_copy(lat_hbm, lat_ref, sems.at[1])
+    plan_copy.start()
+    lat_copy.start()
+    plan_copy.wait()
+    lat_copy.wait()
     out_ref[...] = block_of(lat_ref, plan_ref[0, 1]).T
 
 
@@ -38,7 +45,7 @@
     return jnp.concatenate([q_ref[first + i] for i in range(count)], axis=1)
 
 
-def visit(keys, q_ref, grad_ref, norm_ref, delta_ref, visible, ds_ref, p_ref, grad_out_ref):
+def visit(keys, q_ref, grad_ref, norm_ref, delta_ref, live, visible, ds_ref, p_ref, grad_out_ref):
     heads = q_ref.shape[0]
     per = WIDE // PACKET
     for first in range(0, heads, per):
@@ -48,6 +55,8 @@
         for i in range(per):
             lanes = slice(i * PACKET, (i + 1) * PACKET)
             norm = norm_ref[first + i : first + i + 1, :].astype(F32)
+            if live is not None:
+                norm = jnp.where(live, norm, NEVER)
             delta = delta_ref[first + i : first + i + 1, :].astype(F32)
             prob = jnp.exp(scores[:, lanes] - norm)
             if visible is not None:
@@ -86,7 +95,7 @@
     keys = block_of(lat_ref, b0).T
     k_pos = b0 * BLOCK + lax.broadcasted_iota(jnp.int32, (BLOCK, PACKET), 0)
     q_pos = SHARD - PACKET + lax.broadcasted_iota(jnp.int32, (BLOCK, PACKET), 1)
-    visit(keys, q_ref, rows_ref, norm_ref, delta_ref, k_pos <= q_pos, ds_ref, p_ref, total_ref)
+    visit(keys, q_ref, rows_ref, norm_ref, delta_ref, None, k_pos <= q_pos, ds_ref, p_ref, total_ref)
     pieces_out(total_ref, out_refs, low)
 
 
@@ -94,7 +103,8 @@
     ds_ref = rest[0]
     out_refs = rest[1 : 1 + low]
     p_ref, total_ref = rest[1 + low :]
-    visit(keys_ref[...], q_ref, grad_ref, norm_ref, delta_ref, None, ds_ref, p_ref, total_ref)
+    live = lax.axis_index("seq") > 0
+    visit(keys_ref[...], q_ref, grad_ref, norm_ref, delta_ref, live, None, ds_ref, p_ref, total_ref)
     pieces_out(total_ref, out_refs, low)
 
 
@@ -134,8 +144,11 @@
     out_ref[...] = (mine_ref[...] + got_ref[...].astype(F32)).astype(BF16)
 
 
-def call(kernel, name, ins, outs, scratch=(), smem=0, flops=0, transcendentals=0):
+def call(kernel, name, ins, outs, scratch=(), smem=0, flops=0, transcendentals=0, raw=False):
     specs = [pl.BlockSpec(memory_space=pltpu.SMEM if i < smem else pltpu.VMEM) for i in range(len(ins))]
+    if raw:
+        specs = [pl.BlockSpec(memory_space=pl.ANY) for _ in ins]
+        ins = [pltpu.with_memory_space_constraint(x, pltpu.HBM) for x in ins]
     size = sum(x.size * x.dtype.itemsize for x in ins)
     size += sum(functools.reduce(lambda a, b: a * b, s, jnp.dtype(d).itemsize) for s, d in outs)
     return pl.pallas_call(
@@ -167,14 +180,22 @@
 
     def route(d, back):
         pairs = []
-        for i in range(back, n_seq):
+        for i in range(n_seq):
             for j in range(n_head):
                 to = j // low * low + (j + d) % low
-                pairs.append((i * n_head + j, (i - back) * n_head + to))
+                pairs.append((i * n_head + j, (i - back) % n_seq * n_head + to))
         return pairs
 
-    (sent,) = call(send_block_kernel, "send_block", (plan, lat_t), [((BLOCK, width), BF16)], smem=1)
-    far_keys = lax.ppermute(sent, "seq", [(i, i + 1) for i in range(n_seq - 1)])
+    (sent,) = call(
+        send_block_kernel,
+        "send_block",
+        (plan, lat_t),
+        [((BLOCK, width), BF16)],
+        [pltpu.SMEM(plan.shape, plan.dtype), pltpu.VMEM(lat_t.shape, BF16), pltpu.SemaphoreType.DMA((2,))],
+        flops=visit_flops,
+        raw=True,
+    )
+    far_keys = lax.ppermute(sent, "seq", [(i, (i + 1) % n_seq) for i in range(n_seq)])
 
     scratch = [pltpu.VMEM((BLOCK, columns), BF16), pltpu.VMEM((BLOCK, width), F32)]
     grad_rows, own_ds, *own = call(

time: 44.5 us -> 40 us (0.90)
  the two profiles are of different devices: /device:TPU:5 before, /device:TPU:0 now
where the time goes in v1:
time: 40 us; the launch traced here: 39.8 us
  waiting for transfers between devices  17.2 us (43%)
  Pallas kernels  11.9 us (30%)
  starting transfers between devices  9.92 us (25%)
  between operations  0.71 us (2%)
    pallas_call x6, Pallas kernels, call(): pl.pallas_call(kernel, name=name, out_shape=[jax.ShapeDtypeStruct(s, d) f...  11.9 us
    ppermute x1, waiting for transfers between devices, local(): lax.ppermute(send, 'head', [(j, (j + low) % n_head) for j in range(n_head)])  8.89 us
    ppermute x2, waiting for transfers between devices, local(): lax.ppermute(far[d], ('seq', 'head'), route(d, 1))  5.42 us
    ppermute x2, starting transfers between devices, local(): lax.ppermute(far[d], ('seq', 'head'), route(d, 1))  3.65 us
    ppermute x1, starting transfers between devices, local(): lax.ppermute(own[d], ('seq', 'head'), route(d, 0))  3.1 us
    ppermute x1, waiting for transfers between devices, local(): lax.ppermute(sent, 'seq', [(i, (i + 1) % n_seq) for i in range(n_seq)])  2.89 us
    ppermute x1, starting transfers between devices, local(): lax.ppermute(send, 'head', [(j, (j + low) % n_head) for j in range(n_head)])  2.66 us
  transfers between devices with their start and end apart: 5, of which 4 were waited for; matrix products, arithmetic and copies ran while one was open for 0% of the time, Pallas kernels for 22%

profile of v1, /device:TPU:0, one launch (start us, length us, event | category | flops | bytes accessed | tf_op | source)
XLA Modules:
  0.0 39.8 jit_solution(5020010161529944164)
XLA Ops:
  0.6 0.0 copy-start
  0.6 0.0 copy-start.1
  0.7 0.0 copy-start.2
  0.7 0.0 copy-start.3
  0.7 0.0 copy-start.4
  0.7 0.0 copy-start.5
  0.7 1.5 %send_block.1 = bf16[384,576]{1,0:T(8,128)(2,1)S(1)} custom-call(s32[1,2]{1,0:T(1,128)} %plan_ref.5, bf16[576,768]{1,0:T(8,128)(2,1)} %bitcast.6), custom_call_target="tpu_custom_call" | custom-call | flops 1711276032 | bytes 1327112 | tf_op jit(solution)/shard_map/send_block/pallas_call | solution.py:154
  2.2 0.5 %collective-permute-start = (bf16[384,576]{1,0:T(8,128)(2,1)S(1)}, bf16[384,576]{1,0:T(8,128)(2,1)S(1)}, u32[]{:S(2)}, u32[]{:S(2)}) collective-permute-start(bf16[384,576]{1,0:T(8,128)(2,1)S(1)} %send_block.1), channel_id=1, source_target_pairs={{0,4},{4,8},{8,12},{12,16},{16,20},{20,24},{24,28},{28,0},{1,5},{5... | collective-permute-start | bytes 1327112 | tf_op jit(solution)/shard_map/ppermute | solution.py:198
  2.7 0.0 copy-done
  2.7 0.0 copy-done.1
  2.7 0.0 copy-done.2
  2.7 0.0 copy-done.3
  2.8 0.0 copy-done.4
  2.8 0.0 copy-done.5
  2.8 3.4 %own_visit.1 = (bf16[1024,512]{1,0:T(8,128)(2,1)S(1)}, bf16[384,1024]{1,0:T(8,128)(2,1)S(1)}, f32[192,576]{1,0:T(8,128)S(1)}, bf16[192,576]{1,0:T(8,128)(2,1)S(1)}) custom-call(s32[1,2]{1,0:T(1,128)S(1)} %copy-done.1, bf16[576,768]{1,0:T(8,128)(2,1)S(1)} %bitcast.7, bf16[8,576,128]{2,1,0:T(8,128)(2,1)S(1)} %bitcast.9, bf16[1024,512]{1,0:T(8,128)(2,1)S(1)} %bitcast.11, ...), custom_call_target="tpu_custom_call" | custom-call | flops 1711276032 | bytes 5615624 | tf_op jit(solution)/shard_map/own_visit/pallas_call | solution.py:154
  6.1 3.1 %collective-permute-start.1 = (bf16[192,576]{1,0:T(8,128)(2,1)S(1)}, bf16[192,576]{1,0:T(8,128)(2,1)S(1)}, u32[]{:S(2)}, u32[]{:S(2)}) collective-permute-start(bf16[192,576]{1,0:T(8,128)(2,1)S(1)} %get-tuple-element.15), channel_id=1, source_target_pairs={{0,1},{1,0},{2,3},{3,2},{4,5},{5,4},{6,7},{7,6},{8,9},{9,8},{10,11... | collective-permute-start | bytes 663560 | tf_op jit(solution)/shard_map/ppermute | solution.py:211
  9.2 2.9 %collective-permute-done.keys_ref.far_ref = bf16[384,576]{1,0:T(8,128)(2,1)S(1)} collective-permute-done((bf16[384,576]{1,0:T(8,128)(2,1)S(1)}, bf16[384,576]{1,0:T(8,128)(2,1)S(1)}, u32[]{:S(2)}, u32[]{:S(2)}) %collective-permute-start) | collective-permute-done | bytes 442400 | tf_op jit(solution)/shard_map/ppermute | solution.py:198
  12.1 2.6 %far_visit.1 = (bf16[384,1024]{1,0:T(8,128)(2,1)S(1)}, bf16[192,576]{1,0:T(8,128)(2,1)S(1)}, bf16[192,576]{1,0:T(8,128)(2,1)S(1)}) custom-call(bf16[384,576]{1,0:T(8,128)(2,1)S(1)} %collective-permute-done.keys_ref.far_ref, bf16[8,576,128]{2,1,0:T(8,128)(2,1)S(1)} %bitcast.10, bf16[1024,512]{1,0:T(8,128)(2,1)S(1)} %get-tuple-element.12.grad_ref, ...), custom_call_target="tpu_custom_call" | custom-call | flops 1711276032 | bytes 3903488 | tf_op jit(solution)/shard_map/far_visit/pallas_call | solution.py:154
  14.7 1.1 %collective-permute-start.2 = (bf16[192,576]{1,0:T(8,128)(2,1)S(1)}, bf16[192,576]{1,0:T(8,128)(2,1)S(1)}, u32[]{:S(2)}, u32[]{:S(2)}) collective-permute-start(bf16[192,576]{1,0:T(8,128)(2,1)S(1)} %get-tuple-element.16), channel_id=1, source_target_pairs={{0,29},{1,28},{2,31},{3,30},{4,1},{5,0},{6,3},{7,2},{8,5},{9,4},{1... | collective-permute-start | bytes 663560 | tf_op jit(solution)/shard_map/ppermute | solution.py:222
  15.8 2.6 %collective-permute-start.3 = (bf16[192,576]{1,0:T(8,128)(2,1)S(1)}, bf16[192,576]{1,0:T(8,128)(2,1)S(1)}, u32[]{:S(2)}, u32[]{:S(2)}) collective-permute-start(bf16[192,576]{1,0:T(8,128)(2,1)S(1)} %get-tuple-element.17), channel_id=1, source_target_pairs={{0,28},{1,29},{2,30},{3,31},{4,0},{5,1},{6,2},{7,3},{8,4},{9,5},{1... | collective-permute-start | bytes 663560 | tf_op jit(solution)/shard_map/ppermute | solution.py:222
  18.4 0.0 collective-permute-done.1.rest_1_
  18.4 3.8 %collective-permute-done.2.rest_2_ = bf16[192,576]{1,0:T(8,128)(2,1)S(1)} collective-permute-done((bf16[192,576]{1,0:T(8,128)(2,1)S(1)}, bf16[192,576]{1,0:T(8,128)(2,1)S(1)}, u32[]{:S(2)}, u32[]{:S(2)}) %collective-permute-start.2) | collective-permute-done | bytes 221216 | tf_op jit(solution)/shard_map/ppermute | solution.py:222
  22.1 1.7 %collective-permute-done.3.rest_3_ = bf16[192,576]{1,0:T(8,128)(2,1)S(1)} collective-permute-done((bf16[192,576]{1,0:T(8,128)(2,1)S(1)}, bf16[192,576]{1,0:T(8,128)(2,1)S(1)}, u32[]{:S(2)}, u32[]{:S(2)}) %collective-permute-start.3) | collective-permute-done | bytes 221216 | tf_op jit(solution)/shard_map/ppermute | solution.py:222
  23.8 0.7 %combine.1 = (bf16[192,576]{1,0:T(8,128)(2,1)S(1)}, f32[192,576]{1,0:T(8,128)S(1)}) custom-call(s32[1,2]{1,0:T(1,128)S(1)} %copy-done.1, f32[192,576]{1,0:T(8,128)S(1)} %get-tuple-element.14.rest_0_, bf16[192,576]{1,0:T(8,128)(2,1)S(1)} %collective-permute-done.1.rest_1_, bf16[192,576]{1,0:T(8,128)(2,1)S(1)} %collective-permute-done.2.rest_2_, ...), custom_call_target="tpu_custom_call" | custom-call | bytes 1769480 | tf_op jit(solution)/shard_map/combine/pallas_call | solution.py:154
  24.5 2.7 %collective-permute-start.4 = (bf16[192,576]{1,0:T(8,128)(2,1)S(1)}, bf16[192,576]{1,0:T(8,128)(2,1)S(1)}, u32[]{:S(2)}, u32[]{:S(2)}) collective-permute-start(bf16[192,576]{1,0:T(8,128)(2,1)S(1)} %get-tuple-element.19), channel_id=1, source_target_pairs={{0,2},{1,3},{2,0},{3,1},{4,6},{5,7},{6,4},{7,5},{8,10},{9,11},{10,... | collective-permute-start | bytes 663560 | tf_op jit(solution)/shard_map/ppermute | solution.py:239
  27.2 3.0 %query_grad.1 = bf16[8,576,128]{2,1,0:T(8,128)(2,1)} custom-call(s32[1,2]{1,0:T(1,128)S(1)} %copy-done.1, bf16[576,768]{1,0:T(8,128)(2,1)S(1)} %bitcast.8, bf16[384,576]{1,0:T(8,128)(2,1)S(1)} %collective-permute-done.keys_ref.far_ref, bf16[384,1024]{1,0:T(8,128)(2,1)S(1)} %get-tuple-element.11.own_ds_ref, bf16[384,1024]{1,0:T(8,128)(2,1)S(1)} %get-tuple-element.13.far_ds_ref), custom_call_target="tpu_custom_call" | custom-call | flops 905969664 | bytes 4079624 | tf_op jit(solution)/shard_map/query_grad/pallas_call | solution.py:154
  30.2 8.9 %collective-permute-done.4.got_ref = bf16[192,576]{1,0:T(8,128)(2,1)S(1)} collective-permute-done((bf16[192,576]{1,0:T(8,128)(2,1)S(1)}, bf16[192,576]{1,0:T(8,128)(2,1)S(1)}, u32[]{:S(2)}, u32[]{:S(2)}) %collective-permute-start.4) | collective-permute-done | bytes 221216 | tf_op jit(solution)/shard_map/ppermute | solution.py:239
  39.1 0.8 %last_sum.1 = bf16[192,576]{1,0:T(8,128)(2,1)} custom-call(f32[192,576]{1,0:T(8,128)S(1)} %get-tuple-element.18.mine_ref, bf16[192,576]{1,0:T(8,128)(2,1)S(1)} %collective-permute-done.4.got_ref), custom_call_target="tpu_custom_call" | custom-call | bytes 884736 | tf_op jit(solution)/shard_map/last_sum/pallas_call | solution.py:154
Async XLA Ops:
  0.6 2.1 %copy-start = (bf16[768,576]{0,1:T(8,128)(2,1)S(1)}, bf16[768,576]{0,1:T(8,128)(2,1)}, u32[]{:S(2)}) copy-start(bf16[768,576]{0,1:T(8,128)(2,1)} %param.8) | copy-start | bytes 2654212
  0.6 2.1 %copy-start.1 = (s32[1,2]{1,0:T(1,128)S(1)}, s32[1,2]{1,0:T(1,128)}, u32[]{:S(2)}) copy-start(s32[1,2]{1,0:T(1,128)} %plan_ref.5) | copy-start | bytes 28
  0.7 2.1 %copy-start.2 = (bf16[128,8,576]{0,2,1:T(8,128)(2,1)S(1)}, bf16[128,8,576]{0,2,1:T(8,128)(2,1)}, u32[]{:S(2)}) copy-start(bf16[128,8,576]{0,2,1:T(8,128)(2,1)} %param.6) | copy-start | bytes 3538948
  0.7 2.1 %copy-start.3 = (bf16[128,8,512]{2,1,0:T(8,128)(2,1)S(1)}, bf16[128,8,512]{2,1,0:T(8,128)(2,1)}, u32[]{:S(2)}) copy-start(bf16[128,8,512]{2,1,0:T(8,128)(2,1)} %param.7) | copy-start | bytes 3145732
  0.7 2.1 %copy-start.4 = (bf16[128,8]{0,1:T(8,128)(2,1)S(1)}, bf16[128,8]{0,1:T(8,128)(2,1)}, u32[]{:S(2)}) copy-start(bf16[128,8]{0,1:T(8,128)(2,1)} %param.9) | copy-start | bytes 6148
  0.7 2.1 %copy-start.5 = (bf16[128,8]{0,1:T(8,128)(2,1)S(1)}, bf16[128,8]{0,1:T(8,128)(2,1)}, u32[]{:S(2)}) copy-start(bf16[128,8]{0,1:T(8,128)(2,1)} %param.10) | copy-start | bytes 6148
  2.2 9.9 %collective-permute-start = (bf16[384,576]{1,0:T(8,128)(2,1)S(1)}, bf16[384,576]{1,0:T(8,128)(2,1)S(1)}, u32[]{:S(2)}, u32[]{:S(2)}) collective-permute-start(bf16[384,576]{1,0:T(8,128)(2,1)S(1)} %send_block.1), channel_id=1, source_target_pairs={{0,4},{4,8},{8,12},{12,16},{16,20},{20,24},{24,28},{28,0},{1,5},{5... | collective-permute-start | bytes 1327112 | tf_op jit(solution)/shard_map/ppermute | solution.py:198
  6.1 12.2 %collective-permute-start.1 = (bf16[192,576]{1,0:T(8,128)(2,1)S(1)}, bf16[192,576]{1,0:T(8,128)(2,1)S(1)}, u32[]{:S(2)}, u32[]{:S(2)}) collective-permute-start(bf16[192,576]{1,0:T(8,128)(2,1)S(1)} %get-tuple-element.15), channel_id=1, source_target_pairs={{0,1},{1,0},{2,3},{3,2},{4,5},{5,4},{6,7},{7,6},{8,9},{9,8},{10,11... | collective-permute-start | bytes 663560 | tf_op jit(solution)/shard_map/ppermute | solution.py:211
  14.7 7.4 %collective-permute-start.2 = (bf16[192,576]{1,0:T(8,128)(2,1)S(1)}, bf16[192,576]{1,0:T(8,128)(2,1)S(1)}, u32[]{:S(2)}, u32[]{:S(2)}) collective-permute-start(bf16[192,576]{1,0:T(8,128)(2,1)S(1)} %get-tuple-element.16), channel_id=1, source_target_pairs={{0,29},{1,28},{2,31},{3,30},{4,1},{5,0},{6,3},{7,2},{8,5},{9,4},{1... | collective-permute-start | bytes 663560 | tf_op jit(solution)/shard_map/ppermute | solution.py:222
  15.8 8.0 %collective-permute-start.3 = (bf16[192,576]{1,0:T(8,128)(2,1)S(1)}, bf16[192,576]{1,0:T(8,128)(2,1)S(1)}, u32[]{:S(2)}, u32[]{:S(2)}) collective-permute-start(bf16[192,576]{1,0:T(8,128)(2,1)S(1)} %get-tuple-element.17), channel_id=1, source_target_pairs={{0,28},{1,29},{2,30},{3,31},{4,0},{5,1},{6,2},{7,3},{8,4},{9,5},{1... | collective-permute-start | bytes 663560 | tf_op jit(solution)/shard_map/ppermute | solution.py:222
  24.5 14.5 %collective-permute-start.4 = (bf16[192,576]{1,0:T(8,128)(2,1)S(1)}, bf16[192,576]{1,0:T(8,128)(2,1)S(1)}, u32[]{:S(2)}, u32[]{:S(2)}) collective-permute-start(bf16[192,576]{1,0:T(8,128)(2,1)S(1)} %get-tuple-element.19), channel_id=1, source_target_pairs={{0,2},{1,3},{2,0},{3,1},{4,6},{5,7},{6,4},{7,5},{8,10},{9,11},{10,... | collective-permute-start | bytes 663560 | tf_op jit(solution)/shard_map/ppermute | solution.py:239

commit v2 on v1

--- a/solution.py
+++ b/solution.py
@@ -14,6 +14,7 @@
 WIDE = 256
 VMEM_LIMIT = 24 * 2**20
 NEVER = 1e30
+CHUNKS = 2
 
 F32 = jnp.float32
 BF16 = jnp.bfloat16
@@ -31,14 +32,22 @@
     return lat_ref[:, pl.ds(pl.multiple_of(block * BLOCK, 128), BLOCK)]
 
 
-def send_block_kernel(plan_hbm, lat_hbm, out_ref, plan_ref, lat_ref, sems):
+def send_block_kernel(low, plan_hbm, lat_hbm, *rest):
+    out_refs = rest[:CHUNKS]
+    plan_ref, lat_ref, sems = rest[CHUNKS:]
     plan_copy = pltpu.make_async_copy(plan_hbm, plan_ref, sems.at[0])
     lat_copy = pltpu.make_async_copy(lat_hbm, lat_ref, sems.at[1])
     plan_copy.start()
     lat_copy.start()
     plan_copy.wait()
     lat_copy.wait()
-    out_ref[...] = block_of(lat_ref, plan_ref[0, 1]).T
+    keys = block_of(lat_ref, plan_ref[0, 1]).T
+    rows = BLOCK // low
+    part = rows // CHUNKS
+    for c, out_ref in enumerate(out_refs):
+        for j in range(low):
+            start = j * rows + c * part
+            out_ref[j * part : (j + 1) * part, :] = keys[start : start + part, :]
 
 
 def heads_side_by_side(q_ref, first, count):
@@ -71,7 +80,7 @@
 
 
 def pieces_out(total_ref, out_refs, low):
-    rows = BLOCK // low
+    rows = total_ref.shape[0] // low
     r = lax.rem(lax.axis_index("head"), low)
     for d, out_ref in enumerate(out_refs):
         start = pl.multiple_of(lax.rem(r + d, low) * rows, 16)
@@ -79,9 +88,13 @@
 
 
 def own_kernel(low, plan_ref, lat_ref, q_ref, grad_ref, norm_ref, delta_ref, *rest):
-    rows_ref, ds_ref = rest[:2]
-    out_refs = rest[2 : 2 + low]
-    p_ref, total_ref = rest[2 + low :]
+    rows_ref, ds_ref, sel_ref = rest[:3]
+    out_refs = rest[3 : 3 + low]
+    p_ref, total_ref = rest[3 + low :]
+    t = lax.div(lax.axis_index("head"), low)
+    b1 = plan_ref[0, 1]
+    for i, hit in enumerate((plan_ref[0, 0] == t, plan_ref[0, 0] != t, b1 == t, b1 != t)):
+        sel_ref[i : i + 1, :] = jnp.broadcast_to(jnp.where(hit, 1.0, 0.0), (1, sel_ref.shape[1])).astype(F32)
     heads = q_ref.shape[0]
     group = WIDE // heads
     at = lax.broadcasted_iota(jnp.int32, (WIDE, WIDE), 0)
@@ -108,40 +121,44 @@
     pieces_out(total_ref, out_refs, low)
 
 
-def query_kernel(plan_ref, lat_ref, far_ref, own_ds_ref, far_ds_ref, out_ref):
+def query_kernel(plan_ref, lat_ref, own_ds_ref, *rest):
+    far_refs = rest[:CHUNKS]
+    far_ds_refs = rest[CHUNKS : 2 * CHUNKS]
+    out_ref = rest[-1]
     heads = out_ref.shape[0]
     per = WIDE // PACKET
     own = block_of(lat_ref, plan_ref[0, 0])
-    far = far_ref[...].T
+    fars = [ref[...].T for ref in far_refs]
     for first in range(0, heads, per):
         cols = slice(first * PACKET, (first + per) * PACKET)
-        total = dot(own, own_ds_ref[:, cols]) + dot(far, far_ds_ref[:, cols])
+        total = dot(own, own_ds_ref[:, cols])
+        for far, ds_ref in zip(fars, far_ds_refs):
+            total = total + dot(far, ds_ref[:, cols])
         for i in range(per):
             out_ref[first + i] = total[:, i * PACKET : (i + 1) * PACKET].astype(BF16)
 
 
-def combine_kernel(low, plan_ref, *rest):
+def combine_kernel(low, chunk, sel_ref, *rest):
     own_refs = rest[:low]
     far_refs = rest[low : 2 * low]
     send_ref, mine_ref = rest[2 * low :]
-    own = own_refs[0][...]
+    part = send_ref.shape[0]
+    here = slice(chunk * part, (chunk + 1) * part)
+    own = own_refs[0][here, :]
     for ref in own_refs[1:]:
-        own = own + ref[...].astype(F32)
+        own = own + ref[here, :].astype(F32)
     far = far_refs[0][...].astype(F32)
     for ref in far_refs[1:]:
         far = far + ref[...].astype(F32)
-    t = lax.div(lax.axis_index("head"), low)
-    b0, b1 = plan_ref[0, 0], plan_ref[0, 1]
-
-    def total(block):
-        return jnp.where(b0 == block, own, 0.0) + jnp.where(b1 == block, far, 0.0)
-
-    mine_ref[...] = total(t)
-    send_ref[...] = total(1 - t).astype(BF16)
-
-
-def last_kernel(mine_ref, got_ref, out_ref):
-    out_ref[...] = (mine_ref[...] + got_ref[...].astype(F32)).astype(BF16)
+    send_ref[...] = (own * sel_ref[1:2, :] + far * sel_ref[3:4, :]).astype(BF16)
+    mine_ref[...] = own * sel_ref[0:1, :] + far * sel_ref[2:3, :]
+
+
+def last_kernel(*refs):
+    mine_refs, got_refs, out_ref = refs[:CHUNKS], refs[CHUNKS : 2 * CHUNKS], refs[-1]
+    part = out_ref.shape[0] // CHUNKS
+    for c in range(CHUNKS):
+        out_ref[c * part : (c + 1) * part, :] = (mine_refs[c][...] + got_refs[c][...].astype(F32)).astype(BF16)
 
 
 def call(kernel, name, ins, outs, scratch=(), smem=0, flops=0, transcendentals=0, raw=False):
@@ -186,58 +203,67 @@
                 pairs.append((i * n_head + j, (i - back) % n_seq * n_head + to))
         return pairs
 
-    (sent,) = call(
-        send_block_kernel,
+    part = rows // CHUNKS
+    keys = BLOCK // CHUNKS
+
+    sent = call(
+        functools.partial(send_block_kernel, low),
         "send_block",
         (plan, lat_t),
-        [((BLOCK, width), BF16)],
+        [((keys, width), BF16)] * CHUNKS,
         [pltpu.SMEM(plan.shape, plan.dtype), pltpu.VMEM(lat_t.shape, BF16), pltpu.SemaphoreType.DMA((2,))],
         flops=visit_flops,
         raw=True,
     )
-    far_keys = lax.ppermute(sent, "seq", [(i, (i + 1) % n_seq) for i in range(n_seq)])
-
-    scratch = [pltpu.VMEM((BLOCK, columns), BF16), pltpu.VMEM((BLOCK, width), F32)]
-    grad_rows, own_ds, *own = call(
+    far_keys = [lax.ppermute(x, "seq", [(i, (i + 1) % n_seq) for i in range(n_seq)]) for x in sent]
+
+    grad_rows, own_ds, sel, *own = call(
         functools.partial(own_kernel, low),
         "own_visit",
         (plan, lat_t, q_t, grad, norm_t, delta_t),
-        [((columns, LAT), BF16), ((BLOCK, columns), BF16), ((rows, width), F32)] + [((rows, width), BF16)] * (low - 1),
-        scratch,
+        [((columns, LAT), BF16), ((BLOCK, columns), BF16), ((8, width), F32), ((rows, width), F32)]
+        + [((rows, width), BF16)] * (low - 1),
+        [pltpu.VMEM((BLOCK, columns), BF16), pltpu.VMEM((BLOCK, width), F32)],
         smem=1,
         flops=visit_flops,
         transcendentals=columns * BLOCK,
     )
     own_parts = [own[0]] + [lax.ppermute(own[d], ("seq", "head"), route(d, 0)) for d in range(1, low)]
 
-    far_ds, *far = call(
-        functools.partial(far_kernel, low),
-        "far_visit",
-        (far_keys, q_t, grad_rows, norm_t, delta_t),
-        [((BLOCK, columns), BF16)] + [((rows, width), BF16)] * low,
-        scratch,
-        flops=visit_flops,
-        transcendentals=columns * BLOCK,
-    )
-    far_parts = [lax.ppermute(far[d], ("seq", "head"), route(d, 1)) for d in reversed(range(low))]
+    far_ds, far_parts = [], []
+    for c in range(CHUNKS):
+        ds, *far = call(
+            functools.partial(far_kernel, low),
+            f"far_visit_{c}",
+            (far_keys[c], q_t, grad_rows, norm_t, delta_t),
+            [((keys, columns), BF16)] + [((part, width), BF16)] * low,
+            [pltpu.VMEM((keys, columns), BF16), pltpu.VMEM((keys, width), F32)],
+            flops=visit_flops // CHUNKS,
+            transcendentals=columns * keys,
+        )
+        far_ds.append(ds)
+        far_parts.append([lax.ppermute(far[d], ("seq", "head"), route(d, 1)) for d in reversed(range(low))])
+
+    mine, got = [], []
+    for c in range(CHUNKS):
+        send, kept = call(
+            functools.partial(combine_kernel, low, c),
+            f"combine_{c}",
+            (sel, *own_parts, *far_parts[c]),
+            [((part, width), BF16), ((part, width), F32)],
+        )
+        mine.append(kept)
+        got.append(lax.ppermute(send, "head", [(j, (j + low) % n_head) for j in range(n_head)]))
 
     (query_t,) = call(
         query_kernel,
         "query_grad",
-        (plan, lat_t, far_keys, own_ds, far_ds),
+        (plan, lat_t, own_ds, *far_keys, *far_ds),
         [((heads, width, packet), BF16)],
         smem=1,
         flops=4 * columns * BLOCK * width,
     )
-    send, mine = call(
-        functools.partial(combine_kernel, low),
-        "combine",
-        (plan, *own_parts, *far_parts),
-        [((rows, width), BF16), ((rows, width), F32)],
-        smem=1,
-    )
-    got = lax.ppermute(send, "head", [(j, (j + low) % n_head) for j in range(n_head)])
-    (latent_out,) = call(last_kernel, "last_sum", (mine, got), [((rows, width), BF16)])
+    (latent_out,) = call(last_kernel, "last_sum", (*mine, *got), [((rows, width), BF16)])
     return jnp.transpose(query_t, (2, 0, 1)), latent_out
 
 

time: 40 us -> 35.2 us (0.88)
  waiting for transfers between devices: 17.2 us -> 8.21 us
  starting transfers between devices: 9.92 us -> 14.3 us
    ppermute x2 -> x4, waiting for transfers between devices: 5.42 us -> 1.46 us  [local(): lax.ppermute(far[d], ('seq', 'head'), route(d, 1))]
    ppermute x1 -> x2, waiting for transfers between devices: 2.89 us -> 0.01 us  [local(): lax.ppermute(x, 'seq', [(i, (i + 1) % n_seq) for i in range(n_seq)])]
    ppermute x1 -> x2, starting transfers between devices: 0.5 us -> 3.11 us  [local(): lax.ppermute(x, 'seq', [(i, (i + 1) % n_seq) for i in range(n_seq)])]
    ppermute x1 -> x2, starting transfers between devices: 2.66 us -> 4.97 us  [local(): lax.ppermute(send, 'head', [(j, (j + low) % n_head) for j in range(n_head)])]
    ppermute x1 -> x2, waiting for transfers between devices: 8.89 us -> 6.75 us  [local(): lax.ppermute(send, 'head', [(j, (j + low) % n_head) for j in range(n_head)])]
    ppermute x1, starting transfers between devices: 3.1 us -> 1.65 us  [local(): lax.ppermute(own[d], ('seq', 'head'), route(d, 0))]
    ppermute x2 -> x4, starting transfers between devices: 3.65 us -> 4.56 us  [local(): lax.ppermute(far[d], ('seq', 'head'), route(d, 1))]
    pallas_call x6 -> x8, Pallas kernels: 11.9 us -> 11.8 us  [call(): pl.pallas_call(kernel, name=name, out_shape=[jax.ShapeDtypeStruct(s, d) f...]
  transfers between devices with their start and end apart: 5 -> 9, of which waited for: 4 -> 3; matrix products, arithmetic and copies ran while one was open for 0% -> 0% of each run, Pallas kernels for 22% -> 27%
where the time goes in v2:
time: 35.2 us; the launch traced here: 35.1 us
  starting transfers between devices  14.3 us (41%)
  Pallas kernels  11.8 us (34%)
  waiting for transfers between devices  8.21 us (23%)
  between operations  0.73 us (2%)
    pallas_call x8, Pallas kernels, call(): pl.pallas_call(kernel, name=name, out_shape=[jax.ShapeDtypeStruct(s, d) f...  11.8 us
    ppermute x2, waiting for transfers between devices, local(): lax.ppermute(send, 'head', [(j, (j + low) % n_head) for j in range(n_head)])  6.75 us
    ppermute x2, starting transfers between devices, local(): lax.ppermute(send, 'head', [(j, (j + low) % n_head) for j in range(n_head)])  4.97 us
    ppermute x4, starting transfers between devices, local(): lax.ppermute(far[d], ('seq', 'head'), route(d, 1))  4.56 us
    ppermute x2, starting transfers between devices, local(): lax.ppermute(x, 'seq', [(i, (i + 1) % n_seq) for i in range(n_seq)])  3.11 us
    ppermute x1, starting transfers between devices, local(): lax.ppermute(own[d], ('seq', 'head'), route(d, 0))  1.65 us
    ppermute x4, waiting for transfers between devices, local(): lax.ppermute(far[d], ('seq', 'head'), route(d, 1))  1.46 us
  transfers between devices with their start and end apart: 9, of which 3 were waited for; matrix products, arithmetic and copies ran while one was open for 0% of the time, Pallas kernels for 27%

profile of v2, /device:TPU:0, one launch (start us, length us, event | category | flops | bytes accessed | tf_op | source)
XLA Modules:
  0.0 35.1 jit_solution(11399864690368487374)
XLA Ops:
  0.6 0.0 copy-start
  0.6 0.0 copy-start.1
  0.7 0.0 copy-start.2
  0.7 0.0 copy-start.3
  0.7 0.0 copy-start.4
  0.7 0.0 copy-start.5
  0.7 1.5 %send_block.1 = (bf16[192,576]{1,0:T(8,128)(2,1)S(1)}, bf16[192,576]{1,0:T(8,128)(2,1)S(1)}) custom-call(s32[1,2]{1,0:T(1,128)} %plan_ref.3, bf16[576,768]{1,0:T(8,128)(2,1)} %bitcast.6), custom_call_target="tpu_custom_call" | custom-call | flops 1711276032 | bytes 1327112 | tf_op jit(solution)/shard_map/send_block/pallas_call | solution.py:171
  2.2 0.5 %collective-permute-start.1 = (bf16[192,576]{1,0:T(8,128)(2,1)S(1)}, bf16[192,576]{1,0:T(8,128)(2,1)S(1)}, u32[]{:S(2)}, u32[]{:S(2)}) collective-permute-start(bf16[192,576]{1,0:T(8,128)(2,1)S(1)} %get-tuple-element.21), channel_id=1, source_target_pairs={{0,4},{4,8},{8,12},{12,16},{16,20},{20,24},{24,28},{28,0},{1,5},{5... | collective-permute-start | bytes 663560 | tf_op jit(solution)/shard_map/ppermute | solution.py:218
  2.7 2.6 %collective-permute-start = (bf16[192,576]{1,0:T(8,128)(2,1)S(1)}, bf16[192,576]{1,0:T(8,128)(2,1)S(1)}, u32[]{:S(2)}, u32[]{:S(2)}) collective-permute-start(bf16[192,576]{1,0:T(8,128)(2,1)S(1)} %get-tuple-element.20), channel_id=1, source_target_pairs={{0,4},{4,8},{8,12},{12,16},{16,20},{20,24},{24,28},{28,0},{1,5},{5... | collective-permute-start | bytes 663560 | tf_op jit(solution)/shard_map/ppermute | solution.py:218
  5.3 0.0 copy-done
  5.3 0.0 copy-done.1
  5.3 0.0 copy-done.2
  5.3 0.0 copy-done.3
  5.3 0.0 copy-done.4
  5.4 0.0 copy-done.5
  5.4 3.4 %own_visit.1 = (bf16[1024,512]{1,0:T(8,128)(2,1)S(1)}, bf16[384,1024]{1,0:T(8,128)(2,1)S(1)}, f32[8,576]{1,0:T(8,128)S(1)}, f32[192,576]{1,0:T(8,128)S(1)}, bf16[192,576]{1,0:T(8,128)(2,1)S(1)}) custom-call(s32[1,2]{1,0:T(1,128)S(1)} %copy-done.1, bf16[576,768]{1,0:T(8,128)(2,1)S(1)} %bitcast.7, bf16[8,576,128]{2,1,0:T(8,128)(2,1)S(1)} %bitcast.9, ...), custom_call_target="tpu_custom_call" | custom-call | flops 1711276032 | bytes 5634056 | tf_op jit(solution)/shard_map/own_visit/pallas_call | solution.py:171
  8.8 1.7 %collective-permute-start.2 = (bf16[192,576]{1,0:T(8,128)(2,1)S(1)}, bf16[192,576]{1,0:T(8,128)(2,1)S(1)}, u32[]{:S(2)}, u32[]{:S(2)}) collective-permute-start(bf16[192,576]{1,0:T(8,128)(2,1)S(1)} %get-tuple-element.27), channel_id=1, source_target_pairs={{0,1},{1,0},{2,3},{3,2},{4,5},{5,4},{6,7},{7,6},{8,9},{9,8},{10,11... | collective-permute-start | bytes 663560 | tf_op jit(solution)/shard_map/ppermute | solution.py:231
  10.4 0.0 collective-permute-done.1.keys_ref.rest_1_
  10.4 1.5 %far_visit_1.1 = (bf16[192,1024]{1,0:T(8,128)(2,1)S(1)}, bf16[96,576]{1,0:T(8,128)(2,1)S(1)}, bf16[96,576]{1,0:T(8,128)(2,1)S(1)}) custom-call(bf16[192,576]{1,0:T(8,128)(2,1)S(1)} %collective-permute-done.1.keys_ref.rest_1_, bf16[8,576,128]{2,1,0:T(8,128)(2,1)S(1)} %bitcast.10, bf16[1024,512]{1,0:T(8,128)(2,1)S(1)} %get-tuple-element.22.grad_ref, ...), custom_call_target="tpu_custom_call" | custom-call | flops 855638016 | bytes 3067904 | tf_op jit(solution)/shard_map/far_visit_1/pallas_call | solution.py:171
  11.9 0.6 %collective-permute-start.5 = (bf16[96,576]{1,0:T(8,128)(2,1)S(1)}, bf16[96,576]{1,0:T(8,128)(2,1)S(1)}, u32[]{:S(2)}, u32[]{:S(2)}) collective-permute-start(bf16[96,576]{1,0:T(8,128)(2,1)S(1)} %get-tuple-element.31), channel_id=1, source_target_pairs={{0,29},{1,28},{2,31},{3,30},{4,1},{5,0},{6,3},{7,2},{8,5},{9,4},{1... | collective-permute-start | bytes 331784 | tf_op jit(solution)/shard_map/ppermute | solution.py:245
  12.5 2.1 %collective-permute-start.6 = (bf16[96,576]{1,0:T(8,128)(2,1)S(1)}, bf16[96,576]{1,0:T(8,128)(2,1)S(1)}, u32[]{:S(2)}, u32[]{:S(2)}) collective-permute-start(bf16[96,576]{1,0:T(8,128)(2,1)S(1)} %get-tuple-element.32), channel_id=1, source_target_pairs={{0,28},{1,29},{2,30},{3,31},{4,0},{5,1},{6,2},{7,3},{8,4},{9,5},{1... | collective-permute-start | bytes 331784 | tf_op jit(solution)/shard_map/ppermute | solution.py:245
  14.6 0.0 collective-permute-done.keys_ref.rest_0_
  14.6 1.5 %far_visit_0.1 = (bf16[192,1024]{1,0:T(8,128)(2,1)S(1)}, bf16[96,576]{1,0:T(8,128)(2,1)S(1)}, bf16[96,576]{1,0:T(8,128)(2,1)S(1)}) custom-call(bf16[192,576]{1,0:T(8,128)(2,1)S(1)} %collective-permute-done.keys_ref.rest_0_, bf16[8,576,128]{2,1,0:T(8,128)(2,1)S(1)} %bitcast.11, bf16[1024,512]{1,0:T(8,128)(2,1)S(1)} %get-tuple-element.22.grad_ref, ...), custom_call_target="tpu_custom_call" | custom-call | flops 855638016 | bytes 3067904 | tf_op jit(solution)/shard_map/far_visit_0/pallas_call | solution.py:171
  16.1 0.8 %collective-permute-start.3 = (bf16[96,576]{1,0:T(8,128)(2,1)S(1)}, bf16[96,576]{1,0:T(8,128)(2,1)S(1)}, u32[]{:S(2)}, u32[]{:S(2)}) collective-permute-start(bf16[96,576]{1,0:T(8,128)(2,1)S(1)} %get-tuple-element.28), channel_id=1, source_target_pairs={{0,29},{1,28},{2,31},{3,30},{4,1},{5,0},{6,3},{7,2},{8,5},{9,4},{1... | collective-permute-start | bytes 331784 | tf_op jit(solution)/shard_map/ppermute | solution.py:245
  16.9 1.1 %collective-permute-start.4 = (bf16[96,576]{1,0:T(8,128)(2,1)S(1)}, bf16[96,576]{1,0:T(8,128)(2,1)S(1)}, u32[]{:S(2)}, u32[]{:S(2)}) collective-permute-start(bf16[96,576]{1,0:T(8,128)(2,1)S(1)} %get-tuple-element.29), channel_id=1, source_target_pairs={{0,28},{1,29},{2,30},{3,31},{4,0},{5,1},{6,2},{7,3},{8,4},{9,5},{1... | collective-permute-start | bytes 331784 | tf_op jit(solution)/shard_map/ppermute | solution.py:245
  17.9 0.0 collective-permute-done.2.rest_1_
  17.9 1.5 %collective-permute-done.5.rest_2_ = bf16[96,576]{1,0:T(8,128)(2,1)S(1)} collective-permute-done((bf16[96,576]{1,0:T(8,128)(2,1)S(1)}, bf16[96,576]{1,0:T(8,128)(2,1)S(1)}, u32[]{:S(2)}, u32[]{:S(2)}) %collective-permute-start.5) | collective-permute-done | bytes 110624 | tf_op jit(solution)/shard_map/ppermute | solution.py:245
  19.4 0.0 collective-permute-done.6.rest_3_
  19.4 0.1 combine_1.1
  19.5 2.6 %collective-permute-start.8 = (bf16[96,576]{1,0:T(8,128)(2,1)S(1)}, bf16[96,576]{1,0:T(8,128)(2,1)S(1)}, u32[]{:S(2)}, u32[]{:S(2)}) collective-permute-start(bf16[96,576]{1,0:T(8,128)(2,1)S(1)} %get-tuple-element.35), channel_id=1, source_target_pairs={{0,2},{1,3},{2,0},{3,1},{4,6},{5,7},{6,4},{7,5},{8,10},{9,11},{10,... | collective-permute-start | bytes 331784 | tf_op jit(solution)/shard_map/ppermute | solution.py:256
  22.2 0.0 collective-permute-done.3.rest_2_
  22.2 0.0 collective-permute-done.4.rest_3_
  22.2 0.1 combine_0.1
  22.3 2.3 %collective-permute-start.7 = (bf16[96,576]{1,0:T(8,128)(2,1)S(1)}, bf16[96,576]{1,0:T(8,128)(2,1)S(1)}, u32[]{:S(2)}, u32[]{:S(2)}) collective-permute-start(bf16[96,576]{1,0:T(8,128)(2,1)S(1)} %get-tuple-element.34), channel_id=1, source_target_pairs={{0,2},{1,3},{2,0},{3,1},{4,6},{5,7},{6,4},{7,5},{8,10},{9,11},{10,... | collective-permute-start | bytes 331784 | tf_op jit(solution)/shard_map/ppermute | solution.py:256
  24.6 3.0 %query_grad.1 = bf16[8,576,128]{2,1,0:T(8,128)(2,1)} custom-call(s32[1,2]{1,0:T(1,128)S(1)} %copy-done.1, bf16[576,768]{1,0:T(8,128)(2,1)S(1)} %bitcast.8, bf16[384,1024]{1,0:T(8,128)(2,1)S(1)} %get-tuple-element.19.own_ds_ref, bf16[192,576]{1,0:T(8,128)(2,1)S(1)} %collective-permute-done.keys_ref.rest_0_, ...), custom_call_target="tpu_custom_call" | custom-call | flops 905969664 | bytes 4079624 | tf_op jit(solution)/shard_map/query_grad/pallas_call | solution.py:171
  27.6 4.1 %collective-permute-done.8.refs_3_ = bf16[96,576]{1,0:T(8,128)(2,1)S(1)} collective-permute-done((bf16[96,576]{1,0:T(8,128)(2,1)S(1)}, bf16[96,576]{1,0:T(8,128)(2,1)S(1)}, u32[]{:S(2)}, u32[]{:S(2)}) %collective-permute-start.8) | collective-permute-done | bytes 110624 | tf_op jit(solution)/shard_map/ppermute | solution.py:256
  31.7 2.6 %collective-permute-done.7.refs_2_ = bf16[96,576]{1,0:T(8,128)(2,1)S(1)} collective-permute-done((bf16[96,576]{1,0:T(8,128)(2,1)S(1)}, bf16[96,576]{1,0:T(8,128)(2,1)S(1)}, u32[]{:S(2)}, u32[]{:S(2)}) %collective-permute-start.7) | collective-permute-done | bytes 110624 | tf_op jit(solution)/shard_map/ppermute | solution.py:256
  34.3 0.8 %last_sum.1 = bf16[192,576]{1,0:T(8,128)(2,1)} custom-call(f32[96,576]{1,0:T(8,128)S(1)} %get-tuple-element.30.refs_0_, f32[96,576]{1,0:T(8,128)S(1)} %get-tuple-element.33.refs_1_, bf16[96,576]{1,0:T(8,128)(2,1)S(1)} %collective-permute-done.7.refs_2_, bf16[96,576]{1,0:T(8,128)(2,1)S(1)} %collective-permute-done.8.refs_3_), custom_call_target="tpu_custom_call" | custom-call | bytes 884736 | tf_op jit(solution)/shard_map/last_sum/pallas_call | solution.py:171
Async XLA Ops:
  0.6 4.7 %copy-start = (bf16[768,576]{0,1:T(8,128)(2,1)S(1)}, bf16[768,576]{0,1:T(8,128)(2,1)}, u32[]{:S(2)}) copy-start(bf16[768,576]{0,1:T(8,128)(2,1)} %param.8) | copy-start | bytes 2654212
  0.6 4.7 %copy-start.1 = (s32[1,2]{1,0:T(1,128)S(1)}, s32[1,2]{1,0:T(1,128)}, u32[]{:S(2)}) copy-start(s32[1,2]{1,0:T(1,128)} %plan_ref.3) | copy-start | bytes 28
  0.7 4.7 %copy-start.2 = (bf16[128,8,576]{0,2,1:T(8,128)(2,1)S(1)}, bf16[128,8,576]{0,2,1:T(8,128)(2,1)}, u32[]{:S(2)}) copy-start(bf16[128,8,576]{0,2,1:T(8,128)(2,1)} %param.6) | copy-start | bytes 3538948
  0.7 4.7 %copy-start.3 = (bf16[128,8,512]{2,1,0:T(8,128)(2,1)S(1)}, bf16[128,8,512]{2,1,0:T(8,128)(2,1)}, u32[]{:S(2)}) copy-start(bf16[128,8,512]{2,1,0:T(8,128)(2,1)} %param.7) | copy-start | bytes 3145732
  0.7 4.7 %copy-start.4 = (bf16[128,8]{0,1:T(8,128)(2,1)S(1)}, bf16[128,8]{0,1:T(8,128)(2,1)}, u32[]{:S(2)}) copy-start(bf16[128,8]{0,1:T(8,128)(2,1)} %param.9) | copy-start | bytes 6148
  0.7 4.7 %copy-start.5 = (bf16[128,8]{0,1:T(8,128)(2,1)S(1)}, bf16[128,8]{0,1:T(8,128)(2,1)}, u32[]{:S(2)}) copy-start(bf16[128,8]{0,1:T(8,128)(2,1)} %param.10) | copy-start | bytes 6148
  2.2 8.2 %collective-permute-start.1 = (bf16[192,576]{1,0:T(8,128)(2,1)S(1)}, bf16[192,576]{1,0:T(8,128)(2,1)S(1)}, u32[]{:S(2)}, u32[]{:S(2)}) collective-permute-start(bf16[192,576]{1,0:T(8,128)(2,1)S(1)} %get-tuple-element.21), channel_id=1, source_target_pairs={{0,4},{4,8},{8,12},{12,16},{16,20},{20,24},{24,28},{28,0},{1,5},{5... | collective-permute-start | bytes 663560 | tf_op jit(solution)/shard_map/ppermute | solution.py:218
  2.7 11.9 %collective-permute-start = (bf16[192,576]{1,0:T(8,128)(2,1)S(1)}, bf16[192,576]{1,0:T(8,128)(2,1)S(1)}, u32[]{:S(2)}, u32[]{:S(2)}) collective-permute-start(bf16[192,576]{1,0:T(8,128)(2,1)S(1)} %get-tuple-element.20), channel_id=1, source_target_pairs={{0,4},{4,8},{8,12},{12,16},{16,20},{20,24},{24,28},{28,0},{1,5},{5... | collective-permute-start | bytes 663560 | tf_op jit(solution)/shard_map/ppermute | solution.py:218
  8.8 9.2 %collective-permute-start.2 = (bf16[192,576]{1,0:T(8,128)(2,1)S(1)}, bf16[192,576]{1,0:T(8,128)(2,1)S(1)}, u32[]{:S(2)}, u32[]{:S(2)}) collective-permute-start(bf16[192,576]{1,0:T(8,128)(2,1)S(1)} %get-tuple-element.27), channel_id=1, source_target_pairs={{0,1},{1,0},{2,3},{3,2},{4,5},{5,4},{6,7},{7,6},{8,9},{9,8},{10,11... | collective-permute-start | bytes 663560 | tf_op jit(solution)/shard_map/ppermute | solution.py:231
  11.9 7.5 %collective-permute-start.5 = (bf16[96,576]{1,0:T(8,128)(2,1)S(1)}, bf16[96,576]{1,0:T(8,128)(2,1)S(1)}, u32[]{:S(2)}, u32[]{:S(2)}) collective-permute-start(bf16[96,576]{1,0:T(8,128)(2,1)S(1)} %get-tuple-element.31), channel_id=1, source_target_pairs={{0,29},{1,28},{2,31},{3,30},{4,1},{5,0},{6,3},{7,2},{8,5},{9,4},{1... | collective-permute-start | bytes 331784 | tf_op jit(solution)/shard_map/ppermute | solution.py:245
  12.5 6.9 %collective-permute-start.6 = (bf16[96,576]{1,0:T(8,128)(2,1)S(1)}, bf16[96,576]{1,0:T(8,128)(2,1)S(1)}, u32[]{:S(2)}, u32[]{:S(2)}) collective-permute-start(bf16[96,576]{1,0:T(8,128)(2,1)S(1)} %get-tuple-element.32), channel_id=1, source_target_pairs={{0,28},{1,29},{2,30},{3,31},{4,0},{5,1},{6,2},{7,3},{8,4},{9,5},{1... | collective-permute-start | bytes 331784 | tf_op jit(solution)/shard_map/ppermute | solution.py:245
  16.1 6.1 %collective-permute-start.3 = (bf16[96,576]{1,0:T(8,128)(2,1)S(1)}, bf16[96,576]{1,0:T(8,128)(2,1)S(1)}, u32[]{:S(2)}, u32[]{:S(2)}) collective-permute-start(bf16[96,576]{1,0:T(8,128)(2,1)S(1)} %get-tuple-element.28), channel_id=1, source_target_pairs={{0,29},{1,28},{2,31},{3,30},{4,1},{5,0},{6,3},{7,2},{8,5},{9,4},{1... | collective-permute-start | bytes 331784 | tf_op jit(solution)/shard_map/ppermute | solution.py:245
  16.9 5.3 %collective-permute-start.4 = (bf16[96,576]{1,0:T(8,128)(2,1)S(1)}, bf16[96,576]{1,0:T(8,128)(2,1)S(1)}, u32[]{:S(2)}, u32[]{:S(2)}) collective-permute-start(bf16[96,576]{1,0:T(8,128)(2,1)S(1)} %get-tuple-element.29), channel_id=1, source_target_pairs={{0,28},{1,29},{2,30},{3,31},{4,0},{5,1},{6,2},{7,3},{8,4},{9,5},{1... | collective-permute-start | bytes 331784 | tf_op jit(solution)/shard_map/ppermute | solution.py:245
  19.5 12.2 %collective-permute-start.8 = (bf16[96,576]{1,0:T(8,128)(2,1)S(1)}, bf16[96,576]{1,0:T(8,128)(2,1)S(1)}, u32[]{:S(2)}, u32[]{:S(2)}) collective-permute-start(bf16[96,576]{1,0:T(8,128)(2,1)S(1)} %get-tuple-element.35), channel_id=1, source_target_pairs={{0,2},{1,3},{2,0},{3,1},{4,6},{5,7},{6,4},{7,5},{8,10},{9,11},{10,... | collective-permute-start | bytes 331784 | tf_op jit(solution)/shard_map/ppermute | solution.py:256
  22.3 12.1 %collective-permute-start.7 = (bf16[96,576]{1,0:T(8,128)(2,1)S(1)}, bf16[96,576]{1,0:T(8,128)(2,1)S(1)}, u32[]{:S(2)}, u32[]{:S(2)}) collective-permute-start(bf16[96,576]{1,0:T(8,128)(2,1)S(1)} %get-tuple-element.34), channel_id=1, source_target_pairs={{0,2},{1,3},{2,0},{3,1},{4,6},{5,7},{6,4},{7,5},{8,10},{9,11},{10,... | collective-permute-start | bytes 331784 | tf_op jit(solution)/shard_map/ppermute | solution.py:256

commit v3 on v2

--- a/solution.py
+++ b/solution.py
@@ -15,6 +15,7 @@
 VMEM_LIMIT = 24 * 2**20
 NEVER = 1e30
 CHUNKS = 2
+COPIES = 6
 
 F32 = jnp.float32
 BF16 = jnp.bfloat16
@@ -35,12 +36,15 @@
 def send_block_kernel(low, plan_hbm, lat_hbm, *rest):
     out_refs = rest[:CHUNKS]
     plan_ref, lat_ref, sems = rest[CHUNKS:]
-    plan_copy = pltpu.make_async_copy(plan_hbm, plan_ref, sems.at[0])
-    lat_copy = pltpu.make_async_copy(lat_hbm, lat_ref, sems.at[1])
-    plan_copy.start()
-    lat_copy.start()
-    plan_copy.wait()
-    lat_copy.wait()
+    step = lat_ref.shape[0] // COPIES
+    copies = [pltpu.make_async_copy(plan_hbm, plan_ref, sems.at[COPIES])]
+    for i in range(COPIES):
+        here = pl.ds(i * step, step)
+        copies.append(pltpu.make_async_copy(lat_hbm.at[here], lat_ref.at[here], sems.at[i]))
+    for copy in copies:
+        copy.start()
+    for copy in copies:
+        copy.wait()
     keys = block_of(lat_ref, plan_ref[0, 1]).T
     rows = BLOCK // low
     part = rows // CHUNKS
@@ -79,22 +83,20 @@
     grad_out_ref[:, LAT:] = key_grad[:, LAT:]
 
 
-def pieces_out(total_ref, out_refs, low):
+def pieces_out(total_ref, low, offset, out_refs):
     rows = total_ref.shape[0] // low
     r = lax.rem(lax.axis_index("head"), low)
-    for d, out_ref in enumerate(out_refs):
-        start = pl.multiple_of(lax.rem(r + d, low) * rows, 16)
-        out_ref[...] = total_ref[pl.ds(start, rows), :].astype(out_ref.dtype)
-
-
-def own_kernel(low, plan_ref, lat_ref, q_ref, grad_ref, norm_ref, delta_ref, *rest):
-    rows_ref, ds_ref, sel_ref = rest[:3]
-    out_refs = rest[3 : 3 + low]
-    p_ref, total_ref = rest[3 + low :]
-    t = lax.div(lax.axis_index("head"), low)
-    b1 = plan_ref[0, 1]
-    for i, hit in enumerate((plan_ref[0, 0] == t, plan_ref[0, 0] != t, b1 == t, b1 != t)):
-        sel_ref[i : i + 1, :] = jnp.broadcast_to(jnp.where(hit, 1.0, 0.0), (1, sel_ref.shape[1])).astype(F32)
+    for d, out_ref in out_refs:
+        start = pl.multiple_of(lax.rem(r + d, low) * rows, 16) + offset
+        out_ref[...] = total_ref[pl.ds(start, out_ref.shape[0]), :].astype(out_ref.dtype)
+
+
+def own_kernel(low, plan_hbm, lat_ref, q_ref, grad_ref, norm_ref, delta_ref, *rest):
+    rows_ref, ds_ref, sel_ref, keep_ref = rest[:4]
+    out_refs = rest[4:-4]
+    plan_ref, p_ref, total_ref, sem = rest[-4:]
+    plan_copy = pltpu.make_async_copy(plan_hbm, plan_ref, sem)
+    plan_copy.start()
     heads = q_ref.shape[0]
     group = WIDE // heads
     at = lax.broadcasted_iota(jnp.int32, (WIDE, WIDE), 0)
@@ -104,21 +106,28 @@
         moved = dot(order, grad_ref[g * WIDE : (g + 1) * WIDE, :]).astype(BF16)
         for h in range(heads):
             rows_ref[h * PACKET + g * group : h * PACKET + (g + 1) * group, :] = moved[h * group : (h + 1) * group, :]
-    b0 = plan_ref[0, 0]
+    plan_copy.wait()
+    b0, b1 = plan_ref[0, 0], plan_ref[0, 1]
+    t = lax.div(lax.axis_index("head"), low)
+    for i, hit in enumerate((b0 == t, b0 != t, b1 == t, b1 != t)):
+        sel_ref[i : i + 1, :] = jnp.broadcast_to(jnp.where(hit, 1.0, 0.0), (1, sel_ref.shape[1])).astype(F32)
     keys = block_of(lat_ref, b0).T
     k_pos = b0 * BLOCK + lax.broadcasted_iota(jnp.int32, (BLOCK, PACKET), 0)
     q_pos = SHARD - PACKET + lax.broadcasted_iota(jnp.int32, (BLOCK, PACKET), 1)
     visit(keys, q_ref, rows_ref, norm_ref, delta_ref, None, k_pos <= q_pos, ds_ref, p_ref, total_ref)
-    pieces_out(total_ref, out_refs, low)
-
-
-def far_kernel(low, keys_ref, q_ref, grad_ref, norm_ref, delta_ref, *rest):
-    ds_ref = rest[0]
-    out_refs = rest[1 : 1 + low]
-    p_ref, total_ref = rest[1 + low :]
+    pieces_out(total_ref, low, 0, [(0, keep_ref)])
+    for i, out_ref in enumerate(out_refs):
+        part = out_ref.shape[0]
+        pieces_out(total_ref, low, i % CHUNKS * part, [(1 + i // CHUNKS, out_ref)])
+
+
+def far_kernel(low, held, keys_ref, q_ref, grad_ref, norm_ref, delta_ref, *rest):
+    ds_ref = rest[held]
+    out_refs = rest[held + 1 : held + 1 + low]
+    p_ref, total_ref = rest[-2:]
     live = lax.axis_index("seq") > 0
     visit(keys_ref[...], q_ref, grad_ref, norm_ref, delta_ref, live, None, ds_ref, p_ref, total_ref)
-    pieces_out(total_ref, out_refs, low)
+    pieces_out(total_ref, low, 0, list(enumerate(out_refs)))
 
 
 def query_kernel(plan_ref, lat_ref, own_ds_ref, *rest):
@@ -141,12 +150,12 @@
 def combine_kernel(low, chunk, sel_ref, *rest):
     own_refs = rest[:low]
     far_refs = rest[low : 2 * low]
-    send_ref, mine_ref = rest[2 * low :]
+    send_ref, mine_ref = rest[-2:]
     part = send_ref.shape[0]
     here = slice(chunk * part, (chunk + 1) * part)
     own = own_refs[0][here, :]
     for ref in own_refs[1:]:
-        own = own + ref[here, :].astype(F32)
+        own = own + ref[...].astype(F32)
     far = far_refs[0][...].astype(F32)
     for ref in far_refs[1:]:
         far = far + ref[...].astype(F32)
@@ -155,29 +164,35 @@
 
 
 def last_kernel(*refs):
-    mine_refs, got_refs, out_ref = refs[:CHUNKS], refs[CHUNKS : 2 * CHUNKS], refs[-1]
+    mine_refs, got_refs, out_ref = refs[:CHUNKS][::-1], refs[CHUNKS : 2 * CHUNKS][::-1], refs[-1]
     part = out_ref.shape[0] // CHUNKS
     for c in range(CHUNKS):
         out_ref[c * part : (c + 1) * part, :] = (mine_refs[c][...] + got_refs[c][...].astype(F32)).astype(BF16)
 
 
-def call(kernel, name, ins, outs, scratch=(), smem=0, flops=0, transcendentals=0, raw=False):
-    specs = [pl.BlockSpec(memory_space=pltpu.SMEM if i < smem else pltpu.VMEM) for i in range(len(ins))]
-    if raw:
-        specs = [pl.BlockSpec(memory_space=pl.ANY) for _ in ins]
-        ins = [pltpu.with_memory_space_constraint(x, pltpu.HBM) for x in ins]
+def call(kernel, name, ins, outs, scratch=(), smem=(), raw=(), passed=(), flops=0, transcendentals=0):
+    spaces = [pltpu.SMEM if i in smem else pltpu.VMEM for i in range(len(ins))]
+    ins = list(ins)
+    for i in raw:
+        spaces[i] = pl.ANY
+        ins[i] = pltpu.with_memory_space_constraint(ins[i], pltpu.HBM)
     size = sum(x.size * x.dtype.itemsize for x in ins)
     size += sum(functools.reduce(lambda a, b: a * b, s, jnp.dtype(d).itemsize) for s, d in outs)
+    out_spaces = [pltpu.VMEM] * len(outs) + [pl.ANY] * len(passed)
+    shapes = [jax.ShapeDtypeStruct(s, d) for s, d in outs]
+    shapes += [jax.ShapeDtypeStruct(x.shape, x.dtype) for x in passed]
+    aliases = {len(ins) + i: len(outs) + i for i in range(len(passed))}
     return pl.pallas_call(
         kernel,
         name=name,
-        out_shape=[jax.ShapeDtypeStruct(s, d) for s, d in outs],
-        in_specs=specs,
-        out_specs=[pl.BlockSpec(memory_space=pltpu.VMEM) for _ in outs],
+        out_shape=shapes,
+        in_specs=[pl.BlockSpec(memory_space=space) for space in spaces + [pl.ANY] * len(passed)],
+        out_specs=[pl.BlockSpec(memory_space=space) for space in out_spaces],
         scratch_shapes=scratch,
+        input_output_aliases=aliases,
         compiler_params=pltpu.CompilerParams(vmem_limit_bytes=VMEM_LIMIT),
         cost_estimate=pl.CostEstimate(flops=flops, bytes_accessed=size, transcendentals=transcendentals),
-    )(*ins)
+    )(*ins, *passed)
 
 
 def local(queries, out_grad, latents, log_norm, out_delta, plan):
@@ -211,59 +226,64 @@
         "send_block",
         (plan, lat_t),
         [((keys, width), BF16)] * CHUNKS,
-        [pltpu.SMEM(plan.shape, plan.dtype), pltpu.VMEM(lat_t.shape, BF16), pltpu.SemaphoreType.DMA((2,))],
+        [pltpu.SMEM(plan.shape, plan.dtype), pltpu.VMEM(lat_t.shape, BF16), pltpu.SemaphoreType.DMA((COPIES + 1,))],
         flops=visit_flops,
-        raw=True,
+        raw=(0, 1),
     )
     far_keys = [lax.ppermute(x, "seq", [(i, (i + 1) % n_seq) for i in range(n_seq)]) for x in sent]
 
-    grad_rows, own_ds, sel, *own = call(
+    grad_rows, own_ds, sel, keep, *own = call(
         functools.partial(own_kernel, low),
         "own_visit",
         (plan, lat_t, q_t, grad, norm_t, delta_t),
         [((columns, LAT), BF16), ((BLOCK, columns), BF16), ((8, width), F32), ((rows, width), F32)]
-        + [((rows, width), BF16)] * (low - 1),
-        [pltpu.VMEM((BLOCK, columns), BF16), pltpu.VMEM((BLOCK, width), F32)],
-        smem=1,
-        flops=visit_flops,
-        transcendentals=columns * BLOCK,
+        + [((part, width), BF16)] * (CHUNKS * (low - 1)),
+        [
+            pltpu.SMEM(plan.shape, plan.dtype),
+            pltpu.VMEM((BLOCK, columns), BF16),
+            pltpu.VMEM((BLOCK, width), F32),
+            pltpu.SemaphoreType.DMA,
+        ],
+        raw=(0,),
     )
-    own_parts = [own[0]] + [lax.ppermute(own[d], ("seq", "head"), route(d, 0)) for d in range(1, low)]
-
-    far_ds, far_parts = [], []
+
+    far_ds, own_parts, far_parts = [], [], []
     for c in range(CHUNKS):
+        parts = own[c::CHUNKS]
+        own_parts.append([keep] + [lax.ppermute(parts[d - 1], ("seq", "head"), route(d, 0)) for d in range(1, low)])
+        later = [i for i in range(len(own)) if i % CHUNKS > c]
         ds, *far = call(
-            functools.partial(far_kernel, low),
+            functools.partial(far_kernel, low, len(later)),
             f"far_visit_{c}",
             (far_keys[c], q_t, grad_rows, norm_t, delta_t),
             [((keys, columns), BF16)] + [((part, width), BF16)] * low,
             [pltpu.VMEM((keys, columns), BF16), pltpu.VMEM((keys, width), F32)],
-            flops=visit_flops // CHUNKS,
-            transcendentals=columns * keys,
+            passed=[own[i] for i in later],
         )
+        for i, x in zip(later, far[low:]):
+            own[i] = x
         far_ds.append(ds)
         far_parts.append([lax.ppermute(far[d], ("seq", "head"), route(d, 1)) for d in reversed(range(low))])
 
-    mine, got = [], []
-    for c in range(CHUNKS):
-        send, kept = call(
+    mine, got = [None] * CHUNKS, [None] * CHUNKS
+    for c in reversed(range(CHUNKS)):
+        send, mine[c] = call(
             functools.partial(combine_kernel, low, c),
             f"combine_{c}",
-            (sel, *own_parts, *far_parts[c]),
+            (sel, *own_parts[c], *far_parts[c]),
             [((part, width), BF16), ((part, width), F32)],
         )
-        mine.append(kept)
-        got.append(lax.ppermute(send, "head", [(j, (j + low) % n_head) for j in range(n_head)]))
+        got[c] = lax.ppermute(send, "head", [(j, (j + low) % n_head) for j in range(n_head)])
 
     (query_t,) = call(
         query_kernel,
         "query_grad",
         (plan, lat_t, own_ds, *far_keys, *far_ds),
         [((heads, width, packet), BF16)],
-        smem=1,
+        smem=(0,),
         flops=4 * columns * BLOCK * width,
     )
-    (latent_out,) = call(last_kernel, "last_sum", (*mine, *got), [((rows, width), BF16)])
+    (latent_out,) = call(last_kernel, "last_sum", (*mine[::-1], *got[::-1]), [((rows, width), BF16)])
     return jnp.transpose(query_t, (2, 0, 1)), latent_out
 
 

time: 35.2 us -> 34.2 us (0.972)
  waiting for transfers between devices: 8.21 us -> 5.22 us
  starting transfers between devices: 14.3 us -> 16.2 us
    ppermute x2, waiting for transfers between devices: 6.75 us -> 4.79 us  [local(): lax.ppermute(send, 'head', [(j, (j + low) % n_head) for j in range(n_head)])]
    ppermute x4, starting transfers between devices: 4.56 us -> 5.61 us  [local(): lax.ppermute(far[d], ('seq', 'head'), route(d, 1))]
    ppermute x4, waiting for transfers between devices: 1.46 us -> 0.42 us  [local(): lax.ppermute(far[d], ('seq', 'head'), route(d, 1))]
    ppermute x2, starting transfers between devices: 4.97 us -> 5.43 us  [local(): lax.ppermute(send, 'head', [(j, (j + low) % n_head) for j in range(n_head)])]
    ppermute x1 -> x2, starting transfers between devices: 1.65 us -> 2.1 us  [local(): lax.ppermute(parts[d - 1], ('seq', 'head'), route(d, 0))]
  transfers between devices with their start and end apart: 9 -> 10, of which waited for: 3 -> 4; matrix products, arithmetic and copies ran while one was open for 0% -> 0% of each run, Pallas kernels for 27% -> 28%
where the time goes in v3:
time: 34.2 us; the launch traced here: 34 us
  starting transfers between devices  16.2 us (47%)
  Pallas kernels  11.8 us (35%)
  waiting for transfers between devices  5.22 us (15%)
  between operations  0.73 us (2%)
    pallas_call x8, Pallas kernels, call(): pl.pallas_call(kernel, name=name, out_shape=shapes, in_specs=[pl.BlockSpe...  11.8 us
    ppermute x4, starting transfers between devices, local(): lax.ppermute(far[d], ('seq', 'head'), route(d, 1))  5.61 us
    ppermute x2, starting transfers between devices, local(): lax.ppermute(send, 'head', [(j, (j + low) % n_head) for j in range(n_head)])  5.43 us
    ppermute x2, waiting for transfers between devices, local(): lax.ppermute(send, 'head', [(j, (j + low) % n_head) for j in range(n_head)])  4.79 us
    ppermute x2, starting transfers between devices, local(): lax.ppermute(x, 'seq', [(i, (i + 1) % n_seq) for i in range(n_seq)])  3.11 us
    ppermute x2, starting transfers between devices, local(): lax.ppermute(parts[d - 1], ('seq', 'head'), route(d, 0))  2.1 us
  transfers between devices with their start and end apart: 10, of which 4 were waited for; matrix products, arithmetic and copies ran while one was open for 0% of the time, Pallas kernels for 28%

profile of v3, /device:TPU:0, one launch (start us, length us, event | category | flops | bytes accessed | tf_op | source)
XLA Modules:
  0.0 34.0 jit_solution(17994078793941926512)
XLA Ops:
  0.6 0.0 copy-start
  0.6 0.0 copy-start.1
  0.7 0.0 copy-start.2
  0.7 0.0 copy-start.3
  0.7 0.0 copy-start.4
  0.7 1.6 %send_block.1 = (bf16[192,576]{1,0:T(8,128)(2,1)S(1)}, bf16[192,576]{1,0:T(8,128)(2,1)S(1)}) custom-call(s32[1,2]{1,0:T(1,128)} %plan_ref.1, bf16[576,768]{1,0:T(8,128)(2,1)} %bitcast.9), custom_call_target="tpu_custom_call" | custom-call | flops 1711276032 | bytes 1327112 | tf_op jit(solution)/shard_map/send_block/pallas_call | solution.py:185
  2.3 0.5 %collective-permute-start = (bf16[192,576]{1,0:T(8,128)(2,1)S(1)}, bf16[192,576]{1,0:T(8,128)(2,1)S(1)}, u32[]{:S(2)}, u32[]{:S(2)}) collective-permute-start(bf16[192,576]{1,0:T(8,128)(2,1)S(1)} %get-tuple-element.22), channel_id=1, source_target_pairs={{0,4},{4,8},{8,12},{12,16},{16,20},{20,24},{24,28},{28,0},{1,5},{5... | collective-permute-start | bytes 663560 | tf_op jit(solution)/shard_map/ppermute | solution.py:233
  2.8 2.6 %collective-permute-start.1 = (bf16[192,576]{1,0:T(8,128)(2,1)S(1)}, bf16[192,576]{1,0:T(8,128)(2,1)S(1)}, u32[]{:S(2)}, u32[]{:S(2)}) collective-permute-start(bf16[192,576]{1,0:T(8,128)(2,1)S(1)} %get-tuple-element.23), channel_id=1, source_target_pairs={{0,4},{4,8},{8,12},{12,16},{16,20},{20,24},{24,28},{28,0},{1,5},{5... | collective-permute-start | bytes 663560 | tf_op jit(solution)/shard_map/ppermute | solution.py:233
  5.4 0.0 copy-done
  5.4 0.0 copy-done.1
  5.4 0.0 copy-done.2
  5.4 0.0 copy-done.3
  5.5 0.0 copy-done.4
  5.5 3.3 %own_visit.1 = (bf16[1024,512]{1,0:T(8,128)(2,1)S(1)}, bf16[384,1024]{1,0:T(8,128)(2,1)S(1)}, f32[8,576]{1,0:T(8,128)S(1)}, f32[192,576]{1,0:T(8,128)S(1)}, bf16...) custom-call(s32[1,2]{1,0:T(1,128)} %plan_ref.1, bf16[576,768]{1,0:T(8,128)(2,1)S(1)} %bitcast.10, ...), custom_call_target="tpu_custom_call" | custom-call | bytes 5634056 | tf_op jit(solution)/shard_map/own_visit/pallas_call | solution.py:185
  8.8 1.6 %collective-permute-start.5 = (bf16[96,576]{1,0:T(8,128)(2,1)S(1)}, bf16[96,576]{1,0:T(8,128)(2,1)S(1)}, u32[]{:S(2)}, u32[]{:S(2)}) collective-permute-start(bf16[96,576]{1,0:T(8,128)(2,1)S(1)} %get-tuple-element.34), channel_id=1, source_target_pairs={{0,1},{1,0},{2,3},{3,2},{4,5},{5,4},{6,7},{7,6},{8,9},{9,8},{10,11... | collective-permute-start | bytes 331784 | tf_op jit(solution)/shard_map/ppermute | solution.py:253
  10.4 0.0 collective-permute-done.keys_ref.rest_0_
  10.4 1.5 %far_visit_0.1 = (bf16[192,1024]{1,0:T(8,128)(2,1)S(1)}, bf16[96,576]{1,0:T(8,128)(2,1)S(1)}, bf16[96,576]{1,0:T(8,128)(2,1)S(1)}, bf16[96,576]{1,0:T(8,128)(2,1)S(1)}) custom-call(bf16[192,576]{1,0:T(8,128)(2,1)S(1)} %collective-permute-done.keys_ref.rest_0_, bf16[8,576,128]{2,1,0:T(8,128)(2,1)S(1)} %bitcast.7, ...), custom_call_target="tpu_custom_call", output_to_operand_aliasing={{3}: (5, {})} | custom-call | bytes 3067904 | tf_op jit(solution)/shard_map/far_visit_0/pallas_call | solution.py:185
  11.9 0.6 %collective-permute-start.6 = (bf16[96,576]{1,0:T(8,128)(2,1)S(1)}, bf16[96,576]{1,0:T(8,128)(2,1)S(1)}, u32[]{:S(2)}, u32[]{:S(2)}) collective-permute-start(bf16[96,576]{1,0:T(8,128)(2,1)S(1)} %get-tuple-element.35), channel_id=1, source_target_pairs={{0,29},{1,28},{2,31},{3,30},{4,1},{5,0},{6,3},{7,2},{8,5},{9,4},{1... | collective-permute-start | bytes 331784 | tf_op jit(solution)/shard_map/ppermute | solution.py:266
  12.5 2.2 %collective-permute-start.7 = (bf16[96,576]{1,0:T(8,128)(2,1)S(1)}, bf16[96,576]{1,0:T(8,128)(2,1)S(1)}, u32[]{:S(2)}, u32[]{:S(2)}) collective-permute-start(bf16[96,576]{1,0:T(8,128)(2,1)S(1)} %get-tuple-element.36), channel_id=1, source_target_pairs={{0,28},{1,29},{2,30},{3,31},{4,0},{5,1},{6,2},{7,3},{8,4},{9,5},{1... | collective-permute-start | bytes 331784 | tf_op jit(solution)/shard_map/ppermute | solution.py:266
  14.7 0.4 %collective-permute-start.2 = (bf16[96,576]{1,0:T(8,128)(2,1)S(1)}, bf16[96,576]{1,0:T(8,128)(2,1)S(1)}, u32[]{:S(2)}, u32[]{:S(2)}) collective-permute-start(bf16[96,576]{1,0:T(8,128)(2,1)S(1)} %get-tuple-element.30), channel_id=1, source_target_pairs={{0,1},{1,0},{2,3},{3,2},{4,5},{5,4},{6,7},{7,6},{8,9},{9,8},{10,11... | collective-permute-start | bytes 331784 | tf_op jit(solution)/shard_map/ppermute | solution.py:253
  15.2 0.0 collective-permute-done.1.keys_ref.rest_1_
  15.2 1.5 %far_visit_1.1 = (bf16[192,1024]{1,0:T(8,128)(2,1)S(1)}, bf16[96,576]{1,0:T(8,128)(2,1)S(1)}, bf16[96,576]{1,0:T(8,128)(2,1)S(1)}) custom-call(bf16[192,576]{1,0:T(8,128)(2,1)S(1)} %collective-permute-done.1.keys_ref.rest_1_, bf16[8,576,128]{2,1,0:T(8,128)(2,1)S(1)} %bitcast.8, bf16[1024,512]{1,0:T(8,128)(2,1)S(1)} %get-tuple-element.24.grad_ref, ...), custom_call_target="tpu_custom_call" | custom-call | bytes 3067904 | tf_op jit(solution)/shard_map/far_visit_1/pallas_call | solution.py:185
  16.6 0.0 copy-start.5
  16.6 0.8 %collective-permute-start.3 = (bf16[96,576]{1,0:T(8,128)(2,1)S(1)}, bf16[96,576]{1,0:T(8,128)(2,1)S(1)}, u32[]{:S(2)}, u32[]{:S(2)}) collective-permute-start(bf16[96,576]{1,0:T(8,128)(2,1)S(1)} %get-tuple-element.31), channel_id=1, source_target_pairs={{0,29},{1,28},{2,31},{3,30},{4,1},{5,0},{6,3},{7,2},{8,5},{9,4},{1... | collective-permute-start | bytes 331784 | tf_op jit(solution)/shard_map/ppermute | solution.py:266
  17.4 0.0 collective-permute-done.5.rest_1_
  17.4 2.0 %collective-permute-start.4 = (bf16[96,576]{1,0:T(8,128)(2,1)S(1)}, bf16[96,576]{1,0:T(8,128)(2,1)S(1)}, u32[]{:S(2)}, u32[]{:S(2)}) collective-permute-start(bf16[96,576]{1,0:T(8,128)(2,1)S(1)} %get-tuple-element.32), channel_id=1, source_target_pairs={{0,28},{1,29},{2,30},{3,31},{4,0},{5,1},{6,2},{7,3},{8,4},{9,5},{1... | collective-permute-start | bytes 331784 | tf_op jit(solution)/shard_map/ppermute | solution.py:266
  19.4 0.0 collective-permute-done.6.rest_2_
  19.4 0.0 collective-permute-done.7.rest_3_
  19.4 0.1 combine_0.1
  19.6 2.7 %collective-permute-start.9 = (bf16[96,576]{1,0:T(8,128)(2,1)S(1)}, bf16[96,576]{1,0:T(8,128)(2,1)S(1)}, u32[]{:S(2)}, u32[]{:S(2)}) collective-permute-start(bf16[96,576]{1,0:T(8,128)(2,1)S(1)} %get-tuple-element.39), channel_id=1, source_target_pairs={{0,2},{1,3},{2,0},{3,1},{4,6},{5,7},{6,4},{7,5},{8,10},{9,11},{10,... | collective-permute-start | bytes 331784 | tf_op jit(solution)/shard_map/ppermute | solution.py:276
  22.2 0.0 collective-permute-done.2.rest_1_
  22.2 0.2 collective-permute-done.3.rest_2_
  22.4 0.2 collective-permute-done.4.rest_3_
  22.6 0.1 combine_1.1
  22.7 2.8 %collective-permute-start.8 = (bf16[96,576]{1,0:T(8,128)(2,1)S(1)}, bf16[96,576]{1,0:T(8,128)(2,1)S(1)}, u32[]{:S(2)}, u32[]{:S(2)}) collective-permute-start(bf16[96,576]{1,0:T(8,128)(2,1)S(1)} %get-tuple-element.38), channel_id=1, source_target_pairs={{0,2},{1,3},{2,0},{3,1},{4,6},{5,7},{6,4},{7,5},{8,10},{9,11},{10,... | collective-permute-start | bytes 331784 | tf_op jit(solution)/shard_map/ppermute | solution.py:276
  25.5 0.0 copy-done.5
  25.5 3.0 %query_grad.1 = bf16[8,576,128]{2,1,0:T(8,128)(2,1)} custom-call(s32[1,2]{1,0:T(1,128)S(1)} %copy-done.5, bf16[576,768]{1,0:T(8,128)(2,1)S(1)} %bitcast.11, bf16[384,1024]{1,0:T(8,128)(2,1)S(1)} %get-tuple-element.21.own_ds_ref, bf16[192,576]{1,0:T(8,128)(2,1)S(1)} %collective-permute-done.keys_ref.rest_0_, ...), custom_call_target="tpu_custom_call" | custom-call | flops 905969664 | bytes 4079624 | tf_op jit(solution)/shard_map/query_grad/pallas_call | solution.py:185
  28.5 2.5 %collective-permute-done.9.refs_3_ = bf16[96,576]{1,0:T(8,128)(2,1)S(1)} collective-permute-done((bf16[96,576]{1,0:T(8,128)(2,1)S(1)}, bf16[96,576]{1,0:T(8,128)(2,1)S(1)}, u32[]{:S(2)}, u32[]{:S(2)}) %collective-permute-start.9) | collective-permute-done | bytes 110624 | tf_op jit(solution)/shard_map/ppermute | solution.py:276
  31.0 2.3 %collective-permute-done.8.refs_2_ = bf16[96,576]{1,0:T(8,128)(2,1)S(1)} collective-permute-done((bf16[96,576]{1,0:T(8,128)(2,1)S(1)}, bf16[96,576]{1,0:T(8,128)(2,1)S(1)}, u32[]{:S(2)}, u32[]{:S(2)}) %collective-permute-start.8) | collective-permute-done | bytes 110624 | tf_op jit(solution)/shard_map/ppermute | solution.py:276
  33.3 0.7 %last_sum.1 = bf16[192,576]{1,0:T(8,128)(2,1)} custom-call(f32[96,576]{1,0:T(8,128)S(1)} %get-tuple-element.33.refs_0_, f32[96,576]{1,0:T(8,128)S(1)} %get-tuple-element.37.refs_1_, bf16[96,576]{1,0:T(8,128)(2,1)S(1)} %collective-permute-done.8.refs_2_, bf16[96,576]{1,0:T(8,128)(2,1)S(1)} %collective-permute-done.9.refs_3_), custom_call_target="tpu_custom_call" | custom-call | bytes 884736 | tf_op jit(solution)/shard_map/last_sum/pallas_call | solution.py:185
Async XLA Ops:
  0.6 4.8 %copy-start = (bf16[128,8,576]{0,2,1:T(8,128)(2,1)S(1)}, bf16[128,8,576]{0,2,1:T(8,128)(2,1)}, u32[]{:S(2)}) copy-start(bf16[128,8,576]{0,2,1:T(8,128)(2,1)} %param.6) | copy-start | bytes 3538948
  0.6 4.8 %copy-start.1 = (bf16[768,576]{0,1:T(8,128)(2,1)S(1)}, bf16[768,576]{0,1:T(8,128)(2,1)}, u32[]{:S(2)}) copy-start(bf16[768,576]{0,1:T(8,128)(2,1)} %param.8) | copy-start | bytes 2654212
  0.7 4.8 %copy-start.2 = (bf16[128,8,512]{2,1,0:T(8,128)(2,1)S(1)}, bf16[128,8,512]{2,1,0:T(8,128)(2,1)}, u32[]{:S(2)}) copy-start(bf16[128,8,512]{2,1,0:T(8,128)(2,1)} %param.7) | copy-start | bytes 3145732
  0.7 4.8 %copy-start.3 = (bf16[128,8]{0,1:T(8,128)(2,1)S(1)}, bf16[128,8]{0,1:T(8,128)(2,1)}, u32[]{:S(2)}) copy-start(bf16[128,8]{0,1:T(8,128)(2,1)} %param.9) | copy-start | bytes 6148
  0.7 4.8 %copy-start.4 = (bf16[128,8]{0,1:T(8,128)(2,1)S(1)}, bf16[128,8]{0,1:T(8,128)(2,1)}, u32[]{:S(2)}) copy-start(bf16[128,8]{0,1:T(8,128)(2,1)} %param.10) | copy-start | bytes 6148
  2.3 8.1 %collective-permute-start = (bf16[192,576]{1,0:T(8,128)(2,1)S(1)}, bf16[192,576]{1,0:T(8,128)(2,1)S(1)}, u32[]{:S(2)}, u32[]{:S(2)}) collective-permute-start(bf16[192,576]{1,0:T(8,128)(2,1)S(1)} %get-tuple-element.22), channel_id=1, source_target_pairs={{0,4},{4,8},{8,12},{12,16},{16,20},{20,24},{24,28},{28,0},{1,5},{5... | collective-permute-start | bytes 663560 | tf_op jit(solution)/shard_map/ppermute | solution.py:233
  2.8 12.3 %collective-permute-start.1 = (bf16[192,576]{1,0:T(8,128)(2,1)S(1)}, bf16[192,576]{1,0:T(8,128)(2,1)S(1)}, u32[]{:S(2)}, u32[]{:S(2)}) collective-permute-start(bf16[192,576]{1,0:T(8,128)(2,1)S(1)} %get-tuple-element.23), channel_id=1, source_target_pairs={{0,4},{4,8},{8,12},{12,16},{16,20},{20,24},{24,28},{28,0},{1,5},{5... | collective-permute-start | bytes 663560 | tf_op jit(solution)/shard_map/ppermute | solution.py:233
  8.8 8.7 %collective-permute-start.5 = (bf16[96,576]{1,0:T(8,128)(2,1)S(1)}, bf16[96,576]{1,0:T(8,128)(2,1)S(1)}, u32[]{:S(2)}, u32[]{:S(2)}) collective-permute-start(bf16[96,576]{1,0:T(8,128)(2,1)S(1)} %get-tuple-element.34), channel_id=1, source_target_pairs={{0,1},{1,0},{2,3},{3,2},{4,5},{5,4},{6,7},{7,6},{8,9},{9,8},{10,11... | collective-permute-start | bytes 331784 | tf_op jit(solution)/shard_map/ppermute | solution.py:253
  11.9 7.5 %collective-permute-start.6 = (bf16[96,576]{1,0:T(8,128)(2,1)S(1)}, bf16[96,576]{1,0:T(8,128)(2,1)S(1)}, u32[]{:S(2)}, u32[]{:S(2)}) collective-permute-start(bf16[96,576]{1,0:T(8,128)(2,1)S(1)} %get-tuple-element.35), channel_id=1, source_target_pairs={{0,29},{1,28},{2,31},{3,30},{4,1},{5,0},{6,3},{7,2},{8,5},{9,4},{1... | collective-permute-start | bytes 331784 | tf_op jit(solution)/shard_map/ppermute | solution.py:266
  12.5 6.9 %collective-permute-start.7 = (bf16[96,576]{1,0:T(8,128)(2,1)S(1)}, bf16[96,576]{1,0:T(8,128)(2,1)S(1)}, u32[]{:S(2)}, u32[]{:S(2)}) collective-permute-start(bf16[96,576]{1,0:T(8,128)(2,1)S(1)} %get-tuple-element.36), channel_id=1, source_target_pairs={{0,28},{1,29},{2,30},{3,31},{4,0},{5,1},{6,2},{7,3},{8,4},{9,5},{1... | collective-permute-start | bytes 331784 | tf_op jit(solution)/shard_map/ppermute | solution.py:266
  14.7 7.5 %collective-permute-start.2 = (bf16[96,576]{1,0:T(8,128)(2,1)S(1)}, bf16[96,576]{1,0:T(8,128)(2,1)S(1)}, u32[]{:S(2)}, u32[]{:S(2)}) collective-permute-start(bf16[96,576]{1,0:T(8,128)(2,1)S(1)} %get-tuple-element.30), channel_id=1, source_target_pairs={{0,1},{1,0},{2,3},{3,2},{4,5},{5,4},{6,7},{7,6},{8,9},{9,8},{10,11... | collective-permute-start | bytes 331784 | tf_op jit(solution)/shard_map/ppermute | solution.py:253
  16.6 8.9 %copy-start.5 = (s32[1,2]{1,0:T(1,128)S(1)}, s32[1,2]{1,0:T(1,128)}, u32[]{:S(2)}) copy-start(s32[1,2]{1,0:T(1,128)} %plan_ref.1) | copy-start | bytes 28
  16.6 5.7 %collective-permute-start.3 = (bf16[96,576]{1,0:T(8,128)(2,1)S(1)}, bf16[96,576]{1,0:T(8,128)(2,1)S(1)}, u32[]{:S(2)}, u32[]{:S(2)}) collective-permute-start(bf16[96,576]{1,0:T(8,128)(2,1)S(1)} %get-tuple-element.31), channel_id=1, source_target_pairs={{0,29},{1,28},{2,31},{3,30},{4,1},{5,0},{6,3},{7,2},{8,5},{9,4},{1... | collective-permute-start | bytes 331784 | tf_op jit(solution)/shard_map/ppermute | solution.py:266
  17.4 5.2 %collective-permute-start.4 = (bf16[96,576]{1,0:T(8,128)(2,1)S(1)}, bf16[96,576]{1,0:T(8,128)(2,1)S(1)}, u32[]{:S(2)}, u32[]{:S(2)}) collective-permute-start(bf16[96,576]{1,0:T(8,128)(2,1)S(1)} %get-tuple-element.32), channel_id=1, source_target_pairs={{0,28},{1,29},{2,30},{3,31},{4,0},{5,1},{6,2},{7,3},{8,4},{9,5},{1... | collective-permute-start | bytes 331784 | tf_op jit(solution)/shard_map/ppermute | solution.py:266
  19.6 11.5 %collective-permute-start.9 = (bf16[96,576]{1,0:T(8,128)(2,1)S(1)}, bf16[96,576]{1,0:T(8,128)(2,1)S(1)}, u32[]{:S(2)}, u32[]{:S(2)}) collective-permute-start(bf16[96,576]{1,0:T(8,128)(2,1)S(1)} %get-tuple-element.39), channel_id=1, source_target_pairs={{0,2},{1,3},{2,0},{3,1},{4,6},{5,7},{6,4},{7,5},{8,10},{9,11},{10,... | collective-permute-start | bytes 331784 | tf_op jit(solution)/shard_map/ppermute | solution.py:276
  22.7 10.6 %collective-permute-start.8 = (bf16[96,576]{1,0:T(8,128)(2,1)S(1)}, bf16[96,576]{1,0:T(8,128)(2,1)S(1)}, u32[]{:S(2)}, u32[]{:S(2)}) collective-permute-start(bf16[96,576]{1,0:T(8,128)(2,1)S(1)} %get-tuple-element.38), channel_id=1, source_target_pairs={{0,2},{1,3},{2,0},{3,1},{4,6},{5,7},{6,4},{7,5},{8,10},{9,11},{10,... | collective-permute-start | bytes 331784 | tf_op jit(solution)/shard_map/ppermute | solution.py:276

commit v4 on v3

--- a/solution.py
+++ b/solution.py
@@ -15,7 +15,7 @@
 VMEM_LIMIT = 24 * 2**20
 NEVER = 1e30
 CHUNKS = 2
-COPIES = 6
+COPIES = 1
 
 F32 = jnp.float32
 BF16 = jnp.bfloat16
@@ -73,7 +73,8 @@
             delta = delta_ref[first + i : first + i + 1, :].astype(F32)
             prob = jnp.exp(scores[:, lanes] - norm)
             if visible is not None:
-                prob = jnp.where(visible, prob, 0.0)
+                tail = jnp.where(visible[-PACKET:], prob[-PACKET:], 0.0)
+                prob = jnp.concatenate([prob[:-PACKET], tail], axis=0)
             here = slice((first + i) * PACKET, (first + i + 1) * PACKET)
             ds_ref[:, here] = (prob * (prob_grad[:, lanes] - delta)).astype(BF16)
             p_ref[:, here] = prob.astype(BF16)
@@ -91,12 +92,10 @@
         out_ref[...] = total_ref[pl.ds(start, out_ref.shape[0]), :].astype(out_ref.dtype)
 
 
-def own_kernel(low, plan_hbm, lat_ref, q_ref, grad_ref, norm_ref, delta_ref, *rest):
+def own_kernel(low, plan_ref, lat_ref, q_ref, grad_ref, norm_ref, delta_ref, *rest):
     rows_ref, ds_ref, sel_ref, keep_ref = rest[:4]
-    out_refs = rest[4:-4]
-    plan_ref, p_ref, total_ref, sem = rest[-4:]
-    plan_copy = pltpu.make_async_copy(plan_hbm, plan_ref, sem)
-    plan_copy.start()
+    out_refs = rest[4:-2]
+    p_ref, total_ref = rest[-2:]
     heads = q_ref.shape[0]
     group = WIDE // heads
     at = lax.broadcasted_iota(jnp.int32, (WIDE, WIDE), 0)
@@ -106,12 +105,13 @@
         moved = dot(order, grad_ref[g * WIDE : (g + 1) * WIDE, :]).astype(BF16)
         for h in range(heads):
             rows_ref[h * PACKET + g * group : h * PACKET + (g + 1) * group, :] = moved[h * group : (h + 1) * group, :]
-    plan_copy.wait()
-    b0, b1 = plan_ref[0, 0], plan_ref[0, 1]
+    b0, b1 = plan_ref[0:1, 0:1], plan_ref[0:1, 1:2]
     t = lax.div(lax.axis_index("head"), low)
     for i, hit in enumerate((b0 == t, b0 != t, b1 == t, b1 != t)):
         sel_ref[i : i + 1, :] = jnp.broadcast_to(jnp.where(hit, 1.0, 0.0), (1, sel_ref.shape[1])).astype(F32)
-    keys = block_of(lat_ref, b0).T
+    last = jnp.where(b0 > 0, 1.0, 0.0).astype(BF16)
+    first = jnp.where(b0 > 0, 0.0, 1.0).astype(BF16)
+    keys = (lat_ref[:, :BLOCK] * first + lat_ref[:, BLOCK:] * last).T
     k_pos = b0 * BLOCK + lax.broadcasted_iota(jnp.int32, (BLOCK, PACKET), 0)
     q_pos = SHARD - PACKET + lax.broadcasted_iota(jnp.int32, (BLOCK, PACKET), 1)
     visit(keys, q_ref, rows_ref, norm_ref, delta_ref, None, k_pos <= q_pos, ds_ref, p_ref, total_ref)
@@ -238,20 +238,12 @@
         (plan, lat_t, q_t, grad, norm_t, delta_t),
         [((columns, LAT), BF16), ((BLOCK, columns), BF16), ((8, width), F32), ((rows, width), F32)]
         + [((part, width), BF16)] * (CHUNKS * (low - 1)),
-        [
-            pltpu.SMEM(plan.shape, plan.dtype),
-            pltpu.VMEM((BLOCK, columns), BF16),
-            pltpu.VMEM((BLOCK, width), F32),
-            pltpu.SemaphoreType.DMA,
-        ],
-        raw=(0,),
+        [pltpu.VMEM((BLOCK, columns), BF16), pltpu.VMEM((BLOCK, width), F32)],
     )
 
     far_ds, own_parts, far_parts = [], [], []
     for c in range(CHUNKS):
-        parts = own[c::CHUNKS]
-        own_parts.append([keep] + [lax.ppermute(parts[d - 1], ("seq", "head"), route(d, 0)) for d in range(1, low)])
-        later = [i for i in range(len(own)) if i % CHUNKS > c]
+        later = [i for i in range(len(own)) if i % CHUNKS and i % CHUNKS >= c]
         ds, *far = call(
             functools.partial(far_kernel, low, len(later)),
             f"far_visit_{c}",
@@ -262,6 +254,8 @@
         )
         for i, x in zip(later, far[low:]):
             own[i] = x
+        parts = own[c::CHUNKS]
+        own_parts.append([keep] + [lax.ppermute(parts[d - 1], ("seq", "head"), route(d, 0)) for d in range(1, low)])
         far_ds.append(ds)
         far_parts.append([lax.ppermute(far[d], ("seq", "head"), route(d, 1)) for d in reversed(range(low))])
 

time: 34.2 us -> 34.2 us (level)
  waiting for transfers between devices: 5.22 us -> 5.86 us
  Pallas kernels: 11.8 us -> 11.2 us
    ppermute x2, waiting for transfers between devices: 0.01 us -> 1.43 us  [local(): lax.ppermute(parts[d - 1], ('seq', 'head'), route(d, 0))]
    pallas_call x8, Pallas kernels: 11.8 us -> 11.2 us  [call(): pl.pallas_call(kernel, name=name, out_shape=shapes, in_specs=[pl.BlockSpe...]
    ppermute x2, starting transfers between devices: 5.43 us -> 4.96 us  [local(): lax.ppermute(send, 'head', [(j, (j + low) % n_head) for j in range(n_head)])]
    ppermute x4, starting transfers between devices: 5.61 us -> 6.01 us  [local(): lax.ppermute(far[d], ('seq', 'head'), route(d, 1))]
    ppermute x4, waiting for transfers between devices: 0.42 us -> 0.01 us  [local(): lax.ppermute(far[d], ('seq', 'head'), route(d, 1))]
    ppermute x2, waiting for transfers between devices: 4.79 us -> 4.41 us  [local(): lax.ppermute(send, 'head', [(j, (j + low) % n_head) for j in range(n_head)])]
  transfers between devices with their start and end apart: 10 -> 10, of which waited for: 4 -> 2; matrix products, arithmetic and copies ran while one was open for 0% -> 0% of each run, Pallas kernels for 28% -> 26%
where the time goes in v4:
time: 34.2 us; the launch traced here: 34.1 us
  starting transfers between devices  16.2 us (47%)
  Pallas kernels  11.2 us (33%)
  waiting for transfers between devices  5.86 us (17%)
  between operations  0.73 us (2%)
    pallas_call x8, Pallas kernels, call(): pl.pallas_call(kernel, name=name, out_shape=shapes, in_specs=[pl.BlockSpe...  11.2 us
    ppermute x4, starting transfers between devices, local(): lax.ppermute(far[d], ('seq', 'head'), route(d, 1))  6.01 us
    ppermute x2, starting transfers between devices, local(): lax.ppermute(send, 'head', [(j, (j + low) % n_head) for j in range(n_head)])  4.96 us
    ppermute x2, waiting for transfers between devices, local(): lax.ppermute(send, 'head', [(j, (j + low) % n_head) for j in range(n_head)])  4.41 us
    ppermute x2, starting transfers between devices, local(): lax.ppermute(x, 'seq', [(i, (i + 1) % n_seq) for i in range(n_seq)])  3.11 us
    ppermute x2, starting transfers between devices, local(): lax.ppermute(parts[d - 1], ('seq', 'head'), route(d, 0))  2.16 us
    ppermute x2, waiting for transfers between devices, local(): lax.ppermute(parts[d - 1], ('seq', 'head'), route(d, 0))  1.43 us
  transfers between devices with their start and end apart: 10, of which 2 were waited for; matrix products, arithmetic and copies ran while one was open for 0% of the time, Pallas kernels for 26%

profile of v4, /device:TPU:0, one launch (start us, length us, event | category | flops | bytes accessed | tf_op | source)
XLA Modules:
  0.0 34.1 jit_solution(16859680625968145739)
XLA Ops:
  0.6 0.0 copy-start
  0.6 0.0 copy-start.1
  0.7 0.0 copy-start.2
  0.7 0.0 copy-start.3
  0.7 0.0 copy-start.4
  0.7 0.0 copy-start.5
  0.7 1.5 %send_block.1 = (bf16[192,576]{1,0:T(8,128)(2,1)S(1)}, bf16[192,576]{1,0:T(8,128)(2,1)S(1)}) custom-call(s32[1,2]{1,0:T(1,128)} %plan_ref.3, bf16[576,768]{1,0:T(8,128)(2,1)} %bitcast.9), custom_call_target="tpu_custom_call" | custom-call | flops 1711276032 | bytes 1327112 | tf_op jit(solution)/shard_map/send_block/pallas_call | solution.py:185
  2.2 0.5 %collective-permute-start = (bf16[192,576]{1,0:T(8,128)(2,1)S(1)}, bf16[192,576]{1,0:T(8,128)(2,1)S(1)}, u32[]{:S(2)}, u32[]{:S(2)}) collective-permute-start(bf16[192,576]{1,0:T(8,128)(2,1)S(1)} %get-tuple-element.23), channel_id=1, source_target_pairs={{0,4},{4,8},{8,12},{12,16},{16,20},{20,24},{24,28},{28,0},{1,5},{5... | collective-permute-start | bytes 663560 | tf_op jit(solution)/shard_map/ppermute | solution.py:233
  2.7 2.6 %collective-permute-start.1 = (bf16[192,576]{1,0:T(8,128)(2,1)S(1)}, bf16[192,576]{1,0:T(8,128)(2,1)S(1)}, u32[]{:S(2)}, u32[]{:S(2)}) collective-permute-start(bf16[192,576]{1,0:T(8,128)(2,1)S(1)} %get-tuple-element.24), channel_id=1, source_target_pairs={{0,4},{4,8},{8,12},{12,16},{16,20},{20,24},{24,28},{28,0},{1,5},{5... | collective-permute-start | bytes 663560 | tf_op jit(solution)/shard_map/ppermute | solution.py:233
  5.3 0.0 copy-done
  5.3 0.0 copy-done.1
  5.3 0.0 copy-done.2
  5.3 0.0 copy-done.3
  5.3 0.0 copy-done.4
  5.4 0.0 copy-done.5
  5.4 2.8 %own_visit.1 = (bf16[1024,512]{1,0:T(8,128)(2,1)S(1)}, bf16[384,1024]{1,0:T(8,128)(2,1)S(1)}, f32[8,576]{1,0:T(8,128)S(1)}, f32[192,576]{1,0:T(8,128)S(1)}, bf16...) custom-call(s32[1,2]{1,0:T(1,128)S(1)} %copy-done.5, bf16[576,768]{1,0:T(8,128)(2,1)S(1)} %bitcast.10, ...), custom_call_target="tpu_custom_call" | custom-call | bytes 5634056 | tf_op jit(solution)/shard_map/own_visit/pallas_call | solution.py:185
  8.2 1.6 %collective-permute-start.5 = (bf16[96,576]{1,0:T(8,128)(2,1)S(1)}, bf16[96,576]{1,0:T(8,128)(2,1)S(1)}, u32[]{:S(2)}, u32[]{:S(2)}) collective-permute-start(bf16[96,576]{1,0:T(8,128)(2,1)S(1)} %get-tuple-element.36), channel_id=1, source_target_pairs={{0,1},{1,0},{2,3},{3,2},{4,5},{5,4},{6,7},{7,6},{8,9},{9,8},{10,11... | collective-permute-start | bytes 331784 | tf_op jit(solution)/shard_map/ppermute | solution.py:258
  9.9 0.0 collective-permute-done.keys_ref.rest_0_
  9.9 1.5 %far_visit_0.1 = (bf16[192,1024]{1,0:T(8,128)(2,1)S(1)}, bf16[96,576]{1,0:T(8,128)(2,1)S(1)}, bf16[96,576]{1,0:T(8,128)(2,1)S(1)}, bf16[96,576]{1,0:T(8,128)(2,1)S(1)}) custom-call(bf16[192,576]{1,0:T(8,128)(2,1)S(1)} %collective-permute-done.keys_ref.rest_0_, bf16[8,576,128]{2,1,0:T(8,128)(2,1)S(1)} %bitcast.7, ...), custom_call_target="tpu_custom_call", output_to_operand_aliasing={{3}: (5, {})} | custom-call | bytes 3067904 | tf_op jit(solution)/shard_map/far_visit_0/pallas_call | solution.py:185
  11.3 0.7 %collective-permute-start.6 = (bf16[96,576]{1,0:T(8,128)(2,1)S(1)}, bf16[96,576]{1,0:T(8,128)(2,1)S(1)}, u32[]{:S(2)}, u32[]{:S(2)}) collective-permute-start(bf16[96,576]{1,0:T(8,128)(2,1)S(1)} %get-tuple-element.37), channel_id=1, source_target_pairs={{0,29},{1,28},{2,31},{3,30},{4,1},{5,0},{6,3},{7,2},{8,5},{9,4},{1... | collective-permute-start | bytes 331784 | tf_op jit(solution)/shard_map/ppermute | solution.py:260
  12.0 2.6 %collective-permute-start.7 = (bf16[96,576]{1,0:T(8,128)(2,1)S(1)}, bf16[96,576]{1,0:T(8,128)(2,1)S(1)}, u32[]{:S(2)}, u32[]{:S(2)}) collective-permute-start(bf16[96,576]{1,0:T(8,128)(2,1)S(1)} %get-tuple-element.38), channel_id=1, source_target_pairs={{0,28},{1,29},{2,30},{3,31},{4,0},{5,1},{6,2},{7,3},{8,4},{9,5},{1... | collective-permute-start | bytes 331784 | tf_op jit(solution)/shard_map/ppermute | solution.py:260
  14.6 0.0 collective-permute-done.1.keys_ref.rest_1_
  14.6 1.5 %far_visit_1.1 = (bf16[192,1024]{1,0:T(8,128)(2,1)S(1)}, bf16[96,576]{1,0:T(8,128)(2,1)S(1)}, bf16[96,576]{1,0:T(8,128)(2,1)S(1)}, bf16[96,576]{1,0:T(8,128)(2,1)S(1)}) custom-call(bf16[192,576]{1,0:T(8,128)(2,1)S(1)} %collective-permute-done.1.keys_ref.rest_1_, bf16[8,576,128]{2,1,0:T(8,128)(2,1)S(1)} %bitcast.8, ...), custom_call_target="tpu_custom_call", output_to_operand_aliasing={{3}: (5, {})} | custom-call | bytes 3067904 | tf_op jit(solution)/shard_map/far_visit_1/pallas_call | solution.py:185
  16.1 0.5 %collective-permute-start.2 = (bf16[96,576]{1,0:T(8,128)(2,1)S(1)}, bf16[96,576]{1,0:T(8,128)(2,1)S(1)}, u32[]{:S(2)}, u32[]{:S(2)}) collective-permute-start(bf16[96,576]{1,0:T(8,128)(2,1)S(1)} %get-tuple-element.32), channel_id=1, source_target_pairs={{0,1},{1,0},{2,3},{3,2},{4,5},{5,4},{6,7},{7,6},{8,9},{9,8},{10,11... | collective-permute-start | bytes 331784 | tf_op jit(solution)/shard_map/ppermute | solution.py:258
  16.6 0.7 %collective-permute-start.3 = (bf16[96,576]{1,0:T(8,128)(2,1)S(1)}, bf16[96,576]{1,0:T(8,128)(2,1)S(1)}, u32[]{:S(2)}, u32[]{:S(2)}) collective-permute-start(bf16[96,576]{1,0:T(8,128)(2,1)S(1)} %get-tuple-element.33), channel_id=1, source_target_pairs={{0,29},{1,28},{2,31},{3,30},{4,1},{5,0},{6,3},{7,2},{8,5},{9,4},{1... | collective-permute-start | bytes 331784 | tf_op jit(solution)/shard_map/ppermute | solution.py:260
  17.3 0.0 collective-permute-done.5.rest_1_
  17.3 2.0 %collective-permute-start.4 = (bf16[96,576]{1,0:T(8,128)(2,1)S(1)}, bf16[96,576]{1,0:T(8,128)(2,1)S(1)}, u32[]{:S(2)}, u32[]{:S(2)}) collective-permute-start(bf16[96,576]{1,0:T(8,128)(2,1)S(1)} %get-tuple-element.34), channel_id=1, source_target_pairs={{0,28},{1,29},{2,30},{3,31},{4,0},{5,1},{6,2},{7,3},{8,4},{9,5},{1... | collective-permute-start | bytes 331784 | tf_op jit(solution)/shard_map/ppermute | solution.py:260
  19.3 0.0 collective-permute-done.6.rest_2_
  19.3 0.0 collective-permute-done.7.rest_3_
  19.3 0.1 combine_0.1
  19.4 2.7 %collective-permute-start.9 = (bf16[96,576]{1,0:T(8,128)(2,1)S(1)}, bf16[96,576]{1,0:T(8,128)(2,1)S(1)}, u32[]{:S(2)}, u32[]{:S(2)}) collective-permute-start(bf16[96,576]{1,0:T(8,128)(2,1)S(1)} %get-tuple-element.41), channel_id=1, source_target_pairs={{0,2},{1,3},{2,0},{3,1},{4,6},{5,7},{6,4},{7,5},{8,10},{9,11},{10,... | collective-permute-start | bytes 331784 | tf_op jit(solution)/shard_map/ppermute | solution.py:270
  22.1 1.4 %collective-permute-done.2.rest_1_ = bf16[96,576]{1,0:T(8,128)(2,1)S(1)} collective-permute-done((bf16[96,576]{1,0:T(8,128)(2,1)S(1)}, bf16[96,576]{1,0:T(8,128)(2,1)S(1)}, u32[]{:S(2)}, u32[]{:S(2)}) %collective-permute-start.2) | collective-permute-done | bytes 110624 | tf_op jit(solution)/shard_map/ppermute | solution.py:258
  23.5 0.0 collective-permute-done.3.rest_2_
  23.5 0.0 collective-permute-done.4.rest_3_
  23.5 0.1 combine_1.1
  23.6 2.3 %collective-permute-start.8 = (bf16[96,576]{1,0:T(8,128)(2,1)S(1)}, bf16[96,576]{1,0:T(8,128)(2,1)S(1)}, u32[]{:S(2)}, u32[]{:S(2)}) collective-permute-start(bf16[96,576]{1,0:T(8,128)(2,1)S(1)} %get-tuple-element.40), channel_id=1, source_target_pairs={{0,2},{1,3},{2,0},{3,1},{4,6},{5,7},{6,4},{7,5},{8,10},{9,11},{10,... | collective-permute-start | bytes 331784 | tf_op jit(solution)/shard_map/ppermute | solution.py:270
  25.9 3.0 %query_grad.1 = bf16[8,576,128]{2,1,0:T(8,128)(2,1)} custom-call(s32[1,2]{1,0:T(1,128)S(1)} %copy-done.5, bf16[576,768]{1,0:T(8,128)(2,1)S(1)} %bitcast.11, bf16[384,1024]{1,0:T(8,128)(2,1)S(1)} %get-tuple-element.22.own_ds_ref, bf16[192,576]{1,0:T(8,128)(2,1)S(1)} %collective-permute-done.keys_ref.rest_0_, ...), custom_call_target="tpu_custom_call" | custom-call | flops 905969664 | bytes 4079624 | tf_op jit(solution)/shard_map/query_grad/pallas_call | solution.py:185
  28.9 0.0 collective-permute-done.9.refs_3_
  28.9 4.4 %collective-permute-done.8.refs_2_ = bf16[96,576]{1,0:T(8,128)(2,1)S(1)} collective-permute-done((bf16[96,576]{1,0:T(8,128)(2,1)S(1)}, bf16[96,576]{1,0:T(8,128)(2,1)S(1)}, u32[]{:S(2)}, u32[]{:S(2)}) %collective-permute-start.8) | collective-permute-done | bytes 110624 | tf_op jit(solution)/shard_map/ppermute | solution.py:270
  33.3 0.7 %last_sum.1 = bf16[192,576]{1,0:T(8,128)(2,1)} custom-call(f32[96,576]{1,0:T(8,128)S(1)} %get-tuple-element.35.refs_0_, f32[96,576]{1,0:T(8,128)S(1)} %get-tuple-element.39.refs_1_, bf16[96,576]{1,0:T(8,128)(2,1)S(1)} %collective-permute-done.8.refs_2_, bf16[96,576]{1,0:T(8,128)(2,1)S(1)} %collective-permute-done.9.refs_3_), custom_call_target="tpu_custom_call" | custom-call | bytes 884736 | tf_op jit(solution)/shard_map/last_sum/pallas_call | solution.py:185
Async XLA Ops:
  0.6 4.7 %copy-start = (bf16[128,8,576]{0,2,1:T(8,128)(2,1)S(1)}, bf16[128,8,576]{0,2,1:T(8,128)(2,1)}, u32[]{:S(2)}) copy-start(bf16[128,8,576]{0,2,1:T(8,128)(2,1)} %param.6) | copy-start | bytes 3538948
  0.6 4.7 %copy-start.1 = (bf16[768,576]{0,1:T(8,128)(2,1)S(1)}, bf16[768,576]{0,1:T(8,128)(2,1)}, u32[]{:S(2)}) copy-start(bf16[768,576]{0,1:T(8,128)(2,1)} %param.8) | copy-start | bytes 2654212
  0.7 4.7 %copy-start.2 = (bf16[128,8,512]{2,1,0:T(8,128)(2,1)S(1)}, bf16[128,8,512]{2,1,0:T(8,128)(2,1)}, u32[]{:S(2)}) copy-start(bf16[128,8,512]{2,1,0:T(8,128)(2,1)} %param.7) | copy-start | bytes 3145732
  0.7 4.7 %copy-start.3 = (bf16[128,8]{0,1:T(8,128)(2,1)S(1)}, bf16[128,8]{0,1:T(8,128)(2,1)}, u32[]{:S(2)}) copy-start(bf16[128,8]{0,1:T(8,128)(2,1)} %param.9) | copy-start | bytes 6148
  0.7 4.7 %copy-start.4 = (bf16[128,8]{0,1:T(8,128)(2,1)S(1)}, bf16[128,8]{0,1:T(8,128)(2,1)}, u32[]{:S(2)}) copy-start(bf16[128,8]{0,1:T(8,128)(2,1)} %param.10) | copy-start | bytes 6148
  0.7 4.7 %copy-start.5 = (s32[1,2]{1,0:T(1,128)S(1)}, s32[1,2]{1,0:T(1,128)}, u32[]{:S(2)}) copy-start(s32[1,2]{1,0:T(1,128)} %plan_ref.3) | copy-start | bytes 28
  2.2 7.6 %collective-permute-start = (bf16[192,576]{1,0:T(8,128)(2,1)S(1)}, bf16[192,576]{1,0:T(8,128)(2,1)S(1)}, u32[]{:S(2)}, u32[]{:S(2)}) collective-permute-start(bf16[192,576]{1,0:T(8,128)(2,1)S(1)} %get-tuple-element.23), channel_id=1, source_target_pairs={{0,4},{4,8},{8,12},{12,16},{16,20},{20,24},{24,28},{28,0},{1,5},{5... | collective-permute-start | bytes 663560 | tf_op jit(solution)/shard_map/ppermute | solution.py:233
  2.7 11.9 %collective-permute-start.1 = (bf16[192,576]{1,0:T(8,128)(2,1)S(1)}, bf16[192,576]{1,0:T(8,128)(2,1)S(1)}, u32[]{:S(2)}, u32[]{:S(2)}) collective-permute-start(bf16[192,576]{1,0:T(8,128)(2,1)S(1)} %get-tuple-element.24), channel_id=1, source_target_pairs={{0,4},{4,8},{8,12},{12,16},{16,20},{20,24},{24,28},{28,0},{1,5},{5... | collective-permute-start | bytes 663560 | tf_op jit(solution)/shard_map/ppermute | solution.py:233
  8.2 9.1 %collective-permute-start.5 = (bf16[96,576]{1,0:T(8,128)(2,1)S(1)}, bf16[96,576]{1,0:T(8,128)(2,1)S(1)}, u32[]{:S(2)}, u32[]{:S(2)}) collective-permute-start(bf16[96,576]{1,0:T(8,128)(2,1)S(1)} %get-tuple-element.36), channel_id=1, source_target_pairs={{0,1},{1,0},{2,3},{3,2},{4,5},{5,4},{6,7},{7,6},{8,9},{9,8},{10,11... | collective-permute-start | bytes 331784 | tf_op jit(solution)/shard_map/ppermute | solution.py:258
  11.3 8.0 %collective-permute-start.6 = (bf16[96,576]{1,0:T(8,128)(2,1)S(1)}, bf16[96,576]{1,0:T(8,128)(2,1)S(1)}, u32[]{:S(2)}, u32[]{:S(2)}) collective-permute-start(bf16[96,576]{1,0:T(8,128)(2,1)S(1)} %get-tuple-element.37), channel_id=1, source_target_pairs={{0,29},{1,28},{2,31},{3,30},{4,1},{5,0},{6,3},{7,2},{8,5},{9,4},{1... | collective-permute-start | bytes 331784 | tf_op jit(solution)/shard_map/ppermute | solution.py:260
  12.0 7.3 %collective-permute-start.7 = (bf16[96,576]{1,0:T(8,128)(2,1)S(1)}, bf16[96,576]{1,0:T(8,128)(2,1)S(1)}, u32[]{:S(2)}, u32[]{:S(2)}) collective-permute-start(bf16[96,576]{1,0:T(8,128)(2,1)S(1)} %get-tuple-element.38), channel_id=1, source_target_pairs={{0,28},{1,29},{2,30},{3,31},{4,0},{5,1},{6,2},{7,3},{8,4},{9,5},{1... | collective-permute-start | bytes 331784 | tf_op jit(solution)/shard_map/ppermute | solution.py:260
  16.1 7.5 %collective-permute-start.2 = (bf16[96,576]{1,0:T(8,128)(2,1)S(1)}, bf16[96,576]{1,0:T(8,128)(2,1)S(1)}, u32[]{:S(2)}, u32[]{:S(2)}) collective-permute-start(bf16[96,576]{1,0:T(8,128)(2,1)S(1)} %get-tuple-element.32), channel_id=1, source_target_pairs={{0,1},{1,0},{2,3},{3,2},{4,5},{5,4},{6,7},{7,6},{8,9},{9,8},{10,11... | collective-permute-start | bytes 331784 | tf_op jit(solution)/shard_map/ppermute | solution.py:258
  16.6 6.9 %collective-permute-start.3 = (bf16[96,576]{1,0:T(8,128)(2,1)S(1)}, bf16[96,576]{1,0:T(8,128)(2,1)S(1)}, u32[]{:S(2)}, u32[]{:S(2)}) collective-permute-start(bf16[96,576]{1,0:T(8,128)(2,1)S(1)} %get-tuple-element.33), channel_id=1, source_target_pairs={{0,29},{1,28},{2,31},{3,30},{4,1},{5,0},{6,3},{7,2},{8,5},{9,4},{1... | collective-permute-start | bytes 331784 | tf_op jit(solution)/shard_map/ppermute | solution.py:260
  17.3 6.2 %collective-permute-start.4 = (bf16[96,576]{1,0:T(8,128)(2,1)S(1)}, bf16[96,576]{1,0:T(8,128)(2,1)S(1)}, u32[]{:S(2)}, u32[]{:S(2)}) collective-permute-start(bf16[96,576]{1,0:T(8,128)(2,1)S(1)} %get-tuple-element.34), channel_id=1, source_target_pairs={{0,28},{1,29},{2,30},{3,31},{4,0},{5,1},{6,2},{7,3},{8,4},{9,5},{1... | collective-permute-start | bytes 331784 | tf_op jit(solution)/shard_map/ppermute | solution.py:260
  19.4 9.5 %collective-permute-start.9 = (bf16[96,576]{1,0:T(8,128)(2,1)S(1)}, bf16[96,576]{1,0:T(8,128)(2,1)S(1)}, u32[]{:S(2)}, u32[]{:S(2)}) collective-permute-start(bf16[96,576]{1,0:T(8,128)(2,1)S(1)} %get-tuple-element.41), channel_id=1, source_target_pairs={{0,2},{1,3},{2,0},{3,1},{4,6},{5,7},{6,4},{7,5},{8,10},{9,11},{10,... | collective-permute-start | bytes 331784 | tf_op jit(solution)/shard_map/ppermute | solution.py:270
  23.6 9.7 %collective-permute-start.8 = (bf16[96,576]{1,0:T(8,128)(2,1)S(1)}, bf16[96,576]{1,0:T(8,128)(2,1)S(1)}, u32[]{:S(2)}, u32[]{:S(2)}) collective-permute-start(bf16[96,576]{1,0:T(8,128)(2,1)S(1)} %get-tuple-element.40), channel_id=1, source_target_pairs={{0,2},{1,3},{2,0},{3,1},{4,6},{5,7},{6,4},{7,5},{8,10},{9,11},{10,... | collective-permute-start | bytes 331784 | tf_op jit(solution)/shard_map/ppermute | solution.py:270

commit v5 on v4

--- a/solution.py
+++ b/solution.py
@@ -15,7 +15,7 @@
 VMEM_LIMIT = 24 * 2**20
 NEVER = 1e30
 CHUNKS = 2
-COPIES = 1
+FIRST_SHARE = 1 / 2
 
 F32 = jnp.float32
 BF16 = jnp.bfloat16
@@ -31,26 +31,29 @@
 
 def block_of(lat_ref, block):
     return lat_ref[:, pl.ds(pl.multiple_of(block * BLOCK, 128), BLOCK)]
+
+
+def chunks_of(rows):
+    first = -(-int(rows * FIRST_SHARE) // 16) * 16
+    return [(0, first), (first, rows - first)]
 
 
 def send_block_kernel(low, plan_hbm, lat_hbm, *rest):
     out_refs = rest[:CHUNKS]
     plan_ref, lat_ref, sems = rest[CHUNKS:]
-    step = lat_ref.shape[0] // COPIES
-    copies = [pltpu.make_async_copy(plan_hbm, plan_ref, sems.at[COPIES])]
-    for i in range(COPIES):
-        here = pl.ds(i * step, step)
-        copies.append(pltpu.make_async_copy(lat_hbm.at[here], lat_ref.at[here], sems.at[i]))
+    copies = [
+        pltpu.make_async_copy(plan_hbm, plan_ref, sems.at[0]),
+        pltpu.make_async_copy(lat_hbm, lat_ref, sems.at[1]),
+    ]
     for copy in copies:
         copy.start()
     for copy in copies:
         copy.wait()
     keys = block_of(lat_ref, plan_ref[0, 1]).T
     rows = BLOCK // low
-    part = rows // CHUNKS
-    for c, out_ref in enumerate(out_refs):
+    for (offset, part), out_ref in zip(chunks_of(rows), out_refs):
         for j in range(low):
-            start = j * rows + c * part
+            start = j * rows + offset
             out_ref[j * part : (j + 1) * part, :] = keys[start : start + part, :]
 
 
@@ -116,14 +119,12 @@
     q_pos = SHARD - PACKET + lax.broadcasted_iota(jnp.int32, (BLOCK, PACKET), 1)
     visit(keys, q_ref, rows_ref, norm_ref, delta_ref, None, k_pos <= q_pos, ds_ref, p_ref, total_ref)
     pieces_out(total_ref, low, 0, [(0, keep_ref)])
-    for i, out_ref in enumerate(out_refs):
-        part = out_ref.shape[0]
-        pieces_out(total_ref, low, i % CHUNKS * part, [(1 + i // CHUNKS, out_ref)])
-
-
-def far_kernel(low, held, keys_ref, q_ref, grad_ref, norm_ref, delta_ref, *rest):
-    ds_ref = rest[held]
-    out_refs = rest[held + 1 : held + 1 + low]
+    pieces_out(total_ref, low, 0, list(enumerate(out_refs, 1)))
+
+
+def far_kernel(low, keys_ref, q_ref, grad_ref, norm_ref, delta_ref, *rest):
+    ds_ref = rest[0]
+    out_refs = rest[1 : 1 + low]
     p_ref, total_ref = rest[-2:]
     live = lax.axis_index("seq") > 0
     visit(keys_ref[...], q_ref, grad_ref, norm_ref, delta_ref, live, None, ds_ref, p_ref, total_ref)
@@ -147,15 +148,15 @@
             out_ref[first + i] = total[:, i * PACKET : (i + 1) * PACKET].astype(BF16)
 
 
-def combine_kernel(low, chunk, sel_ref, *rest):
+def combine_kernel(low, offset, sel_ref, *rest):
     own_refs = rest[:low]
     far_refs = rest[low : 2 * low]
     send_ref, mine_ref = rest[-2:]
     part = send_ref.shape[0]
-    here = slice(chunk * part, (chunk + 1) * part)
+    here = slice(offset, offset + part)
     own = own_refs[0][here, :]
     for ref in own_refs[1:]:
-        own = own + ref[...].astype(F32)
+        own = own + ref[here, :].astype(F32)
     far = far_refs[0][...].astype(F32)
     for ref in far_refs[1:]:
         far = far + ref[...].astype(F32)
@@ -165,34 +166,29 @@
 
 def last_kernel(*refs):
     mine_refs, got_refs, out_ref = refs[:CHUNKS][::-1], refs[CHUNKS : 2 * CHUNKS][::-1], refs[-1]
-    part = out_ref.shape[0] // CHUNKS
-    for c in range(CHUNKS):
-        out_ref[c * part : (c + 1) * part, :] = (mine_refs[c][...] + got_refs[c][...].astype(F32)).astype(BF16)
-
-
-def call(kernel, name, ins, outs, scratch=(), smem=(), raw=(), passed=(), flops=0, transcendentals=0):
+    for (offset, part), mine_ref, got_ref in zip(chunks_of(out_ref.shape[0]), mine_refs, got_refs):
+        out_ref[offset : offset + part, :] = (mine_ref[...] + got_ref[...].astype(F32)).astype(BF16)
+
+
+def call(kernel, name, ins, outs, scratch=(), smem=(), raw=(), flops=0, size=None):
     spaces = [pltpu.SMEM if i in smem else pltpu.VMEM for i in range(len(ins))]
     ins = list(ins)
     for i in raw:
         spaces[i] = pl.ANY
         ins[i] = pltpu.with_memory_space_constraint(ins[i], pltpu.HBM)
-    size = sum(x.size * x.dtype.itemsize for x in ins)
-    size += sum(functools.reduce(lambda a, b: a * b, s, jnp.dtype(d).itemsize) for s, d in outs)
-    out_spaces = [pltpu.VMEM] * len(outs) + [pl.ANY] * len(passed)
-    shapes = [jax.ShapeDtypeStruct(s, d) for s, d in outs]
-    shapes += [jax.ShapeDtypeStruct(x.shape, x.dtype) for x in passed]
-    aliases = {len(ins) + i: len(outs) + i for i in range(len(passed))}
+    if size is None:
+        size = sum(x.size * x.dtype.itemsize for x in ins)
+        size += sum(functools.reduce(lambda a, b: a * b, s, jnp.dtype(d).itemsize) for s, d in outs)
     return pl.pallas_call(
         kernel,
         name=name,
-        out_shape=shapes,
-        in_specs=[pl.BlockSpec(memory_space=space) for space in spaces + [pl.ANY] * len(passed)],
-        out_specs=[pl.BlockSpec(memory_space=space) for space in out_spaces],
+        out_shape=[jax.ShapeDtypeStruct(s, d) for s, d in outs],
+        in_specs=[pl.BlockSpec(memory_space=space) for space in spaces],
+        out_specs=[pl.BlockSpec(memory_space=pltpu.VMEM) for _ in outs],
         scratch_shapes=scratch,
-        input_output_aliases=aliases,
         compiler_params=pltpu.CompilerParams(vmem_limit_bytes=VMEM_LIMIT),
-        cost_estimate=pl.CostEstimate(flops=flops, bytes_accessed=size, transcendentals=transcendentals),
-    )(*ins, *passed)
+        cost_estimate=pl.CostEstimate(flops=flops, bytes_accessed=size, transcendentals=0),
+    )(*ins)
 
 
 def local(queries, out_grad, latents, log_norm, out_delta, plan):
@@ -218,15 +214,14 @@
                 pairs.append((i * n_head + j, (i - back) % n_seq * n_head + to))
         return pairs
 
-    part = rows // CHUNKS
-    keys = BLOCK // CHUNKS
+    chunks = chunks_of(rows)
 
     sent = call(
         functools.partial(send_block_kernel, low),
         "send_block",
         (plan, lat_t),
-        [((keys, width), BF16)] * CHUNKS,
-        [pltpu.SMEM(plan.shape, plan.dtype), pltpu.VMEM(lat_t.shape, BF16), pltpu.SemaphoreType.DMA((COPIES + 1,))],
+        [((low * part, width), BF16) for _, part in chunks],
+        [pltpu.SMEM(plan.shape, plan.dtype), pltpu.VMEM(lat_t.shape, BF16), pltpu.SemaphoreType.DMA((2,))],
         flops=visit_flops,
         raw=(0, 1),
     )
@@ -237,34 +232,31 @@
         "own_visit",
         (plan, lat_t, q_t, grad, norm_t, delta_t),
         [((columns, LAT), BF16), ((BLOCK, columns), BF16), ((8, width), F32), ((rows, width), F32)]
-        + [((part, width), BF16)] * (CHUNKS * (low - 1)),
+        + [((rows, width), BF16)] * (low - 1),
         [pltpu.VMEM((BLOCK, columns), BF16), pltpu.VMEM((BLOCK, width), F32)],
     )
-
-    far_ds, own_parts, far_parts = [], [], []
-    for c in range(CHUNKS):
-        later = [i for i in range(len(own)) if i % CHUNKS and i % CHUNKS >= c]
+    own_parts = [keep] + [lax.ppermute(own[d - 1], ("seq", "head"), route(d, 0)) for d in range(1, low)]
+
+    far_ds, far_parts = [], []
+    for c, (_, part) in enumerate(chunks):
+        keys = low * part
         ds, *far = call(
-            functools.partial(far_kernel, low, len(later)),
+            functools.partial(far_kernel, low),
             f"far_visit_{c}",
             (far_keys[c], q_t, grad_rows, norm_t, delta_t),
             [((keys, columns), BF16)] + [((part, width), BF16)] * low,
             [pltpu.VMEM((keys, columns), BF16), pltpu.VMEM((keys, width), F32)],
-            passed=[own[i] for i in later],
+            size=0,
         )
-        for i, x in zip(later, far[low:]):
-            own[i] = x
-        parts = own[c::CHUNKS]
-        own_parts.append([keep] + [lax.ppermute(parts[d - 1], ("seq", "head"), route(d, 0)) for d in range(1, low)])
         far_ds.append(ds)
         far_parts.append([lax.ppermute(far[d], ("seq", "head"), route(d, 1)) for d in reversed(range(low))])
 
     mine, got = [None] * CHUNKS, [None] * CHUNKS
-    for c in reversed(range(CHUNKS)):
+    for c, (offset, part) in reversed(list(enumerate(chunks))):
         send, mine[c] = call(
-            functools.partial(combine_kernel, low, c),
+            functools.partial(combine_kernel, low, offset),
             f"combine_{c}",
-            (sel, *own_parts[c], *far_parts[c]),
+            (sel, *own_parts, *far_parts[c]),
             [((part, width), BF16), ((part, width), F32)],
         )
         got[c] = lax.ppermute(send, "head", [(j, (j + low) % n_head) for j in range(n_head)])

time: 34.2 us -> 34.5 us (level)
  waiting for transfers between devices: 5.86 us -> 7.34 us
  starting transfers between devices: 16.2 us -> 14.9 us
    ppermute x2, waiting for transfers between devices: 4.41 us -> 6.09 us  [local(): lax.ppermute(send, 'head', [(j, (j + low) % n_head) for j in range(n_head)])]
    ppermute x2 -> x1, waiting for transfers between devices: 1.43 us -> 0.01 us  [local(): lax.ppermute(own[d - 1], ('seq', 'head'), route(d, 0))]
    ppermute x4, waiting for transfers between devices: 0.01 us -> 1.24 us  [local(): lax.ppermute(far[d], ('seq', 'head'), route(d, 1))]
    ppermute x4, starting transfers between devices: 6.01 us -> 4.9 us  [local(): lax.ppermute(far[d], ('seq', 'head'), route(d, 1))]
    ppermute x2 -> x1, starting transfers between devices: 2.16 us -> 1.64 us  [local(): lax.ppermute(own[d - 1], ('seq', 'head'), route(d, 0))]
  transfers between devices with their start and end apart: 10 -> 9, of which waited for: 2 -> 4; matrix products, arithmetic and copies ran while one was open for 0% -> 0% of each run, Pallas kernels for 26% -> 26%
where the time goes in v5:
time: 34.5 us; the launch traced here: 34.3 us
  starting transfers between devices  14.9 us (43%)
  Pallas kernels  11.3 us (33%)
  waiting for transfers between devices  7.34 us (21%)
  between operations  0.73 us (2%)
    pallas_call x8, Pallas kernels, call(): pl.pallas_call(kernel, name=name, out_shape=[jax.ShapeDtypeStruct(s, d) f...  11.3 us
    ppermute x2, waiting for transfers between devices, local(): lax.ppermute(send, 'head', [(j, (j + low) % n_head) for j in range(n_head)])  6.09 us
    ppermute x2, starting transfers between devices, local(): lax.ppermute(send, 'head', [(j, (j + low) % n_head) for j in range(n_head)])  5.3 us
    ppermute x4, starting transfers between devices, local(): lax.ppermute(far[d], ('seq', 'head'), route(d, 1))  4.9 us
    ppermute x2, starting transfers between devices, local(): lax.ppermute(x, 'seq', [(i, (i + 1) % n_seq) for i in range(n_seq)])  3.11 us
    ppermute x1, starting transfers between devices, local(): lax.ppermute(own[d - 1], ('seq', 'head'), route(d, 0))  1.64 us
    ppermute x4, waiting for transfers between devices, local(): lax.ppermute(far[d], ('seq', 'head'), route(d, 1))  1.24 us
  transfers between devices with their start and end apart: 9, of which 4 were waited for; matrix products, arithmetic and copies ran while one was open for 0% of the time, Pallas kernels for 26%

profile of v5, /device:TPU:0, one launch (start us, length us, event | category | flops | bytes accessed | tf_op | source)
XLA Modules:
  0.0 34.3 jit_solution(15706457999270769749)
XLA Ops:
  0.6 0.0 copy-start
  0.6 0.0 copy-start.1
  0.7 0.0 copy-start.2
  0.7 0.0 copy-start.3
  0.7 0.0 copy-start.4
  0.7 0.0 copy-start.5
  0.7 1.5 %send_block.1 = (bf16[192,576]{1,0:T(8,128)(2,1)S(1)}, bf16[192,576]{1,0:T(8,128)(2,1)S(1)}) custom-call(s32[1,2]{1,0:T(1,128)} %plan_ref.3, bf16[576,768]{1,0:T(8,128)(2,1)} %bitcast.9), custom_call_target="tpu_custom_call" | custom-call | flops 1711276032 | bytes 1327112 | tf_op jit(solution)/shard_map/send_block/pallas_call | solution.py:182
  2.2 0.5 %collective-permute-start = (bf16[192,576]{1,0:T(8,128)(2,1)S(1)}, bf16[192,576]{1,0:T(8,128)(2,1)S(1)}, u32[]{:S(2)}, u32[]{:S(2)}) collective-permute-start(bf16[192,576]{1,0:T(8,128)(2,1)S(1)} %get-tuple-element.20), channel_id=1, source_target_pairs={{0,4},{4,8},{8,12},{12,16},{16,20},{20,24},{24,28},{28,0},{1,5},{5... | collective-permute-start | bytes 663560 | tf_op jit(solution)/shard_map/ppermute | solution.py:228
  2.7 2.6 %collective-permute-start.1 = (bf16[192,576]{1,0:T(8,128)(2,1)S(1)}, bf16[192,576]{1,0:T(8,128)(2,1)S(1)}, u32[]{:S(2)}, u32[]{:S(2)}) collective-permute-start(bf16[192,576]{1,0:T(8,128)(2,1)S(1)} %get-tuple-element.21), channel_id=1, source_target_pairs={{0,4},{4,8},{8,12},{12,16},{16,20},{20,24},{24,28},{28,0},{1,5},{5... | collective-permute-start | bytes 663560 | tf_op jit(solution)/shard_map/ppermute | solution.py:228
  5.3 0.0 copy-done
  5.3 0.0 copy-done.1
  5.3 0.0 copy-done.2
  5.3 0.0 copy-done.3
  5.3 0.0 copy-done.4
  5.4 0.0 copy-done.5
  5.4 2.9 %own_visit.1 = (bf16[1024,512]{1,0:T(8,128)(2,1)S(1)}, bf16[384,1024]{1,0:T(8,128)(2,1)S(1)}, f32[8,576]{1,0:T(8,128)S(1)}, f32[192,576]{1,0:T(8,128)S(1)}, bf16[192,576]{1,0:T(8,128)(2,1)S(1)}) custom-call(s32[1,2]{1,0:T(1,128)S(1)} %copy-done.5, bf16[576,768]{1,0:T(8,128)(2,1)S(1)} %bitcast.10, bf16[8,576,128]{2,1,0:T(8,128)(2,1)S(1)} %bitcast.6, ...), custom_call_target="tpu_custom_call" | custom-call | bytes 5634056 | tf_op jit(solution)/shard_map/own_visit/pallas_call | solution.py:182
  8.3 1.6 %collective-permute-start.2 = (bf16[192,576]{1,0:T(8,128)(2,1)S(1)}, bf16[192,576]{1,0:T(8,128)(2,1)S(1)}, u32[]{:S(2)}, u32[]{:S(2)}) collective-permute-start(bf16[192,576]{1,0:T(8,128)(2,1)S(1)} %get-tuple-element.27), channel_id=1, source_target_pairs={{0,1},{1,0},{2,3},{3,2},{4,5},{5,4},{6,7},{7,6},{8,9},{9,8},{10,11... | collective-permute-start | bytes 663560 | tf_op jit(solution)/shard_map/ppermute | solution.py:238
  9.9 0.0 collective-permute-done.keys_ref.rest_0_
  9.9 1.5 %far_visit_0.1 = (bf16[192,1024]{1,0:T(8,128)(2,1)S(1)}, bf16[96,576]{1,0:T(8,128)(2,1)S(1)}, bf16[96,576]{1,0:T(8,128)(2,1)S(1)}) custom-call(bf16[192,576]{1,0:T(8,128)(2,1)S(1)} %collective-permute-done.keys_ref.rest_0_, bf16[8,576,128]{2,1,0:T(8,128)(2,1)S(1)} %bitcast.7, bf16[1024,512]{1,0:T(8,128)(2,1)S(1)} %get-tuple-element.22.grad_ref, ...), custom_call_target="tpu_custom_call" | custom-call | tf_op jit(solution)/shard_map/far_visit_0/pallas_call | solution.py:182
  11.4 0.7 %collective-permute-start.5 = (bf16[96,576]{1,0:T(8,128)(2,1)S(1)}, bf16[96,576]{1,0:T(8,128)(2,1)S(1)}, u32[]{:S(2)}, u32[]{:S(2)}) collective-permute-start(bf16[96,576]{1,0:T(8,128)(2,1)S(1)} %get-tuple-element.31), channel_id=1, source_target_pairs={{0,29},{1,28},{2,31},{3,30},{4,1},{5,0},{6,3},{7,2},{8,5},{9,4},{1... | collective-permute-start | bytes 331784 | tf_op jit(solution)/shard_map/ppermute | solution.py:252
  12.0 2.6 %collective-permute-start.6 = (bf16[96,576]{1,0:T(8,128)(2,1)S(1)}, bf16[96,576]{1,0:T(8,128)(2,1)S(1)}, u32[]{:S(2)}, u32[]{:S(2)}) collective-permute-start(bf16[96,576]{1,0:T(8,128)(2,1)S(1)} %get-tuple-element.32), channel_id=1, source_target_pairs={{0,28},{1,29},{2,30},{3,31},{4,0},{5,1},{6,2},{7,3},{8,4},{9,5},{1... | collective-permute-start | bytes 331784 | tf_op jit(solution)/shard_map/ppermute | solution.py:252
  14.6 0.0 collective-permute-done.1.keys_ref.rest_1_
  14.6 1.5 %far_visit_1.1 = (bf16[192,1024]{1,0:T(8,128)(2,1)S(1)}, bf16[96,576]{1,0:T(8,128)(2,1)S(1)}, bf16[96,576]{1,0:T(8,128)(2,1)S(1)}) custom-call(bf16[192,576]{1,0:T(8,128)(2,1)S(1)} %collective-permute-done.1.keys_ref.rest_1_, bf16[8,576,128]{2,1,0:T(8,128)(2,1)S(1)} %bitcast.8, bf16[1024,512]{1,0:T(8,128)(2,1)S(1)} %get-tuple-element.22.grad_ref, ...), custom_call_target="tpu_custom_call" | custom-call | tf_op jit(solution)/shard_map/far_visit_1/pallas_call | solution.py:182
  16.1 0.3 collective-permute-start.3
  16.3 1.4 %collective-permute-start.4 = (bf16[96,576]{1,0:T(8,128)(2,1)S(1)}, bf16[96,576]{1,0:T(8,128)(2,1)S(1)}, u32[]{:S(2)}, u32[]{:S(2)}) collective-permute-start(bf16[96,576]{1,0:T(8,128)(2,1)S(1)} %get-tuple-element.29), channel_id=1, source_target_pairs={{0,28},{1,29},{2,30},{3,31},{4,0},{5,1},{6,2},{7,3},{8,4},{9,5},{1... | collective-permute-start | bytes 331784 | tf_op jit(solution)/shard_map/ppermute | solution.py:252
  17.7 0.0 collective-permute-done.2.rest_1_
  17.7 1.1 %collective-permute-done.5.rest_2_ = bf16[96,576]{1,0:T(8,128)(2,1)S(1)} collective-permute-done((bf16[96,576]{1,0:T(8,128)(2,1)S(1)}, bf16[96,576]{1,0:T(8,128)(2,1)S(1)}, u32[]{:S(2)}, u32[]{:S(2)}) %collective-permute-start.5) | collective-permute-done | bytes 110624 | tf_op jit(solution)/shard_map/ppermute | solution.py:252
  18.8 0.0 collective-permute-done.6.rest_3_
  18.8 0.1 combine_0.1
  18.9 2.6 %collective-permute-start.8 = (bf16[96,576]{1,0:T(8,128)(2,1)S(1)}, bf16[96,576]{1,0:T(8,128)(2,1)S(1)}, u32[]{:S(2)}, u32[]{:S(2)}) collective-permute-start(bf16[96,576]{1,0:T(8,128)(2,1)S(1)} %get-tuple-element.35), channel_id=1, source_target_pairs={{0,2},{1,3},{2,0},{3,1},{4,6},{5,7},{6,4},{7,5},{8,10},{9,11},{10,... | collective-permute-start | bytes 331784 | tf_op jit(solution)/shard_map/ppermute | solution.py:262
  21.6 0.2 collective-permute-done.3.rest_2_
  21.7 0.0 collective-permute-done.4.rest_3_
  21.8 0.1 combine_1.1
  21.9 2.7 %collective-permute-start.7 = (bf16[96,576]{1,0:T(8,128)(2,1)S(1)}, bf16[96,576]{1,0:T(8,128)(2,1)S(1)}, u32[]{:S(2)}, u32[]{:S(2)}) collective-permute-start(bf16[96,576]{1,0:T(8,128)(2,1)S(1)} %get-tuple-element.34), channel_id=1, source_target_pairs={{0,2},{1,3},{2,0},{3,1},{4,6},{5,7},{6,4},{7,5},{8,10},{9,11},{10,... | collective-permute-start | bytes 331784 | tf_op jit(solution)/shard_map/ppermute | solution.py:262
  24.5 3.0 %query_grad.1 = bf16[8,576,128]{2,1,0:T(8,128)(2,1)} custom-call(s32[1,2]{1,0:T(1,128)S(1)} %copy-done.5, bf16[576,768]{1,0:T(8,128)(2,1)S(1)} %bitcast.11, bf16[384,1024]{1,0:T(8,128)(2,1)S(1)} %get-tuple-element.19.own_ds_ref, bf16[192,576]{1,0:T(8,128)(2,1)S(1)} %collective-permute-done.keys_ref.rest_0_, ...), custom_call_target="tpu_custom_call" | custom-call | flops 905969664 | bytes 4079624 | tf_op jit(solution)/shard_map/query_grad/pallas_call | solution.py:182
  27.5 3.5 %collective-permute-done.8.refs_3_ = bf16[96,576]{1,0:T(8,128)(2,1)S(1)} collective-permute-done((bf16[96,576]{1,0:T(8,128)(2,1)S(1)}, bf16[96,576]{1,0:T(8,128)(2,1)S(1)}, u32[]{:S(2)}, u32[]{:S(2)}) %collective-permute-start.8) | collective-permute-done | bytes 110624 | tf_op jit(solution)/shard_map/ppermute | solution.py:262
  31.0 2.6 %collective-permute-done.7.refs_2_ = bf16[96,576]{1,0:T(8,128)(2,1)S(1)} collective-permute-done((bf16[96,576]{1,0:T(8,128)(2,1)S(1)}, bf16[96,576]{1,0:T(8,128)(2,1)S(1)}, u32[]{:S(2)}, u32[]{:S(2)}) %collective-permute-start.7) | collective-permute-done | bytes 110624 | tf_op jit(solution)/shard_map/ppermute | solution.py:262
  33.6 0.8 %last_sum.1 = bf16[192,576]{1,0:T(8,128)(2,1)} custom-call(f32[96,576]{1,0:T(8,128)S(1)} %get-tuple-element.30.refs_0_, f32[96,576]{1,0:T(8,128)S(1)} %get-tuple-element.33.refs_1_, bf16[96,576]{1,0:T(8,128)(2,1)S(1)} %collective-permute-done.7.refs_2_, bf16[96,576]{1,0:T(8,128)(2,1)S(1)} %collective-permute-done.8.refs_3_), custom_call_target="tpu_custom_call" | custom-call | bytes 884736 | tf_op jit(solution)/shard_map/last_sum/pallas_call | solution.py:182
Async XLA Ops:
  0.6 4.7 %copy-start = (bf16[128,8,576]{0,2,1:T(8,128)(2,1)S(1)}, bf16[128,8,576]{0,2,1:T(8,128)(2,1)}, u32[]{:S(2)}) copy-start(bf16[128,8,576]{0,2,1:T(8,128)(2,1)} %param.6) | copy-start | bytes 3538948
  0.6 4.7 %copy-start.1 = (bf16[768,576]{0,1:T(8,128)(2,1)S(1)}, bf16[768,576]{0,1:T(8,128)(2,1)}, u32[]{:S(2)}) copy-start(bf16[768,576]{0,1:T(8,128)(2,1)} %param.8) | copy-start | bytes 2654212
  0.7 4.7 %copy-start.2 = (bf16[128,8,512]{2,1,0:T(8,128)(2,1)S(1)}, bf16[128,8,512]{2,1,0:T(8,128)(2,1)}, u32[]{:S(2)}) copy-start(bf16[128,8,512]{2,1,0:T(8,128)(2,1)} %param.7) | copy-start | bytes 3145732
  0.7 4.7 %copy-start.3 = (bf16[128,8]{0,1:T(8,128)(2,1)S(1)}, bf16[128,8]{0,1:T(8,128)(2,1)}, u32[]{:S(2)}) copy-start(bf16[128,8]{0,1:T(8,128)(2,1)} %param.9) | copy-start | bytes 6148
  0.7 4.7 %copy-start.4 = (bf16[128,8]{0,1:T(8,128)(2,1)S(1)}, bf16[128,8]{0,1:T(8,128)(2,1)}, u32[]{:S(2)}) copy-start(bf16[128,8]{0,1:T(8,128)(2,1)} %param.10) | copy-start | bytes 6148
  0.7 4.7 %copy-start.5 = (s32[1,2]{1,0:T(1,128)S(1)}, s32[1,2]{1,0:T(1,128)}, u32[]{:S(2)}) copy-start(s32[1,2]{1,0:T(1,128)} %plan_ref.3) | copy-start | bytes 28
  2.2 7.7 %collective-permute-start = (bf16[192,576]{1,0:T(8,128)(2,1)S(1)}, bf16[192,576]{1,0:T(8,128)(2,1)S(1)}, u32[]{:S(2)}, u32[]{:S(2)}) collective-permute-start(bf16[192,576]{1,0:T(8,128)(2,1)S(1)} %get-tuple-element.20), channel_id=1, source_target_pairs={{0,4},{4,8},{8,12},{12,16},{16,20},{20,24},{24,28},{28,0},{1,5},{5... | collective-permute-start | bytes 663560 | tf_op jit(solution)/shard_map/ppermute | solution.py:228
  2.7 11.9 %collective-permute-start.1 = (bf16[192,576]{1,0:T(8,128)(2,1)S(1)}, bf16[192,576]{1,0:T(8,128)(2,1)S(1)}, u32[]{:S(2)}, u32[]{:S(2)}) collective-permute-start(bf16[192,576]{1,0:T(8,128)(2,1)S(1)} %get-tuple-element.21), channel_id=1, source_target_pairs={{0,4},{4,8},{8,12},{12,16},{16,20},{20,24},{24,28},{28,0},{1,5},{5... | collective-permute-start | bytes 663560 | tf_op jit(solution)/shard_map/ppermute | solution.py:228
  8.3 9.5 %collective-permute-start.2 = (bf16[192,576]{1,0:T(8,128)(2,1)S(1)}, bf16[192,576]{1,0:T(8,128)(2,1)S(1)}, u32[]{:S(2)}, u32[]{:S(2)}) collective-permute-start(bf16[192,576]{1,0:T(8,128)(2,1)S(1)} %get-tuple-element.27), channel_id=1, source_target_pairs={{0,1},{1,0},{2,3},{3,2},{4,5},{5,4},{6,7},{7,6},{8,9},{9,8},{10,11... | collective-permute-start | bytes 663560 | tf_op jit(solution)/shard_map/ppermute | solution.py:238
  11.4 7.4 %collective-permute-start.5 = (bf16[96,576]{1,0:T(8,128)(2,1)S(1)}, bf16[96,576]{1,0:T(8,128)(2,1)S(1)}, u32[]{:S(2)}, u32[]{:S(2)}) collective-permute-start(bf16[96,576]{1,0:T(8,128)(2,1)S(1)} %get-tuple-element.31), channel_id=1, source_target_pairs={{0,29},{1,28},{2,31},{3,30},{4,1},{5,0},{6,3},{7,2},{8,5},{9,4},{1... | collective-permute-start | bytes 331784 | tf_op jit(solution)/shard_map/ppermute | solution.py:252
  12.0 6.8 %collective-permute-start.6 = (bf16[96,576]{1,0:T(8,128)(2,1)S(1)}, bf16[96,576]{1,0:T(8,128)(2,1)S(1)}, u32[]{:S(2)}, u32[]{:S(2)}) collective-permute-start(bf16[96,576]{1,0:T(8,128)(2,1)S(1)} %get-tuple-element.32), channel_id=1, source_target_pairs={{0,28},{1,29},{2,30},{3,31},{4,0},{5,1},{6,2},{7,3},{8,4},{9,5},{1... | collective-permute-start | bytes 331784 | tf_op jit(solution)/shard_map/ppermute | solution.py:252
  16.1 5.7 %collective-permute-start.3 = (bf16[96,576]{1,0:T(8,128)(2,1)S(1)}, bf16[96,576]{1,0:T(8,128)(2,1)S(1)}, u32[]{:S(2)}, u32[]{:S(2)}) collective-permute-start(bf16[96,576]{1,0:T(8,128)(2,1)S(1)} %get-tuple-element.28), channel_id=1, source_target_pairs={{0,29},{1,28},{2,31},{3,30},{4,1},{5,0},{6,3},{7,2},{8,5},{9,4},{1... | collective-permute-start | bytes 331784 | tf_op jit(solution)/shard_map/ppermute | solution.py:252
  16.3 5.4 %collective-permute-start.4 = (bf16[96,576]{1,0:T(8,128)(2,1)S(1)}, bf16[96,576]{1,0:T(8,128)(2,1)S(1)}, u32[]{:S(2)}, u32[]{:S(2)}) collective-permute-start(bf16[96,576]{1,0:T(8,128)(2,1)S(1)} %get-tuple-element.29), channel_id=1, source_target_pairs={{0,28},{1,29},{2,30},{3,31},{4,0},{5,1},{6,2},{7,3},{8,4},{9,5},{1... | collective-permute-start | bytes 331784 | tf_op jit(solution)/shard_map/ppermute | solution.py:252
  18.9 12.0 %collective-permute-start.8 = (bf16[96,576]{1,0:T(8,128)(2,1)S(1)}, bf16[96,576]{1,0:T(8,128)(2,1)S(1)}, u32[]{:S(2)}, u32[]{:S(2)}) collective-permute-start(bf16[96,576]{1,0:T(8,128)(2,1)S(1)} %get-tuple-element.35), channel_id=1, source_target_pairs={{0,2},{1,3},{2,0},{3,1},{4,6},{5,7},{6,4},{7,5},{8,10},{9,11},{10,... | collective-permute-start | bytes 331784 | tf_op jit(solution)/shard_map/ppermute | solution.py:262
  21.9 11.7 %collective-permute-start.7 = (bf16[96,576]{1,0:T(8,128)(2,1)S(1)}, bf16[96,576]{1,0:T(8,128)(2,1)S(1)}, u32[]{:S(2)}, u32[]{:S(2)}) collective-permute-start(bf16[96,576]{1,0:T(8,128)(2,1)S(1)} %get-tuple-element.34), channel_id=1, source_target_pairs={{0,2},{1,3},{2,0},{3,1},{4,6},{5,7},{6,4},{7,5},{8,10},{9,11},{10,... | collective-permute-start | bytes 331784 | tf_op jit(solution)/shard_map/ppermute | solution.py:262

commit v6 on v5

--- a/solution.py
+++ b/solution.py
@@ -29,13 +29,17 @@
     return lax.dot_general(a, b, (((1,), (1,)), ((), ())), preferred_element_type=F32)
 
 
-def block_of(lat_ref, block):
-    return lat_ref[:, pl.ds(pl.multiple_of(block * BLOCK, 128), BLOCK)]
-
-
 def chunks_of(rows):
     first = -(-int(rows * FIRST_SHARE) // 16) * 16
     return [(0, first), (first, rows - first)]
+
+
+def chunk_rows(keys, low, out_refs):
+    rows = BLOCK // low
+    for (offset, part), out_ref in zip(chunks_of(rows), out_refs):
+        for j in range(low):
+            start = j * rows + offset
+            out_ref[j * part : (j + 1) * part, :] = keys[start : start + part, :]
 
 
 def send_block_kernel(low, plan_hbm, lat_hbm, *rest):
@@ -49,12 +53,8 @@
         copy.start()
     for copy in copies:
         copy.wait()
-    keys = block_of(lat_ref, plan_ref[0, 1]).T
-    rows = BLOCK // low
-    for (offset, part), out_ref in zip(chunks_of(rows), out_refs):
-        for j in range(low):
-            start = j * rows + offset
-            out_ref[j * part : (j + 1) * part, :] = keys[start : start + part, :]
+    block = pl.multiple_of(plan_ref[0, 1] * BLOCK, 128)
+    chunk_rows(lat_ref[:, pl.ds(block, BLOCK)].T, low, out_refs)
 
 
 def heads_side_by_side(q_ref, first, count):
@@ -76,8 +76,7 @@
             delta = delta_ref[first + i : first + i + 1, :].astype(F32)
             prob = jnp.exp(scores[:, lanes] - norm)
             if visible is not None:
-                tail = jnp.where(visible[-PACKET:], prob[-PACKET:], 0.0)
-                prob = jnp.concatenate([prob[:-PACKET], tail], axis=0)
+                prob = jnp.where(visible, prob, 0.0)
             here = slice((first + i) * PACKET, (first + i + 1) * PACKET)
             ds_ref[:, here] = (prob * (prob_grad[:, lanes] - delta)).astype(BF16)
             p_ref[:, here] = prob.astype(BF16)
@@ -95,10 +94,23 @@
         out_ref[...] = total_ref[pl.ds(start, out_ref.shape[0]), :].astype(out_ref.dtype)
 
 
-def own_kernel(low, plan_ref, lat_ref, q_ref, grad_ref, norm_ref, delta_ref, *rest):
-    rows_ref, ds_ref, sel_ref, keep_ref = rest[:4]
-    out_refs = rest[4:-2]
-    p_ref, total_ref = rest[-2:]
+def own_chunk(plan_ref, keys, offset, part, refs, low, q_ref, rows_ref, norm_ref, delta_ref):
+    ds_ref, keep_ref, *out_refs, p_ref, total_ref = refs
+    rows = BLOCK // low
+    at = lax.broadcasted_iota(jnp.int32, (part, PACKET), 0)
+    at = jnp.concatenate([at + (j * rows + offset) for j in range(low)], axis=0)
+    k_pos = plan_ref[0:1, 0:1] * BLOCK + at
+    q_pos = SHARD - PACKET + lax.broadcasted_iota(jnp.int32, at.shape, 1)
+    visit(keys, q_ref, rows_ref, norm_ref, delta_ref, None, k_pos <= q_pos, ds_ref, p_ref, total_ref)
+    pieces_out(total_ref, low, 0, list(enumerate([keep_ref, *out_refs])))
+
+
+def own_first_kernel(low, held, plan_ref, lat_ref, q_ref, grad_ref, norm_ref, delta_ref, *rest):
+    rest = rest[held:]
+    rows_ref, sel_ref = rest[:2]
+    keys_refs = rest[2 : 2 + CHUNKS]
+    ds_ref, keep_ref = rest[2 + CHUNKS : 4 + CHUNKS]
+    out_refs = rest[4 + CHUNKS : 3 + CHUNKS + low]
     heads = q_ref.shape[0]
     group = WIDE // heads
     at = lax.broadcasted_iota(jnp.int32, (WIDE, WIDE), 0)
@@ -115,48 +127,46 @@
     last = jnp.where(b0 > 0, 1.0, 0.0).astype(BF16)
     first = jnp.where(b0 > 0, 0.0, 1.0).astype(BF16)
     keys = (lat_ref[:, :BLOCK] * first + lat_ref[:, BLOCK:] * last).T
-    k_pos = b0 * BLOCK + lax.broadcasted_iota(jnp.int32, (BLOCK, PACKET), 0)
-    q_pos = SHARD - PACKET + lax.broadcasted_iota(jnp.int32, (BLOCK, PACKET), 1)
-    visit(keys, q_ref, rows_ref, norm_ref, delta_ref, None, k_pos <= q_pos, ds_ref, p_ref, total_ref)
-    pieces_out(total_ref, low, 0, [(0, keep_ref)])
-    pieces_out(total_ref, low, 0, list(enumerate(out_refs, 1)))
+    chunk_rows(keys, low, keys_refs)
+    (offset, part), *_ = chunks_of(BLOCK // low)
+    refs = [ds_ref, keep_ref, *out_refs, *rest[-2:]]
+    own_chunk(plan_ref, keys_refs[0][...], offset, part, refs, low, q_ref, rows_ref, norm_ref, delta_ref)
+
+
+def own_next_kernel(low, offset, plan_ref, keys_ref, q_ref, rows_ref, norm_ref, delta_ref, *rest):
+    part = keys_ref.shape[0] // low
+    own_chunk(plan_ref, keys_ref[...], offset, part, rest, low, q_ref, rows_ref, norm_ref, delta_ref)
 
 
 def far_kernel(low, keys_ref, q_ref, grad_ref, norm_ref, delta_ref, *rest):
-    ds_ref = rest[0]
-    out_refs = rest[1 : 1 + low]
+    ds_ref = rest[-3 - low]
+    out_refs = rest[-2 - low : -2]
     p_ref, total_ref = rest[-2:]
     live = lax.axis_index("seq") > 0
     visit(keys_ref[...], q_ref, grad_ref, norm_ref, delta_ref, live, None, ds_ref, p_ref, total_ref)
     pieces_out(total_ref, low, 0, list(enumerate(out_refs)))
 
 
-def query_kernel(plan_ref, lat_ref, own_ds_ref, *rest):
-    far_refs = rest[:CHUNKS]
-    far_ds_refs = rest[CHUNKS : 2 * CHUNKS]
-    out_ref = rest[-1]
+def query_kernel(*refs):
+    count = len(refs) // 2
+    keys_refs, ds_refs, out_ref = refs[:count], refs[count:-1], refs[-1]
     heads = out_ref.shape[0]
     per = WIDE // PACKET
-    own = block_of(lat_ref, plan_ref[0, 0])
-    fars = [ref[...].T for ref in far_refs]
+    keys = [ref[...].T for ref in keys_refs]
     for first in range(0, heads, per):
         cols = slice(first * PACKET, (first + per) * PACKET)
-        total = dot(own, own_ds_ref[:, cols])
-        for far, ds_ref in zip(fars, far_ds_refs):
-            total = total + dot(far, ds_ref[:, cols])
+        total = sum(dot(k, ds_ref[:, cols]) for k, ds_ref in zip(keys, ds_refs))
         for i in range(per):
             out_ref[first + i] = total[:, i * PACKET : (i + 1) * PACKET].astype(BF16)
 
 
-def combine_kernel(low, offset, sel_ref, *rest):
+def combine_kernel(low, sel_ref, *rest):
     own_refs = rest[:low]
     far_refs = rest[low : 2 * low]
     send_ref, mine_ref = rest[-2:]
-    part = send_ref.shape[0]
-    here = slice(offset, offset + part)
-    own = own_refs[0][here, :]
+    own = own_refs[0][...]
     for ref in own_refs[1:]:
-        own = own + ref[here, :].astype(F32)
+        own = own + ref[...].astype(F32)
     far = far_refs[0][...].astype(F32)
     for ref in far_refs[1:]:
         far = far + ref[...].astype(F32)
@@ -170,25 +180,25 @@
         out_ref[offset : offset + part, :] = (mine_ref[...] + got_ref[...].astype(F32)).astype(BF16)
 
 
-def call(kernel, name, ins, outs, scratch=(), smem=(), raw=(), flops=0, size=None):
-    spaces = [pltpu.SMEM if i in smem else pltpu.VMEM for i in range(len(ins))]
+def call(kernel, name, ins, outs, scratch=(), raw=(), passed=(), flops=0, size=0):
+    spaces = [pltpu.VMEM] * len(ins) + [pl.ANY] * len(passed)
     ins = list(ins)
     for i in raw:
         spaces[i] = pl.ANY
         ins[i] = pltpu.with_memory_space_constraint(ins[i], pltpu.HBM)
-    if size is None:
-        size = sum(x.size * x.dtype.itemsize for x in ins)
-        size += sum(functools.reduce(lambda a, b: a * b, s, jnp.dtype(d).itemsize) for s, d in outs)
+    shapes = [jax.ShapeDtypeStruct(s, d) for s, d in outs]
+    shapes += [jax.ShapeDtypeStruct(x.shape, x.dtype) for x in passed]
     return pl.pallas_call(
         kernel,
         name=name,
-        out_shape=[jax.ShapeDtypeStruct(s, d) for s, d in outs],
+        out_shape=shapes,
         in_specs=[pl.BlockSpec(memory_space=space) for space in spaces],
-        out_specs=[pl.BlockSpec(memory_space=pltpu.VMEM) for _ in outs],
+        out_specs=[pl.BlockSpec(memory_space=space) for space in [pltpu.VMEM] * len(outs) + [pl.ANY] * len(passed)],
         scratch_shapes=scratch,
+        input_output_aliases={len(ins) + i: len(outs) + i for i in range(len(passed))},
         compiler_params=pltpu.CompilerParams(vmem_limit_bytes=VMEM_LIMIT),
         cost_estimate=pl.CostEstimate(flops=flops, bytes_accessed=size, transcendentals=0),
-    )(*ins)
+    )(*ins, *passed)
 
 
 def local(queries, out_grad, latents, log_norm, out_delta, plan):
@@ -225,38 +235,62 @@
         flops=visit_flops,
         raw=(0, 1),
     )
-    far_keys = [lax.ppermute(x, "seq", [(i, (i + 1) % n_seq) for i in range(n_seq)]) for x in sent]
-
-    grad_rows, own_ds, sel, keep, *own = call(
-        functools.partial(own_kernel, low),
-        "own_visit",
+
+    def forward(x):
+        return lax.ppermute(x, "seq", [(i, (i + 1) % n_seq) for i in range(n_seq)])
+
+    def own_outs(part):
+        return [((low * part, columns), BF16), ((part, width), F32)] + [((part, width), BF16)] * (low - 1)
+
+    def scratch(part):
+        return [pltpu.VMEM((low * part, columns), BF16), pltpu.VMEM((low * part, width), F32)]
+
+    far_keys = [forward(sent[0])]
+    (_, part), *_ = chunks
+    grad_rows, sel, *first = call(
+        functools.partial(own_first_kernel, low, CHUNKS - 1),
+        "own_visit_0",
         (plan, lat_t, q_t, grad, norm_t, delta_t),
-        [((columns, LAT), BF16), ((BLOCK, columns), BF16), ((8, width), F32), ((rows, width), F32)]
-        + [((rows, width), BF16)] * (low - 1),
-        [pltpu.VMEM((BLOCK, columns), BF16), pltpu.VMEM((BLOCK, width), F32)],
+        [((columns, LAT), BF16), ((8, width), F32)] + [((low * p, width), BF16) for _, p in chunks] + own_outs(part),
+        scratch(part),
+        passed=sent[1:],
     )
-    own_parts = [keep] + [lax.ppermute(own[d - 1], ("seq", "head"), route(d, 0)) for d in range(1, low)]
+    own_keys, first = first[:CHUNKS], first[CHUNKS:]
+    own, later = [first[: 1 + low]], first[1 + low :]
+    far_keys += [forward(x) for x in later]
+    for c, (offset, part) in list(enumerate(chunks))[1:]:
+        own.append(
+            call(
+                functools.partial(own_next_kernel, low, offset),
+                f"own_visit_{c}",
+                (plan, own_keys[c], q_t, grad_rows, norm_t, delta_t),
+                own_outs(part),
+                scratch(part),
+            )
+        )
+    own_parts = []
+    for _, keep, *pieces in own:
+        sends = enumerate(pieces, 1)
+        own_parts.append([keep] + [lax.ppermute(x, ("seq", "head"), route(d, 0)) for d, x in sends])
 
     far_ds, far_parts = [], []
     for c, (_, part) in enumerate(chunks):
-        keys = low * part
         ds, *far = call(
             functools.partial(far_kernel, low),
             f"far_visit_{c}",
-            (far_keys[c], q_t, grad_rows, norm_t, delta_t),
-            [((keys, columns), BF16)] + [((part, width), BF16)] * low,
-            [pltpu.VMEM((keys, columns), BF16), pltpu.VMEM((keys, width), F32)],
-            size=0,
+            (far_keys[c], q_t, grad_rows, norm_t, delta_t, *(far_ds[-1:] or [own[-1][0]])),
+            [((low * part, columns), BF16)] + [((part, width), BF16)] * low,
+            scratch(part),
         )
         far_ds.append(ds)
         far_parts.append([lax.ppermute(far[d], ("seq", "head"), route(d, 1)) for d in reversed(range(low))])
 
     mine, got = [None] * CHUNKS, [None] * CHUNKS
-    for c, (offset, part) in reversed(list(enumerate(chunks))):
+    for c, (_, part) in reversed(list(enumerate(chunks))):
         send, mine[c] = call(
-            functools.partial(combine_kernel, low, offset),
+            functools.partial(combine_kernel, low),
             f"combine_{c}",
-            (sel, *own_parts, *far_parts[c]),
+            (sel, *own_parts[c], *far_parts[c]),
             [((part, width), BF16), ((part, width), F32)],
         )
         got[c] = lax.ppermute(send, "head", [(j, (j + low) % n_head) for j in range(n_head)])
@@ -264,9 +298,8 @@
     (query_t,) = call(
         query_kernel,
         "query_grad",
-        (plan, lat_t, own_ds, *far_keys, *far_ds),
+        (*own_keys, *far_keys, *(x[0] for x in own), *far_ds),
         [((heads, width, packet), BF16)],
-        smem=(0,),
         flops=4 * columns * BLOCK * width,
     )
     (latent_out,) = call(last_kernel, "last_sum", (*mine[::-1], *got[::-1]), [((rows, width), BF16)])

time: 34.5 us -> 34 us (0.986)
  waiting for transfers between devices: 7.34 us -> 6.61 us
    ppermute x3 -> x4, starting transfers between devices: 4.75 us -> 5.26 us  [the longest x2 3.16 us: forward(): return lax.ppermute(x, 'seq', [(i, (i + 1) % n_seq) for i in range(n_seq)])]
    ppermute x2, waiting for transfers between devices: 6.09 us -> 5.66 us  [local(): lax.ppermute(send, 'head', [(j, (j + low) % n_head) for j in range(n_head)])]
    pallas_call x8 -> x9, Pallas kernels: 11.3 us -> 11.4 us  [call(): pl.pallas_call(kernel, name=name, out_shape=shapes, in_specs=[pl.BlockSpe...]
  transfers between devices with their start and end apart: 9 -> 10, of which waited for: 4 -> 4; matrix products, arithmetic and copies ran while one was open for 0% -> 0% of each run, Pallas kernels for 26% -> 27%
where the time goes in v6:
time: 34 us; the launch traced here: 33.9 us
  starting transfers between devices  15.2 us (45%)
  Pallas kernels  11.4 us (34%)
  waiting for transfers between devices  6.61 us (19%)
  between operations  0.73 us (2%)
    pallas_call x9, Pallas kernels, call(): pl.pallas_call(kernel, name=name, out_shape=shapes, in_specs=[pl.BlockSpe...  11.4 us
    ppermute x2, waiting for transfers between devices, local(): lax.ppermute(send, 'head', [(j, (j + low) % n_head) for j in range(n_head)])  5.66 us
    ppermute x2, starting transfers between devices, local(): lax.ppermute(send, 'head', [(j, (j + low) % n_head) for j in range(n_head)])  5.35 us
    ppermute x4, starting transfers between devices, local(): lax.ppermute(far[d], ('seq', 'head'), route(d, 1))  4.56 us
    ppermute x2, starting transfers between devices, forward(): return lax.ppermute(x, 'seq', [(i, (i + 1) % n_seq) for i in range(n_seq)])  3.16 us
    ppermute x2, starting transfers between devices, local(): lax.ppermute(x, ('seq', 'head'), route(d, 0))  2.09 us
    ppermute x4, waiting for transfers between devices, local(): lax.ppermute(far[d], ('seq', 'head'), route(d, 1))  0.94 us
  transfers between devices with their start and end apart: 10, of which 4 were waited for; matrix products, arithmetic and copies ran while one was open for 0% of the time, Pallas kernels for 27%

profile of v6, /device:TPU:0, one launch (start us, length us, event | category | flops | bytes accessed | tf_op | source)
XLA Modules:
  0.0 33.9 jit_solution(12728793197430858161)
XLA Ops:
  0.6 0.0 copy-start
  0.6 0.0 copy-start.1
  0.7 0.0 copy-start.2
  0.7 0.0 copy-start.3
  0.7 0.0 copy-start.4
  0.7 0.0 copy-start.5
  0.7 1.5 %send_block.1 = (bf16[192,576]{1,0:T(8,128)(2,1)S(1)}, bf16[192,576]{1,0:T(8,128)(2,1)S(1)}) custom-call(s32[1,2]{1,0:T(1,128)} %plan_ref.3, bf16[576,768]{1,0:T(8,128)(2,1)} %bitcast.11), custom_call_target="tpu_custom_call" | custom-call | flops 1711276032 | tf_op jit(solution)/shard_map/send_block/pallas_call | solution.py:191
  2.2 0.5 %collective-permute-start = (bf16[192,576]{1,0:T(8,128)(2,1)S(1)}, bf16[192,576]{1,0:T(8,128)(2,1)S(1)}, u32[]{:S(2)}, u32[]{:S(2)}) collective-permute-start(bf16[192,576]{1,0:T(8,128)(2,1)S(1)} %get-tuple-element.28), channel_id=1, source_target_pairs={{0,4},{4,8},{8,12},{12,16},{16,20},{20,24},{24,28},{28,0},{1,5},{5... | collective-permute-start | bytes 663560 | tf_op jit(solution)/shard_map/ppermute | solution.py:240
  2.7 0.0 copy-done
  2.7 0.0 copy-done.1
  2.7 0.0 copy-done.2
  2.7 0.0 copy-done.3
  2.7 0.0 copy-done.4
  2.8 0.0 copy-done.5
  2.8 2.1 %own_visit_0.1 = (bf16[1024,512]{1,0:T(8,128)(2,1)S(1)}, f32[8,576]{1,0:T(8,128)S(1)}, bf16[192,576]{1,0:T(8,128)(2,1)S(1)}, bf16[192,576]{1,0:T(8,128)(2,1)S(1)...) custom-call(s32[1,2]{1,0:T(1,128)S(1)} %copy-done.5, ...), custom_call_target="tpu_custom_call", output_to_operand_aliasing={{7}: (6, {})} | custom-call | tf_op jit(solution)/shard_map/own_visit_0/pallas_call | solution.py:191
  4.8 2.7 %collective-permute-start.1 = (bf16[192,576]{1,0:T(8,128)(2,1)S(1)}, bf16[192,576]{1,0:T(8,128)(2,1)S(1)}, u32[]{:S(2)}, u32[]{:S(2)}) collective-permute-start(bf16[192,576]{1,0:T(8,128)(2,1)S(1)} %get-tuple-element.29), channel_id=1, source_target_pairs={{0,4},{4,8},{8,12},{12,16},{16,20},{20,24},{24,28},{28,0},{1,5},{5... | collective-permute-start | bytes 663560 | tf_op jit(solution)/shard_map/ppermute | solution.py:240
  7.5 1.6 %collective-permute-start.5 = (bf16[96,576]{1,0:T(8,128)(2,1)S(1)}, bf16[96,576]{1,0:T(8,128)(2,1)S(1)}, u32[]{:S(2)}, u32[]{:S(2)}) collective-permute-start(bf16[96,576]{1,0:T(8,128)(2,1)S(1)} %get-tuple-element.42), channel_id=1, source_target_pairs={{0,1},{1,0},{2,3},{3,2},{4,5},{5,4},{6,7},{7,6},{8,9},{9,8},{10,11... | collective-permute-start | bytes 331784 | tf_op jit(solution)/shard_map/ppermute | solution.py:274
  9.1 1.5 %own_visit_1.1 = (bf16[192,1024]{1,0:T(8,128)(2,1)S(1)}, f32[96,576]{1,0:T(8,128)S(1)}, bf16[96,576]{1,0:T(8,128)(2,1)S(1)}) custom-call(s32[1,2]{1,0:T(1,128)S(1)} %copy-done.5, bf16[192,576]{1,0:T(8,128)(2,1)S(1)} %get-tuple-element.27.keys_ref.refs_1_, bf16[8,576,128]{2,1,0:T(8,128)(2,1)S(1)} %bitcast.7, ...), custom_call_target="tpu_custom_call" | custom-call | tf_op jit(solution)/shard_map/own_visit_1/pallas_call | solution.py:191
  10.5 0.5 %collective-permute-start.2 = (bf16[96,576]{1,0:T(8,128)(2,1)S(1)}, bf16[96,576]{1,0:T(8,128)(2,1)S(1)}, u32[]{:S(2)}, u32[]{:S(2)}) collective-permute-start(bf16[96,576]{1,0:T(8,128)(2,1)S(1)} %get-tuple-element.37), channel_id=1, source_target_pairs={{0,1},{1,0},{2,3},{3,2},{4,5},{5,4},{6,7},{7,6},{8,9},{9,8},{10,11... | collective-permute-start | bytes 331784 | tf_op jit(solution)/shard_map/ppermute | solution.py:274
  11.0 0.0 collective-permute-done.keys_ref.refs_2_
  11.1 1.4 %far_visit_0.1 = (bf16[192,1024]{1,0:T(8,128)(2,1)S(1)}, bf16[96,576]{1,0:T(8,128)(2,1)S(1)}, bf16[96,576]{1,0:T(8,128)(2,1)S(1)}) custom-call(bf16[192,576]{1,0:T(8,128)(2,1)S(1)} %collective-permute-done.keys_ref.refs_2_, bf16[8,576,128]{2,1,0:T(8,128)(2,1)S(1)} %bitcast.8, bf16[1024,512]{1,0:T(8,128)(2,1)S(1)} %get-tuple-element.31.rows_ref.grad_ref, ...), custom_call_target="tpu_custom_call" | custom-call | tf_op jit(solution)/shard_map/far_visit_0/pallas_call | solution.py:191
  12.5 2.0 %collective-permute-start.6 = (bf16[96,576]{1,0:T(8,128)(2,1)S(1)}, bf16[96,576]{1,0:T(8,128)(2,1)S(1)}, u32[]{:S(2)}, u32[]{:S(2)}) collective-permute-start(bf16[96,576]{1,0:T(8,128)(2,1)S(1)} %get-tuple-element.43), channel_id=1, source_target_pairs={{0,29},{1,28},{2,31},{3,30},{4,1},{5,0},{6,3},{7,2},{8,5},{9,4},{1... | collective-permute-start | bytes 331784 | tf_op jit(solution)/shard_map/ppermute | solution.py:286
  14.5 0.8 %collective-permute-start.7 = (bf16[96,576]{1,0:T(8,128)(2,1)S(1)}, bf16[96,576]{1,0:T(8,128)(2,1)S(1)}, u32[]{:S(2)}, u32[]{:S(2)}) collective-permute-start(bf16[96,576]{1,0:T(8,128)(2,1)S(1)} %get-tuple-element.44), channel_id=1, source_target_pairs={{0,28},{1,29},{2,30},{3,31},{4,0},{5,1},{6,2},{7,3},{8,4},{9,5},{1... | collective-permute-start | bytes 331784 | tf_op jit(solution)/shard_map/ppermute | solution.py:286
  15.3 0.0 collective-permute-done.1.keys_ref.refs_3_
  15.3 1.5 %far_visit_1.1 = (bf16[192,1024]{1,0:T(8,128)(2,1)S(1)}, bf16[96,576]{1,0:T(8,128)(2,1)S(1)}, bf16[96,576]{1,0:T(8,128)(2,1)S(1)}) custom-call(bf16[192,576]{1,0:T(8,128)(2,1)S(1)} %collective-permute-done.1.keys_ref.refs_3_, bf16[8,576,128]{2,1,0:T(8,128)(2,1)S(1)} %bitcast.9, bf16[1024,512]{1,0:T(8,128)(2,1)S(1)} %get-tuple-element.31.rows_ref.grad_ref, ...), custom_call_target="tpu_custom_call" | custom-call | tf_op jit(solution)/shard_map/far_visit_1/pallas_call | solution.py:191
  16.8 0.8 %collective-permute-start.3 = (bf16[96,576]{1,0:T(8,128)(2,1)S(1)}, bf16[96,576]{1,0:T(8,128)(2,1)S(1)}, u32[]{:S(2)}, u32[]{:S(2)}) collective-permute-start(bf16[96,576]{1,0:T(8,128)(2,1)S(1)} %get-tuple-element.38), channel_id=1, source_target_pairs={{0,29},{1,28},{2,31},{3,30},{4,1},{5,0},{6,3},{7,2},{8,5},{9,4},{1... | collective-permute-start | bytes 331784 | tf_op jit(solution)/shard_map/ppermute | solution.py:286
  17.6 0.0 collective-permute-done.5.rest_1_
  17.6 1.0 %collective-permute-start.4 = (bf16[96,576]{1,0:T(8,128)(2,1)S(1)}, bf16[96,576]{1,0:T(8,128)(2,1)S(1)}, u32[]{:S(2)}, u32[]{:S(2)}) collective-permute-start(bf16[96,576]{1,0:T(8,128)(2,1)S(1)} %get-tuple-element.39), channel_id=1, source_target_pairs={{0,28},{1,29},{2,30},{3,31},{4,0},{5,1},{6,2},{7,3},{8,4},{9,5},{1... | collective-permute-start | bytes 331784 | tf_op jit(solution)/shard_map/ppermute | solution.py:286
  18.5 0.0 collective-permute-done.6.rest_2_
  18.5 0.0 collective-permute-done.7.rest_3_
  18.5 0.1 combine_0.1
  18.6 2.7 %collective-permute-start.9 = (bf16[96,576]{1,0:T(8,128)(2,1)S(1)}, bf16[96,576]{1,0:T(8,128)(2,1)S(1)}, u32[]{:S(2)}, u32[]{:S(2)}) collective-permute-start(bf16[96,576]{1,0:T(8,128)(2,1)S(1)} %get-tuple-element.47), channel_id=1, source_target_pairs={{0,2},{1,3},{2,0},{3,1},{4,6},{5,7},{6,4},{7,5},{8,10},{9,11},{10,... | collective-permute-start | bytes 331784 | tf_op jit(solution)/shard_map/ppermute | solution.py:296
  21.3 0.0 collective-permute-done.2.rest_1_
  21.3 0.3 collective-permute-done.3.rest_2_
  21.6 0.7 %collective-permute-done.4.rest_3_ = bf16[96,576]{1,0:T(8,128)(2,1)S(1)} collective-permute-done((bf16[96,576]{1,0:T(8,128)(2,1)S(1)}, bf16[96,576]{1,0:T(8,128)(2,1)S(1)}, u32[]{:S(2)}, u32[]{:S(2)}) %collective-permute-start.4) | collective-permute-done | bytes 110624 | tf_op jit(solution)/shard_map/ppermute | solution.py:286
  22.2 0.1 combine_1.1
  22.3 2.7 %collective-permute-start.8 = (bf16[96,576]{1,0:T(8,128)(2,1)S(1)}, bf16[96,576]{1,0:T(8,128)(2,1)S(1)}, u32[]{:S(2)}, u32[]{:S(2)}) collective-permute-start(bf16[96,576]{1,0:T(8,128)(2,1)S(1)} %get-tuple-element.46), channel_id=1, source_target_pairs={{0,2},{1,3},{2,0},{3,1},{4,6},{5,7},{6,4},{7,5},{8,10},{9,11},{10,... | collective-permute-start | bytes 331784 | tf_op jit(solution)/shard_map/ppermute | solution.py:296
  25.0 2.4 %query_grad.1 = bf16[8,576,128]{2,1,0:T(8,128)(2,1)} custom-call(bf16[192,576]{1,0:T(8,128)(2,1)S(1)} %get-tuple-element.26.refs_0_, bf16[192,576]{1,0:T(8,128)(2,1)S(1)} %get-tuple-element.27.keys_ref.refs_1_, bf16[192,576]{1,0:T(8,128)(2,1)S(1)} %collective-permute-done.keys_ref.refs_2_, bf16[192,576]{1,0:T(8,128)(2,1)S(1)} %collective-permute-done.1.keys_ref.refs_3_, ...), custom_call_target="tpu_custom_call" | custom-call | flops 905969664 | tf_op jit(solution)/shard_map/query_grad/pallas_call | solution.py:191
  27.5 3.0 %collective-permute-done.9.refs_3_ = bf16[96,576]{1,0:T(8,128)(2,1)S(1)} collective-permute-done((bf16[96,576]{1,0:T(8,128)(2,1)S(1)}, bf16[96,576]{1,0:T(8,128)(2,1)S(1)}, u32[]{:S(2)}, u32[]{:S(2)}) %collective-permute-start.9) | collective-permute-done | bytes 110624 | tf_op jit(solution)/shard_map/ppermute | solution.py:296
  30.5 2.6 %collective-permute-done.8.refs_2_ = bf16[96,576]{1,0:T(8,128)(2,1)S(1)} collective-permute-done((bf16[96,576]{1,0:T(8,128)(2,1)S(1)}, bf16[96,576]{1,0:T(8,128)(2,1)S(1)}, u32[]{:S(2)}, u32[]{:S(2)}) %collective-permute-start.8) | collective-permute-done | bytes 110624 | tf_op jit(solution)/shard_map/ppermute | solution.py:296
  33.1 0.7 %last_sum.1 = bf16[192,576]{1,0:T(8,128)(2,1)} custom-call(f32[96,576]{1,0:T(8,128)S(1)} %get-tuple-element.40.refs_0_, f32[96,576]{1,0:T(8,128)S(1)} %get-tuple-element.45.refs_1_, bf16[96,576]{1,0:T(8,128)(2,1)S(1)} %collective-permute-done.8.refs_2_, bf16[96,576]{1,0:T(8,128)(2,1)S(1)} %collective-permute-done.9.refs_3_), custom_call_target="tpu_custom_call" | custom-call | tf_op jit(solution)/shard_map/last_sum/pallas_call | solution.py:191
Async XLA Ops:
  0.6 2.1 %copy-start = (bf16[128,8,576]{0,2,1:T(8,128)(2,1)S(1)}, bf16[128,8,576]{0,2,1:T(8,128)(2,1)}, u32[]{:S(2)}) copy-start(bf16[128,8,576]{0,2,1:T(8,128)(2,1)} %param.6) | copy-start | bytes 3538948
  0.6 2.1 %copy-start.1 = (bf16[128,8,512]{2,1,0:T(8,128)(2,1)S(1)}, bf16[128,8,512]{2,1,0:T(8,128)(2,1)}, u32[]{:S(2)}) copy-start(bf16[128,8,512]{2,1,0:T(8,128)(2,1)} %param.7) | copy-start | bytes 3145732
  0.7 2.1 %copy-start.2 = (bf16[768,576]{0,1:T(8,128)(2,1)S(1)}, bf16[768,576]{0,1:T(8,128)(2,1)}, u32[]{:S(2)}) copy-start(bf16[768,576]{0,1:T(8,128)(2,1)} %param.8) | copy-start | bytes 2654212
  0.7 2.1 %copy-start.3 = (bf16[128,8]{0,1:T(8,128)(2,1)S(1)}, bf16[128,8]{0,1:T(8,128)(2,1)}, u32[]{:S(2)}) copy-start(bf16[128,8]{0,1:T(8,128)(2,1)} %param.9) | copy-start | bytes 6148
  0.7 2.1 %copy-start.4 = (bf16[128,8]{0,1:T(8,128)(2,1)S(1)}, bf16[128,8]{0,1:T(8,128)(2,1)}, u32[]{:S(2)}) copy-start(bf16[128,8]{0,1:T(8,128)(2,1)} %param.10) | copy-start | bytes 6148
  0.7 2.1 %copy-start.5 = (s32[1,2]{1,0:T(1,128)S(1)}, s32[1,2]{1,0:T(1,128)}, u32[]{:S(2)}) copy-start(s32[1,2]{1,0:T(1,128)} %plan_ref.3) | copy-start | bytes 28
  2.2 8.8 %collective-permute-start = (bf16[192,576]{1,0:T(8,128)(2,1)S(1)}, bf16[192,576]{1,0:T(8,128)(2,1)S(1)}, u32[]{:S(2)}, u32[]{:S(2)}) collective-permute-start(bf16[192,576]{1,0:T(8,128)(2,1)S(1)} %get-tuple-element.28), channel_id=1, source_target_pairs={{0,4},{4,8},{8,12},{12,16},{16,20},{20,24},{24,28},{28,0},{1,5},{5... | collective-permute-start | bytes 663560 | tf_op jit(solution)/shard_map/ppermute | solution.py:240
  4.8 10.4 %collective-permute-start.1 = (bf16[192,576]{1,0:T(8,128)(2,1)S(1)}, bf16[192,576]{1,0:T(8,128)(2,1)S(1)}, u32[]{:S(2)}, u32[]{:S(2)}) collective-permute-start(bf16[192,576]{1,0:T(8,128)(2,1)S(1)} %get-tuple-element.29), channel_id=1, source_target_pairs={{0,4},{4,8},{8,12},{12,16},{16,20},{20,24},{24,28},{28,0},{1,5},{5... | collective-permute-start | bytes 663560 | tf_op jit(solution)/shard_map/ppermute | solution.py:240
  7.5 10.1 %collective-permute-start.5 = (bf16[96,576]{1,0:T(8,128)(2,1)S(1)}, bf16[96,576]{1,0:T(8,128)(2,1)S(1)}, u32[]{:S(2)}, u32[]{:S(2)}) collective-permute-start(bf16[96,576]{1,0:T(8,128)(2,1)S(1)} %get-tuple-element.42), channel_id=1, source_target_pairs={{0,1},{1,0},{2,3},{3,2},{4,5},{5,4},{6,7},{7,6},{8,9},{9,8},{10,11... | collective-permute-start | bytes 331784 | tf_op jit(solution)/shard_map/ppermute | solution.py:274
  10.5 10.8 %collective-permute-start.2 = (bf16[96,576]{1,0:T(8,128)(2,1)S(1)}, bf16[96,576]{1,0:T(8,128)(2,1)S(1)}, u32[]{:S(2)}, u32[]{:S(2)}) collective-permute-start(bf16[96,576]{1,0:T(8,128)(2,1)S(1)} %get-tuple-element.37), channel_id=1, source_target_pairs={{0,1},{1,0},{2,3},{3,2},{4,5},{5,4},{6,7},{7,6},{8,9},{9,8},{10,11... | collective-permute-start | bytes 331784 | tf_op jit(solution)/shard_map/ppermute | solution.py:274
  12.5 6.0 %collective-permute-start.6 = (bf16[96,576]{1,0:T(8,128)(2,1)S(1)}, bf16[96,576]{1,0:T(8,128)(2,1)S(1)}, u32[]{:S(2)}, u32[]{:S(2)}) collective-permute-start(bf16[96,576]{1,0:T(8,128)(2,1)S(1)} %get-tuple-element.43), channel_id=1, source_target_pairs={{0,29},{1,28},{2,31},{3,30},{4,1},{5,0},{6,3},{7,2},{8,5},{9,4},{1... | collective-permute-start | bytes 331784 | tf_op jit(solution)/shard_map/ppermute | solution.py:286
  14.5 4.0 %collective-permute-start.7 = (bf16[96,576]{1,0:T(8,128)(2,1)S(1)}, bf16[96,576]{1,0:T(8,128)(2,1)S(1)}, u32[]{:S(2)}, u32[]{:S(2)}) collective-permute-start(bf16[96,576]{1,0:T(8,128)(2,1)S(1)} %get-tuple-element.44), channel_id=1, source_target_pairs={{0,28},{1,29},{2,30},{3,31},{4,0},{5,1},{6,2},{7,3},{8,4},{9,5},{1... | collective-permute-start | bytes 331784 | tf_op jit(solution)/shard_map/ppermute | solution.py:286
  16.8 4.8 %collective-permute-start.3 = (bf16[96,576]{1,0:T(8,128)(2,1)S(1)}, bf16[96,576]{1,0:T(8,128)(2,1)S(1)}, u32[]{:S(2)}, u32[]{:S(2)}) collective-permute-start(bf16[96,576]{1,0:T(8,128)(2,1)S(1)} %get-tuple-element.38), channel_id=1, source_target_pairs={{0,29},{1,28},{2,31},{3,30},{4,1},{5,0},{6,3},{7,2},{8,5},{9,4},{1... | collective-permute-start | bytes 331784 | tf_op jit(solution)/shard_map/ppermute | solution.py:286
  17.6 4.7 %collective-permute-start.4 = (bf16[96,576]{1,0:T(8,128)(2,1)S(1)}, bf16[96,576]{1,0:T(8,128)(2,1)S(1)}, u32[]{:S(2)}, u32[]{:S(2)}) collective-permute-start(bf16[96,576]{1,0:T(8,128)(2,1)S(1)} %get-tuple-element.39), channel_id=1, source_target_pairs={{0,28},{1,29},{2,30},{3,31},{4,0},{5,1},{6,2},{7,3},{8,4},{9,5},{1... | collective-permute-start | bytes 331784 | tf_op jit(solution)/shard_map/ppermute | solution.py:286
  18.6 11.9 %collective-permute-start.9 = (bf16[96,576]{1,0:T(8,128)(2,1)S(1)}, bf16[96,576]{1,0:T(8,128)(2,1)S(1)}, u32[]{:S(2)}, u32[]{:S(2)}) collective-permute-start(bf16[96,576]{1,0:T(8,128)(2,1)S(1)} %get-tuple-element.47), channel_id=1, source_target_pairs={{0,2},{1,3},{2,0},{3,1},{4,6},{5,7},{6,4},{7,5},{8,10},{9,11},{10,... | collective-permute-start | bytes 331784 | tf_op jit(solution)/shard_map/ppermute | solution.py:296
  22.3 10.8 %collective-permute-start.8 = (bf16[96,576]{1,0:T(8,128)(2,1)S(1)}, bf16[96,576]{1,0:T(8,128)(2,1)S(1)}, u32[]{:S(2)}, u32[]{:S(2)}) collective-permute-start(bf16[96,576]{1,0:T(8,128)(2,1)S(1)} %get-tuple-element.46), channel_id=1, source_target_pairs={{0,2},{1,3},{2,0},{3,1},{4,6},{5,7},{6,4},{7,5},{8,10},{9,11},{10,... | collective-permute-start | bytes 331784 | tf_op jit(solution)/shard_map/ppermute | solution.py:296

commit v7 on v6

--- a/solution.py
+++ b/solution.py
@@ -15,7 +15,10 @@
 VMEM_LIMIT = 24 * 2**20
 NEVER = 1e30
 CHUNKS = 2
-FIRST_SHARE = 1 / 2
+FIRST_SHARE = 5 / 12
+COST_SUM = 10**9
+COST_COMBINE = 10**9
+COST_OWN = 3 * 10**9
 
 F32 = jnp.float32
 BF16 = jnp.bfloat16
@@ -45,16 +48,22 @@
 def send_block_kernel(low, plan_hbm, lat_hbm, *rest):
     out_refs = rest[:CHUNKS]
     plan_ref, lat_ref, sems = rest[CHUNKS:]
-    copies = [
-        pltpu.make_async_copy(plan_hbm, plan_ref, sems.at[0]),
-        pltpu.make_async_copy(lat_hbm, lat_ref, sems.at[1]),
-    ]
-    for copy in copies:
-        copy.start()
-    for copy in copies:
-        copy.wait()
-    block = pl.multiple_of(plan_ref[0, 1] * BLOCK, 128)
-    chunk_rows(lat_ref[:, pl.ds(block, BLOCK)].T, low, out_refs)
+
+    def block_copy(block):
+        here = pl.ds(pl.multiple_of(block * BLOCK, 128), BLOCK)
+        return pltpu.make_async_copy(lat_hbm.at[:, here], lat_ref.at[block], sems.at[block])
+
+    blocks = lat_ref.shape[0]
+    plan_copy = pltpu.make_async_copy(plan_hbm, plan_ref, sems.at[blocks])
+    plan_copy.start()
+    for block in range(blocks):
+        block_copy(block).start()
+    plan_copy.wait()
+    sent = plan_ref[0, 1]
+    block_copy(sent).wait()
+    chunk_rows(lat_ref[sent].T, low, out_refs)
+    for i in range(1, blocks):
+        block_copy(lax.rem(sent + i, blocks)).wait()
 
 
 def heads_side_by_side(q_ref, first, count):
@@ -174,10 +183,16 @@
     mine_ref[...] = own * sel_ref[0:1, :] + far * sel_ref[2:3, :]
 
 
+def first_sum_kernel(mine_ref, got_ref, out_ref):
+    out_ref[...] = (mine_ref[...] + got_ref[...].astype(F32)).astype(BF16)
+
+
 def last_kernel(*refs):
-    mine_refs, got_refs, out_ref = refs[:CHUNKS][::-1], refs[CHUNKS : 2 * CHUNKS][::-1], refs[-1]
-    for (offset, part), mine_ref, got_ref in zip(chunks_of(out_ref.shape[0]), mine_refs, got_refs):
-        out_ref[offset : offset + part, :] = (mine_ref[...] + got_ref[...].astype(F32)).astype(BF16)
+    *done_refs, mine_ref, got_ref, out_ref = refs
+    *firsts, (offset, part) = chunks_of(out_ref.shape[0])
+    for (at, size), done_ref in zip(firsts, done_refs):
+        out_ref[at : at + size, :] = done_ref[...]
+    out_ref[offset : offset + part, :] = (mine_ref[...] + got_ref[...].astype(F32)).astype(BF16)
 
 
 def call(kernel, name, ins, outs, scratch=(), raw=(), passed=(), flops=0, size=0):
@@ -225,13 +240,14 @@
         return pairs
 
     chunks = chunks_of(rows)
+    blocks = SHARD // BLOCK
 
     sent = call(
         functools.partial(send_block_kernel, low),
         "send_block",
         (plan, lat_t),
         [((low * part, width), BF16) for _, part in chunks],
-        [pltpu.SMEM(plan.shape, plan.dtype), pltpu.VMEM(lat_t.shape, BF16), pltpu.SemaphoreType.DMA((2,))],
+        [pltpu.SMEM(plan.shape, plan.dtype), pltpu.VMEM((blocks, width, BLOCK), BF16), pltpu.SemaphoreType.DMA((blocks + 1,))],
         flops=visit_flops,
         raw=(0, 1),
     )
@@ -266,6 +282,7 @@
                 (plan, own_keys[c], q_t, grad_rows, norm_t, delta_t),
                 own_outs(part),
                 scratch(part),
+                flops=COST_OWN,
             )
         )
     own_parts = []
@@ -292,6 +309,7 @@
             f"combine_{c}",
             (sel, *own_parts[c], *far_parts[c]),
             [((part, width), BF16), ((part, width), F32)],
+            flops=COST_COMBINE,
         )
         got[c] = lax.ppermute(send, "head", [(j, (j + low) % n_head) for j in range(n_head)])
 
@@ -302,7 +320,11 @@
         [((heads, width, packet), BF16)],
         flops=4 * columns * BLOCK * width,
     )
-    (latent_out,) = call(last_kernel, "last_sum", (*mine[::-1], *got[::-1]), [((rows, width), BF16)])
+    done = [
+        call(first_sum_kernel, f"sum_{c}", (mine[c], got[c]), [((part, width), BF16)], flops=COST_SUM)[0]
+        for c, (_, part) in list(enumerate(chunks))[:-1]
+    ]
+    (latent_out,) = call(last_kernel, "last_sum", (*done, mine[-1], got[-1]), [((rows, width), BF16)])
     return jnp.transpose(query_t, (2, 0, 1)), latent_out
 
 

time: 34 us -> 35.2 us (1.035)
  waiting for transfers between devices: 6.61 us -> 9.44 us
  starting transfers between devices: 15.2 us -> 13.4 us
    ppermute x4, waiting for transfers between devices: 0.94 us -> 3.33 us  [local(): lax.ppermute(far[d], ('seq', 'head'), route(d, 1))]
    ppermute x2, starting transfers between devices: 5.35 us -> 3.35 us  [local(): lax.ppermute(send, 'head', [(j, (j + low) % n_head) for j in range(n_head)])]
    ppermute x2, starting transfers between devices: 2.09 us -> 2.77 us  [local(): lax.ppermute(x, ('seq', 'head'), route(d, 0))]
    ppermute x2, waiting for transfers between devices: 5.66 us -> 6.09 us  [local(): lax.ppermute(send, 'head', [(j, (j + low) % n_head) for j in range(n_head)])]
    pallas_call x9 -> x10, Pallas kernels: 11.4 us -> 11.4 us  [call(): pl.pallas_call(kernel, name=name, out_shape=shapes, in_specs=[pl.BlockSpe...]
  transfers between devices with their start and end apart: 10 -> 10, of which waited for: 4 -> 2; matrix products, arithmetic and copies ran while one was open for 0% -> 0% of each run, Pallas kernels for 27% -> 26%
where the time goes in v7:
time: 35.2 us; the launch traced here: 35 us
  starting transfers between devices  13.4 us (38%)
  Pallas kernels  11.4 us (32%)
  waiting for transfers between devices  9.44 us (27%)
  between operations  0.74 us (2%)
    pallas_call x10, Pallas kernels, call(): pl.pallas_call(kernel, name=name, out_shape=shapes, in_specs=[pl.BlockSpe...  11.4 us
    ppermute x2, waiting for transfers between devices, local(): lax.ppermute(send, 'head', [(j, (j + low) % n_head) for j in range(n_head)])  6.09 us
    ppermute x4, starting transfers between devices, local(): lax.ppermute(far[d], ('seq', 'head'), route(d, 1))  4.23 us
    ppermute x2, starting transfers between devices, local(): lax.ppermute(send, 'head', [(j, (j + low) % n_head) for j in range(n_head)])  3.35 us
    ppermute x4, waiting for transfers between devices, local(): lax.ppermute(far[d], ('seq', 'head'), route(d, 1))  3.33 us
    ppermute x2, starting transfers between devices, forward(): return lax.ppermute(x, 'seq', [(i, (i + 1) % n_seq) for i in range(n_seq)])  3.02 us
    ppermute x2, starting transfers between devices, local(): lax.ppermute(x, ('seq', 'head'), route(d, 0))  2.77 us
  transfers between devices with their start and end apart: 10, of which 2 were waited for; matrix products, arithmetic and copies ran while one was open for 0% of the time, Pallas kernels for 26%

profile of v7, /device:TPU:0, one launch (start us, length us, event | category | flops | bytes accessed | tf_op | source)
XLA Modules:
  0.0 35.0 jit_solution(4814691580543141011)
XLA Ops:
  0.6 0.0 copy-start
  0.6 0.0 copy-start.1
  0.7 0.0 copy-start.2
  0.7 0.0 copy-start.3
  0.7 0.0 copy-start.4
  0.7 0.0 copy-start.5
  0.7 1.5 %send_block.1 = (bf16[160,576]{1,0:T(8,128)(2,1)S(1)}, bf16[224,576]{1,0:T(8,128)(2,1)S(1)}) custom-call(s32[1,2]{1,0:T(1,128)} %plan_ref.3, bf16[576,768]{1,0:T(8,128)(2,1)} %bitcast.11), custom_call_target="tpu_custom_call" | custom-call | flops 1711276032 | tf_op jit(solution)/shard_map/send_block/pallas_call | solution.py:206
  2.2 0.5 %collective-permute-start = (bf16[160,576]{1,0:T(8,128)(2,1)S(1)}, bf16[160,576]{1,0:T(8,128)(2,1)S(1)}, u32[]{:S(2)}, u32[]{:S(2)}) collective-permute-start(bf16[160,576]{1,0:T(8,128)(2,1)S(1)} %get-tuple-element.28), channel_id=1, source_target_pairs={{0,4},{4,8},{8,12},{12,16},{16,20},{20,24},{24,28},{28,0},{1,5},{5... | collective-permute-start | bytes 552968 | tf_op jit(solution)/shard_map/ppermute | solution.py:256
  2.7 0.0 copy-done
  2.7 0.0 copy-done.1
  2.7 0.0 copy-done.2
  2.7 0.0 copy-done.3
  2.7 0.0 copy-done.4
  2.7 0.0 copy-done.5
  2.8 1.9 %own_visit_0.1 = (bf16[1024,512]{1,0:T(8,128)(2,1)S(1)}, f32[8,576]{1,0:T(8,128)S(1)}, bf16[160,576]{1,0:T(8,128)(2,1)S(1)}, bf16[224,576]{1,0:T(8,128)(2,1)S(1)...) custom-call(s32[1,2]{1,0:T(1,128)S(1)} %copy-done.5, ...), custom_call_target="tpu_custom_call", output_to_operand_aliasing={{7}: (6, {})} | custom-call | tf_op jit(solution)/shard_map/own_visit_0/pallas_call | solution.py:206
  4.6 2.5 %collective-permute-start.1 = (bf16[224,576]{1,0:T(8,128)(2,1)S(1)}, bf16[224,576]{1,0:T(8,128)(2,1)S(1)}, u32[]{:S(2)}, u32[]{:S(2)}) collective-permute-start(bf16[224,576]{1,0:T(8,128)(2,1)S(1)} %get-tuple-element.29), channel_id=1, source_target_pairs={{0,4},{4,8},{8,12},{12,16},{16,20},{20,24},{24,28},{28,0},{1,5},{5... | collective-permute-start | bytes 774152 | tf_op jit(solution)/shard_map/ppermute | solution.py:256
  7.1 1.6 %collective-permute-start.2 = (bf16[80,576]{1,0:T(8,128)(2,1)S(1)}, bf16[80,576]{1,0:T(8,128)(2,1)S(1)}, u32[]{:S(2)}, u32[]{:S(2)}) collective-permute-start(bf16[80,576]{1,0:T(8,128)(2,1)S(1)} %get-tuple-element.37), channel_id=1, source_target_pairs={{0,1},{1,0},{2,3},{3,2},{4,5},{5,4},{6,7},{7,6},{8,9},{9,8},{10,11... | collective-permute-start | bytes 276488 | tf_op jit(solution)/shard_map/ppermute | solution.py:291
  8.7 1.7 %own_visit_1.1 = (bf16[224,1024]{1,0:T(8,128)(2,1)S(1)}, f32[112,576]{1,0:T(8,128)S(1)}, bf16[112,576]{1,0:T(8,128)(2,1)S(1)}) custom-call(s32[1,2]{1,0:T(1,128)S(1)} %copy-done.5, bf16[224,576]{1,0:T(8,128)(2,1)S(1)} %get-tuple-element.27.keys_ref.refs_1_, bf16[8,576,128]{2,1,0:T(8,128)(2,1)S(1)} %bitcast.7, ...), custom_call_target="tpu_custom_call" | custom-call | flops 3000000000 | tf_op jit(solution)/shard_map/own_visit_1/pallas_call | solution.py:206
  10.4 0.0 collective-permute-done.keys_ref.refs_2_
  10.4 1.3 %far_visit_0.1 = (bf16[160,1024]{1,0:T(8,128)(2,1)S(1)}, bf16[80,576]{1,0:T(8,128)(2,1)S(1)}, bf16[80,576]{1,0:T(8,128)(2,1)S(1)}) custom-call(bf16[160,576]{1,0:T(8,128)(2,1)S(1)} %collective-permute-done.keys_ref.refs_2_, bf16[8,576,128]{2,1,0:T(8,128)(2,1)S(1)} %bitcast.8, bf16[1024,512]{1,0:T(8,128)(2,1)S(1)} %get-tuple-element.31.rows_ref.grad_ref, ...), custom_call_target="tpu_custom_call" | custom-call | tf_op jit(solution)/shard_map/far_visit_0/pallas_call | solution.py:206
  11.7 1.1 %collective-permute-start.3 = (bf16[80,576]{1,0:T(8,128)(2,1)S(1)}, bf16[80,576]{1,0:T(8,128)(2,1)S(1)}, u32[]{:S(2)}, u32[]{:S(2)}) collective-permute-start(bf16[80,576]{1,0:T(8,128)(2,1)S(1)} %get-tuple-element.38), channel_id=1, source_target_pairs={{0,29},{1,28},{2,31},{3,30},{4,1},{5,0},{6,3},{7,2},{8,5},{9,4},{1... | collective-permute-start | bytes 276488 | tf_op jit(solution)/shard_map/ppermute | solution.py:303
  12.8 1.1 %collective-permute-start.4 = (bf16[80,576]{1,0:T(8,128)(2,1)S(1)}, bf16[80,576]{1,0:T(8,128)(2,1)S(1)}, u32[]{:S(2)}, u32[]{:S(2)}) collective-permute-start(bf16[80,576]{1,0:T(8,128)(2,1)S(1)} %get-tuple-element.39), channel_id=1, source_target_pairs={{0,28},{1,29},{2,30},{3,31},{4,0},{5,1},{6,2},{7,3},{8,4},{9,5},{1... | collective-permute-start | bytes 276488 | tf_op jit(solution)/shard_map/ppermute | solution.py:303
  13.9 1.2 %collective-permute-start.6 = (bf16[112,576]{1,0:T(8,128)(2,1)S(1)}, bf16[112,576]{1,0:T(8,128)(2,1)S(1)}, u32[]{:S(2)}, u32[]{:S(2)}) collective-permute-start(bf16[112,576]{1,0:T(8,128)(2,1)S(1)} %get-tuple-element.43), channel_id=1, source_target_pairs={{0,1},{1,0},{2,3},{3,2},{4,5},{5,4},{6,7},{7,6},{8,9},{9,8},{10,11... | collective-permute-start | bytes 387080 | tf_op jit(solution)/shard_map/ppermute | solution.py:291
  15.1 0.0 collective-permute-done.1.keys_ref.refs_3_
  15.1 1.6 %far_visit_1.1 = (bf16[224,1024]{1,0:T(8,128)(2,1)S(1)}, bf16[112,576]{1,0:T(8,128)(2,1)S(1)}, bf16[112,576]{1,0:T(8,128)(2,1)S(1)}) custom-call(bf16[224,576]{1,0:T(8,128)(2,1)S(1)} %collective-permute-done.1.keys_ref.refs_3_, bf16[8,576,128]{2,1,0:T(8,128)(2,1)S(1)} %bitcast.9, bf16[1024,512]{1,0:T(8,128)(2,1)S(1)} %get-tuple-element.31.rows_ref.grad_ref, ...), custom_call_target="tpu_custom_call" | custom-call | tf_op jit(solution)/shard_map/far_visit_1/pallas_call | solution.py:206
  16.7 0.8 %collective-permute-start.7 = (bf16[112,576]{1,0:T(8,128)(2,1)S(1)}, bf16[112,576]{1,0:T(8,128)(2,1)S(1)}, u32[]{:S(2)}, u32[]{:S(2)}) collective-permute-start(bf16[112,576]{1,0:T(8,128)(2,1)S(1)} %get-tuple-element.44), channel_id=1, source_target_pairs={{0,29},{1,28},{2,31},{3,30},{4,1},{5,0},{6,3},{7,2},{8,5},{9,4},{1... | collective-permute-start | bytes 387080 | tf_op jit(solution)/shard_map/ppermute | solution.py:303
  17.5 0.0 collective-permute-done.2.rest_1_
  17.5 1.2 %collective-permute-start.8 = (bf16[112,576]{1,0:T(8,128)(2,1)S(1)}, bf16[112,576]{1,0:T(8,128)(2,1)S(1)}, u32[]{:S(2)}, u32[]{:S(2)}) collective-permute-start(bf16[112,576]{1,0:T(8,128)(2,1)S(1)} %get-tuple-element.45), channel_id=1, source_target_pairs={{0,28},{1,29},{2,30},{3,31},{4,0},{5,1},{6,2},{7,3},{8,4},{9,5},{1... | collective-permute-start | bytes 387080 | tf_op jit(solution)/shard_map/ppermute | solution.py:303
  18.8 0.0 collective-permute-done.3.rest_2_
  18.8 0.0 collective-permute-done.4.rest_3_
  18.8 0.1 combine_0.1
  18.9 2.7 %collective-permute-start.5 = (bf16[80,576]{1,0:T(8,128)(2,1)S(1)}, bf16[80,576]{1,0:T(8,128)(2,1)S(1)}, u32[]{:S(2)}, u32[]{:S(2)}) collective-permute-start(bf16[80,576]{1,0:T(8,128)(2,1)S(1)} %get-tuple-element.41), channel_id=1, source_target_pairs={{0,2},{1,3},{2,0},{3,1},{4,6},{5,7},{6,4},{7,5},{8,10},{9,11},{10,... | collective-permute-start | bytes 276488 | tf_op jit(solution)/shard_map/ppermute | solution.py:314
  21.5 0.0 collective-permute-done.6.rest_1_
  21.5 3.3 %collective-permute-done.7.rest_2_ = bf16[112,576]{1,0:T(8,128)(2,1)S(1)} collective-permute-done((bf16[112,576]{1,0:T(8,128)(2,1)S(1)}, bf16[112,576]{1,0:T(8,128)(2,1)S(1)}, u32[]{:S(2)}, u32[]{:S(2)}) %collective-permute-start.7) | collective-permute-done | bytes 129056 | tf_op jit(solution)/shard_map/ppermute | solution.py:303
  24.9 0.0 collective-permute-done.8.rest_3_
  24.9 0.1 combine_1.1
  25.0 0.7 %collective-permute-start.9 = (bf16[112,576]{1,0:T(8,128)(2,1)S(1)}, bf16[112,576]{1,0:T(8,128)(2,1)S(1)}, u32[]{:S(2)}, u32[]{:S(2)}) collective-permute-start(bf16[112,576]{1,0:T(8,128)(2,1)S(1)} %get-tuple-element.47), channel_id=1, source_target_pairs={{0,2},{1,3},{2,0},{3,1},{4,6},{5,7},{6,4},{7,5},{8,10},{9,11},{10,... | collective-permute-start | bytes 387080 | tf_op jit(solution)/shard_map/ppermute | solution.py:314
  25.7 2.4 %query_grad.1 = bf16[8,576,128]{2,1,0:T(8,128)(2,1)} custom-call(bf16[160,576]{1,0:T(8,128)(2,1)S(1)} %get-tuple-element.26.refs_0_, bf16[224,576]{1,0:T(8,128)(2,1)S(1)} %get-tuple-element.27.keys_ref.refs_1_, bf16[160,576]{1,0:T(8,128)(2,1)S(1)} %collective-permute-done.keys_ref.refs_2_, bf16[224,576]{1,0:T(8,128)(2,1)S(1)} %collective-permute-done.1.keys_ref.refs_3_, ...), custom_call_target="tpu_custom_call" | custom-call | flops 905969664 | tf_op jit(solution)/shard_map/query_grad/pallas_call | solution.py:206
  28.1 0.0 collective-permute-done.5.got_ref
  28.2 6.1 %collective-permute-done.9.refs_2_ = bf16[112,576]{1,0:T(8,128)(2,1)S(1)} collective-permute-done((bf16[112,576]{1,0:T(8,128)(2,1)S(1)}, bf16[112,576]{1,0:T(8,128)(2,1)S(1)}, u32[]{:S(2)}, u32[]{:S(2)}) %collective-permute-start.9) | collective-permute-done | bytes 129056 | tf_op jit(solution)/shard_map/ppermute | solution.py:314
  34.3 0.7 %last_sum.1 = bf16[192,576]{1,0:T(8,128)(2,1)} custom-call(bf16[80,576]{1,0:T(8,128)(2,1)S(1)} %sum_0.1.refs_0_, f32[112,576]{1,0:T(8,128)S(1)} %get-tuple-element.46.refs_1_, bf16[112,576]{1,0:T(8,128)(2,1)S(1)} %collective-permute-done.9.refs_2_), custom_call_target="tpu_custom_call" | custom-call | tf_op jit(solution)/shard_map/last_sum/pallas_call | solution.py:206
  (1 shorter events, 0.0 us)
Async XLA Ops:
  0.6 2.1 %copy-start = (bf16[128,8,576]{0,2,1:T(8,128)(2,1)S(1)}, bf16[128,8,576]{0,2,1:T(8,128)(2,1)}, u32[]{:S(2)}) copy-start(bf16[128,8,576]{0,2,1:T(8,128)(2,1)} %param.6) | copy-start | bytes 3538948
  0.6 2.1 %copy-start.1 = (bf16[128,8,512]{2,1,0:T(8,128)(2,1)S(1)}, bf16[128,8,512]{2,1,0:T(8,128)(2,1)}, u32[]{:S(2)}) copy-start(bf16[128,8,512]{2,1,0:T(8,128)(2,1)} %param.7) | copy-start | bytes 3145732
  0.7 2.1 %copy-start.2 = (bf16[768,576]{0,1:T(8,128)(2,1)S(1)}, bf16[768,576]{0,1:T(8,128)(2,1)}, u32[]{:S(2)}) copy-start(bf16[768,576]{0,1:T(8,128)(2,1)} %param.8) | copy-start | bytes 2654212
  0.7 2.1 %copy-start.3 = (bf16[128,8]{0,1:T(8,128)(2,1)S(1)}, bf16[128,8]{0,1:T(8,128)(2,1)}, u32[]{:S(2)}) copy-start(bf16[128,8]{0,1:T(8,128)(2,1)} %param.9) | copy-start | bytes 6148
  0.7 2.1 %copy-start.4 = (bf16[128,8]{0,1:T(8,128)(2,1)S(1)}, bf16[128,8]{0,1:T(8,128)(2,1)}, u32[]{:S(2)}) copy-start(bf16[128,8]{0,1:T(8,128)(2,1)} %param.10) | copy-start | bytes 6148
  0.7 2.1 %copy-start.5 = (s32[1,2]{1,0:T(1,128)S(1)}, s32[1,2]{1,0:T(1,128)}, u32[]{:S(2)}) copy-start(s32[1,2]{1,0:T(1,128)} %plan_ref.3) | copy-start | bytes 28
  2.2 8.2 %collective-permute-start = (bf16[160,576]{1,0:T(8,128)(2,1)S(1)}, bf16[160,576]{1,0:T(8,128)(2,1)S(1)}, u32[]{:S(2)}, u32[]{:S(2)}) collective-permute-start(bf16[160,576]{1,0:T(8,128)(2,1)S(1)} %get-tuple-element.28), channel_id=1, source_target_pairs={{0,4},{4,8},{8,12},{12,16},{16,20},{20,24},{24,28},{28,0},{1,5},{5... | collective-permute-start | bytes 552968 | tf_op jit(solution)/shard_map/ppermute | solution.py:256
  4.6 10.5 %collective-permute-start.1 = (bf16[224,576]{1,0:T(8,128)(2,1)S(1)}, bf16[224,576]{1,0:T(8,128)(2,1)S(1)}, u32[]{:S(2)}, u32[]{:S(2)}) collective-permute-start(bf16[224,576]{1,0:T(8,128)(2,1)S(1)} %get-tuple-element.29), channel_id=1, source_target_pairs={{0,4},{4,8},{8,12},{12,16},{16,20},{20,24},{24,28},{28,0},{1,5},{5... | collective-permute-start | bytes 774152 | tf_op jit(solution)/shard_map/ppermute | solution.py:256
  7.1 10.4 %collective-permute-start.2 = (bf16[80,576]{1,0:T(8,128)(2,1)S(1)}, bf16[80,576]{1,0:T(8,128)(2,1)S(1)}, u32[]{:S(2)}, u32[]{:S(2)}) collective-permute-start(bf16[80,576]{1,0:T(8,128)(2,1)S(1)} %get-tuple-element.37), channel_id=1, source_target_pairs={{0,1},{1,0},{2,3},{3,2},{4,5},{5,4},{6,7},{7,6},{8,9},{9,8},{10,11... | collective-permute-start | bytes 276488 | tf_op jit(solution)/shard_map/ppermute | solution.py:291
  11.7 7.1 %collective-permute-start.3 = (bf16[80,576]{1,0:T(8,128)(2,1)S(1)}, bf16[80,576]{1,0:T(8,128)(2,1)S(1)}, u32[]{:S(2)}, u32[]{:S(2)}) collective-permute-start(bf16[80,576]{1,0:T(8,128)(2,1)S(1)} %get-tuple-element.38), channel_id=1, source_target_pairs={{0,29},{1,28},{2,31},{3,30},{4,1},{5,0},{6,3},{7,2},{8,5},{9,4},{1... | collective-permute-start | bytes 276488 | tf_op jit(solution)/shard_map/ppermute | solution.py:303
  12.8 6.0 %collective-permute-start.4 = (bf16[80,576]{1,0:T(8,128)(2,1)S(1)}, bf16[80,576]{1,0:T(8,128)(2,1)S(1)}, u32[]{:S(2)}, u32[]{:S(2)}) collective-permute-start(bf16[80,576]{1,0:T(8,128)(2,1)S(1)} %get-tuple-element.39), channel_id=1, source_target_pairs={{0,28},{1,29},{2,30},{3,31},{4,0},{5,1},{6,2},{7,3},{8,4},{9,5},{1... | collective-permute-start | bytes 276488 | tf_op jit(solution)/shard_map/ppermute | solution.py:303
  13.9 7.6 %collective-permute-start.6 = (bf16[112,576]{1,0:T(8,128)(2,1)S(1)}, bf16[112,576]{1,0:T(8,128)(2,1)S(1)}, u32[]{:S(2)}, u32[]{:S(2)}) collective-permute-start(bf16[112,576]{1,0:T(8,128)(2,1)S(1)} %get-tuple-element.43), channel_id=1, source_target_pairs={{0,1},{1,0},{2,3},{3,2},{4,5},{5,4},{6,7},{7,6},{8,9},{9,8},{10,11... | collective-permute-start | bytes 387080 | tf_op jit(solution)/shard_map/ppermute | solution.py:291
  16.7 8.1 %collective-permute-start.7 = (bf16[112,576]{1,0:T(8,128)(2,1)S(1)}, bf16[112,576]{1,0:T(8,128)(2,1)S(1)}, u32[]{:S(2)}, u32[]{:S(2)}) collective-permute-start(bf16[112,576]{1,0:T(8,128)(2,1)S(1)} %get-tuple-element.44), channel_id=1, source_target_pairs={{0,29},{1,28},{2,31},{3,30},{4,1},{5,0},{6,3},{7,2},{8,5},{9,4},{1... | collective-permute-start | bytes 387080 | tf_op jit(solution)/shard_map/ppermute | solution.py:303
  17.5 7.3 %collective-permute-start.8 = (bf16[112,576]{1,0:T(8,128)(2,1)S(1)}, bf16[112,576]{1,0:T(8,128)(2,1)S(1)}, u32[]{:S(2)}, u32[]{:S(2)}) collective-permute-start(bf16[112,576]{1,0:T(8,128)(2,1)S(1)} %get-tuple-element.45), channel_id=1, source_target_pairs={{0,28},{1,29},{2,30},{3,31},{4,0},{5,1},{6,2},{7,3},{8,4},{9,5},{1... | collective-permute-start | bytes 387080 | tf_op jit(solution)/shard_map/ppermute | solution.py:303
  18.9 9.3 %collective-permute-start.5 = (bf16[80,576]{1,0:T(8,128)(2,1)S(1)}, bf16[80,576]{1,0:T(8,128)(2,1)S(1)}, u32[]{:S(2)}, u32[]{:S(2)}) collective-permute-start(bf16[80,576]{1,0:T(8,128)(2,1)S(1)} %get-tuple-element.41), channel_id=1, source_target_pairs={{0,2},{1,3},{2,0},{3,1},{4,6},{5,7},{6,4},{7,5},{8,10},{9,11},{10,... | collective-permute-start | bytes 276488 | tf_op jit(solution)/shard_map/ppermute | solution.py:314
  25.0 9.3 %collective-permute-start.9 = (bf16[112,576]{1,0:T(8,128)(2,1)S(1)}, bf16[112,576]{1,0:T(8,128)(2,1)S(1)}, u32[]{:S(2)}, u32[]{:S(2)}) collective-permute-start(bf16[112,576]{1,0:T(8,128)(2,1)S(1)} %get-tuple-element.47), channel_id=1, source_target_pairs={{0,2},{1,3},{2,0},{3,1},{4,6},{5,7},{6,4},{7,5},{8,10},{9,11},{10,... | collective-permute-start | bytes 387080 | tf_op jit(solution)/shard_map/ppermute | solution.py:314

commit v8 on v7

--- a/solution.py
+++ b/solution.py
@@ -15,10 +15,10 @@
 VMEM_LIMIT = 24 * 2**20
 NEVER = 1e30
 CHUNKS = 2
-FIRST_SHARE = 5 / 12
+FIRST_SHARE = 1 / 2
 COST_SUM = 10**9
 COST_COMBINE = 10**9
-COST_OWN = 3 * 10**9
+COST_OWN = 0
 
 F32 = jnp.float32
 BF16 = jnp.bfloat16
@@ -37,12 +37,17 @@
     return [(0, first), (first, rows - first)]
 
 
+def piece_at(place, low):
+    return lax.rem(lax.axis_index("head") + place, low)
+
+
 def chunk_rows(keys, low, out_refs):
     rows = BLOCK // low
-    for (offset, part), out_ref in zip(chunks_of(rows), out_refs):
-        for j in range(low):
+    for j in range(low):
+        place = lax.rem(j + low - piece_at(0, low), low)
+        for (offset, part), out_ref in zip(chunks_of(rows), out_refs):
             start = j * rows + offset
-            out_ref[j * part : (j + 1) * part, :] = keys[start : start + part, :]
+            out_ref[pl.ds(pl.multiple_of(place * part, 16), part), :] = keys[start : start + part, :]
 
 
 def send_block_kernel(low, plan_hbm, lat_hbm, *rest):
@@ -70,7 +75,7 @@
     return jnp.concatenate([q_ref[first + i] for i in range(count)], axis=1)
 
 
-def visit(keys, q_ref, grad_ref, norm_ref, delta_ref, live, visible, ds_ref, p_ref, grad_out_ref):
+def visit(keys, q_ref, grad_ref, norm_ref, delta_ref, live, visible, ds_ref, p_ref, out_refs):
     heads = q_ref.shape[0]
     per = WIDE // PACKET
     for first in range(0, heads, per):
@@ -89,37 +94,30 @@
             here = slice((first + i) * PACKET, (first + i + 1) * PACKET)
             ds_ref[:, here] = (prob * (prob_grad[:, lanes] - delta)).astype(BF16)
             p_ref[:, here] = prob.astype(BF16)
+    value_grad = dot(p_ref[...], grad_ref[...])
     key_grad = dot_nt(ds_ref[...], heads_side_by_side(q_ref, 0, heads))
-    value_grad = dot(p_ref[...], grad_ref[...])
-    grad_out_ref[:, :LAT] = key_grad[:, :LAT] + value_grad
-    grad_out_ref[:, LAT:] = key_grad[:, LAT:]
-
-
-def pieces_out(total_ref, low, offset, out_refs):
-    rows = total_ref.shape[0] // low
-    r = lax.rem(lax.axis_index("head"), low)
-    for d, out_ref in out_refs:
-        start = pl.multiple_of(lax.rem(r + d, low) * rows, 16) + offset
-        out_ref[...] = total_ref[pl.ds(start, out_ref.shape[0]), :].astype(out_ref.dtype)
-
-
-def own_chunk(plan_ref, keys, offset, part, refs, low, q_ref, rows_ref, norm_ref, delta_ref):
-    ds_ref, keep_ref, *out_refs, p_ref, total_ref = refs
-    rows = BLOCK // low
+    part = keys.shape[0] // len(out_refs)
+    for d, out_ref in enumerate(out_refs):
+        here = slice(d * part, (d + 1) * part)
+        out_ref[:, :LAT] = (key_grad[here, :LAT] + value_grad[here, :]).astype(out_ref.dtype)
+        out_ref[:, LAT:] = key_grad[here, LAT:].astype(out_ref.dtype)
+
+
+def own_chunk(plan_ref, keys, offset, refs, low, q_ref, rows_ref, norm_ref, delta_ref):
+    ds_ref, *out_refs, p_ref = refs
+    rows, part = BLOCK // low, keys.shape[0] // low
     at = lax.broadcasted_iota(jnp.int32, (part, PACKET), 0)
-    at = jnp.concatenate([at + (j * rows + offset) for j in range(low)], axis=0)
+    at = jnp.concatenate([at + (piece_at(d, low) * rows + offset) for d in range(low)], axis=0)
     k_pos = plan_ref[0:1, 0:1] * BLOCK + at
     q_pos = SHARD - PACKET + lax.broadcasted_iota(jnp.int32, at.shape, 1)
-    visit(keys, q_ref, rows_ref, norm_ref, delta_ref, None, k_pos <= q_pos, ds_ref, p_ref, total_ref)
-    pieces_out(total_ref, low, 0, list(enumerate([keep_ref, *out_refs])))
+    visit(keys, q_ref, rows_ref, norm_ref, delta_ref, None, k_pos <= q_pos, ds_ref, p_ref, out_refs)
 
 
 def own_first_kernel(low, held, plan_ref, lat_ref, q_ref, grad_ref, norm_ref, delta_ref, *rest):
     rest = rest[held:]
     rows_ref, sel_ref = rest[:2]
     keys_refs = rest[2 : 2 + CHUNKS]
-    ds_ref, keep_ref = rest[2 + CHUNKS : 4 + CHUNKS]
-    out_refs = rest[4 + CHUNKS : 3 + CHUNKS + low]
+    refs = [*rest[2 + CHUNKS : 3 + CHUNKS + low], rest[-1]]
     heads = q_ref.shape[0]
     group = WIDE // heads
     at = lax.broadcasted_iota(jnp.int32, (WIDE, WIDE), 0)
@@ -137,23 +135,18 @@
     first = jnp.where(b0 > 0, 0.0, 1.0).astype(BF16)
     keys = (lat_ref[:, :BLOCK] * first + lat_ref[:, BLOCK:] * last).T
     chunk_rows(keys, low, keys_refs)
-    (offset, part), *_ = chunks_of(BLOCK // low)
-    refs = [ds_ref, keep_ref, *out_refs, *rest[-2:]]
-    own_chunk(plan_ref, keys_refs[0][...], offset, part, refs, low, q_ref, rows_ref, norm_ref, delta_ref)
+    (offset, _), *_ = chunks_of(BLOCK // low)
+    own_chunk(plan_ref, keys_refs[0][...], offset, refs, low, q_ref, rows_ref, norm_ref, delta_ref)
 
 
 def own_next_kernel(low, offset, plan_ref, keys_ref, q_ref, rows_ref, norm_ref, delta_ref, *rest):
-    part = keys_ref.shape[0] // low
-    own_chunk(plan_ref, keys_ref[...], offset, part, rest, low, q_ref, rows_ref, norm_ref, delta_ref)
+    own_chunk(plan_ref, keys_ref[...], offset, rest, low, q_ref, rows_ref, norm_ref, delta_ref)
 
 
 def far_kernel(low, keys_ref, q_ref, grad_ref, norm_ref, delta_ref, *rest):
-    ds_ref = rest[-3 - low]
-    out_refs = rest[-2 - low : -2]
-    p_ref, total_ref = rest[-2:]
+    ds_ref, *out_refs, p_ref = rest[-2 - low :]
     live = lax.axis_index("seq") > 0
-    visit(keys_ref[...], q_ref, grad_ref, norm_ref, delta_ref, live, None, ds_ref, p_ref, total_ref)
-    pieces_out(total_ref, low, 0, list(enumerate(out_refs)))
+    visit(keys_ref[...], q_ref, grad_ref, norm_ref, delta_ref, live, None, ds_ref, p_ref, out_refs)
 
 
 def query_kernel(*refs):
@@ -259,7 +252,7 @@
         return [((low * part, columns), BF16), ((part, width), F32)] + [((part, width), BF16)] * (low - 1)
 
     def scratch(part):
-        return [pltpu.VMEM((low * part, columns), BF16), pltpu.VMEM((low * part, width), F32)]
+        return [pltpu.VMEM((low * part, columns), BF16)]
 
     far_keys = [forward(sent[0])]
     (_, part), *_ = chunks

time: 35.2 us -> 34.3 us (0.974)
  waiting for transfers between devices: 9.44 us -> 5.99 us
  starting transfers between devices: 13.4 us -> 15.9 us
    ppermute x4, waiting for transfers between devices: 3.33 us -> 0.57 us  [local(): lax.ppermute(far[d], ('seq', 'head'), route(d, 1))]
    ppermute x2, starting transfers between devices: 3.35 us -> 5.37 us  [local(): lax.ppermute(send, 'head', [(j, (j + low) % n_head) for j in range(n_head)])]
    ppermute x4, starting transfers between devices: 4.23 us -> 5.18 us  [local(): lax.ppermute(far[d], ('seq', 'head'), route(d, 1))]
    ppermute x2, waiting for transfers between devices: 6.09 us -> 5.41 us  [local(): lax.ppermute(send, 'head', [(j, (j + low) % n_head) for j in range(n_head)])]
    ppermute x2, starting transfers between devices: 2.77 us -> 2.15 us  [local(): lax.ppermute(x, ('seq', 'head'), route(d, 0))]
  transfers between devices with their start and end apart: 10 -> 10, of which waited for: 2 -> 4; matrix products, arithmetic and copies ran while one was open for 0% -> 0% of each run, Pallas kernels for 26% -> 27%
where the time goes in v8:
time: 34.3 us; the launch traced here: 34.2 us
  starting transfers between devices  15.9 us (46%)
  Pallas kernels  11.5 us (34%)
  waiting for transfers between devices  5.99 us (17%)
  between operations  0.75 us (2%)
    pallas_call x10, Pallas kernels, call(): pl.pallas_call(kernel, name=name, out_shape=shapes, in_specs=[pl.BlockSpe...  11.5 us
    ppermute x2, waiting for transfers between devices, local(): lax.ppermute(send, 'head', [(j, (j + low) % n_head) for j in range(n_head)])  5.41 us
    ppermute x2, starting transfers between devices, local(): lax.ppermute(send, 'head', [(j, (j + low) % n_head) for j in range(n_head)])  5.37 us
    ppermute x4, starting transfers between devices, local(): lax.ppermute(far[d], ('seq', 'head'), route(d, 1))  5.18 us
    ppermute x2, starting transfers between devices, forward(): return lax.ppermute(x, 'seq', [(i, (i + 1) % n_seq) for i in range(n_seq)])  3.16 us
    ppermute x2, starting transfers between devices, local(): lax.ppermute(x, ('seq', 'head'), route(d, 0))  2.15 us
  transfers between devices with their start and end apart: 10, of which 4 were waited for; matrix products, arithmetic and copies ran while one was open for 0% of the time, Pallas kernels for 27%

profile of v8, /device:TPU:0, one launch (start us, length us, event | category | flops | bytes accessed | tf_op | source)
XLA Modules:
  0.0 34.2 jit_solution(15735548774354342377)
XLA Ops:
  0.6 0.0 copy-start
  0.6 0.0 copy-start.1
  0.7 0.0 copy-start.2
  0.7 0.0 copy-start.3
  0.7 0.0 copy-start.4
  0.7 0.0 copy-start.5
  0.7 1.5 %send_block.1 = (bf16[192,576]{1,0:T(8,128)(2,1)S(1)}, bf16[192,576]{1,0:T(8,128)(2,1)S(1)}) custom-call(s32[1,2]{1,0:T(1,128)} %plan_ref.3, bf16[576,768]{1,0:T(8,128)(2,1)} %bitcast.11), custom_call_target="tpu_custom_call" | custom-call | flops 1711276032 | tf_op jit(solution)/shard_map/send_block/pallas_call | solution.py:199
  2.2 0.5 %collective-permute-start = (bf16[192,576]{1,0:T(8,128)(2,1)S(1)}, bf16[192,576]{1,0:T(8,128)(2,1)S(1)}, u32[]{:S(2)}, u32[]{:S(2)}) collective-permute-start(bf16[192,576]{1,0:T(8,128)(2,1)S(1)} %get-tuple-element.28), channel_id=1, source_target_pairs={{0,4},{4,8},{8,12},{12,16},{16,20},{20,24},{24,28},{28,0},{1,5},{5... | collective-permute-start | bytes 663560 | tf_op jit(solution)/shard_map/ppermute | solution.py:249
  2.7 0.0 copy-done
  2.7 0.0 copy-done.1
  2.7 0.0 copy-done.2
  2.7 0.0 copy-done.3
  2.7 0.0 copy-done.4
  2.7 0.0 copy-done.5
  2.8 1.9 %own_visit_0.1 = (bf16[1024,512]{1,0:T(8,128)(2,1)S(1)}, f32[8,576]{1,0:T(8,128)S(1)}, bf16[192,576]{1,0:T(8,128)(2,1)S(1)}, bf16[192,576]{1,0:T(8,128)(2,1)S(1)...) custom-call(s32[1,2]{1,0:T(1,128)S(1)} %copy-done.5, ...), custom_call_target="tpu_custom_call", output_to_operand_aliasing={{7}: (6, {})} | custom-call | tf_op jit(solution)/shard_map/own_visit_0/pallas_call | solution.py:199
  4.7 2.7 %collective-permute-start.1 = (bf16[192,576]{1,0:T(8,128)(2,1)S(1)}, bf16[192,576]{1,0:T(8,128)(2,1)S(1)}, u32[]{:S(2)}, u32[]{:S(2)}) collective-permute-start(bf16[192,576]{1,0:T(8,128)(2,1)S(1)} %get-tuple-element.29), channel_id=1, source_target_pairs={{0,4},{4,8},{8,12},{12,16},{16,20},{20,24},{24,28},{28,0},{1,5},{5... | collective-permute-start | bytes 663560 | tf_op jit(solution)/shard_map/ppermute | solution.py:249
  7.3 1.6 %collective-permute-start.2 = (bf16[96,576]{1,0:T(8,128)(2,1)S(1)}, bf16[96,576]{1,0:T(8,128)(2,1)S(1)}, u32[]{:S(2)}, u32[]{:S(2)}) collective-permute-start(bf16[96,576]{1,0:T(8,128)(2,1)S(1)} %get-tuple-element.37), channel_id=1, source_target_pairs={{0,1},{1,0},{2,3},{3,2},{4,5},{5,4},{6,7},{7,6},{8,9},{9,8},{10,11... | collective-permute-start | bytes 331784 | tf_op jit(solution)/shard_map/ppermute | solution.py:284
  8.9 1.5 %own_visit_1.1 = (bf16[192,1024]{1,0:T(8,128)(2,1)S(1)}, f32[96,576]{1,0:T(8,128)S(1)}, bf16[96,576]{1,0:T(8,128)(2,1)S(1)}) custom-call(s32[1,2]{1,0:T(1,128)S(1)} %copy-done.5, bf16[192,576]{1,0:T(8,128)(2,1)S(1)} %get-tuple-element.27.keys_ref.refs_1_, bf16[8,576,128]{2,1,0:T(8,128)(2,1)S(1)} %bitcast.7, ...), custom_call_target="tpu_custom_call" | custom-call | tf_op jit(solution)/shard_map/own_visit_1/pallas_call | solution.py:199
  10.5 0.0 collective-permute-done.keys_ref.refs_2_
  10.5 1.5 %far_visit_0.1 = (bf16[192,1024]{1,0:T(8,128)(2,1)S(1)}, bf16[96,576]{1,0:T(8,128)(2,1)S(1)}, bf16[96,576]{1,0:T(8,128)(2,1)S(1)}) custom-call(bf16[192,576]{1,0:T(8,128)(2,1)S(1)} %collective-permute-done.keys_ref.refs_2_, bf16[8,576,128]{2,1,0:T(8,128)(2,1)S(1)} %bitcast.8, bf16[1024,512]{1,0:T(8,128)(2,1)S(1)} %get-tuple-element.31.rows_ref.grad_ref, ...), custom_call_target="tpu_custom_call" | custom-call | tf_op jit(solution)/shard_map/far_visit_0/pallas_call | solution.py:199
  12.0 1.0 %collective-permute-start.3 = (bf16[96,576]{1,0:T(8,128)(2,1)S(1)}, bf16[96,576]{1,0:T(8,128)(2,1)S(1)}, u32[]{:S(2)}, u32[]{:S(2)}) collective-permute-start(bf16[96,576]{1,0:T(8,128)(2,1)S(1)} %get-tuple-element.38), channel_id=1, source_target_pairs={{0,29},{1,28},{2,31},{3,30},{4,1},{5,0},{6,3},{7,2},{8,5},{9,4},{1... | collective-permute-start | bytes 331784 | tf_op jit(solution)/shard_map/ppermute | solution.py:296
  13.0 1.7 %collective-permute-start.4 = (bf16[96,576]{1,0:T(8,128)(2,1)S(1)}, bf16[96,576]{1,0:T(8,128)(2,1)S(1)}, u32[]{:S(2)}, u32[]{:S(2)}) collective-permute-start(bf16[96,576]{1,0:T(8,128)(2,1)S(1)} %get-tuple-element.39), channel_id=1, source_target_pairs={{0,28},{1,29},{2,30},{3,31},{4,0},{5,1},{6,2},{7,3},{8,4},{9,5},{1... | collective-permute-start | bytes 331784 | tf_op jit(solution)/shard_map/ppermute | solution.py:296
  14.7 0.6 %collective-permute-start.6 = (bf16[96,576]{1,0:T(8,128)(2,1)S(1)}, bf16[96,576]{1,0:T(8,128)(2,1)S(1)}, u32[]{:S(2)}, u32[]{:S(2)}) collective-permute-start(bf16[96,576]{1,0:T(8,128)(2,1)S(1)} %get-tuple-element.43), channel_id=1, source_target_pairs={{0,1},{1,0},{2,3},{3,2},{4,5},{5,4},{6,7},{7,6},{8,9},{9,8},{10,11... | collective-permute-start | bytes 331784 | tf_op jit(solution)/shard_map/ppermute | solution.py:284
  15.3 0.0 collective-permute-done.1.keys_ref.refs_3_
  15.3 1.6 %far_visit_1.1 = (bf16[192,1024]{1,0:T(8,128)(2,1)S(1)}, bf16[96,576]{1,0:T(8,128)(2,1)S(1)}, bf16[96,576]{1,0:T(8,128)(2,1)S(1)}) custom-call(bf16[192,576]{1,0:T(8,128)(2,1)S(1)} %collective-permute-done.1.keys_ref.refs_3_, bf16[8,576,128]{2,1,0:T(8,128)(2,1)S(1)} %bitcast.9, bf16[1024,512]{1,0:T(8,128)(2,1)S(1)} %get-tuple-element.31.rows_ref.grad_ref, ...), custom_call_target="tpu_custom_call" | custom-call | tf_op jit(solution)/shard_map/far_visit_1/pallas_call | solution.py:199
  16.8 0.8 %collective-permute-start.7 = (bf16[96,576]{1,0:T(8,128)(2,1)S(1)}, bf16[96,576]{1,0:T(8,128)(2,1)S(1)}, u32[]{:S(2)}, u32[]{:S(2)}) collective-permute-start(bf16[96,576]{1,0:T(8,128)(2,1)S(1)} %get-tuple-element.44), channel_id=1, source_target_pairs={{0,29},{1,28},{2,31},{3,30},{4,1},{5,0},{6,3},{7,2},{8,5},{9,4},{1... | collective-permute-start | bytes 331784 | tf_op jit(solution)/shard_map/ppermute | solution.py:296
  17.7 0.0 collective-permute-done.2.rest_1_
  17.7 1.7 %collective-permute-start.8 = (bf16[96,576]{1,0:T(8,128)(2,1)S(1)}, bf16[96,576]{1,0:T(8,128)(2,1)S(1)}, u32[]{:S(2)}, u32[]{:S(2)}) collective-permute-start(bf16[96,576]{1,0:T(8,128)(2,1)S(1)} %get-tuple-element.45), channel_id=1, source_target_pairs={{0,28},{1,29},{2,30},{3,31},{4,0},{5,1},{6,2},{7,3},{8,4},{9,5},{1... | collective-permute-start | bytes 331784 | tf_op jit(solution)/shard_map/ppermute | solution.py:296
  19.4 0.0 collective-permute-done.3.rest_2_
  19.4 0.0 collective-permute-done.4.rest_3_
  19.4 0.1 combine_0.1
  19.5 2.7 %collective-permute-start.5 = (bf16[96,576]{1,0:T(8,128)(2,1)S(1)}, bf16[96,576]{1,0:T(8,128)(2,1)S(1)}, u32[]{:S(2)}, u32[]{:S(2)}) collective-permute-start(bf16[96,576]{1,0:T(8,128)(2,1)S(1)} %get-tuple-element.41), channel_id=1, source_target_pairs={{0,2},{1,3},{2,0},{3,1},{4,6},{5,7},{6,4},{7,5},{8,10},{9,11},{10,... | collective-permute-start | bytes 331784 | tf_op jit(solution)/shard_map/ppermute | solution.py:307
  22.2 0.0 collective-permute-done.6.rest_1_
  22.2 0.4 %collective-permute-done.7.rest_2_ = bf16[96,576]{1,0:T(8,128)(2,1)S(1)} collective-permute-done((bf16[96,576]{1,0:T(8,128)(2,1)S(1)}, bf16[96,576]{1,0:T(8,128)(2,1)S(1)}, u32[]{:S(2)}, u32[]{:S(2)}) %collective-permute-start.7) | collective-permute-done | bytes 110624 | tf_op jit(solution)/shard_map/ppermute | solution.py:296
  22.5 0.2 collective-permute-done.8.rest_3_
  22.7 0.1 combine_1.1
  22.8 2.7 %collective-permute-start.9 = (bf16[96,576]{1,0:T(8,128)(2,1)S(1)}, bf16[96,576]{1,0:T(8,128)(2,1)S(1)}, u32[]{:S(2)}, u32[]{:S(2)}) collective-permute-start(bf16[96,576]{1,0:T(8,128)(2,1)S(1)} %get-tuple-element.47), channel_id=1, source_target_pairs={{0,2},{1,3},{2,0},{3,1},{4,6},{5,7},{6,4},{7,5},{8,10},{9,11},{10,... | collective-permute-start | bytes 331784 | tf_op jit(solution)/shard_map/ppermute | solution.py:307
  25.6 2.4 %query_grad.1 = bf16[8,576,128]{2,1,0:T(8,128)(2,1)} custom-call(bf16[192,576]{1,0:T(8,128)(2,1)S(1)} %get-tuple-element.26.refs_0_, bf16[192,576]{1,0:T(8,128)(2,1)S(1)} %get-tuple-element.27.keys_ref.refs_1_, bf16[192,576]{1,0:T(8,128)(2,1)S(1)} %collective-permute-done.keys_ref.refs_2_, bf16[192,576]{1,0:T(8,128)(2,1)S(1)} %collective-permute-done.1.keys_ref.refs_3_, ...), custom_call_target="tpu_custom_call" | custom-call | flops 905969664 | tf_op jit(solution)/shard_map/query_grad/pallas_call | solution.py:199
  28.0 3.0 %collective-permute-done.5.got_ref = bf16[96,576]{1,0:T(8,128)(2,1)S(1)} collective-permute-done((bf16[96,576]{1,0:T(8,128)(2,1)S(1)}, bf16[96,576]{1,0:T(8,128)(2,1)S(1)}, u32[]{:S(2)}, u32[]{:S(2)}) %collective-permute-start.5) | collective-permute-done | bytes 110624 | tf_op jit(solution)/shard_map/ppermute | solution.py:307
  31.0 2.4 %collective-permute-done.9.refs_2_ = bf16[96,576]{1,0:T(8,128)(2,1)S(1)} collective-permute-done((bf16[96,576]{1,0:T(8,128)(2,1)S(1)}, bf16[96,576]{1,0:T(8,128)(2,1)S(1)}, u32[]{:S(2)}, u32[]{:S(2)}) %collective-permute-start.9) | collective-permute-done | bytes 110624 | tf_op jit(solution)/shard_map/ppermute | solution.py:307
  33.4 0.7 %last_sum.1 = bf16[192,576]{1,0:T(8,128)(2,1)} custom-call(bf16[96,576]{1,0:T(8,128)(2,1)S(1)} %sum_0.1.refs_0_, f32[96,576]{1,0:T(8,128)S(1)} %get-tuple-element.46.refs_1_, bf16[96,576]{1,0:T(8,128)(2,1)S(1)} %collective-permute-done.9.refs_2_), custom_call_target="tpu_custom_call" | custom-call | tf_op jit(solution)/shard_map/last_sum/pallas_call | solution.py:199
  (1 shorter events, 0.0 us)
Async XLA Ops:
  0.6 2.1 %copy-start = (bf16[128,8,576]{0,2,1:T(8,128)(2,1)S(1)}, bf16[128,8,576]{0,2,1:T(8,128)(2,1)}, u32[]{:S(2)}) copy-start(bf16[128,8,576]{0,2,1:T(8,128)(2,1)} %param.6) | copy-start | bytes 3538948
  0.6 2.1 %copy-start.1 = (bf16[128,8,512]{2,1,0:T(8,128)(2,1)S(1)}, bf16[128,8,512]{2,1,0:T(8,128)(2,1)}, u32[]{:S(2)}) copy-start(bf16[128,8,512]{2,1,0:T(8,128)(2,1)} %param.7) | copy-start | bytes 3145732
  0.7 2.1 %copy-start.2 = (bf16[768,576]{0,1:T(8,128)(2,1)S(1)}, bf16[768,576]{0,1:T(8,128)(2,1)}, u32[]{:S(2)}) copy-start(bf16[768,576]{0,1:T(8,128)(2,1)} %param.8) | copy-start | bytes 2654212
  0.7 2.1 %copy-start.3 = (bf16[128,8]{0,1:T(8,128)(2,1)S(1)}, bf16[128,8]{0,1:T(8,128)(2,1)}, u32[]{:S(2)}) copy-start(bf16[128,8]{0,1:T(8,128)(2,1)} %param.9) | copy-start | bytes 6148
  0.7 2.1 %copy-start.4 = (bf16[128,8]{0,1:T(8,128)(2,1)S(1)}, bf16[128,8]{0,1:T(8,128)(2,1)}, u32[]{:S(2)}) copy-start(bf16[128,8]{0,1:T(8,128)(2,1)} %param.10) | copy-start | bytes 6148
  0.7 2.1 %copy-start.5 = (s32[1,2]{1,0:T(1,128)S(1)}, s32[1,2]{1,0:T(1,128)}, u32[]{:S(2)}) copy-start(s32[1,2]{1,0:T(1,128)} %plan_ref.3) | copy-start | bytes 28
  2.2 8.2 %collective-permute-start = (bf16[192,576]{1,0:T(8,128)(2,1)S(1)}, bf16[192,576]{1,0:T(8,128)(2,1)S(1)}, u32[]{:S(2)}, u32[]{:S(2)}) collective-permute-start(bf16[192,576]{1,0:T(8,128)(2,1)S(1)} %get-tuple-element.28), channel_id=1, source_target_pairs={{0,4},{4,8},{8,12},{12,16},{16,20},{20,24},{24,28},{28,0},{1,5},{5... | collective-permute-start | bytes 663560 | tf_op jit(solution)/shard_map/ppermute | solution.py:249
  4.7 10.6 %collective-permute-start.1 = (bf16[192,576]{1,0:T(8,128)(2,1)S(1)}, bf16[192,576]{1,0:T(8,128)(2,1)S(1)}, u32[]{:S(2)}, u32[]{:S(2)}) collective-permute-start(bf16[192,576]{1,0:T(8,128)(2,1)S(1)} %get-tuple-element.29), channel_id=1, source_target_pairs={{0,4},{4,8},{8,12},{12,16},{16,20},{20,24},{24,28},{28,0},{1,5},{5... | collective-permute-start | bytes 663560 | tf_op jit(solution)/shard_map/ppermute | solution.py:249
  7.3 10.3 %collective-permute-start.2 = (bf16[96,576]{1,0:T(8,128)(2,1)S(1)}, bf16[96,576]{1,0:T(8,128)(2,1)S(1)}, u32[]{:S(2)}, u32[]{:S(2)}) collective-permute-start(bf16[96,576]{1,0:T(8,128)(2,1)S(1)} %get-tuple-element.37), channel_id=1, source_target_pairs={{0,1},{1,0},{2,3},{3,2},{4,5},{5,4},{6,7},{7,6},{8,9},{9,8},{10,11... | collective-permute-start | bytes 331784 | tf_op jit(solution)/shard_map/ppermute | solution.py:284
  12.0 7.4 %collective-permute-start.3 = (bf16[96,576]{1,0:T(8,128)(2,1)S(1)}, bf16[96,576]{1,0:T(8,128)(2,1)S(1)}, u32[]{:S(2)}, u32[]{:S(2)}) collective-permute-start(bf16[96,576]{1,0:T(8,128)(2,1)S(1)} %get-tuple-element.38), channel_id=1, source_target_pairs={{0,29},{1,28},{2,31},{3,30},{4,1},{5,0},{6,3},{7,2},{8,5},{9,4},{1... | collective-permute-start | bytes 331784 | tf_op jit(solution)/shard_map/ppermute | solution.py:296
  13.0 6.4 %collective-permute-start.4 = (bf16[96,576]{1,0:T(8,128)(2,1)S(1)}, bf16[96,576]{1,0:T(8,128)(2,1)S(1)}, u32[]{:S(2)}, u32[]{:S(2)}) collective-permute-start(bf16[96,576]{1,0:T(8,128)(2,1)S(1)} %get-tuple-element.39), channel_id=1, source_target_pairs={{0,28},{1,29},{2,30},{3,31},{4,0},{5,1},{6,2},{7,3},{8,4},{9,5},{1... | collective-permute-start | bytes 331784 | tf_op jit(solution)/shard_map/ppermute | solution.py:296
  14.7 7.5 %collective-permute-start.6 = (bf16[96,576]{1,0:T(8,128)(2,1)S(1)}, bf16[96,576]{1,0:T(8,128)(2,1)S(1)}, u32[]{:S(2)}, u32[]{:S(2)}) collective-permute-start(bf16[96,576]{1,0:T(8,128)(2,1)S(1)} %get-tuple-element.43), channel_id=1, source_target_pairs={{0,1},{1,0},{2,3},{3,2},{4,5},{5,4},{6,7},{7,6},{8,9},{9,8},{10,11... | collective-permute-start | bytes 331784 | tf_op jit(solution)/shard_map/ppermute | solution.py:284
  16.8 5.7 %collective-permute-start.7 = (bf16[96,576]{1,0:T(8,128)(2,1)S(1)}, bf16[96,576]{1,0:T(8,128)(2,1)S(1)}, u32[]{:S(2)}, u32[]{:S(2)}) collective-permute-start(bf16[96,576]{1,0:T(8,128)(2,1)S(1)} %get-tuple-element.44), channel_id=1, source_target_pairs={{0,29},{1,28},{2,31},{3,30},{4,1},{5,0},{6,3},{7,2},{8,5},{9,4},{1... | collective-permute-start | bytes 331784 | tf_op jit(solution)/shard_map/ppermute | solution.py:296
  17.7 5.1 %collective-permute-start.8 = (bf16[96,576]{1,0:T(8,128)(2,1)S(1)}, bf16[96,576]{1,0:T(8,128)(2,1)S(1)}, u32[]{:S(2)}, u32[]{:S(2)}) collective-permute-start(bf16[96,576]{1,0:T(8,128)(2,1)S(1)} %get-tuple-element.45), channel_id=1, source_target_pairs={{0,28},{1,29},{2,30},{3,31},{4,0},{5,1},{6,2},{7,3},{8,4},{9,5},{1... | collective-permute-start | bytes 331784 | tf_op jit(solution)/shard_map/ppermute | solution.py:296
  19.5 11.5 %collective-permute-start.5 = (bf16[96,576]{1,0:T(8,128)(2,1)S(1)}, bf16[96,576]{1,0:T(8,128)(2,1)S(1)}, u32[]{:S(2)}, u32[]{:S(2)}) collective-permute-start(bf16[96,576]{1,0:T(8,128)(2,1)S(1)} %get-tuple-element.41), channel_id=1, source_target_pairs={{0,2},{1,3},{2,0},{3,1},{4,6},{5,7},{6,4},{7,5},{8,10},{9,11},{10,... | collective-permute-start | bytes 331784 | tf_op jit(solution)/shard_map/ppermute | solution.py:307
  22.8 10.6 %collective-permute-start.9 = (bf16[96,576]{1,0:T(8,128)(2,1)S(1)}, bf16[96,576]{1,0:T(8,128)(2,1)S(1)}, u32[]{:S(2)}, u32[]{:S(2)}) collective-permute-start(bf16[96,576]{1,0:T(8,128)(2,1)S(1)} %get-tuple-element.47), channel_id=1, source_target_pairs={{0,2},{1,3},{2,0},{3,1},{4,6},{5,7},{6,4},{7,5},{8,10},{9,11},{10,... | collective-permute-start | bytes 331784 | tf_op jit(solution)/shard_map/ppermute | solution.py:307

commit v9 on v7

--- a/solution.py
+++ b/solution.py
@@ -15,10 +15,10 @@
 VMEM_LIMIT = 24 * 2**20
 NEVER = 1e30
 CHUNKS = 2
-FIRST_SHARE = 5 / 12
+FIRST_SHARE = 1 / 2
 COST_SUM = 10**9
 COST_COMBINE = 10**9
-COST_OWN = 3 * 10**9
+COST_OWN = 0
 
 F32 = jnp.float32
 BF16 = jnp.bfloat16
@@ -47,7 +47,7 @@
 
 def send_block_kernel(low, plan_hbm, lat_hbm, *rest):
     out_refs = rest[:CHUNKS]
-    plan_ref, lat_ref, sems = rest[CHUNKS:]
+    lat_ref, plan_ref, sems = rest[CHUNKS:]
 
     def block_copy(block):
         here = pl.ds(pl.multiple_of(block * BLOCK, 128), BLOCK)
@@ -135,7 +135,7 @@
         sel_ref[i : i + 1, :] = jnp.broadcast_to(jnp.where(hit, 1.0, 0.0), (1, sel_ref.shape[1])).astype(F32)
     last = jnp.where(b0 > 0, 1.0, 0.0).astype(BF16)
     first = jnp.where(b0 > 0, 0.0, 1.0).astype(BF16)
-    keys = (lat_ref[:, :BLOCK] * first + lat_ref[:, BLOCK:] * last).T
+    keys = (lat_ref[0] * first + lat_ref[1] * last).T
     chunk_rows(keys, low, keys_refs)
     (offset, part), *_ = chunks_of(BLOCK // low)
     refs = [ds_ref, keep_ref, *out_refs, *rest[-2:]]
@@ -242,12 +242,12 @@
     chunks = chunks_of(rows)
     blocks = SHARD // BLOCK
 
-    sent = call(
+    *sent, lat_blocks = call(
         functools.partial(send_block_kernel, low),
         "send_block",
         (plan, lat_t),
-        [((low * part, width), BF16) for _, part in chunks],
-        [pltpu.SMEM(plan.shape, plan.dtype), pltpu.VMEM((blocks, width, BLOCK), BF16), pltpu.SemaphoreType.DMA((blocks + 1,))],
+        [((low * part, width), BF16) for _, part in chunks] + [((blocks, width, BLOCK), BF16)],
+        [pltpu.SMEM(plan.shape, plan.dtype), pltpu.SemaphoreType.DMA((blocks + 1,))],
         flops=visit_flops,
         raw=(0, 1),
     )
@@ -266,7 +266,7 @@
     grad_rows, sel, *first = call(
         functools.partial(own_first_kernel, low, CHUNKS - 1),
         "own_visit_0",
-        (plan, lat_t, q_t, grad, norm_t, delta_t),
+        (plan, lat_blocks, q_t, grad, norm_t, delta_t),
         [((columns, LAT), BF16), ((8, width), F32)] + [((low * p, width), BF16) for _, p in chunks] + own_outs(part),
         scratch(part),
         passed=sent[1:],

time: 35.2 us -> 34.1 us (0.969)
  waiting for transfers between devices: 9.44 us -> 5.79 us
  starting transfers between devices: 13.4 us -> 16.1 us
    ppermute x4, waiting for transfers between devices: 3.33 us -> 0.5 us  [local(): lax.ppermute(far[d], ('seq', 'head'), route(d, 1))]
    ppermute x2, starting transfers between devices: 3.35 us -> 5.47 us  [local(): lax.ppermute(send, 'head', [(j, (j + low) % n_head) for j in range(n_head)])]
    ppermute x4, starting transfers between devices: 4.23 us -> 5.36 us  [local(): lax.ppermute(far[d], ('seq', 'head'), route(d, 1))]
    ppermute x2, waiting for transfers between devices: 6.09 us -> 5.28 us  [local(): lax.ppermute(send, 'head', [(j, (j + low) % n_head) for j in range(n_head)])]
    ppermute x2, starting transfers between devices: 2.77 us -> 2.2 us  [local(): lax.ppermute(x, ('seq', 'head'), route(d, 0))]
  transfers between devices with their start and end apart: 10 -> 10, of which waited for: 2 -> 4; matrix products, arithmetic and copies ran while one was open for 0% -> 0% of each run, Pallas kernels for 26% -> 27%
where the time goes in v9:
time: 34.1 us; the launch traced here: 34 us
  starting transfers between devices  16.1 us (47%)
  Pallas kernels  11.4 us (33%)
  waiting for transfers between devices  5.79 us (17%)
  between operations  0.72 us (2%)
    pallas_call x10, Pallas kernels, call(): pl.pallas_call(kernel, name=name, out_shape=shapes, in_specs=[pl.BlockSpe...  11.4 us
    ppermute x2, starting transfers between devices, local(): lax.ppermute(send, 'head', [(j, (j + low) % n_head) for j in range(n_head)])  5.47 us
    ppermute x4, starting transfers between devices, local(): lax.ppermute(far[d], ('seq', 'head'), route(d, 1))  5.36 us
    ppermute x2, waiting for transfers between devices, local(): lax.ppermute(send, 'head', [(j, (j + low) % n_head) for j in range(n_head)])  5.28 us
    ppermute x2, starting transfers between devices, forward(): return lax.ppermute(x, 'seq', [(i, (i + 1) % n_seq) for i in range(n_seq)])  3.02 us
    ppermute x2, starting transfers between devices, local(): lax.ppermute(x, ('seq', 'head'), route(d, 0))  2.2 us
  transfers between devices with their start and end apart: 10, of which 4 were waited for; matrix products, arithmetic and copies ran while one was open for 0% of the time, Pallas kernels for 27%

profile of v9, /device:TPU:0, one launch (start us, length us, event | category | flops | bytes accessed | tf_op | source)
XLA Modules:
  0.0 34.0 jit_solution(712313472557826560)
XLA Ops:
  0.6 0.0 copy-start
  0.6 0.0 copy-start.1
  0.7 0.0 copy-start.2
  0.7 0.0 copy-start.3
  0.7 0.0 copy-start.4
  0.7 1.5 %send_block.1 = (bf16[192,576]{1,0:T(8,128)(2,1)S(1)}, bf16[192,576]{1,0:T(8,128)(2,1)S(1)}, bf16[2,576,384]{2,1,0:T(8,128)(2,1)S(1)}) custom-call(s32[1,2]{1,0:T(1,128)} %plan_ref.3, bf16[576,768]{1,0:T(8,128)(2,1)} %bitcast.20), custom_call_target="tpu_custom_call" | custom-call | flops 1711276032 | tf_op jit(solution)/shard_map/send_block/pallas_call | solution.py:206
  2.2 0.4 %collective-permute-start = (bf16[192,576]{1,0:T(8,128)(2,1)S(1)}, bf16[192,576]{1,0:T(8,128)(2,1)S(1)}, u32[]{:S(2)}, u32[]{:S(2)}) collective-permute-start(bf16[192,576]{1,0:T(8,128)(2,1)S(1)} %get-tuple-element.30), channel_id=1, source_target_pairs={{0,4},{4,8},{8,12},{12,16},{16,20},{20,24},{24,28},{28,0},{1,5},{5... | collective-permute-start | bytes 663560 | tf_op jit(solution)/shard_map/ppermute | solution.py:256
  2.6 0.0 copy-done
  2.6 0.0 copy-done.1
  2.6 0.0 copy-done.2
  2.6 0.0 copy-done.3
  2.6 0.0 copy-done.4
  2.6 2.1 %own_visit_0.1 = (bf16[1024,512]{1,0:T(8,128)(2,1)S(1)}, f32[8,576]{1,0:T(8,128)S(1)}, bf16[192,576]{1,0:T(8,128)(2,1)S(1)}, bf16[192,576]{1,0:T(8,128)(2,1)S(1)...) custom-call(s32[1,2]{1,0:T(1,128)S(1)} %copy-done.4, ...), custom_call_target="tpu_custom_call", output_to_operand_aliasing={{7}: (6, {})} | custom-call | tf_op jit(solution)/shard_map/own_visit_0/pallas_call | solution.py:206
  4.7 2.7 %collective-permute-start.1 = (bf16[192,576]{1,0:T(8,128)(2,1)S(1)}, bf16[192,576]{1,0:T(8,128)(2,1)S(1)}, u32[]{:S(2)}, u32[]{:S(2)}) collective-permute-start(bf16[192,576]{1,0:T(8,128)(2,1)S(1)} %get-tuple-element.31), channel_id=1, source_target_pairs={{0,4},{4,8},{8,12},{12,16},{16,20},{20,24},{24,28},{28,0},{1,5},{5... | collective-permute-start | bytes 663560 | tf_op jit(solution)/shard_map/ppermute | solution.py:256
  7.3 1.6 %collective-permute-start.2 = (bf16[96,576]{1,0:T(8,128)(2,1)S(1)}, bf16[96,576]{1,0:T(8,128)(2,1)S(1)}, u32[]{:S(2)}, u32[]{:S(2)}) collective-permute-start(bf16[96,576]{1,0:T(8,128)(2,1)S(1)} %get-tuple-element.39), channel_id=1, source_target_pairs={{0,1},{1,0},{2,3},{3,2},{4,5},{5,4},{6,7},{7,6},{8,9},{9,8},{10,11... | collective-permute-start | bytes 331784 | tf_op jit(solution)/shard_map/ppermute | solution.py:291
  8.9 1.5 %own_visit_1.1 = (bf16[192,1024]{1,0:T(8,128)(2,1)S(1)}, f32[96,576]{1,0:T(8,128)S(1)}, bf16[96,576]{1,0:T(8,128)(2,1)S(1)}) custom-call(s32[1,2]{1,0:T(1,128)S(1)} %copy-done.4, bf16[192,576]{1,0:T(8,128)(2,1)S(1)} %get-tuple-element.29.keys_ref.refs_1_, bf16[8,576,128]{2,1,0:T(8,128)(2,1)S(1)} %bitcast.7, ...), custom_call_target="tpu_custom_call" | custom-call | tf_op jit(solution)/shard_map/own_visit_1/pallas_call | solution.py:206
  10.4 0.0 collective-permute-done.keys_ref.refs_2_
  10.4 1.4 %far_visit_0.1 = (bf16[192,1024]{1,0:T(8,128)(2,1)S(1)}, bf16[96,576]{1,0:T(8,128)(2,1)S(1)}, bf16[96,576]{1,0:T(8,128)(2,1)S(1)}) custom-call(bf16[192,576]{1,0:T(8,128)(2,1)S(1)} %collective-permute-done.keys_ref.refs_2_, bf16[8,576,128]{2,1,0:T(8,128)(2,1)S(1)} %bitcast.8, bf16[1024,512]{1,0:T(8,128)(2,1)S(1)} %get-tuple-element.33.rows_ref.grad_ref, ...), custom_call_target="tpu_custom_call" | custom-call | tf_op jit(solution)/shard_map/far_visit_0/pallas_call | solution.py:206
  11.8 0.9 %collective-permute-start.3 = (bf16[96,576]{1,0:T(8,128)(2,1)S(1)}, bf16[96,576]{1,0:T(8,128)(2,1)S(1)}, u32[]{:S(2)}, u32[]{:S(2)}) collective-permute-start(bf16[96,576]{1,0:T(8,128)(2,1)S(1)} %get-tuple-element.40), channel_id=1, source_target_pairs={{0,29},{1,28},{2,31},{3,30},{4,1},{5,0},{6,3},{7,2},{8,5},{9,4},{1... | collective-permute-start | bytes 331784 | tf_op jit(solution)/shard_map/ppermute | solution.py:303
  12.7 1.9 %collective-permute-start.4 = (bf16[96,576]{1,0:T(8,128)(2,1)S(1)}, bf16[96,576]{1,0:T(8,128)(2,1)S(1)}, u32[]{:S(2)}, u32[]{:S(2)}) collective-permute-start(bf16[96,576]{1,0:T(8,128)(2,1)S(1)} %get-tuple-element.41), channel_id=1, source_target_pairs={{0,28},{1,29},{2,30},{3,31},{4,0},{5,1},{6,2},{7,3},{8,4},{9,5},{1... | collective-permute-start | bytes 331784 | tf_op jit(solution)/shard_map/ppermute | solution.py:303
  14.6 0.6 %collective-permute-start.6 = (bf16[96,576]{1,0:T(8,128)(2,1)S(1)}, bf16[96,576]{1,0:T(8,128)(2,1)S(1)}, u32[]{:S(2)}, u32[]{:S(2)}) collective-permute-start(bf16[96,576]{1,0:T(8,128)(2,1)S(1)} %get-tuple-element.45), channel_id=1, source_target_pairs={{0,1},{1,0},{2,3},{3,2},{4,5},{5,4},{6,7},{7,6},{8,9},{9,8},{10,11... | collective-permute-start | bytes 331784 | tf_op jit(solution)/shard_map/ppermute | solution.py:291
  15.2 0.0 collective-permute-done.1.keys_ref.refs_3_
  15.2 1.5 %far_visit_1.1 = (bf16[192,1024]{1,0:T(8,128)(2,1)S(1)}, bf16[96,576]{1,0:T(8,128)(2,1)S(1)}, bf16[96,576]{1,0:T(8,128)(2,1)S(1)}) custom-call(bf16[192,576]{1,0:T(8,128)(2,1)S(1)} %collective-permute-done.1.keys_ref.refs_3_, bf16[8,576,128]{2,1,0:T(8,128)(2,1)S(1)} %bitcast.9, bf16[1024,512]{1,0:T(8,128)(2,1)S(1)} %get-tuple-element.33.rows_ref.grad_ref, ...), custom_call_target="tpu_custom_call" | custom-call | tf_op jit(solution)/shard_map/far_visit_1/pallas_call | solution.py:206
  16.7 0.6 %collective-permute-start.7 = (bf16[96,576]{1,0:T(8,128)(2,1)S(1)}, bf16[96,576]{1,0:T(8,128)(2,1)S(1)}, u32[]{:S(2)}, u32[]{:S(2)}) collective-permute-start(bf16[96,576]{1,0:T(8,128)(2,1)S(1)} %get-tuple-element.46), channel_id=1, source_target_pairs={{0,29},{1,28},{2,31},{3,30},{4,1},{5,0},{6,3},{7,2},{8,5},{9,4},{1... | collective-permute-start | bytes 331784 | tf_op jit(solution)/shard_map/ppermute | solution.py:303
  17.3 0.0 collective-permute-done.2.rest_1_
  17.3 2.0 %collective-permute-start.8 = (bf16[96,576]{1,0:T(8,128)(2,1)S(1)}, bf16[96,576]{1,0:T(8,128)(2,1)S(1)}, u32[]{:S(2)}, u32[]{:S(2)}) collective-permute-start(bf16[96,576]{1,0:T(8,128)(2,1)S(1)} %get-tuple-element.47), channel_id=1, source_target_pairs={{0,28},{1,29},{2,30},{3,31},{4,0},{5,1},{6,2},{7,3},{8,4},{9,5},{1... | collective-permute-start | bytes 331784 | tf_op jit(solution)/shard_map/ppermute | solution.py:303
  19.3 0.0 collective-permute-done.3.rest_2_
  19.3 0.0 collective-permute-done.4.rest_3_
  19.3 0.1 combine_0.1
  19.4 2.7 %collective-permute-start.5 = (bf16[96,576]{1,0:T(8,128)(2,1)S(1)}, bf16[96,576]{1,0:T(8,128)(2,1)S(1)}, u32[]{:S(2)}, u32[]{:S(2)}) collective-permute-start(bf16[96,576]{1,0:T(8,128)(2,1)S(1)} %get-tuple-element.43), channel_id=1, source_target_pairs={{0,2},{1,3},{2,0},{3,1},{4,6},{5,7},{6,4},{7,5},{8,10},{9,11},{10,... | collective-permute-start | bytes 331784 | tf_op jit(solution)/shard_map/ppermute | solution.py:314
  22.1 0.0 collective-permute-done.6.rest_1_
  22.1 0.3 collective-permute-done.7.rest_2_
  22.4 0.2 collective-permute-done.8.rest_3_
  22.6 0.1 combine_1.1
  22.7 2.8 %collective-permute-start.9 = (bf16[96,576]{1,0:T(8,128)(2,1)S(1)}, bf16[96,576]{1,0:T(8,128)(2,1)S(1)}, u32[]{:S(2)}, u32[]{:S(2)}) collective-permute-start(bf16[96,576]{1,0:T(8,128)(2,1)S(1)} %get-tuple-element.49), channel_id=1, source_target_pairs={{0,2},{1,3},{2,0},{3,1},{4,6},{5,7},{6,4},{7,5},{8,10},{9,11},{10,... | collective-permute-start | bytes 331784 | tf_op jit(solution)/shard_map/ppermute | solution.py:314
  25.5 2.4 %query_grad.1 = bf16[8,576,128]{2,1,0:T(8,128)(2,1)} custom-call(bf16[192,576]{1,0:T(8,128)(2,1)S(1)} %get-tuple-element.28.refs_0_, bf16[192,576]{1,0:T(8,128)(2,1)S(1)} %get-tuple-element.29.keys_ref.refs_1_, bf16[192,576]{1,0:T(8,128)(2,1)S(1)} %collective-permute-done.keys_ref.refs_2_, bf16[192,576]{1,0:T(8,128)(2,1)S(1)} %collective-permute-done.1.keys_ref.refs_3_, ...), custom_call_target="tpu_custom_call" | custom-call | flops 905969664 | tf_op jit(solution)/shard_map/query_grad/pallas_call | solution.py:206
  27.9 2.9 %collective-permute-done.5.got_ref = bf16[96,576]{1,0:T(8,128)(2,1)S(1)} collective-permute-done((bf16[96,576]{1,0:T(8,128)(2,1)S(1)}, bf16[96,576]{1,0:T(8,128)(2,1)S(1)}, u32[]{:S(2)}, u32[]{:S(2)}) %collective-permute-start.5) | collective-permute-done | bytes 110624 | tf_op jit(solution)/shard_map/ppermute | solution.py:314
  30.9 2.4 %collective-permute-done.9.refs_2_ = bf16[96,576]{1,0:T(8,128)(2,1)S(1)} collective-permute-done((bf16[96,576]{1,0:T(8,128)(2,1)S(1)}, bf16[96,576]{1,0:T(8,128)(2,1)S(1)}, u32[]{:S(2)}, u32[]{:S(2)}) %collective-permute-start.9) | collective-permute-done | bytes 110624 | tf_op jit(solution)/shard_map/ppermute | solution.py:314
  33.2 0.7 %last_sum.1 = bf16[192,576]{1,0:T(8,128)(2,1)} custom-call(bf16[96,576]{1,0:T(8,128)(2,1)S(1)} %sum_0.1.refs_0_, f32[96,576]{1,0:T(8,128)S(1)} %get-tuple-element.48.refs_1_, bf16[96,576]{1,0:T(8,128)(2,1)S(1)} %collective-permute-done.9.refs_2_), custom_call_target="tpu_custom_call" | custom-call | tf_op jit(solution)/shard_map/last_sum/pallas_call | solution.py:206
  (1 shorter events, 0.0 us)
Async XLA Ops:
  0.6 1.9 %copy-start = (bf16[128,8,576]{0,2,1:T(8,128)(2,1)S(1)}, bf16[128,8,576]{0,2,1:T(8,128)(2,1)}, u32[]{:S(2)}) copy-start(bf16[128,8,576]{0,2,1:T(8,128)(2,1)} %param.6) | copy-start | bytes 3538948
  0.6 1.9 %copy-start.1 = (bf16[128,8,512]{2,1,0:T(8,128)(2,1)S(1)}, bf16[128,8,512]{2,1,0:T(8,128)(2,1)}, u32[]{:S(2)}) copy-start(bf16[128,8,512]{2,1,0:T(8,128)(2,1)} %param.7) | copy-start | bytes 3145732
  0.7 1.9 %copy-start.2 = (bf16[128,8]{0,1:T(8,128)(2,1)S(1)}, bf16[128,8]{0,1:T(8,128)(2,1)}, u32[]{:S(2)}) copy-start(bf16[128,8]{0,1:T(8,128)(2,1)} %param.9) | copy-start | bytes 6148
  0.7 1.9 %copy-start.3 = (bf16[128,8]{0,1:T(8,128)(2,1)S(1)}, bf16[128,8]{0,1:T(8,128)(2,1)}, u32[]{:S(2)}) copy-start(bf16[128,8]{0,1:T(8,128)(2,1)} %param.10) | copy-start | bytes 6148
  0.7 1.9 %copy-start.4 = (s32[1,2]{1,0:T(1,128)S(1)}, s32[1,2]{1,0:T(1,128)}, u32[]{:S(2)}) copy-start(s32[1,2]{1,0:T(1,128)} %plan_ref.3) | copy-start | bytes 28
  2.2 8.2 %collective-permute-start = (bf16[192,576]{1,0:T(8,128)(2,1)S(1)}, bf16[192,576]{1,0:T(8,128)(2,1)S(1)}, u32[]{:S(2)}, u32[]{:S(2)}) collective-permute-start(bf16[192,576]{1,0:T(8,128)(2,1)S(1)} %get-tuple-element.30), channel_id=1, source_target_pairs={{0,4},{4,8},{8,12},{12,16},{16,20},{20,24},{24,28},{28,0},{1,5},{5... | collective-permute-start | bytes 663560 | tf_op jit(solution)/shard_map/ppermute | solution.py:256
  4.7 10.5 %collective-permute-start.1 = (bf16[192,576]{1,0:T(8,128)(2,1)S(1)}, bf16[192,576]{1,0:T(8,128)(2,1)S(1)}, u32[]{:S(2)}, u32[]{:S(2)}) collective-permute-start(bf16[192,576]{1,0:T(8,128)(2,1)S(1)} %get-tuple-element.31), channel_id=1, source_target_pairs={{0,4},{4,8},{8,12},{12,16},{16,20},{20,24},{24,28},{28,0},{1,5},{5... | collective-permute-start | bytes 663560 | tf_op jit(solution)/shard_map/ppermute | solution.py:256
  7.3 10.0 %collective-permute-start.2 = (bf16[96,576]{1,0:T(8,128)(2,1)S(1)}, bf16[96,576]{1,0:T(8,128)(2,1)S(1)}, u32[]{:S(2)}, u32[]{:S(2)}) collective-permute-start(bf16[96,576]{1,0:T(8,128)(2,1)S(1)} %get-tuple-element.39), channel_id=1, source_target_pairs={{0,1},{1,0},{2,3},{3,2},{4,5},{5,4},{6,7},{7,6},{8,9},{9,8},{10,11... | collective-permute-start | bytes 331784 | tf_op jit(solution)/shard_map/ppermute | solution.py:291
  11.8 7.5 %collective-permute-start.3 = (bf16[96,576]{1,0:T(8,128)(2,1)S(1)}, bf16[96,576]{1,0:T(8,128)(2,1)S(1)}, u32[]{:S(2)}, u32[]{:S(2)}) collective-permute-start(bf16[96,576]{1,0:T(8,128)(2,1)S(1)} %get-tuple-element.40), channel_id=1, source_target_pairs={{0,29},{1,28},{2,31},{3,30},{4,1},{5,0},{6,3},{7,2},{8,5},{9,4},{1... | collective-permute-start | bytes 331784 | tf_op jit(solution)/shard_map/ppermute | solution.py:303
  12.7 6.6 %collective-permute-start.4 = (bf16[96,576]{1,0:T(8,128)(2,1)S(1)}, bf16[96,576]{1,0:T(8,128)(2,1)S(1)}, u32[]{:S(2)}, u32[]{:S(2)}) collective-permute-start(bf16[96,576]{1,0:T(8,128)(2,1)S(1)} %get-tuple-element.41), channel_id=1, source_target_pairs={{0,28},{1,29},{2,30},{3,31},{4,0},{5,1},{6,2},{7,3},{8,4},{9,5},{1... | collective-permute-start | bytes 331784 | tf_op jit(solution)/shard_map/ppermute | solution.py:303
  14.6 7.5 %collective-permute-start.6 = (bf16[96,576]{1,0:T(8,128)(2,1)S(1)}, bf16[96,576]{1,0:T(8,128)(2,1)S(1)}, u32[]{:S(2)}, u32[]{:S(2)}) collective-permute-start(bf16[96,576]{1,0:T(8,128)(2,1)S(1)} %get-tuple-element.45), channel_id=1, source_target_pairs={{0,1},{1,0},{2,3},{3,2},{4,5},{5,4},{6,7},{7,6},{8,9},{9,8},{10,11... | collective-permute-start | bytes 331784 | tf_op jit(solution)/shard_map/ppermute | solution.py:291
  16.7 5.7 %collective-permute-start.7 = (bf16[96,576]{1,0:T(8,128)(2,1)S(1)}, bf16[96,576]{1,0:T(8,128)(2,1)S(1)}, u32[]{:S(2)}, u32[]{:S(2)}) collective-permute-start(bf16[96,576]{1,0:T(8,128)(2,1)S(1)} %get-tuple-element.46), channel_id=1, source_target_pairs={{0,29},{1,28},{2,31},{3,30},{4,1},{5,0},{6,3},{7,2},{8,5},{9,4},{1... | collective-permute-start | bytes 331784 | tf_op jit(solution)/shard_map/ppermute | solution.py:303
  17.3 5.3 %collective-permute-start.8 = (bf16[96,576]{1,0:T(8,128)(2,1)S(1)}, bf16[96,576]{1,0:T(8,128)(2,1)S(1)}, u32[]{:S(2)}, u32[]{:S(2)}) collective-permute-start(bf16[96,576]{1,0:T(8,128)(2,1)S(1)} %get-tuple-element.47), channel_id=1, source_target_pairs={{0,28},{1,29},{2,30},{3,31},{4,0},{5,1},{6,2},{7,3},{8,4},{9,5},{1... | collective-permute-start | bytes 331784 | tf_op jit(solution)/shard_map/ppermute | solution.py:303
  19.4 11.4 %collective-permute-start.5 = (bf16[96,576]{1,0:T(8,128)(2,1)S(1)}, bf16[96,576]{1,0:T(8,128)(2,1)S(1)}, u32[]{:S(2)}, u32[]{:S(2)}) collective-permute-start(bf16[96,576]{1,0:T(8,128)(2,1)S(1)} %get-tuple-element.43), channel_id=1, source_target_pairs={{0,2},{1,3},{2,0},{3,1},{4,6},{5,7},{6,4},{7,5},{8,10},{9,11},{10,... | collective-permute-start | bytes 331784 | tf_op jit(solution)/shard_map/ppermute | solution.py:314
  22.7 10.6 %collective-permute-start.9 = (bf16[96,576]{1,0:T(8,128)(2,1)S(1)}, bf16[96,576]{1,0:T(8,128)(2,1)S(1)}, u32[]{:S(2)}, u32[]{:S(2)}) collective-permute-start(bf16[96,576]{1,0:T(8,128)(2,1)S(1)} %get-tuple-element.49), channel_id=1, source_target_pairs={{0,2},{1,3},{2,0},{3,1},{4,6},{5,7},{6,4},{7,5},{8,10},{9,11},{10,... | collective-permute-start | bytes 331784 | tf_op jit(solution)/shard_map/ppermute | solution.py:314

commit v10 on v4

--- a/solution.py
+++ b/solution.py
@@ -15,7 +15,6 @@
 VMEM_LIMIT = 24 * 2**20
 NEVER = 1e30
 CHUNKS = 2
-COPIES = 1
 
 F32 = jnp.float32
 BF16 = jnp.bfloat16
@@ -29,29 +28,31 @@
     return lax.dot_general(a, b, (((1,), (1,)), ((), ())), preferred_element_type=F32)
 
 
-def block_of(lat_ref, block):
-    return lat_ref[:, pl.ds(pl.multiple_of(block * BLOCK, 128), BLOCK)]
-
-
 def send_block_kernel(low, plan_hbm, lat_hbm, *rest):
     out_refs = rest[:CHUNKS]
-    plan_ref, lat_ref, sems = rest[CHUNKS:]
-    step = lat_ref.shape[0] // COPIES
-    copies = [pltpu.make_async_copy(plan_hbm, plan_ref, sems.at[COPIES])]
-    for i in range(COPIES):
-        here = pl.ds(i * step, step)
-        copies.append(pltpu.make_async_copy(lat_hbm.at[here], lat_ref.at[here], sems.at[i]))
-    for copy in copies:
-        copy.start()
-    for copy in copies:
-        copy.wait()
-    keys = block_of(lat_ref, plan_ref[0, 1]).T
+    lat_ref, plan_ref, sems = rest[CHUNKS:]
+
+    def block_copy(block):
+        here = pl.ds(pl.multiple_of(block * BLOCK, 128), BLOCK)
+        return pltpu.make_async_copy(lat_hbm.at[:, here], lat_ref.at[block], sems.at[block])
+
+    blocks = lat_ref.shape[0]
+    plan_copy = pltpu.make_async_copy(plan_hbm, plan_ref, sems.at[blocks])
+    plan_copy.start()
+    for block in range(blocks):
+        block_copy(block).start()
+    plan_copy.wait()
+    sent = plan_ref[0, 1]
+    block_copy(sent).wait()
+    keys = lat_ref[sent].T
     rows = BLOCK // low
     part = rows // CHUNKS
     for c, out_ref in enumerate(out_refs):
         for j in range(low):
             start = j * rows + c * part
             out_ref[j * part : (j + 1) * part, :] = keys[start : start + part, :]
+    for i in range(1, blocks):
+        block_copy(lax.rem(sent + i, blocks)).wait()
 
 
 def heads_side_by_side(q_ref, first, count):
@@ -111,7 +112,7 @@
         sel_ref[i : i + 1, :] = jnp.broadcast_to(jnp.where(hit, 1.0, 0.0), (1, sel_ref.shape[1])).astype(F32)
     last = jnp.where(b0 > 0, 1.0, 0.0).astype(BF16)
     first = jnp.where(b0 > 0, 0.0, 1.0).astype(BF16)
-    keys = (lat_ref[:, :BLOCK] * first + lat_ref[:, BLOCK:] * last).T
+    keys = (lat_ref[0] * first + lat_ref[1] * last).T
     k_pos = b0 * BLOCK + lax.broadcasted_iota(jnp.int32, (BLOCK, PACKET), 0)
     q_pos = SHARD - PACKET + lax.broadcasted_iota(jnp.int32, (BLOCK, PACKET), 1)
     visit(keys, q_ref, rows_ref, norm_ref, delta_ref, None, k_pos <= q_pos, ds_ref, p_ref, total_ref)
@@ -136,7 +137,10 @@
     out_ref = rest[-1]
     heads = out_ref.shape[0]
     per = WIDE // PACKET
-    own = block_of(lat_ref, plan_ref[0, 0])
+    b0 = plan_ref[0:1, 0:1]
+    last = jnp.where(b0 > 0, 1.0, 0.0).astype(BF16)
+    first_block = jnp.where(b0 > 0, 0.0, 1.0).astype(BF16)
+    own = lat_ref[0] * first_block + lat_ref[1] * last
     fars = [ref[...].T for ref in far_refs]
     for first in range(0, heads, per):
         cols = slice(first * PACKET, (first + per) * PACKET)
@@ -221,12 +225,13 @@
     part = rows // CHUNKS
     keys = BLOCK // CHUNKS
 
-    sent = call(
+    blocks = SHARD // BLOCK
+    *sent, lat_blocks = call(
         functools.partial(send_block_kernel, low),
         "send_block",
         (plan, lat_t),
-        [((keys, width), BF16)] * CHUNKS,
-        [pltpu.SMEM(plan.shape, plan.dtype), pltpu.VMEM(lat_t.shape, BF16), pltpu.SemaphoreType.DMA((COPIES + 1,))],
+        [((keys, width), BF16)] * CHUNKS + [((blocks, width, BLOCK), BF16)],
+        [pltpu.SMEM(plan.shape, plan.dtype), pltpu.SemaphoreType.DMA((blocks + 1,))],
         flops=visit_flops,
         raw=(0, 1),
     )
@@ -235,7 +240,7 @@
     grad_rows, own_ds, sel, keep, *own = call(
         functools.partial(own_kernel, low),
         "own_visit",
-        (plan, lat_t, q_t, grad, norm_t, delta_t),
+        (plan, lat_blocks, q_t, grad, norm_t, delta_t),
         [((columns, LAT), BF16), ((BLOCK, columns), BF16), ((8, width), F32), ((rows, width), F32)]
         + [((part, width), BF16)] * (CHUNKS * (low - 1)),
         [pltpu.VMEM((BLOCK, columns), BF16), pltpu.VMEM((BLOCK, width), F32)],
@@ -243,7 +248,9 @@
 
     far_ds, own_parts, far_parts = [], [], []
     for c in range(CHUNKS):
-        later = [i for i in range(len(own)) if i % CHUNKS and i % CHUNKS >= c]
+        parts = own[c::CHUNKS]
+        own_parts.append([keep] + [lax.ppermute(parts[d - 1], ("seq", "head"), route(d, 0)) for d in range(1, low)])
+        later = [i for i in range(len(own)) if i % CHUNKS > c]
         ds, *far = call(
             functools.partial(far_kernel, low, len(later)),
             f"far_visit_{c}",
@@ -254,8 +261,6 @@
         )
         for i, x in zip(later, far[low:]):
             own[i] = x
-        parts = own[c::CHUNKS]
-        own_parts.append([keep] + [lax.ppermute(parts[d - 1], ("seq", "head"), route(d, 0)) for d in range(1, low)])
         far_ds.append(ds)
         far_parts.append([lax.ppermute(far[d], ("seq", "head"), route(d, 1)) for d in reversed(range(low))])
 
@@ -272,9 +277,8 @@
     (query_t,) = call(
         query_kernel,
         "query_grad",
-        (plan, lat_t, own_ds, *far_keys, *far_ds),
+        (plan, lat_blocks, own_ds, *far_keys, *far_ds),
         [((heads, width, packet), BF16)],
-        smem=(0,),
         flops=4 * columns * BLOCK * width,
     )
     (latent_out,) = call(last_kernel, "last_sum", (*mine[::-1], *got[::-1]), [((rows, width), BF16)])

time: 34.2 us -> 34 us (level)
  starting transfers between devices: 16.2 us -> 17 us
  Pallas kernels: 11.2 us -> 10.7 us
  waiting for transfers between devices: 5.86 us -> 5.46 us
    ppermute x2, waiting for transfers between devices: 1.43 us -> 0.01 us  [local(): lax.ppermute(parts[d - 1], ('seq', 'head'), route(d, 0))]
    ppermute x2, waiting for transfers between devices: 4.41 us -> 5.33 us  [local(): lax.ppermute(send, 'head', [(j, (j + low) % n_head) for j in range(n_head)])]
    ppermute x2, starting transfers between devices: 4.96 us -> 5.74 us  [local(): lax.ppermute(send, 'head', [(j, (j + low) % n_head) for j in range(n_head)])]
    pallas_call x8, Pallas kernels: 11.2 us -> 10.7 us  [call(): pl.pallas_call(kernel, name=name, out_shape=shapes, in_specs=[pl.BlockSpe...]
  transfers between devices with their start and end apart: 10 -> 10, of which waited for: 2 -> 3; matrix products, arithmetic and copies ran while one was open for 0% -> 0% of each run, Pallas kernels for 26% -> 25%
where the time goes in v10:
time: 34 us; the launch traced here: 33.9 us
  starting transfers between devices  17 us (50%)
  Pallas kernels  10.7 us (31%)
  waiting for transfers between devices  5.46 us (16%)
  between operations  0.71 us (2%)
    pallas_call x8, Pallas kernels, call(): pl.pallas_call(kernel, name=name, out_shape=shapes, in_specs=[pl.BlockSpe...  10.7 us
    ppermute x4, starting transfers between devices, local(): lax.ppermute(far[d], ('seq', 'head'), route(d, 1))  6.08 us
    ppermute x2, starting transfers between devices, local(): lax.ppermute(send, 'head', [(j, (j + low) % n_head) for j in range(n_head)])  5.74 us
    ppermute x2, waiting for transfers between devices, local(): lax.ppermute(send, 'head', [(j, (j + low) % n_head) for j in range(n_head)])  5.33 us
    ppermute x2, starting transfers between devices, local(): lax.ppermute(x, 'seq', [(i, (i + 1) % n_seq) for i in range(n_seq)])  3.11 us
    ppermute x2, starting transfers between devices, local(): lax.ppermute(parts[d - 1], ('seq', 'head'), route(d, 0))  2.09 us
  transfers between devices with their start and end apart: 10, of which 3 were waited for; matrix products, arithmetic and copies ran while one was open for 0% of the time, Pallas kernels for 25%

profile of v10, /device:TPU:0, one launch (start us, length us, event | category | flops | bytes accessed | tf_op | source)
XLA Modules:
  0.0 33.9 jit_solution(4131109019008187241)
XLA Ops:
  0.6 0.0 copy-start
  0.6 0.0 copy-start.1
  0.7 0.0 copy-start.2
  0.7 0.0 copy-start.3
  0.7 0.0 copy-start.4
  0.7 1.5 %send_block.1 = (bf16[192,576]{1,0:T(8,128)(2,1)S(1)}, bf16[192,576]{1,0:T(8,128)(2,1)S(1)}, bf16[2,576,384]{2,1,0:T(8,128)(2,1)S(1)}) custom-call(s32[1,2]{1,0:T(1,128)} %plan_ref.3, bf16[576,768]{1,0:T(8,128)(2,1)} %bitcast.17), custom_call_target="tpu_custom_call" | custom-call | flops 1711276032 | bytes 2211848 | tf_op jit(solution)/shard_map/send_block/pallas_call | solution.py:189
  2.2 0.4 %collective-permute-start = (bf16[192,576]{1,0:T(8,128)(2,1)S(1)}, bf16[192,576]{1,0:T(8,128)(2,1)S(1)}, u32[]{:S(2)}, u32[]{:S(2)}) collective-permute-start(bf16[192,576]{1,0:T(8,128)(2,1)S(1)} %get-tuple-element.24), channel_id=1, source_target_pairs={{0,4},{4,8},{8,12},{12,16},{16,20},{20,24},{24,28},{28,0},{1,5},{5... | collective-permute-start | bytes 663560 | tf_op jit(solution)/shard_map/ppermute | solution.py:238
  2.6 2.7 %collective-permute-start.1 = (bf16[192,576]{1,0:T(8,128)(2,1)S(1)}, bf16[192,576]{1,0:T(8,128)(2,1)S(1)}, u32[]{:S(2)}, u32[]{:S(2)}) collective-permute-start(bf16[192,576]{1,0:T(8,128)(2,1)S(1)} %get-tuple-element.25), channel_id=1, source_target_pairs={{0,4},{4,8},{8,12},{12,16},{16,20},{20,24},{24,28},{28,0},{1,5},{5... | collective-permute-start | bytes 663560 | tf_op jit(solution)/shard_map/ppermute | solution.py:238
  5.3 0.0 copy-done
  5.3 0.0 copy-done.1
  5.3 0.0 copy-done.2
  5.3 0.0 copy-done.3
  5.3 0.0 copy-done.4
  5.3 2.8 %own_visit.1 = (bf16[1024,512]{1,0:T(8,128)(2,1)S(1)}, bf16[384,1024]{1,0:T(8,128)(2,1)S(1)}, f32[8,576]{1,0:T(8,128)S(1)}, f32[192,576]{1,0:T(8,128)S(1)}, bf16...) custom-call(s32[1,2]{1,0:T(1,128)S(1)} %copy-done.4, bf16[2,576,384]{2,1,0:T(8,128)(2,1)S(1)} %get-tuple-element.22.lat_ref, ...), custom_call_target="tpu_custom_call" | custom-call | bytes 5634056 | tf_op jit(solution)/shard_map/own_visit/pallas_call | solution.py:189
  8.2 1.6 %collective-permute-start.5 = (bf16[96,576]{1,0:T(8,128)(2,1)S(1)}, bf16[96,576]{1,0:T(8,128)(2,1)S(1)}, u32[]{:S(2)}, u32[]{:S(2)}) collective-permute-start(bf16[96,576]{1,0:T(8,128)(2,1)S(1)} %get-tuple-element.36), channel_id=1, source_target_pairs={{0,1},{1,0},{2,3},{3,2},{4,5},{5,4},{6,7},{7,6},{8,9},{9,8},{10,11... | collective-permute-start | bytes 331784 | tf_op jit(solution)/shard_map/ppermute | solution.py:252
  9.8 0.0 collective-permute-done.keys_ref.rest_0_
  9.8 1.5 %far_visit_0.1 = (bf16[192,1024]{1,0:T(8,128)(2,1)S(1)}, bf16[96,576]{1,0:T(8,128)(2,1)S(1)}, bf16[96,576]{1,0:T(8,128)(2,1)S(1)}, bf16[96,576]{1,0:T(8,128)(2,1)S(1)}) custom-call(bf16[192,576]{1,0:T(8,128)(2,1)S(1)} %collective-permute-done.keys_ref.rest_0_, bf16[8,576,128]{2,1,0:T(8,128)(2,1)S(1)} %bitcast.7, ...), custom_call_target="tpu_custom_call", output_to_operand_aliasing={{3}: (5, {})} | custom-call | bytes 3067904 | tf_op jit(solution)/shard_map/far_visit_0/pallas_call | solution.py:189
  11.3 0.7 %collective-permute-start.6 = (bf16[96,576]{1,0:T(8,128)(2,1)S(1)}, bf16[96,576]{1,0:T(8,128)(2,1)S(1)}, u32[]{:S(2)}, u32[]{:S(2)}) collective-permute-start(bf16[96,576]{1,0:T(8,128)(2,1)S(1)} %get-tuple-element.37), channel_id=1, source_target_pairs={{0,29},{1,28},{2,31},{3,30},{4,1},{5,0},{6,3},{7,2},{8,5},{9,4},{1... | collective-permute-start | bytes 331784 | tf_op jit(solution)/shard_map/ppermute | solution.py:265
  12.0 2.4 %collective-permute-start.7 = (bf16[96,576]{1,0:T(8,128)(2,1)S(1)}, bf16[96,576]{1,0:T(8,128)(2,1)S(1)}, u32[]{:S(2)}, u32[]{:S(2)}) collective-permute-start(bf16[96,576]{1,0:T(8,128)(2,1)S(1)} %get-tuple-element.38), channel_id=1, source_target_pairs={{0,28},{1,29},{2,30},{3,31},{4,0},{5,1},{6,2},{7,3},{8,4},{9,5},{1... | collective-permute-start | bytes 331784 | tf_op jit(solution)/shard_map/ppermute | solution.py:265
  14.4 0.4 %collective-permute-start.2 = (bf16[96,576]{1,0:T(8,128)(2,1)S(1)}, bf16[96,576]{1,0:T(8,128)(2,1)S(1)}, u32[]{:S(2)}, u32[]{:S(2)}) collective-permute-start(bf16[96,576]{1,0:T(8,128)(2,1)S(1)} %get-tuple-element.32), channel_id=1, source_target_pairs={{0,1},{1,0},{2,3},{3,2},{4,5},{5,4},{6,7},{7,6},{8,9},{9,8},{10,11... | collective-permute-start | bytes 331784 | tf_op jit(solution)/shard_map/ppermute | solution.py:252
  14.9 0.0 collective-permute-done.1.keys_ref.rest_1_
  14.9 1.5 %far_visit_1.1 = (bf16[192,1024]{1,0:T(8,128)(2,1)S(1)}, bf16[96,576]{1,0:T(8,128)(2,1)S(1)}, bf16[96,576]{1,0:T(8,128)(2,1)S(1)}) custom-call(bf16[192,576]{1,0:T(8,128)(2,1)S(1)} %collective-permute-done.1.keys_ref.rest_1_, bf16[8,576,128]{2,1,0:T(8,128)(2,1)S(1)} %bitcast.8, bf16[1024,512]{1,0:T(8,128)(2,1)S(1)} %get-tuple-element.26.grad_ref, ...), custom_call_target="tpu_custom_call" | custom-call | bytes 3067904 | tf_op jit(solution)/shard_map/far_visit_1/pallas_call | solution.py:189
  16.4 0.8 %collective-permute-start.3 = (bf16[96,576]{1,0:T(8,128)(2,1)S(1)}, bf16[96,576]{1,0:T(8,128)(2,1)S(1)}, u32[]{:S(2)}, u32[]{:S(2)}) collective-permute-start(bf16[96,576]{1,0:T(8,128)(2,1)S(1)} %get-tuple-element.33), channel_id=1, source_target_pairs={{0,29},{1,28},{2,31},{3,30},{4,1},{5,0},{6,3},{7,2},{8,5},{9,4},{1... | collective-permute-start | bytes 331784 | tf_op jit(solution)/shard_map/ppermute | solution.py:265
  17.2 0.0 collective-permute-done.5.rest_1_
  17.2 2.1 %collective-permute-start.4 = (bf16[96,576]{1,0:T(8,128)(2,1)S(1)}, bf16[96,576]{1,0:T(8,128)(2,1)S(1)}, u32[]{:S(2)}, u32[]{:S(2)}) collective-permute-start(bf16[96,576]{1,0:T(8,128)(2,1)S(1)} %get-tuple-element.34), channel_id=1, source_target_pairs={{0,28},{1,29},{2,30},{3,31},{4,0},{5,1},{6,2},{7,3},{8,4},{9,5},{1... | collective-permute-start | bytes 331784 | tf_op jit(solution)/shard_map/ppermute | solution.py:265
  19.3 0.0 collective-permute-done.6.rest_2_
  19.3 0.0 collective-permute-done.7.rest_3_
  19.3 0.1 combine_0.1
  19.4 2.7 %collective-permute-start.9 = (bf16[96,576]{1,0:T(8,128)(2,1)S(1)}, bf16[96,576]{1,0:T(8,128)(2,1)S(1)}, u32[]{:S(2)}, u32[]{:S(2)}) collective-permute-start(bf16[96,576]{1,0:T(8,128)(2,1)S(1)} %get-tuple-element.41), channel_id=1, source_target_pairs={{0,2},{1,3},{2,0},{3,1},{4,6},{5,7},{6,4},{7,5},{8,10},{9,11},{10,... | collective-permute-start | bytes 331784 | tf_op jit(solution)/shard_map/ppermute | solution.py:275
  22.1 0.0 collective-permute-done.2.rest_1_
  22.1 0.0 collective-permute-done.3.rest_2_
  22.1 0.1 collective-permute-done.4.rest_3_
  22.2 0.1 combine_1.1
  22.3 3.1 %collective-permute-start.8 = (bf16[96,576]{1,0:T(8,128)(2,1)S(1)}, bf16[96,576]{1,0:T(8,128)(2,1)S(1)}, u32[]{:S(2)}, u32[]{:S(2)}) collective-permute-start(bf16[96,576]{1,0:T(8,128)(2,1)S(1)} %get-tuple-element.40), channel_id=1, source_target_pairs={{0,2},{1,3},{2,0},{3,1},{4,6},{5,7},{6,4},{7,5},{8,10},{9,11},{10,... | collective-permute-start | bytes 331784 | tf_op jit(solution)/shard_map/ppermute | solution.py:275
  25.4 2.4 %query_grad.1 = bf16[8,576,128]{2,1,0:T(8,128)(2,1)} custom-call(s32[1,2]{1,0:T(1,128)S(1)} %copy-done.4, bf16[2,576,384]{2,1,0:T(8,128)(2,1)S(1)} %get-tuple-element.22.lat_ref, bf16[384,1024]{1,0:T(8,128)(2,1)S(1)} %get-tuple-element.23.own_ds_ref, bf16[192,576]{1,0:T(8,128)(2,1)S(1)} %collective-permute-done.keys_ref.rest_0_, ...), custom_call_target="tpu_custom_call" | custom-call | flops 905969664 | bytes 4079624 | tf_op jit(solution)/shard_map/query_grad/pallas_call | solution.py:189
  27.8 3.1 %collective-permute-done.9.refs_3_ = bf16[96,576]{1,0:T(8,128)(2,1)S(1)} collective-permute-done((bf16[96,576]{1,0:T(8,128)(2,1)S(1)}, bf16[96,576]{1,0:T(8,128)(2,1)S(1)}, u32[]{:S(2)}, u32[]{:S(2)}) %collective-permute-start.9) | collective-permute-done | bytes 110624 | tf_op jit(solution)/shard_map/ppermute | solution.py:275
  30.9 2.2 %collective-permute-done.8.refs_2_ = bf16[96,576]{1,0:T(8,128)(2,1)S(1)} collective-permute-done((bf16[96,576]{1,0:T(8,128)(2,1)S(1)}, bf16[96,576]{1,0:T(8,128)(2,1)S(1)}, u32[]{:S(2)}, u32[]{:S(2)}) %collective-permute-start.8) | collective-permute-done | bytes 110624 | tf_op jit(solution)/shard_map/ppermute | solution.py:275
  33.1 0.7 %last_sum.1 = bf16[192,576]{1,0:T(8,128)(2,1)} custom-call(f32[96,576]{1,0:T(8,128)S(1)} %get-tuple-element.35.refs_0_, f32[96,576]{1,0:T(8,128)S(1)} %get-tuple-element.39.refs_1_, bf16[96,576]{1,0:T(8,128)(2,1)S(1)} %collective-permute-done.8.refs_2_, bf16[96,576]{1,0:T(8,128)(2,1)S(1)} %collective-permute-done.9.refs_3_), custom_call_target="tpu_custom_call" | custom-call | bytes 884736 | tf_op jit(solution)/shard_map/last_sum/pallas_call | solution.py:189
Async XLA Ops:
  0.6 4.7 %copy-start = (bf16[128,8,576]{0,2,1:T(8,128)(2,1)S(1)}, bf16[128,8,576]{0,2,1:T(8,128)(2,1)}, u32[]{:S(2)}) copy-start(bf16[128,8,576]{0,2,1:T(8,128)(2,1)} %param.6) | copy-start | bytes 3538948
  0.6 4.7 %copy-start.1 = (bf16[128,8,512]{2,1,0:T(8,128)(2,1)S(1)}, bf16[128,8,512]{2,1,0:T(8,128)(2,1)}, u32[]{:S(2)}) copy-start(bf16[128,8,512]{2,1,0:T(8,128)(2,1)} %param.7) | copy-start | bytes 3145732
  0.7 4.7 %copy-start.2 = (bf16[128,8]{0,1:T(8,128)(2,1)S(1)}, bf16[128,8]{0,1:T(8,128)(2,1)}, u32[]{:S(2)}) copy-start(bf16[128,8]{0,1:T(8,128)(2,1)} %param.9) | copy-start | bytes 6148
  0.7 4.7 %copy-start.3 = (bf16[128,8]{0,1:T(8,128)(2,1)S(1)}, bf16[128,8]{0,1:T(8,128)(2,1)}, u32[]{:S(2)}) copy-start(bf16[128,8]{0,1:T(8,128)(2,1)} %param.10) | copy-start | bytes 6148
  0.7 4.7 %copy-start.4 = (s32[1,2]{1,0:T(1,128)S(1)}, s32[1,2]{1,0:T(1,128)}, u32[]{:S(2)}) copy-start(s32[1,2]{1,0:T(1,128)} %plan_ref.3) | copy-start | bytes 28
  2.2 7.6 %collective-permute-start = (bf16[192,576]{1,0:T(8,128)(2,1)S(1)}, bf16[192,576]{1,0:T(8,128)(2,1)S(1)}, u32[]{:S(2)}, u32[]{:S(2)}) collective-permute-start(bf16[192,576]{1,0:T(8,128)(2,1)S(1)} %get-tuple-element.24), channel_id=1, source_target_pairs={{0,4},{4,8},{8,12},{12,16},{16,20},{20,24},{24,28},{28,0},{1,5},{5... | collective-permute-start | bytes 663560 | tf_op jit(solution)/shard_map/ppermute | solution.py:238
  2.6 12.3 %collective-permute-start.1 = (bf16[192,576]{1,0:T(8,128)(2,1)S(1)}, bf16[192,576]{1,0:T(8,128)(2,1)S(1)}, u32[]{:S(2)}, u32[]{:S(2)}) collective-permute-start(bf16[192,576]{1,0:T(8,128)(2,1)S(1)} %get-tuple-element.25), channel_id=1, source_target_pairs={{0,4},{4,8},{8,12},{12,16},{16,20},{20,24},{24,28},{28,0},{1,5},{5... | collective-permute-start | bytes 663560 | tf_op jit(solution)/shard_map/ppermute | solution.py:238
  8.2 9.0 %collective-permute-start.5 = (bf16[96,576]{1,0:T(8,128)(2,1)S(1)}, bf16[96,576]{1,0:T(8,128)(2,1)S(1)}, u32[]{:S(2)}, u32[]{:S(2)}) collective-permute-start(bf16[96,576]{1,0:T(8,128)(2,1)S(1)} %get-tuple-element.36), channel_id=1, source_target_pairs={{0,1},{1,0},{2,3},{3,2},{4,5},{5,4},{6,7},{7,6},{8,9},{9,8},{10,11... | collective-permute-start | bytes 331784 | tf_op jit(solution)/shard_map/ppermute | solution.py:252
  11.3 8.0 %collective-permute-start.6 = (bf16[96,576]{1,0:T(8,128)(2,1)S(1)}, bf16[96,576]{1,0:T(8,128)(2,1)S(1)}, u32[]{:S(2)}, u32[]{:S(2)}) collective-permute-start(bf16[96,576]{1,0:T(8,128)(2,1)S(1)} %get-tuple-element.37), channel_id=1, source_target_pairs={{0,29},{1,28},{2,31},{3,30},{4,1},{5,0},{6,3},{7,2},{8,5},{9,4},{1... | collective-permute-start | bytes 331784 | tf_op jit(solution)/shard_map/ppermute | solution.py:265
  12.0 7.3 %collective-permute-start.7 = (bf16[96,576]{1,0:T(8,128)(2,1)S(1)}, bf16[96,576]{1,0:T(8,128)(2,1)S(1)}, u32[]{:S(2)}, u32[]{:S(2)}) collective-permute-start(bf16[96,576]{1,0:T(8,128)(2,1)S(1)} %get-tuple-element.38), channel_id=1, source_target_pairs={{0,28},{1,29},{2,30},{3,31},{4,0},{5,1},{6,2},{7,3},{8,4},{9,5},{1... | collective-permute-start | bytes 331784 | tf_op jit(solution)/shard_map/ppermute | solution.py:265
  14.4 7.6 %collective-permute-start.2 = (bf16[96,576]{1,0:T(8,128)(2,1)S(1)}, bf16[96,576]{1,0:T(8,128)(2,1)S(1)}, u32[]{:S(2)}, u32[]{:S(2)}) collective-permute-start(bf16[96,576]{1,0:T(8,128)(2,1)S(1)} %get-tuple-element.32), channel_id=1, source_target_pairs={{0,1},{1,0},{2,3},{3,2},{4,5},{5,4},{6,7},{7,6},{8,9},{9,8},{10,11... | collective-permute-start | bytes 331784 | tf_op jit(solution)/shard_map/ppermute | solution.py:252
  16.4 5.7 %collective-permute-start.3 = (bf16[96,576]{1,0:T(8,128)(2,1)S(1)}, bf16[96,576]{1,0:T(8,128)(2,1)S(1)}, u32[]{:S(2)}, u32[]{:S(2)}) collective-permute-start(bf16[96,576]{1,0:T(8,128)(2,1)S(1)} %get-tuple-element.33), channel_id=1, source_target_pairs={{0,29},{1,28},{2,31},{3,30},{4,1},{5,0},{6,3},{7,2},{8,5},{9,4},{1... | collective-permute-start | bytes 331784 | tf_op jit(solution)/shard_map/ppermute | solution.py:265
  17.2 5.0 %collective-permute-start.4 = (bf16[96,576]{1,0:T(8,128)(2,1)S(1)}, bf16[96,576]{1,0:T(8,128)(2,1)S(1)}, u32[]{:S(2)}, u32[]{:S(2)}) collective-permute-start(bf16[96,576]{1,0:T(8,128)(2,1)S(1)} %get-tuple-element.34), channel_id=1, source_target_pairs={{0,28},{1,29},{2,30},{3,31},{4,0},{5,1},{6,2},{7,3},{8,4},{9,5},{1... | collective-permute-start | bytes 331784 | tf_op jit(solution)/shard_map/ppermute | solution.py:265
  19.4 11.5 %collective-permute-start.9 = (bf16[96,576]{1,0:T(8,128)(2,1)S(1)}, bf16[96,576]{1,0:T(8,128)(2,1)S(1)}, u32[]{:S(2)}, u32[]{:S(2)}) collective-permute-start(bf16[96,576]{1,0:T(8,128)(2,1)S(1)} %get-tuple-element.41), channel_id=1, source_target_pairs={{0,2},{1,3},{2,0},{3,1},{4,6},{5,7},{6,4},{7,5},{8,10},{9,11},{10,... | collective-permute-start | bytes 331784 | tf_op jit(solution)/shard_map/ppermute | solution.py:275
  22.3 10.9 %collective-permute-start.8 = (bf16[96,576]{1,0:T(8,128)(2,1)S(1)}, bf16[96,576]{1,0:T(8,128)(2,1)S(1)}, u32[]{:S(2)}, u32[]{:S(2)}) collective-permute-start(bf16[96,576]{1,0:T(8,128)(2,1)S(1)} %get-tuple-element.40), channel_id=1, source_target_pairs={{0,2},{1,3},{2,0},{3,1},{4,6},{5,7},{6,4},{7,5},{8,10},{9,11},{10,... | collective-permute-start | bytes 331784 | tf_op jit(solution)/shard_map/ppermute | solution.py:275

commit v11 on v10

--- a/solution.py
+++ b/solution.py
@@ -12,6 +12,7 @@
 BLOCK = 384
 SHARD = 768
 WIDE = 256
+VISIT_WIDE = 512
 VMEM_LIMIT = 24 * 2**20
 NEVER = 1e30
 CHUNKS = 2
@@ -61,7 +62,7 @@
 
 def visit(keys, q_ref, grad_ref, norm_ref, delta_ref, live, visible, ds_ref, p_ref, grad_out_ref):
     heads = q_ref.shape[0]
-    per = WIDE // PACKET
+    per = VISIT_WIDE // PACKET
     for first in range(0, heads, per):
         cols = slice(first * PACKET, (first + per) * PACKET)
         scores = dot(keys, heads_side_by_side(q_ref, first, per))

time: 34 us -> 34.1 us (level)
  transfers between devices with their start and end apart: 10 -> 10, of which waited for: 3 -> 4; matrix products, arithmetic and copies ran while one was open for 0% -> 0% of each run, Pallas kernels for 25% -> 25%
where the time goes in v11:
time: 34.1 us; the launch traced here: 33.9 us
  starting transfers between devices  16.8 us (49%)
  Pallas kernels  10.8 us (32%)
  waiting for transfers between devices  5.56 us (16%)
  between operations  0.71 us (2%)
    pallas_call x8, Pallas kernels, call(): pl.pallas_call(kernel, name=name, out_shape=shapes, in_specs=[pl.BlockSpe...  10.8 us
    ppermute x4, starting transfers between devices, local(): lax.ppermute(far[d], ('seq', 'head'), route(d, 1))  6.1 us
    ppermute x2, starting transfers between devices, local(): lax.ppermute(send, 'head', [(j, (j + low) % n_head) for j in range(n_head)])  5.63 us
    ppermute x2, waiting for transfers between devices, local(): lax.ppermute(send, 'head', [(j, (j + low) % n_head) for j in range(n_head)])  5.41 us
    ppermute x2, starting transfers between devices, local(): lax.ppermute(x, 'seq', [(i, (i + 1) % n_seq) for i in range(n_seq)])  2.97 us
    ppermute x2, starting transfers between devices, local(): lax.ppermute(parts[d - 1], ('seq', 'head'), route(d, 0))  2.09 us
  transfers between devices with their start and end apart: 10, of which 4 were waited for; matrix products, arithmetic and copies ran while one was open for 0% of the time, Pallas kernels for 25%

profile of v11, /device:TPU:0, one launch (start us, length us, event | category | flops | bytes accessed | tf_op | source)
XLA Modules:
  0.0 33.9 jit_solution(4018232834106213100)
XLA Ops:
  0.6 0.0 copy-start
  0.6 0.0 copy-start.1
  0.7 0.0 copy-start.2
  0.7 0.0 copy-start.3
  0.7 0.0 copy-start.4
  0.7 1.5 %send_block.1 = (bf16[192,576]{1,0:T(8,128)(2,1)S(1)}, bf16[192,576]{1,0:T(8,128)(2,1)S(1)}, bf16[2,576,384]{2,1,0:T(8,128)(2,1)S(1)}) custom-call(s32[1,2]{1,0:T(1,128)} %plan_ref.3, bf16[576,768]{1,0:T(8,128)(2,1)} %bitcast.17), custom_call_target="tpu_custom_call" | custom-call | flops 1711276032 | bytes 2211848 | tf_op jit(solution)/shard_map/send_block/pallas_call | solution.py:190
  2.2 0.5 %collective-permute-start = (bf16[192,576]{1,0:T(8,128)(2,1)S(1)}, bf16[192,576]{1,0:T(8,128)(2,1)S(1)}, u32[]{:S(2)}, u32[]{:S(2)}) collective-permute-start(bf16[192,576]{1,0:T(8,128)(2,1)S(1)} %get-tuple-element.24), channel_id=1, source_target_pairs={{0,4},{4,8},{8,12},{12,16},{16,20},{20,24},{24,28},{28,0},{1,5},{5... | collective-permute-start | bytes 663560 | tf_op jit(solution)/shard_map/ppermute | solution.py:239
  2.7 2.5 %collective-permute-start.1 = (bf16[192,576]{1,0:T(8,128)(2,1)S(1)}, bf16[192,576]{1,0:T(8,128)(2,1)S(1)}, u32[]{:S(2)}, u32[]{:S(2)}) collective-permute-start(bf16[192,576]{1,0:T(8,128)(2,1)S(1)} %get-tuple-element.25), channel_id=1, source_target_pairs={{0,4},{4,8},{8,12},{12,16},{16,20},{20,24},{24,28},{28,0},{1,5},{5... | collective-permute-start | bytes 663560 | tf_op jit(solution)/shard_map/ppermute | solution.py:239
  5.2 0.0 copy-done
  5.2 0.0 copy-done.1
  5.2 0.0 copy-done.2
  5.2 0.0 copy-done.3
  5.2 0.0 copy-done.4
  5.2 2.8 %own_visit.1 = (bf16[1024,512]{1,0:T(8,128)(2,1)S(1)}, bf16[384,1024]{1,0:T(8,128)(2,1)S(1)}, f32[8,576]{1,0:T(8,128)S(1)}, f32[192,576]{1,0:T(8,128)S(1)}, bf16...) custom-call(s32[1,2]{1,0:T(1,128)S(1)} %copy-done.4, bf16[2,576,384]{2,1,0:T(8,128)(2,1)S(1)} %get-tuple-element.22.lat_ref, ...), custom_call_target="tpu_custom_call" | custom-call | bytes 5634056 | tf_op jit(solution)/shard_map/own_visit/pallas_call | solution.py:190
  8.0 1.6 %collective-permute-start.5 = (bf16[96,576]{1,0:T(8,128)(2,1)S(1)}, bf16[96,576]{1,0:T(8,128)(2,1)S(1)}, u32[]{:S(2)}, u32[]{:S(2)}) collective-permute-start(bf16[96,576]{1,0:T(8,128)(2,1)S(1)} %get-tuple-element.36), channel_id=1, source_target_pairs={{0,1},{1,0},{2,3},{3,2},{4,5},{5,4},{6,7},{7,6},{8,9},{9,8},{10,11... | collective-permute-start | bytes 331784 | tf_op jit(solution)/shard_map/ppermute | solution.py:253
  9.7 0.0 collective-permute-done.keys_ref.rest_0_
  9.7 1.5 %far_visit_0.1 = (bf16[192,1024]{1,0:T(8,128)(2,1)S(1)}, bf16[96,576]{1,0:T(8,128)(2,1)S(1)}, bf16[96,576]{1,0:T(8,128)(2,1)S(1)}, bf16[96,576]{1,0:T(8,128)(2,1)S(1)}) custom-call(bf16[192,576]{1,0:T(8,128)(2,1)S(1)} %collective-permute-done.keys_ref.rest_0_, bf16[8,576,128]{2,1,0:T(8,128)(2,1)S(1)} %bitcast.7, ...), custom_call_target="tpu_custom_call", output_to_operand_aliasing={{3}: (5, {})} | custom-call | bytes 3067904 | tf_op jit(solution)/shard_map/far_visit_0/pallas_call | solution.py:190
  11.2 0.9 %collective-permute-start.6 = (bf16[96,576]{1,0:T(8,128)(2,1)S(1)}, bf16[96,576]{1,0:T(8,128)(2,1)S(1)}, u32[]{:S(2)}, u32[]{:S(2)}) collective-permute-start(bf16[96,576]{1,0:T(8,128)(2,1)S(1)} %get-tuple-element.37), channel_id=1, source_target_pairs={{0,29},{1,28},{2,31},{3,30},{4,1},{5,0},{6,3},{7,2},{8,5},{9,4},{1... | collective-permute-start | bytes 331784 | tf_op jit(solution)/shard_map/ppermute | solution.py:266
  12.1 2.6 %collective-permute-start.7 = (bf16[96,576]{1,0:T(8,128)(2,1)S(1)}, bf16[96,576]{1,0:T(8,128)(2,1)S(1)}, u32[]{:S(2)}, u32[]{:S(2)}) collective-permute-start(bf16[96,576]{1,0:T(8,128)(2,1)S(1)} %get-tuple-element.38), channel_id=1, source_target_pairs={{0,28},{1,29},{2,30},{3,31},{4,0},{5,1},{6,2},{7,3},{8,4},{9,5},{1... | collective-permute-start | bytes 331784 | tf_op jit(solution)/shard_map/ppermute | solution.py:266
  14.7 0.4 %collective-permute-start.2 = (bf16[96,576]{1,0:T(8,128)(2,1)S(1)}, bf16[96,576]{1,0:T(8,128)(2,1)S(1)}, u32[]{:S(2)}, u32[]{:S(2)}) collective-permute-start(bf16[96,576]{1,0:T(8,128)(2,1)S(1)} %get-tuple-element.32), channel_id=1, source_target_pairs={{0,1},{1,0},{2,3},{3,2},{4,5},{5,4},{6,7},{7,6},{8,9},{9,8},{10,11... | collective-permute-start | bytes 331784 | tf_op jit(solution)/shard_map/ppermute | solution.py:253
  15.1 0.0 collective-permute-done.1.keys_ref.rest_1_
  15.1 1.5 %far_visit_1.1 = (bf16[192,1024]{1,0:T(8,128)(2,1)S(1)}, bf16[96,576]{1,0:T(8,128)(2,1)S(1)}, bf16[96,576]{1,0:T(8,128)(2,1)S(1)}) custom-call(bf16[192,576]{1,0:T(8,128)(2,1)S(1)} %collective-permute-done.1.keys_ref.rest_1_, bf16[8,576,128]{2,1,0:T(8,128)(2,1)S(1)} %bitcast.8, bf16[1024,512]{1,0:T(8,128)(2,1)S(1)} %get-tuple-element.26.grad_ref, ...), custom_call_target="tpu_custom_call" | custom-call | bytes 3067904 | tf_op jit(solution)/shard_map/far_visit_1/pallas_call | solution.py:190
  16.7 0.8 %collective-permute-start.3 = (bf16[96,576]{1,0:T(8,128)(2,1)S(1)}, bf16[96,576]{1,0:T(8,128)(2,1)S(1)}, u32[]{:S(2)}, u32[]{:S(2)}) collective-permute-start(bf16[96,576]{1,0:T(8,128)(2,1)S(1)} %get-tuple-element.33), channel_id=1, source_target_pairs={{0,29},{1,28},{2,31},{3,30},{4,1},{5,0},{6,3},{7,2},{8,5},{9,4},{1... | collective-permute-start | bytes 331784 | tf_op jit(solution)/shard_map/ppermute | solution.py:266
  17.5 0.0 collective-permute-done.5.rest_1_
  17.5 1.9 %collective-permute-start.4 = (bf16[96,576]{1,0:T(8,128)(2,1)S(1)}, bf16[96,576]{1,0:T(8,128)(2,1)S(1)}, u32[]{:S(2)}, u32[]{:S(2)}) collective-permute-start(bf16[96,576]{1,0:T(8,128)(2,1)S(1)} %get-tuple-element.34), channel_id=1, source_target_pairs={{0,28},{1,29},{2,30},{3,31},{4,0},{5,1},{6,2},{7,3},{8,4},{9,5},{1... | collective-permute-start | bytes 331784 | tf_op jit(solution)/shard_map/ppermute | solution.py:266
  19.3 0.0 collective-permute-done.6.rest_2_
  19.3 0.0 collective-permute-done.7.rest_3_
  19.3 0.1 combine_0.1
  19.4 2.7 %collective-permute-start.9 = (bf16[96,576]{1,0:T(8,128)(2,1)S(1)}, bf16[96,576]{1,0:T(8,128)(2,1)S(1)}, u32[]{:S(2)}, u32[]{:S(2)}) collective-permute-start(bf16[96,576]{1,0:T(8,128)(2,1)S(1)} %get-tuple-element.41), channel_id=1, source_target_pairs={{0,2},{1,3},{2,0},{3,1},{4,6},{5,7},{6,4},{7,5},{8,10},{9,11},{10,... | collective-permute-start | bytes 331784 | tf_op jit(solution)/shard_map/ppermute | solution.py:276
  22.1 0.0 collective-permute-done.2.rest_1_
  22.1 0.1 collective-permute-done.3.rest_2_
  22.2 0.1 collective-permute-done.4.rest_3_
  22.2 0.1 combine_1.1
  22.4 3.0 %collective-permute-start.8 = (bf16[96,576]{1,0:T(8,128)(2,1)S(1)}, bf16[96,576]{1,0:T(8,128)(2,1)S(1)}, u32[]{:S(2)}, u32[]{:S(2)}) collective-permute-start(bf16[96,576]{1,0:T(8,128)(2,1)S(1)} %get-tuple-element.40), channel_id=1, source_target_pairs={{0,2},{1,3},{2,0},{3,1},{4,6},{5,7},{6,4},{7,5},{8,10},{9,11},{10,... | collective-permute-start | bytes 331784 | tf_op jit(solution)/shard_map/ppermute | solution.py:276
  25.3 2.4 %query_grad.1 = bf16[8,576,128]{2,1,0:T(8,128)(2,1)} custom-call(s32[1,2]{1,0:T(1,128)S(1)} %copy-done.4, bf16[2,576,384]{2,1,0:T(8,128)(2,1)S(1)} %get-tuple-element.22.lat_ref, bf16[384,1024]{1,0:T(8,128)(2,1)S(1)} %get-tuple-element.23.own_ds_ref, bf16[192,576]{1,0:T(8,128)(2,1)S(1)} %collective-permute-done.keys_ref.rest_0_, ...), custom_call_target="tpu_custom_call" | custom-call | flops 905969664 | bytes 4079624 | tf_op jit(solution)/shard_map/query_grad/pallas_call | solution.py:190
  27.8 3.2 %collective-permute-done.9.refs_3_ = bf16[96,576]{1,0:T(8,128)(2,1)S(1)} collective-permute-done((bf16[96,576]{1,0:T(8,128)(2,1)S(1)}, bf16[96,576]{1,0:T(8,128)(2,1)S(1)}, u32[]{:S(2)}, u32[]{:S(2)}) %collective-permute-start.9) | collective-permute-done | bytes 110624 | tf_op jit(solution)/shard_map/ppermute | solution.py:276
  30.9 2.2 %collective-permute-done.8.refs_2_ = bf16[96,576]{1,0:T(8,128)(2,1)S(1)} collective-permute-done((bf16[96,576]{1,0:T(8,128)(2,1)S(1)}, bf16[96,576]{1,0:T(8,128)(2,1)S(1)}, u32[]{:S(2)}, u32[]{:S(2)}) %collective-permute-start.8) | collective-permute-done | bytes 110624 | tf_op jit(solution)/shard_map/ppermute | solution.py:276
  33.2 0.7 %last_sum.1 = bf16[192,576]{1,0:T(8,128)(2,1)} custom-call(f32[96,576]{1,0:T(8,128)S(1)} %get-tuple-element.35.refs_0_, f32[96,576]{1,0:T(8,128)S(1)} %get-tuple-element.39.refs_1_, bf16[96,576]{1,0:T(8,128)(2,1)S(1)} %collective-permute-done.8.refs_2_, bf16[96,576]{1,0:T(8,128)(2,1)S(1)} %collective-permute-done.9.refs_3_), custom_call_target="tpu_custom_call" | custom-call | bytes 884736 | tf_op jit(solution)/shard_map/last_sum/pallas_call | solution.py:190
Async XLA Ops:
  0.6 4.5 %copy-start = (bf16[128,8,576]{0,2,1:T(8,128)(2,1)S(1)}, bf16[128,8,576]{0,2,1:T(8,128)(2,1)}, u32[]{:S(2)}) copy-start(bf16[128,8,576]{0,2,1:T(8,128)(2,1)} %param.6) | copy-start | bytes 3538948
  0.6 4.5 %copy-start.1 = (bf16[128,8,512]{2,1,0:T(8,128)(2,1)S(1)}, bf16[128,8,512]{2,1,0:T(8,128)(2,1)}, u32[]{:S(2)}) copy-start(bf16[128,8,512]{2,1,0:T(8,128)(2,1)} %param.7) | copy-start | bytes 3145732
  0.7 4.5 %copy-start.2 = (bf16[128,8]{0,1:T(8,128)(2,1)S(1)}, bf16[128,8]{0,1:T(8,128)(2,1)}, u32[]{:S(2)}) copy-start(bf16[128,8]{0,1:T(8,128)(2,1)} %param.9) | copy-start | bytes 6148
  0.7 4.5 %copy-start.3 = (bf16[128,8]{0,1:T(8,128)(2,1)S(1)}, bf16[128,8]{0,1:T(8,128)(2,1)}, u32[]{:S(2)}) copy-start(bf16[128,8]{0,1:T(8,128)(2,1)} %param.10) | copy-start | bytes 6148
  0.7 4.5 %copy-start.4 = (s32[1,2]{1,0:T(1,128)S(1)}, s32[1,2]{1,0:T(1,128)}, u32[]{:S(2)}) copy-start(s32[1,2]{1,0:T(1,128)} %plan_ref.3) | copy-start | bytes 28
  2.2 7.5 %collective-permute-start = (bf16[192,576]{1,0:T(8,128)(2,1)S(1)}, bf16[192,576]{1,0:T(8,128)(2,1)S(1)}, u32[]{:S(2)}, u32[]{:S(2)}) collective-permute-start(bf16[192,576]{1,0:T(8,128)(2,1)S(1)} %get-tuple-element.24), channel_id=1, source_target_pairs={{0,4},{4,8},{8,12},{12,16},{16,20},{20,24},{24,28},{28,0},{1,5},{5... | collective-permute-start | bytes 663560 | tf_op jit(solution)/shard_map/ppermute | solution.py:239
  2.7 12.4 %collective-permute-start.1 = (bf16[192,576]{1,0:T(8,128)(2,1)S(1)}, bf16[192,576]{1,0:T(8,128)(2,1)S(1)}, u32[]{:S(2)}, u32[]{:S(2)}) collective-permute-start(bf16[192,576]{1,0:T(8,128)(2,1)S(1)} %get-tuple-element.25), channel_id=1, source_target_pairs={{0,4},{4,8},{8,12},{12,16},{16,20},{20,24},{24,28},{28,0},{1,5},{5... | collective-permute-start | bytes 663560 | tf_op jit(solution)/shard_map/ppermute | solution.py:239
  8.0 9.4 %collective-permute-start.5 = (bf16[96,576]{1,0:T(8,128)(2,1)S(1)}, bf16[96,576]{1,0:T(8,128)(2,1)S(1)}, u32[]{:S(2)}, u32[]{:S(2)}) collective-permute-start(bf16[96,576]{1,0:T(8,128)(2,1)S(1)} %get-tuple-element.36), channel_id=1, source_target_pairs={{0,1},{1,0},{2,3},{3,2},{4,5},{5,4},{6,7},{7,6},{8,9},{9,8},{10,11... | collective-permute-start | bytes 331784 | tf_op jit(solution)/shard_map/ppermute | solution.py:253
  11.2 8.1 %collective-permute-start.6 = (bf16[96,576]{1,0:T(8,128)(2,1)S(1)}, bf16[96,576]{1,0:T(8,128)(2,1)S(1)}, u32[]{:S(2)}, u32[]{:S(2)}) collective-permute-start(bf16[96,576]{1,0:T(8,128)(2,1)S(1)} %get-tuple-element.37), channel_id=1, source_target_pairs={{0,29},{1,28},{2,31},{3,30},{4,1},{5,0},{6,3},{7,2},{8,5},{9,4},{1... | collective-permute-start | bytes 331784 | tf_op jit(solution)/shard_map/ppermute | solution.py:266
  12.1 7.2 %collective-permute-start.7 = (bf16[96,576]{1,0:T(8,128)(2,1)S(1)}, bf16[96,576]{1,0:T(8,128)(2,1)S(1)}, u32[]{:S(2)}, u32[]{:S(2)}) collective-permute-start(bf16[96,576]{1,0:T(8,128)(2,1)S(1)} %get-tuple-element.38), channel_id=1, source_target_pairs={{0,28},{1,29},{2,30},{3,31},{4,0},{5,1},{6,2},{7,3},{8,4},{9,5},{1... | collective-permute-start | bytes 331784 | tf_op jit(solution)/shard_map/ppermute | solution.py:266
  14.7 7.4 %collective-permute-start.2 = (bf16[96,576]{1,0:T(8,128)(2,1)S(1)}, bf16[96,576]{1,0:T(8,128)(2,1)S(1)}, u32[]{:S(2)}, u32[]{:S(2)}) collective-permute-start(bf16[96,576]{1,0:T(8,128)(2,1)S(1)} %get-tuple-element.32), channel_id=1, source_target_pairs={{0,1},{1,0},{2,3},{3,2},{4,5},{5,4},{6,7},{7,6},{8,9},{9,8},{10,11... | collective-permute-start | bytes 331784 | tf_op jit(solution)/shard_map/ppermute | solution.py:253
  16.7 5.5 %collective-permute-start.3 = (bf16[96,576]{1,0:T(8,128)(2,1)S(1)}, bf16[96,576]{1,0:T(8,128)(2,1)S(1)}, u32[]{:S(2)}, u32[]{:S(2)}) collective-permute-start(bf16[96,576]{1,0:T(8,128)(2,1)S(1)} %get-tuple-element.33), channel_id=1, source_target_pairs={{0,29},{1,28},{2,31},{3,30},{4,1},{5,0},{6,3},{7,2},{8,5},{9,4},{1... | collective-permute-start | bytes 331784 | tf_op jit(solution)/shard_map/ppermute | solution.py:266
  17.5 4.8 %collective-permute-start.4 = (bf16[96,576]{1,0:T(8,128)(2,1)S(1)}, bf16[96,576]{1,0:T(8,128)(2,1)S(1)}, u32[]{:S(2)}, u32[]{:S(2)}) collective-permute-start(bf16[96,576]{1,0:T(8,128)(2,1)S(1)} %get-tuple-element.34), channel_id=1, source_target_pairs={{0,28},{1,29},{2,30},{3,31},{4,0},{5,1},{6,2},{7,3},{8,4},{9,5},{1... | collective-permute-start | bytes 331784 | tf_op jit(solution)/shard_map/ppermute | solution.py:266
  19.4 11.5 %collective-permute-start.9 = (bf16[96,576]{1,0:T(8,128)(2,1)S(1)}, bf16[96,576]{1,0:T(8,128)(2,1)S(1)}, u32[]{:S(2)}, u32[]{:S(2)}) collective-permute-start(bf16[96,576]{1,0:T(8,128)(2,1)S(1)} %get-tuple-element.41), channel_id=1, source_target_pairs={{0,2},{1,3},{2,0},{3,1},{4,6},{5,7},{6,4},{7,5},{8,10},{9,11},{10,... | collective-permute-start | bytes 331784 | tf_op jit(solution)/shard_map/ppermute | solution.py:276
  22.4 10.8 %collective-permute-start.8 = (bf16[96,576]{1,0:T(8,128)(2,1)S(1)}, bf16[96,576]{1,0:T(8,128)(2,1)S(1)}, u32[]{:S(2)}, u32[]{:S(2)}) collective-permute-start(bf16[96,576]{1,0:T(8,128)(2,1)S(1)} %get-tuple-element.40), channel_id=1, source_target_pairs={{0,2},{1,3},{2,0},{3,1},{4,6},{5,7},{6,4},{7,5},{8,10},{9,11},{10,... | collective-permute-start | bytes 331784 | tf_op jit(solution)/shard_map/ppermute | solution.py:276

commit v12 on v10

--- a/solution.py
+++ b/solution.py
@@ -79,10 +79,16 @@
             here = slice((first + i) * PACKET, (first + i + 1) * PACKET)
             ds_ref[:, here] = (prob * (prob_grad[:, lanes] - delta)).astype(BF16)
             p_ref[:, here] = prob.astype(BF16)
-    key_grad = dot_nt(ds_ref[...], heads_side_by_side(q_ref, 0, heads))
-    value_grad = dot(p_ref[...], grad_ref[...])
-    grad_out_ref[:, :LAT] = key_grad[:, :LAT] + value_grad
-    grad_out_ref[:, LAT:] = key_grad[:, LAT:]
+        if (first + per) % (heads // 2) == 0:
+            half = slice((first + per) * PACKET - heads // 2 * PACKET, (first + per) * PACKET)
+            key_grad = dot_nt(ds_ref[:, half], heads_side_by_side(q_ref, first + per - heads // 2, heads // 2))
+            value_grad = dot(p_ref[:, half], grad_ref[half, :])
+            if first + per > heads // 2:
+                grad_out_ref[:, :LAT] += key_grad[:, :LAT] + value_grad
+                grad_out_ref[:, LAT:] += key_grad[:, LAT:]
+            else:
+                grad_out_ref[:, :LAT] = key_grad[:, :LAT] + value_grad
+                grad_out_ref[:, LAT:] = key_grad[:, LAT:]
 
 
 def pieces_out(total_ref, low, offset, out_refs):

time: 34 us -> 34.2 us (level)
  transfers between devices with their start and end apart: 10 -> 10, of which waited for: 3 -> 2; matrix products, arithmetic and copies ran while one was open for 0% -> 0% of each run, Pallas kernels for 25% -> 25%
where the time goes in v12:
time: 34.2 us; the launch traced here: 34.1 us
  starting transfers between devices  17 us (50%)
  Pallas kernels  10.7 us (31%)
  waiting for transfers between devices  5.69 us (17%)
  between operations  0.72 us (2%)
    pallas_call x8, Pallas kernels, call(): pl.pallas_call(kernel, name=name, out_shape=shapes, in_specs=[pl.BlockSpe...  10.7 us
    ppermute x4, starting transfers between devices, local(): lax.ppermute(far[d], ('seq', 'head'), route(d, 1))  6.25 us
    ppermute x2, waiting for transfers between devices, local(): lax.ppermute(send, 'head', [(j, (j + low) % n_head) for j in range(n_head)])  5.67 us
    ppermute x2, starting transfers between devices, local(): lax.ppermute(send, 'head', [(j, (j + low) % n_head) for j in range(n_head)])  5.51 us
    ppermute x2, starting transfers between devices, local(): lax.ppermute(x, 'seq', [(i, (i + 1) % n_seq) for i in range(n_seq)])  3.11 us
    ppermute x2, starting transfers between devices, local(): lax.ppermute(parts[d - 1], ('seq', 'head'), route(d, 0))  2.09 us
  transfers between devices with their start and end apart: 10, of which 2 were waited for; matrix products, arithmetic and copies ran while one was open for 0% of the time, Pallas kernels for 25%

profile of v12, /device:TPU:0, one launch (start us, length us, event | category | flops | bytes accessed | tf_op | source)
XLA Modules:
  0.0 34.1 jit_solution(6967478024920751911)
XLA Ops:
  0.6 0.0 copy-start
  0.6 0.0 copy-start.1
  0.7 0.0 copy-start.2
  0.7 0.0 copy-start.3
  0.7 0.0 copy-start.4
  0.7 1.4 %send_block.1 = (bf16[192,576]{1,0:T(8,128)(2,1)S(1)}, bf16[192,576]{1,0:T(8,128)(2,1)S(1)}, bf16[2,576,384]{2,1,0:T(8,128)(2,1)S(1)}) custom-call(s32[1,2]{1,0:T(1,128)} %plan_ref.3, bf16[576,768]{1,0:T(8,128)(2,1)} %bitcast.17), custom_call_target="tpu_custom_call" | custom-call | flops 1711276032 | bytes 2211848 | tf_op jit(solution)/shard_map/send_block/pallas_call | solution.py:195
  2.1 0.5 %collective-permute-start = (bf16[192,576]{1,0:T(8,128)(2,1)S(1)}, bf16[192,576]{1,0:T(8,128)(2,1)S(1)}, u32[]{:S(2)}, u32[]{:S(2)}) collective-permute-start(bf16[192,576]{1,0:T(8,128)(2,1)S(1)} %get-tuple-element.24), channel_id=1, source_target_pairs={{0,4},{4,8},{8,12},{12,16},{16,20},{20,24},{24,28},{28,0},{1,5},{5... | collective-permute-start | bytes 663560 | tf_op jit(solution)/shard_map/ppermute | solution.py:244
  2.6 2.6 %collective-permute-start.1 = (bf16[192,576]{1,0:T(8,128)(2,1)S(1)}, bf16[192,576]{1,0:T(8,128)(2,1)S(1)}, u32[]{:S(2)}, u32[]{:S(2)}) collective-permute-start(bf16[192,576]{1,0:T(8,128)(2,1)S(1)} %get-tuple-element.25), channel_id=1, source_target_pairs={{0,4},{4,8},{8,12},{12,16},{16,20},{20,24},{24,28},{28,0},{1,5},{5... | collective-permute-start | bytes 663560 | tf_op jit(solution)/shard_map/ppermute | solution.py:244
  5.2 0.0 copy-done
  5.2 0.0 copy-done.1
  5.2 0.0 copy-done.2
  5.2 0.0 copy-done.3
  5.2 0.0 copy-done.4
  5.2 2.8 %own_visit.1 = (bf16[1024,512]{1,0:T(8,128)(2,1)S(1)}, bf16[384,1024]{1,0:T(8,128)(2,1)S(1)}, f32[8,576]{1,0:T(8,128)S(1)}, f32[192,576]{1,0:T(8,128)S(1)}, bf16...) custom-call(s32[1,2]{1,0:T(1,128)S(1)} %copy-done.4, bf16[2,576,384]{2,1,0:T(8,128)(2,1)S(1)} %get-tuple-element.22.lat_ref, ...), custom_call_target="tpu_custom_call" | custom-call | bytes 5634056 | tf_op jit(solution)/shard_map/own_visit/pallas_call | solution.py:195
  8.0 1.6 %collective-permute-start.5 = (bf16[96,576]{1,0:T(8,128)(2,1)S(1)}, bf16[96,576]{1,0:T(8,128)(2,1)S(1)}, u32[]{:S(2)}, u32[]{:S(2)}) collective-permute-start(bf16[96,576]{1,0:T(8,128)(2,1)S(1)} %get-tuple-element.36), channel_id=1, source_target_pairs={{0,1},{1,0},{2,3},{3,2},{4,5},{5,4},{6,7},{7,6},{8,9},{9,8},{10,11... | collective-permute-start | bytes 331784 | tf_op jit(solution)/shard_map/ppermute | solution.py:258
  9.6 0.0 collective-permute-done.keys_ref.rest_0_
  9.7 1.6 %far_visit_0.1 = (bf16[192,1024]{1,0:T(8,128)(2,1)S(1)}, bf16[96,576]{1,0:T(8,128)(2,1)S(1)}, bf16[96,576]{1,0:T(8,128)(2,1)S(1)}, bf16[96,576]{1,0:T(8,128)(2,1)S(1)}) custom-call(bf16[192,576]{1,0:T(8,128)(2,1)S(1)} %collective-permute-done.keys_ref.rest_0_, bf16[8,576,128]{2,1,0:T(8,128)(2,1)S(1)} %bitcast.7, ...), custom_call_target="tpu_custom_call", output_to_operand_aliasing={{3}: (5, {})} | custom-call | bytes 3067904 | tf_op jit(solution)/shard_map/far_visit_0/pallas_call | solution.py:195
  11.2 0.8 %collective-permute-start.6 = (bf16[96,576]{1,0:T(8,128)(2,1)S(1)}, bf16[96,576]{1,0:T(8,128)(2,1)S(1)}, u32[]{:S(2)}, u32[]{:S(2)}) collective-permute-start(bf16[96,576]{1,0:T(8,128)(2,1)S(1)} %get-tuple-element.37), channel_id=1, source_target_pairs={{0,29},{1,28},{2,31},{3,30},{4,1},{5,0},{6,3},{7,2},{8,5},{9,4},{1... | collective-permute-start | bytes 331784 | tf_op jit(solution)/shard_map/ppermute | solution.py:271
  12.0 2.7 %collective-permute-start.7 = (bf16[96,576]{1,0:T(8,128)(2,1)S(1)}, bf16[96,576]{1,0:T(8,128)(2,1)S(1)}, u32[]{:S(2)}, u32[]{:S(2)}) collective-permute-start(bf16[96,576]{1,0:T(8,128)(2,1)S(1)} %get-tuple-element.38), channel_id=1, source_target_pairs={{0,28},{1,29},{2,30},{3,31},{4,0},{5,1},{6,2},{7,3},{8,4},{9,5},{1... | collective-permute-start | bytes 331784 | tf_op jit(solution)/shard_map/ppermute | solution.py:271
  14.7 0.4 %collective-permute-start.2 = (bf16[96,576]{1,0:T(8,128)(2,1)S(1)}, bf16[96,576]{1,0:T(8,128)(2,1)S(1)}, u32[]{:S(2)}, u32[]{:S(2)}) collective-permute-start(bf16[96,576]{1,0:T(8,128)(2,1)S(1)} %get-tuple-element.32), channel_id=1, source_target_pairs={{0,1},{1,0},{2,3},{3,2},{4,5},{5,4},{6,7},{7,6},{8,9},{9,8},{10,11... | collective-permute-start | bytes 331784 | tf_op jit(solution)/shard_map/ppermute | solution.py:258
  15.1 0.0 collective-permute-done.1.keys_ref.rest_1_
  15.1 1.6 %far_visit_1.1 = (bf16[192,1024]{1,0:T(8,128)(2,1)S(1)}, bf16[96,576]{1,0:T(8,128)(2,1)S(1)}, bf16[96,576]{1,0:T(8,128)(2,1)S(1)}) custom-call(bf16[192,576]{1,0:T(8,128)(2,1)S(1)} %collective-permute-done.1.keys_ref.rest_1_, bf16[8,576,128]{2,1,0:T(8,128)(2,1)S(1)} %bitcast.8, bf16[1024,512]{1,0:T(8,128)(2,1)S(1)} %get-tuple-element.26.grad_ref, ...), custom_call_target="tpu_custom_call" | custom-call | bytes 3067904 | tf_op jit(solution)/shard_map/far_visit_1/pallas_call | solution.py:195
  16.7 0.8 %collective-permute-start.3 = (bf16[96,576]{1,0:T(8,128)(2,1)S(1)}, bf16[96,576]{1,0:T(8,128)(2,1)S(1)}, u32[]{:S(2)}, u32[]{:S(2)}) collective-permute-start(bf16[96,576]{1,0:T(8,128)(2,1)S(1)} %get-tuple-element.33), channel_id=1, source_target_pairs={{0,29},{1,28},{2,31},{3,30},{4,1},{5,0},{6,3},{7,2},{8,5},{9,4},{1... | collective-permute-start | bytes 331784 | tf_op jit(solution)/shard_map/ppermute | solution.py:271
  17.5 0.0 collective-permute-done.5.rest_1_
  17.5 2.0 %collective-permute-start.4 = (bf16[96,576]{1,0:T(8,128)(2,1)S(1)}, bf16[96,576]{1,0:T(8,128)(2,1)S(1)}, u32[]{:S(2)}, u32[]{:S(2)}) collective-permute-start(bf16[96,576]{1,0:T(8,128)(2,1)S(1)} %get-tuple-element.34), channel_id=1, source_target_pairs={{0,28},{1,29},{2,30},{3,31},{4,0},{5,1},{6,2},{7,3},{8,4},{9,5},{1... | collective-permute-start | bytes 331784 | tf_op jit(solution)/shard_map/ppermute | solution.py:271
  19.5 0.0 collective-permute-done.6.rest_2_
  19.5 0.0 collective-permute-done.7.rest_3_
  19.5 0.1 combine_0.1
  19.6 2.7 %collective-permute-start.9 = (bf16[96,576]{1,0:T(8,128)(2,1)S(1)}, bf16[96,576]{1,0:T(8,128)(2,1)S(1)}, u32[]{:S(2)}, u32[]{:S(2)}) collective-permute-start(bf16[96,576]{1,0:T(8,128)(2,1)S(1)} %get-tuple-element.41), channel_id=1, source_target_pairs={{0,2},{1,3},{2,0},{3,1},{4,6},{5,7},{6,4},{7,5},{8,10},{9,11},{10,... | collective-permute-start | bytes 331784 | tf_op jit(solution)/shard_map/ppermute | solution.py:281
  22.3 0.0 collective-permute-done.2.rest_1_
  22.3 0.0 collective-permute-done.3.rest_2_
  22.3 0.0 collective-permute-done.4.rest_3_
  22.3 0.1 combine_1.1
  22.4 2.8 %collective-permute-start.8 = (bf16[96,576]{1,0:T(8,128)(2,1)S(1)}, bf16[96,576]{1,0:T(8,128)(2,1)S(1)}, u32[]{:S(2)}, u32[]{:S(2)}) collective-permute-start(bf16[96,576]{1,0:T(8,128)(2,1)S(1)} %get-tuple-element.40), channel_id=1, source_target_pairs={{0,2},{1,3},{2,0},{3,1},{4,6},{5,7},{6,4},{7,5},{8,10},{9,11},{10,... | collective-permute-start | bytes 331784 | tf_op jit(solution)/shard_map/ppermute | solution.py:281
  25.2 2.4 %query_grad.1 = bf16[8,576,128]{2,1,0:T(8,128)(2,1)} custom-call(s32[1,2]{1,0:T(1,128)S(1)} %copy-done.4, bf16[2,576,384]{2,1,0:T(8,128)(2,1)S(1)} %get-tuple-element.22.lat_ref, bf16[384,1024]{1,0:T(8,128)(2,1)S(1)} %get-tuple-element.23.own_ds_ref, bf16[192,576]{1,0:T(8,128)(2,1)S(1)} %collective-permute-done.keys_ref.rest_0_, ...), custom_call_target="tpu_custom_call" | custom-call | flops 905969664 | bytes 4079624 | tf_op jit(solution)/shard_map/query_grad/pallas_call | solution.py:195
  27.7 3.7 %collective-permute-done.9.refs_3_ = bf16[96,576]{1,0:T(8,128)(2,1)S(1)} collective-permute-done((bf16[96,576]{1,0:T(8,128)(2,1)S(1)}, bf16[96,576]{1,0:T(8,128)(2,1)S(1)}, u32[]{:S(2)}, u32[]{:S(2)}) %collective-permute-start.9) | collective-permute-done | bytes 110624 | tf_op jit(solution)/shard_map/ppermute | solution.py:281
  31.4 2.0 %collective-permute-done.8.refs_2_ = bf16[96,576]{1,0:T(8,128)(2,1)S(1)} collective-permute-done((bf16[96,576]{1,0:T(8,128)(2,1)S(1)}, bf16[96,576]{1,0:T(8,128)(2,1)S(1)}, u32[]{:S(2)}, u32[]{:S(2)}) %collective-permute-start.8) | collective-permute-done | bytes 110624 | tf_op jit(solution)/shard_map/ppermute | solution.py:281
  33.3 0.7 %last_sum.1 = bf16[192,576]{1,0:T(8,128)(2,1)} custom-call(f32[96,576]{1,0:T(8,128)S(1)} %get-tuple-element.35.refs_0_, f32[96,576]{1,0:T(8,128)S(1)} %get-tuple-element.39.refs_1_, bf16[96,576]{1,0:T(8,128)(2,1)S(1)} %collective-permute-done.8.refs_2_, bf16[96,576]{1,0:T(8,128)(2,1)S(1)} %collective-permute-done.9.refs_3_), custom_call_target="tpu_custom_call" | custom-call | bytes 884736 | tf_op jit(solution)/shard_map/last_sum/pallas_call | solution.py:195
Async XLA Ops:
  0.6 4.5 %copy-start = (bf16[128,8,576]{0,2,1:T(8,128)(2,1)S(1)}, bf16[128,8,576]{0,2,1:T(8,128)(2,1)}, u32[]{:S(2)}) copy-start(bf16[128,8,576]{0,2,1:T(8,128)(2,1)} %param.6) | copy-start | bytes 3538948
  0.6 4.5 %copy-start.1 = (bf16[128,8,512]{2,1,0:T(8,128)(2,1)S(1)}, bf16[128,8,512]{2,1,0:T(8,128)(2,1)}, u32[]{:S(2)}) copy-start(bf16[128,8,512]{2,1,0:T(8,128)(2,1)} %param.7) | copy-start | bytes 3145732
  0.7 4.5 %copy-start.2 = (bf16[128,8]{0,1:T(8,128)(2,1)S(1)}, bf16[128,8]{0,1:T(8,128)(2,1)}, u32[]{:S(2)}) copy-start(bf16[128,8]{0,1:T(8,128)(2,1)} %param.9) | copy-start | bytes 6148
  0.7 4.5 %copy-start.3 = (bf16[128,8]{0,1:T(8,128)(2,1)S(1)}, bf16[128,8]{0,1:T(8,128)(2,1)}, u32[]{:S(2)}) copy-start(bf16[128,8]{0,1:T(8,128)(2,1)} %param.10) | copy-start | bytes 6148
  0.7 4.5 %copy-start.4 = (s32[1,2]{1,0:T(1,128)S(1)}, s32[1,2]{1,0:T(1,128)}, u32[]{:S(2)}) copy-start(s32[1,2]{1,0:T(1,128)} %plan_ref.3) | copy-start | bytes 28
  2.1 7.6 %collective-permute-start = (bf16[192,576]{1,0:T(8,128)(2,1)S(1)}, bf16[192,576]{1,0:T(8,128)(2,1)S(1)}, u32[]{:S(2)}, u32[]{:S(2)}) collective-permute-start(bf16[192,576]{1,0:T(8,128)(2,1)S(1)} %get-tuple-element.24), channel_id=1, source_target_pairs={{0,4},{4,8},{8,12},{12,16},{16,20},{20,24},{24,28},{28,0},{1,5},{5... | collective-permute-start | bytes 663560 | tf_op jit(solution)/shard_map/ppermute | solution.py:244
  2.6 12.6 %collective-permute-start.1 = (bf16[192,576]{1,0:T(8,128)(2,1)S(1)}, bf16[192,576]{1,0:T(8,128)(2,1)S(1)}, u32[]{:S(2)}, u32[]{:S(2)}) collective-permute-start(bf16[192,576]{1,0:T(8,128)(2,1)S(1)} %get-tuple-element.25), channel_id=1, source_target_pairs={{0,4},{4,8},{8,12},{12,16},{16,20},{20,24},{24,28},{28,0},{1,5},{5... | collective-permute-start | bytes 663560 | tf_op jit(solution)/shard_map/ppermute | solution.py:244
  8.0 9.5 %collective-permute-start.5 = (bf16[96,576]{1,0:T(8,128)(2,1)S(1)}, bf16[96,576]{1,0:T(8,128)(2,1)S(1)}, u32[]{:S(2)}, u32[]{:S(2)}) collective-permute-start(bf16[96,576]{1,0:T(8,128)(2,1)S(1)} %get-tuple-element.36), channel_id=1, source_target_pairs={{0,1},{1,0},{2,3},{3,2},{4,5},{5,4},{6,7},{7,6},{8,9},{9,8},{10,11... | collective-permute-start | bytes 331784 | tf_op jit(solution)/shard_map/ppermute | solution.py:258
  11.2 8.3 %collective-permute-start.6 = (bf16[96,576]{1,0:T(8,128)(2,1)S(1)}, bf16[96,576]{1,0:T(8,128)(2,1)S(1)}, u32[]{:S(2)}, u32[]{:S(2)}) collective-permute-start(bf16[96,576]{1,0:T(8,128)(2,1)S(1)} %get-tuple-element.37), channel_id=1, source_target_pairs={{0,29},{1,28},{2,31},{3,30},{4,1},{5,0},{6,3},{7,2},{8,5},{9,4},{1... | collective-permute-start | bytes 331784 | tf_op jit(solution)/shard_map/ppermute | solution.py:271
  12.0 7.5 %collective-permute-start.7 = (bf16[96,576]{1,0:T(8,128)(2,1)S(1)}, bf16[96,576]{1,0:T(8,128)(2,1)S(1)}, u32[]{:S(2)}, u32[]{:S(2)}) collective-permute-start(bf16[96,576]{1,0:T(8,128)(2,1)S(1)} %get-tuple-element.38), channel_id=1, source_target_pairs={{0,28},{1,29},{2,30},{3,31},{4,0},{5,1},{6,2},{7,3},{8,4},{9,5},{1... | collective-permute-start | bytes 331784 | tf_op jit(solution)/shard_map/ppermute | solution.py:271
  14.7 7.6 %collective-permute-start.2 = (bf16[96,576]{1,0:T(8,128)(2,1)S(1)}, bf16[96,576]{1,0:T(8,128)(2,1)S(1)}, u32[]{:S(2)}, u32[]{:S(2)}) collective-permute-start(bf16[96,576]{1,0:T(8,128)(2,1)S(1)} %get-tuple-element.32), channel_id=1, source_target_pairs={{0,1},{1,0},{2,3},{3,2},{4,5},{5,4},{6,7},{7,6},{8,9},{9,8},{10,11... | collective-permute-start | bytes 331784 | tf_op jit(solution)/shard_map/ppermute | solution.py:258
  16.7 5.6 %collective-permute-start.3 = (bf16[96,576]{1,0:T(8,128)(2,1)S(1)}, bf16[96,576]{1,0:T(8,128)(2,1)S(1)}, u32[]{:S(2)}, u32[]{:S(2)}) collective-permute-start(bf16[96,576]{1,0:T(8,128)(2,1)S(1)} %get-tuple-element.33), channel_id=1, source_target_pairs={{0,29},{1,28},{2,31},{3,30},{4,1},{5,0},{6,3},{7,2},{8,5},{9,4},{1... | collective-permute-start | bytes 331784 | tf_op jit(solution)/shard_map/ppermute | solution.py:271
  17.5 4.8 %collective-permute-start.4 = (bf16[96,576]{1,0:T(8,128)(2,1)S(1)}, bf16[96,576]{1,0:T(8,128)(2,1)S(1)}, u32[]{:S(2)}, u32[]{:S(2)}) collective-permute-start(bf16[96,576]{1,0:T(8,128)(2,1)S(1)} %get-tuple-element.34), channel_id=1, source_target_pairs={{0,28},{1,29},{2,30},{3,31},{4,0},{5,1},{6,2},{7,3},{8,4},{9,5},{1... | collective-permute-start | bytes 331784 | tf_op jit(solution)/shard_map/ppermute | solution.py:271
  19.6 11.8 %collective-permute-start.9 = (bf16[96,576]{1,0:T(8,128)(2,1)S(1)}, bf16[96,576]{1,0:T(8,128)(2,1)S(1)}, u32[]{:S(2)}, u32[]{:S(2)}) collective-permute-start(bf16[96,576]{1,0:T(8,128)(2,1)S(1)} %get-tuple-element.41), channel_id=1, source_target_pairs={{0,2},{1,3},{2,0},{3,1},{4,6},{5,7},{6,4},{7,5},{8,10},{9,11},{10,... | collective-permute-start | bytes 331784 | tf_op jit(solution)/shard_map/ppermute | solution.py:281
  22.4 11.0 %collective-permute-start.8 = (bf16[96,576]{1,0:T(8,128)(2,1)S(1)}, bf16[96,576]{1,0:T(8,128)(2,1)S(1)}, u32[]{:S(2)}, u32[]{:S(2)}) collective-permute-start(bf16[96,576]{1,0:T(8,128)(2,1)S(1)} %get-tuple-element.40), channel_id=1, source_target_pairs={{0,2},{1,3},{2,0},{3,1},{4,6},{5,7},{6,4},{7,5},{8,10},{9,11},{10,... | collective-permute-start | bytes 331784 | tf_op jit(solution)/shard_map/ppermute | solution.py:281

commit v13 on v10

--- a/solution.py
+++ b/solution.py
@@ -15,6 +15,7 @@
 VMEM_LIMIT = 24 * 2**20
 NEVER = 1e30
 CHUNKS = 2
+FIRST_SHARE = 7 / 12
 
 F32 = jnp.float32
 BF16 = jnp.bfloat16
@@ -26,6 +27,11 @@
 
 def dot_nt(a, b):
     return lax.dot_general(a, b, (((1,), (1,)), ((), ())), preferred_element_type=F32)
+
+
+def chunks_of(rows):
+    first = -(-int(rows * FIRST_SHARE) // 16) * 16
+    return [(0, first), (first, rows - first)]
 
 
 def send_block_kernel(low, plan_hbm, lat_hbm, *rest):
@@ -46,10 +52,9 @@
     block_copy(sent).wait()
     keys = lat_ref[sent].T
     rows = BLOCK // low
-    part = rows // CHUNKS
-    for c, out_ref in enumerate(out_refs):
+    for (offset, part), out_ref in zip(chunks_of(rows), out_refs):
         for j in range(low):
-            start = j * rows + c * part
+            start = j * rows + offset
             out_ref[j * part : (j + 1) * part, :] = keys[start : start + part, :]
     for i in range(1, blocks):
         block_copy(lax.rem(sent + i, blocks)).wait()
@@ -118,8 +123,8 @@
     visit(keys, q_ref, rows_ref, norm_ref, delta_ref, None, k_pos <= q_pos, ds_ref, p_ref, total_ref)
     pieces_out(total_ref, low, 0, [(0, keep_ref)])
     for i, out_ref in enumerate(out_refs):
-        part = out_ref.shape[0]
-        pieces_out(total_ref, low, i % CHUNKS * part, [(1 + i // CHUNKS, out_ref)])
+        offset, _ = chunks_of(BLOCK // low)[i % CHUNKS]
+        pieces_out(total_ref, low, offset, [(1 + i // CHUNKS, out_ref)])
 
 
 def far_kernel(low, held, keys_ref, q_ref, grad_ref, norm_ref, delta_ref, *rest):
@@ -151,12 +156,12 @@
             out_ref[first + i] = total[:, i * PACKET : (i + 1) * PACKET].astype(BF16)
 
 
-def combine_kernel(low, chunk, sel_ref, *rest):
+def combine_kernel(low, offset, sel_ref, *rest):
     own_refs = rest[:low]
     far_refs = rest[low : 2 * low]
     send_ref, mine_ref = rest[-2:]
     part = send_ref.shape[0]
-    here = slice(chunk * part, (chunk + 1) * part)
+    here = slice(offset, offset + part)
     own = own_refs[0][here, :]
     for ref in own_refs[1:]:
         own = own + ref[...].astype(F32)
@@ -169,9 +174,8 @@
 
 def last_kernel(*refs):
     mine_refs, got_refs, out_ref = refs[:CHUNKS][::-1], refs[CHUNKS : 2 * CHUNKS][::-1], refs[-1]
-    part = out_ref.shape[0] // CHUNKS
-    for c in range(CHUNKS):
-        out_ref[c * part : (c + 1) * part, :] = (mine_refs[c][...] + got_refs[c][...].astype(F32)).astype(BF16)
+    for (offset, part), mine_ref, got_ref in zip(chunks_of(out_ref.shape[0]), mine_refs, got_refs):
+        out_ref[offset : offset + part, :] = (mine_ref[...] + got_ref[...].astype(F32)).astype(BF16)
 
 
 def call(kernel, name, ins, outs, scratch=(), smem=(), raw=(), passed=(), flops=0, transcendentals=0):
@@ -222,15 +226,14 @@
                 pairs.append((i * n_head + j, (i - back) % n_seq * n_head + to))
         return pairs
 
-    part = rows // CHUNKS
-    keys = BLOCK // CHUNKS
+    chunks = chunks_of(rows)
 
     blocks = SHARD // BLOCK
     *sent, lat_blocks = call(
         functools.partial(send_block_kernel, low),
         "send_block",
         (plan, lat_t),
-        [((keys, width), BF16)] * CHUNKS + [((blocks, width, BLOCK), BF16)],
+        [((low * part, width), BF16) for _, part in chunks] + [((blocks, width, BLOCK), BF16)],
         [pltpu.SMEM(plan.shape, plan.dtype), pltpu.SemaphoreType.DMA((blocks + 1,))],
         flops=visit_flops,
         raw=(0, 1),
@@ -242,12 +245,13 @@
         "own_visit",
         (plan, lat_blocks, q_t, grad, norm_t, delta_t),
         [((columns, LAT), BF16), ((BLOCK, columns), BF16), ((8, width), F32), ((rows, width), F32)]
-        + [((part, width), BF16)] * (CHUNKS * (low - 1)),
+        + [((part, width), BF16) for _, part in chunks] * (low - 1),
         [pltpu.VMEM((BLOCK, columns), BF16), pltpu.VMEM((BLOCK, width), F32)],
     )
 
     far_ds, own_parts, far_parts = [], [], []
-    for c in range(CHUNKS):
+    for c, (_, part) in enumerate(chunks):
+        keys = low * part
         parts = own[c::CHUNKS]
         own_parts.append([keep] + [lax.ppermute(parts[d - 1], ("seq", "head"), route(d, 0)) for d in range(1, low)])
         later = [i for i in range(len(own)) if i % CHUNKS > c]
@@ -265,9 +269,9 @@
         far_parts.append([lax.ppermute(far[d], ("seq", "head"), route(d, 1)) for d in reversed(range(low))])
 
     mine, got = [None] * CHUNKS, [None] * CHUNKS
-    for c in reversed(range(CHUNKS)):
+    for c, (offset, part) in reversed(list(enumerate(chunks))):
         send, mine[c] = call(
-            functools.partial(combine_kernel, low, c),
+            functools.partial(combine_kernel, low, offset),
             f"combine_{c}",
             (sel, *own_parts[c], *far_parts[c]),
             [((part, width), BF16), ((part, width), F32)],

time: 34 us -> 34.8 us (1.024)
  waiting for transfers between devices: 5.46 us -> 9.12 us
  starting transfers between devices: 17 us -> 14.4 us
    ppermute x2, waiting for transfers between devices: 0.01 us -> 4.61 us  [local(): lax.ppermute(parts[d - 1], ('seq', 'head'), route(d, 0))]
    ppermute x2, starting transfers between devices: 5.74 us -> 2.73 us  [local(): lax.ppermute(send, 'head', [(j, (j + low) % n_head) for j in range(n_head)])]
    ppermute x2, starting transfers between devices: 2.09 us -> 3.25 us  [local(): lax.ppermute(parts[d - 1], ('seq', 'head'), route(d, 0))]
    ppermute x4, starting transfers between devices: 6.08 us -> 5.19 us  [local(): lax.ppermute(far[d], ('seq', 'head'), route(d, 1))]
    ppermute x2, waiting for transfers between devices: 5.33 us -> 4.5 us  [local(): lax.ppermute(send, 'head', [(j, (j + low) % n_head) for j in range(n_head)])]
  transfers between devices with their start and end apart: 10 -> 10, of which waited for: 3 -> 2; matrix products, arithmetic and copies ran while one was open for 0% -> 0% of each run, Pallas kernels for 25% -> 24%
where the time goes in v13:
time: 34.8 us; the launch traced here: 34.9 us
  starting transfers between devices  14.4 us (41%)
  Pallas kernels  10.6 us (30%)
  waiting for transfers between devices  9.12 us (26%)
  between operations  0.74 us (2%)
    pallas_call x8, Pallas kernels, call(): pl.pallas_call(kernel, name=name, out_shape=shapes, in_specs=[pl.BlockSpe...  10.6 us
    ppermute x4, starting transfers between devices, local(): lax.ppermute(far[d], ('seq', 'head'), route(d, 1))  5.19 us
    ppermute x2, waiting for transfers between devices, local(): lax.ppermute(parts[d - 1], ('seq', 'head'), route(d, 0))  4.61 us
    ppermute x2, waiting for transfers between devices, local(): lax.ppermute(send, 'head', [(j, (j + low) % n_head) for j in range(n_head)])  4.5 us
    ppermute x2, starting transfers between devices, local(): lax.ppermute(parts[d - 1], ('seq', 'head'), route(d, 0))  3.25 us
    ppermute x2, starting transfers between devices, local(): lax.ppermute(x, 'seq', [(i, (i + 1) % n_seq) for i in range(n_seq)])  3.24 us
    ppermute x2, starting transfers between devices, local(): lax.ppermute(send, 'head', [(j, (j + low) % n_head) for j in range(n_head)])  2.73 us
  transfers between devices with their start and end apart: 10, of which 2 were waited for; matrix products, arithmetic and copies ran while one was open for 0% of the time, Pallas kernels for 24%

profile of v13, /device:TPU:0, one launch (start us, length us, event | category | flops | bytes accessed | tf_op | source)
XLA Modules:
  0.0 34.9 jit_solution(9008315079786396566)
XLA Ops:
  0.6 0.0 copy-start
  0.6 0.0 copy-start.1
  0.7 0.0 copy-start.2
  0.7 0.0 copy-start.3
  0.7 0.0 copy-start.4
  0.7 1.4 %send_block.1 = (bf16[224,576]{1,0:T(8,128)(2,1)S(1)}, bf16[160,576]{1,0:T(8,128)(2,1)S(1)}, bf16[2,576,384]{2,1,0:T(8,128)(2,1)S(1)}) custom-call(s32[1,2]{1,0:T(1,128)} %plan_ref.3, bf16[576,768]{1,0:T(8,128)(2,1)} %bitcast.17), custom_call_target="tpu_custom_call" | custom-call | flops 1711276032 | bytes 2211848 | tf_op jit(solution)/shard_map/send_block/pallas_call | solution.py:193
  2.1 0.5 %collective-permute-start = (bf16[224,576]{1,0:T(8,128)(2,1)S(1)}, bf16[224,576]{1,0:T(8,128)(2,1)S(1)}, u32[]{:S(2)}, u32[]{:S(2)}) collective-permute-start(bf16[224,576]{1,0:T(8,128)(2,1)S(1)} %get-tuple-element.24), channel_id=1, source_target_pairs={{0,4},{4,8},{8,12},{12,16},{16,20},{20,24},{24,28},{28,0},{1,5},{5... | collective-permute-start | bytes 774152 | tf_op jit(solution)/shard_map/ppermute | solution.py:241
  2.6 2.7 %collective-permute-start.1 = (bf16[160,576]{1,0:T(8,128)(2,1)S(1)}, bf16[160,576]{1,0:T(8,128)(2,1)S(1)}, u32[]{:S(2)}, u32[]{:S(2)}) collective-permute-start(bf16[160,576]{1,0:T(8,128)(2,1)S(1)} %get-tuple-element.25), channel_id=1, source_target_pairs={{0,4},{4,8},{8,12},{12,16},{16,20},{20,24},{24,28},{28,0},{1,5},{5... | collective-permute-start | bytes 552968 | tf_op jit(solution)/shard_map/ppermute | solution.py:241
  5.3 0.0 copy-done
  5.3 0.0 copy-done.1
  5.3 0.0 copy-done.2
  5.3 0.0 copy-done.3
  5.3 0.0 copy-done.4
  5.3 2.9 %own_visit.1 = (bf16[1024,512]{1,0:T(8,128)(2,1)S(1)}, bf16[384,1024]{1,0:T(8,128)(2,1)S(1)}, f32[8,576]{1,0:T(8,128)S(1)}, f32[192,576]{1,0:T(8,128)S(1)}, bf16...) custom-call(s32[1,2]{1,0:T(1,128)S(1)} %copy-done.4, bf16[2,576,384]{2,1,0:T(8,128)(2,1)S(1)} %get-tuple-element.22.lat_ref, ...), custom_call_target="tpu_custom_call" | custom-call | bytes 5634056 | tf_op jit(solution)/shard_map/own_visit/pallas_call | solution.py:193
  8.2 1.7 %collective-permute-start.5 = (bf16[112,576]{1,0:T(8,128)(2,1)S(1)}, bf16[112,576]{1,0:T(8,128)(2,1)S(1)}, u32[]{:S(2)}, u32[]{:S(2)}) collective-permute-start(bf16[112,576]{1,0:T(8,128)(2,1)S(1)} %get-tuple-element.36), channel_id=1, source_target_pairs={{0,1},{1,0},{2,3},{3,2},{4,5},{5,4},{6,7},{7,6},{8,9},{9,8},{10,11... | collective-permute-start | bytes 387080 | tf_op jit(solution)/shard_map/ppermute | solution.py:256
  9.9 0.0 collective-permute-done.keys_ref.rest_0_
  9.9 1.6 %far_visit_0.1 = (bf16[224,1024]{1,0:T(8,128)(2,1)S(1)}, bf16[112,576]{1,0:T(8,128)(2,1)S(1)}, bf16[112,576]{1,0:T(8,128)(2,1)S(1)}, bf16[80,576]{1,0:T(8,128)(2,1)S(1)}) custom-call(bf16[224,576]{1,0:T(8,128)(2,1)S(1)} %collective-permute-done.keys_ref.rest_0_, bf16[8,576,128]{2,1,0:T(8,128)(2,1)S(1)} %bitcast.7, ...), custom_call_target="tpu_custom_call", output_to_operand_aliasing={{3}: (5, {})} | custom-call | bytes 3207168 | tf_op jit(solution)/shard_map/far_visit_0/pallas_call | solution.py:193
  11.5 1.0 %collective-permute-start.6 = (bf16[112,576]{1,0:T(8,128)(2,1)S(1)}, bf16[112,576]{1,0:T(8,128)(2,1)S(1)}, u32[]{:S(2)}, u32[]{:S(2)}) collective-permute-start(bf16[112,576]{1,0:T(8,128)(2,1)S(1)} %get-tuple-element.37), channel_id=1, source_target_pairs={{0,29},{1,28},{2,31},{3,30},{4,1},{5,0},{6,3},{7,2},{8,5},{9,4},{1... | collective-permute-start | bytes 387080 | tf_op jit(solution)/shard_map/ppermute | solution.py:269
  12.5 2.7 %collective-permute-start.7 = (bf16[112,576]{1,0:T(8,128)(2,1)S(1)}, bf16[112,576]{1,0:T(8,128)(2,1)S(1)}, u32[]{:S(2)}, u32[]{:S(2)}) collective-permute-start(bf16[112,576]{1,0:T(8,128)(2,1)S(1)} %get-tuple-element.38), channel_id=1, source_target_pairs={{0,28},{1,29},{2,30},{3,31},{4,0},{5,1},{6,2},{7,3},{8,4},{9,5},{1... | collective-permute-start | bytes 387080 | tf_op jit(solution)/shard_map/ppermute | solution.py:269
  15.2 0.0 collective-permute-done.1.keys_ref.rest_1_
  15.2 1.4 %far_visit_1.1 = (bf16[160,1024]{1,0:T(8,128)(2,1)S(1)}, bf16[80,576]{1,0:T(8,128)(2,1)S(1)}, bf16[80,576]{1,0:T(8,128)(2,1)S(1)}) custom-call(bf16[160,576]{1,0:T(8,128)(2,1)S(1)} %collective-permute-done.1.keys_ref.rest_1_, bf16[8,576,128]{2,1,0:T(8,128)(2,1)S(1)} %bitcast.8, bf16[1024,512]{1,0:T(8,128)(2,1)S(1)} %get-tuple-element.26.grad_ref, ...), custom_call_target="tpu_custom_call" | custom-call | bytes 2928640 | tf_op jit(solution)/shard_map/far_visit_1/pallas_call | solution.py:193
  16.5 0.1 collective-permute-start.3
  16.6 1.4 %collective-permute-start.4 = (bf16[80,576]{1,0:T(8,128)(2,1)S(1)}, bf16[80,576]{1,0:T(8,128)(2,1)S(1)}, u32[]{:S(2)}, u32[]{:S(2)}) collective-permute-start(bf16[80,576]{1,0:T(8,128)(2,1)S(1)} %get-tuple-element.34), channel_id=1, source_target_pairs={{0,28},{1,29},{2,30},{3,31},{4,0},{5,1},{6,2},{7,3},{8,4},{9,5},{1... | collective-permute-start | bytes 276488 | tf_op jit(solution)/shard_map/ppermute | solution.py:269
  18.1 0.0 collective-permute-done.5.rest_1_
  18.1 1.6 %collective-permute-start.2 = (bf16[80,576]{1,0:T(8,128)(2,1)S(1)}, bf16[80,576]{1,0:T(8,128)(2,1)S(1)}, u32[]{:S(2)}, u32[]{:S(2)}) collective-permute-start(bf16[80,576]{1,0:T(8,128)(2,1)S(1)} %get-tuple-element.32), channel_id=1, source_target_pairs={{0,1},{1,0},{2,3},{3,2},{4,5},{5,4},{6,7},{7,6},{8,9},{9,8},{10,11... | collective-permute-start | bytes 276488 | tf_op jit(solution)/shard_map/ppermute | solution.py:256
  19.6 0.0 collective-permute-done.6.rest_2_
  19.6 0.0 collective-permute-done.7.rest_3_
  19.6 0.1 combine_0.1
  19.8 2.7 %collective-permute-start.9 = (bf16[112,576]{1,0:T(8,128)(2,1)S(1)}, bf16[112,576]{1,0:T(8,128)(2,1)S(1)}, u32[]{:S(2)}, u32[]{:S(2)}) collective-permute-start(bf16[112,576]{1,0:T(8,128)(2,1)S(1)} %get-tuple-element.41), channel_id=1, source_target_pairs={{0,2},{1,3},{2,0},{3,1},{4,6},{5,7},{6,4},{7,5},{8,10},{9,11},{10,... | collective-permute-start | bytes 387080 | tf_op jit(solution)/shard_map/ppermute | solution.py:279
  22.4 0.0 collective-permute-done.3.rest_2_
  22.4 0.0 collective-permute-done.4.rest_3_
  22.4 4.6 %collective-permute-done.2.rest_1_ = bf16[80,576]{1,0:T(8,128)(2,1)S(1)} collective-permute-done((bf16[80,576]{1,0:T(8,128)(2,1)S(1)}, bf16[80,576]{1,0:T(8,128)(2,1)S(1)}, u32[]{:S(2)}, u32[]{:S(2)}) %collective-permute-start.2) | collective-permute-done | bytes 92192 | tf_op jit(solution)/shard_map/ppermute | solution.py:256
  27.0 0.1 combine_1.1
  27.1 0.1 collective-permute-start.8
  27.2 2.4 %query_grad.1 = bf16[8,576,128]{2,1,0:T(8,128)(2,1)} custom-call(s32[1,2]{1,0:T(1,128)S(1)} %copy-done.4, bf16[2,576,384]{2,1,0:T(8,128)(2,1)S(1)} %get-tuple-element.22.lat_ref, bf16[384,1024]{1,0:T(8,128)(2,1)S(1)} %get-tuple-element.23.own_ds_ref, bf16[224,576]{1,0:T(8,128)(2,1)S(1)} %collective-permute-done.keys_ref.rest_0_, ...), custom_call_target="tpu_custom_call" | custom-call | flops 905969664 | bytes 4079624 | tf_op jit(solution)/shard_map/query_grad/pallas_call | solution.py:193
  29.7 4.5 %collective-permute-done.8.refs_2_ = bf16[80,576]{1,0:T(8,128)(2,1)S(1)} collective-permute-done((bf16[80,576]{1,0:T(8,128)(2,1)S(1)}, bf16[80,576]{1,0:T(8,128)(2,1)S(1)}, u32[]{:S(2)}, u32[]{:S(2)}) %collective-permute-start.8) | collective-permute-done | bytes 92192 | tf_op jit(solution)/shard_map/ppermute | solution.py:279
  34.2 0.0 collective-permute-done.9.refs_3_
  34.2 0.7 %last_sum.1 = bf16[192,576]{1,0:T(8,128)(2,1)} custom-call(f32[80,576]{1,0:T(8,128)S(1)} %get-tuple-element.35.refs_0_, f32[112,576]{1,0:T(8,128)S(1)} %get-tuple-element.39.refs_1_, bf16[80,576]{1,0:T(8,128)(2,1)S(1)} %collective-permute-done.8.refs_2_, bf16[112,576]{1,0:T(8,128)(2,1)S(1)} %collective-permute-done.9.refs_3_), custom_call_target="tpu_custom_call" | custom-call | bytes 884736 | tf_op jit(solution)/shard_map/last_sum/pallas_call | solution.py:193
Async XLA Ops:
  0.6 4.7 %copy-start = (bf16[128,8,576]{0,2,1:T(8,128)(2,1)S(1)}, bf16[128,8,576]{0,2,1:T(8,128)(2,1)}, u32[]{:S(2)}) copy-start(bf16[128,8,576]{0,2,1:T(8,128)(2,1)} %param.6) | copy-start | bytes 3538948
  0.6 4.7 %copy-start.1 = (bf16[128,8,512]{2,1,0:T(8,128)(2,1)S(1)}, bf16[128,8,512]{2,1,0:T(8,128)(2,1)}, u32[]{:S(2)}) copy-start(bf16[128,8,512]{2,1,0:T(8,128)(2,1)} %param.7) | copy-start | bytes 3145732
  0.7 4.7 %copy-start.2 = (bf16[128,8]{0,1:T(8,128)(2,1)S(1)}, bf16[128,8]{0,1:T(8,128)(2,1)}, u32[]{:S(2)}) copy-start(bf16[128,8]{0,1:T(8,128)(2,1)} %param.9) | copy-start | bytes 6148
  0.7 4.7 %copy-start.3 = (bf16[128,8]{0,1:T(8,128)(2,1)S(1)}, bf16[128,8]{0,1:T(8,128)(2,1)}, u32[]{:S(2)}) copy-start(bf16[128,8]{0,1:T(8,128)(2,1)} %param.10) | copy-start | bytes 6148
  0.7 4.7 %copy-start.4 = (s32[1,2]{1,0:T(1,128)S(1)}, s32[1,2]{1,0:T(1,128)}, u32[]{:S(2)}) copy-start(s32[1,2]{1,0:T(1,128)} %plan_ref.3) | copy-start | bytes 28
  2.1 7.8 %collective-permute-start = (bf16[224,576]{1,0:T(8,128)(2,1)S(1)}, bf16[224,576]{1,0:T(8,128)(2,1)S(1)}, u32[]{:S(2)}, u32[]{:S(2)}) collective-permute-start(bf16[224,576]{1,0:T(8,128)(2,1)S(1)} %get-tuple-element.24), channel_id=1, source_target_pairs={{0,4},{4,8},{8,12},{12,16},{16,20},{20,24},{24,28},{28,0},{1,5},{5... | collective-permute-start | bytes 774152 | tf_op jit(solution)/shard_map/ppermute | solution.py:241
  2.6 12.6 %collective-permute-start.1 = (bf16[160,576]{1,0:T(8,128)(2,1)S(1)}, bf16[160,576]{1,0:T(8,128)(2,1)S(1)}, u32[]{:S(2)}, u32[]{:S(2)}) collective-permute-start(bf16[160,576]{1,0:T(8,128)(2,1)S(1)} %get-tuple-element.25), channel_id=1, source_target_pairs={{0,4},{4,8},{8,12},{12,16},{16,20},{20,24},{24,28},{28,0},{1,5},{5... | collective-permute-start | bytes 552968 | tf_op jit(solution)/shard_map/ppermute | solution.py:241
  8.2 9.9 %collective-permute-start.5 = (bf16[112,576]{1,0:T(8,128)(2,1)S(1)}, bf16[112,576]{1,0:T(8,128)(2,1)S(1)}, u32[]{:S(2)}, u32[]{:S(2)}) collective-permute-start(bf16[112,576]{1,0:T(8,128)(2,1)S(1)} %get-tuple-element.36), channel_id=1, source_target_pairs={{0,1},{1,0},{2,3},{3,2},{4,5},{5,4},{6,7},{7,6},{8,9},{9,8},{10,11... | collective-permute-start | bytes 387080 | tf_op jit(solution)/shard_map/ppermute | solution.py:256
  11.5 8.1 %collective-permute-start.6 = (bf16[112,576]{1,0:T(8,128)(2,1)S(1)}, bf16[112,576]{1,0:T(8,128)(2,1)S(1)}, u32[]{:S(2)}, u32[]{:S(2)}) collective-permute-start(bf16[112,576]{1,0:T(8,128)(2,1)S(1)} %get-tuple-element.37), channel_id=1, source_target_pairs={{0,29},{1,28},{2,31},{3,30},{4,1},{5,0},{6,3},{7,2},{8,5},{9,4},{1... | collective-permute-start | bytes 387080 | tf_op jit(solution)/shard_map/ppermute | solution.py:269
  12.5 7.2 %collective-permute-start.7 = (bf16[112,576]{1,0:T(8,128)(2,1)S(1)}, bf16[112,576]{1,0:T(8,128)(2,1)S(1)}, u32[]{:S(2)}, u32[]{:S(2)}) collective-permute-start(bf16[112,576]{1,0:T(8,128)(2,1)S(1)} %get-tuple-element.38), channel_id=1, source_target_pairs={{0,28},{1,29},{2,30},{3,31},{4,0},{5,1},{6,2},{7,3},{8,4},{9,5},{1... | collective-permute-start | bytes 387080 | tf_op jit(solution)/shard_map/ppermute | solution.py:269
  16.5 5.9 %collective-permute-start.3 = (bf16[80,576]{1,0:T(8,128)(2,1)S(1)}, bf16[80,576]{1,0:T(8,128)(2,1)S(1)}, u32[]{:S(2)}, u32[]{:S(2)}) collective-permute-start(bf16[80,576]{1,0:T(8,128)(2,1)S(1)} %get-tuple-element.33), channel_id=1, source_target_pairs={{0,29},{1,28},{2,31},{3,30},{4,1},{5,0},{6,3},{7,2},{8,5},{9,4},{1... | collective-permute-start | bytes 276488 | tf_op jit(solution)/shard_map/ppermute | solution.py:269
  16.6 5.8 %collective-permute-start.4 = (bf16[80,576]{1,0:T(8,128)(2,1)S(1)}, bf16[80,576]{1,0:T(8,128)(2,1)S(1)}, u32[]{:S(2)}, u32[]{:S(2)}) collective-permute-start(bf16[80,576]{1,0:T(8,128)(2,1)S(1)} %get-tuple-element.34), channel_id=1, source_target_pairs={{0,28},{1,29},{2,30},{3,31},{4,0},{5,1},{6,2},{7,3},{8,4},{9,5},{1... | collective-permute-start | bytes 276488 | tf_op jit(solution)/shard_map/ppermute | solution.py:269
  18.1 9.0 %collective-permute-start.2 = (bf16[80,576]{1,0:T(8,128)(2,1)S(1)}, bf16[80,576]{1,0:T(8,128)(2,1)S(1)}, u32[]{:S(2)}, u32[]{:S(2)}) collective-permute-start(bf16[80,576]{1,0:T(8,128)(2,1)S(1)} %get-tuple-element.32), channel_id=1, source_target_pairs={{0,1},{1,0},{2,3},{3,2},{4,5},{5,4},{6,7},{7,6},{8,9},{9,8},{10,11... | collective-permute-start | bytes 276488 | tf_op jit(solution)/shard_map/ppermute | solution.py:256
  19.8 14.4 %collective-permute-start.9 = (bf16[112,576]{1,0:T(8,128)(2,1)S(1)}, bf16[112,576]{1,0:T(8,128)(2,1)S(1)}, u32[]{:S(2)}, u32[]{:S(2)}) collective-permute-start(bf16[112,576]{1,0:T(8,128)(2,1)S(1)} %get-tuple-element.41), channel_id=1, source_target_pairs={{0,2},{1,3},{2,0},{3,1},{4,6},{5,7},{6,4},{7,5},{8,10},{9,11},{10,... | collective-permute-start | bytes 387080 | tf_op jit(solution)/shard_map/ppermute | solution.py:279
  27.1 7.0 %collective-permute-start.8 = (bf16[80,576]{1,0:T(8,128)(2,1)S(1)}, bf16[80,576]{1,0:T(8,128)(2,1)S(1)}, u32[]{:S(2)}, u32[]{:S(2)}) collective-permute-start(bf16[80,576]{1,0:T(8,128)(2,1)S(1)} %get-tuple-element.40), channel_id=1, source_target_pairs={{0,2},{1,3},{2,0},{3,1},{4,6},{5,7},{6,4},{7,5},{8,10},{9,11},{10,... | collective-permute-start | bytes 276488 | tf_op jit(solution)/shard_map/ppermute | solution.py:279

commit v14 on v10

--- a/solution.py
+++ b/solution.py
@@ -152,8 +152,8 @@
 
 
 def combine_kernel(low, chunk, sel_ref, *rest):
-    own_refs = rest[:low]
-    far_refs = rest[low : 2 * low]
+    far_refs = rest[:low]
+    own_refs = rest[low : 2 * low]
     send_ref, mine_ref = rest[-2:]
     part = send_ref.shape[0]
     here = slice(chunk * part, (chunk + 1) * part)
@@ -248,9 +248,7 @@
 
     far_ds, own_parts, far_parts = [], [], []
     for c in range(CHUNKS):
-        parts = own[c::CHUNKS]
-        own_parts.append([keep] + [lax.ppermute(parts[d - 1], ("seq", "head"), route(d, 0)) for d in range(1, low)])
-        later = [i for i in range(len(own)) if i % CHUNKS > c]
+        later = [i for i in range(len(own)) if i % CHUNKS and i % CHUNKS >= c]
         ds, *far = call(
             functools.partial(far_kernel, low, len(later)),
             f"far_visit_{c}",
@@ -261,6 +259,8 @@
         )
         for i, x in zip(later, far[low:]):
             own[i] = x
+        parts = own[c::CHUNKS]
+        own_parts.append([keep] + [lax.ppermute(parts[d - 1], ("seq", "head"), route(d, 0)) for d in range(1, low)])
         far_ds.append(ds)
         far_parts.append([lax.ppermute(far[d], ("seq", "head"), route(d, 1)) for d in reversed(range(low))])
 
@@ -269,7 +269,7 @@
         send, mine[c] = call(
             functools.partial(combine_kernel, low, c),
             f"combine_{c}",
-            (sel, *own_parts[c], *far_parts[c]),
+            (sel, *far_parts[c], *own_parts[c]),
             [((part, width), BF16), ((part, width), F32)],
         )
         got[c] = lax.ppermute(send, "head", [(j, (j + low) % n_head) for j in range(n_head)])

time: 34 us -> 35.8 us (1.053)
  waiting for transfers between devices: 5.46 us -> 10.2 us
  starting transfers between devices: 17 us -> 14.1 us
    ppermute x2, waiting for transfers between devices: 0.01 us -> 4.79 us  [local(): lax.ppermute(parts[d - 1], ('seq', 'head'), route(d, 0))]
    ppermute x2, starting transfers between devices: 5.74 us -> 2.73 us  [local(): lax.ppermute(send, 'head', [(j, (j + low) % n_head) for j in range(n_head)])]
    ppermute x2, starting transfers between devices: 2.09 us -> 3.22 us  [local(): lax.ppermute(parts[d - 1], ('seq', 'head'), route(d, 0))]
    ppermute x4, starting transfers between devices: 6.08 us -> 5.08 us  [local(): lax.ppermute(far[d], ('seq', 'head'), route(d, 1))]
  transfers between devices with their start and end apart: 10 -> 10, of which waited for: 3 -> 2; matrix products, arithmetic and copies ran while one was open for 0% -> 0% of each run, Pallas kernels for 25% -> 24%
where the time goes in v14:
time: 35.8 us; the launch traced here: 35.6 us
  starting transfers between devices  14.1 us (39%)
  Pallas kernels  10.6 us (30%)
  waiting for transfers between devices  10.2 us (28%)
  between operations  0.72 us (2%)
    pallas_call x8, Pallas kernels, call(): pl.pallas_call(kernel, name=name, out_shape=shapes, in_specs=[pl.BlockSpe...  10.6 us
    ppermute x2, waiting for transfers between devices, local(): lax.ppermute(send, 'head', [(j, (j + low) % n_head) for j in range(n_head)])  5.38 us
    ppermute x4, starting transfers between devices, local(): lax.ppermute(far[d], ('seq', 'head'), route(d, 1))  5.08 us
    ppermute x2, waiting for transfers between devices, local(): lax.ppermute(parts[d - 1], ('seq', 'head'), route(d, 0))  4.79 us
    ppermute x2, starting transfers between devices, local(): lax.ppermute(parts[d - 1], ('seq', 'head'), route(d, 0))  3.22 us
    ppermute x2, starting transfers between devices, local(): lax.ppermute(x, 'seq', [(i, (i + 1) % n_seq) for i in range(n_seq)])  3.11 us
    ppermute x2, starting transfers between devices, local(): lax.ppermute(send, 'head', [(j, (j + low) % n_head) for j in range(n_head)])  2.73 us
  transfers between devices with their start and end apart: 10, of which 2 were waited for; matrix products, arithmetic and copies ran while one was open for 0% of the time, Pallas kernels for 24%

profile of v14, /device:TPU:0, one launch (start us, length us, event | category | flops | bytes accessed | tf_op | source)
XLA Modules:
  0.0 35.6 jit_solution(17723156923478933660)
XLA Ops:
  0.6 0.0 copy-start
  0.6 0.0 copy-start.1
  0.7 0.0 copy-start.2
  0.7 0.0 copy-start.3
  0.7 0.0 copy-start.4
  0.7 1.4 %send_block.1 = (bf16[192,576]{1,0:T(8,128)(2,1)S(1)}, bf16[192,576]{1,0:T(8,128)(2,1)S(1)}, bf16[2,576,384]{2,1,0:T(8,128)(2,1)S(1)}) custom-call(s32[1,2]{1,0:T(1,128)} %plan_ref.3, bf16[576,768]{1,0:T(8,128)(2,1)} %bitcast.17), custom_call_target="tpu_custom_call" | custom-call | flops 1711276032 | bytes 2211848 | tf_op jit(solution)/shard_map/send_block/pallas_call | solution.py:189
  2.1 0.5 %collective-permute-start = (bf16[192,576]{1,0:T(8,128)(2,1)S(1)}, bf16[192,576]{1,0:T(8,128)(2,1)S(1)}, u32[]{:S(2)}, u32[]{:S(2)}) collective-permute-start(bf16[192,576]{1,0:T(8,128)(2,1)S(1)} %get-tuple-element.25), channel_id=1, source_target_pairs={{0,4},{4,8},{8,12},{12,16},{16,20},{20,24},{24,28},{28,0},{1,5},{5... | collective-permute-start | bytes 663560 | tf_op jit(solution)/shard_map/ppermute | solution.py:238
  2.6 2.6 %collective-permute-start.1 = (bf16[192,576]{1,0:T(8,128)(2,1)S(1)}, bf16[192,576]{1,0:T(8,128)(2,1)S(1)}, u32[]{:S(2)}, u32[]{:S(2)}) collective-permute-start(bf16[192,576]{1,0:T(8,128)(2,1)S(1)} %get-tuple-element.26), channel_id=1, source_target_pairs={{0,4},{4,8},{8,12},{12,16},{16,20},{20,24},{24,28},{28,0},{1,5},{5... | collective-permute-start | bytes 663560 | tf_op jit(solution)/shard_map/ppermute | solution.py:238
  5.2 0.0 copy-done
  5.2 0.0 copy-done.1
  5.2 0.0 copy-done.2
  5.2 0.0 copy-done.3
  5.2 0.0 copy-done.4
  5.2 2.9 %own_visit.1 = (bf16[1024,512]{1,0:T(8,128)(2,1)S(1)}, bf16[384,1024]{1,0:T(8,128)(2,1)S(1)}, f32[8,576]{1,0:T(8,128)S(1)}, f32[192,576]{1,0:T(8,128)S(1)}, bf16...) custom-call(s32[1,2]{1,0:T(1,128)S(1)} %copy-done.4, bf16[2,576,384]{2,1,0:T(8,128)(2,1)S(1)} %get-tuple-element.23.lat_ref, ...), custom_call_target="tpu_custom_call" | custom-call | bytes 5634056 | tf_op jit(solution)/shard_map/own_visit/pallas_call | solution.py:189
  8.1 1.6 %collective-permute-start.7 = (bf16[96,576]{1,0:T(8,128)(2,1)S(1)}, bf16[96,576]{1,0:T(8,128)(2,1)S(1)}, u32[]{:S(2)}, u32[]{:S(2)}) collective-permute-start(bf16[96,576]{1,0:T(8,128)(2,1)S(1)} %get-tuple-element.40), channel_id=1, source_target_pairs={{0,1},{1,0},{2,3},{3,2},{4,5},{5,4},{6,7},{7,6},{8,9},{9,8},{10,11... | collective-permute-start | bytes 331784 | tf_op jit(solution)/shard_map/ppermute | solution.py:263
  9.7 0.0 collective-permute-done.keys_ref.rest_0_
  9.7 1.5 %far_visit_0.1 = (bf16[192,1024]{1,0:T(8,128)(2,1)S(1)}, bf16[96,576]{1,0:T(8,128)(2,1)S(1)}, bf16[96,576]{1,0:T(8,128)(2,1)S(1)}, bf16[96,576]{1,0:T(8,128)(2,1)S(1)}) custom-call(bf16[192,576]{1,0:T(8,128)(2,1)S(1)} %collective-permute-done.keys_ref.rest_0_, bf16[8,576,128]{2,1,0:T(8,128)(2,1)S(1)} %bitcast.7, ...), custom_call_target="tpu_custom_call", output_to_operand_aliasing={{3}: (5, {})} | custom-call | bytes 3067904 | tf_op jit(solution)/shard_map/far_visit_0/pallas_call | solution.py:189
  11.2 0.7 %collective-permute-start.5 = (bf16[96,576]{1,0:T(8,128)(2,1)S(1)}, bf16[96,576]{1,0:T(8,128)(2,1)S(1)}, u32[]{:S(2)}, u32[]{:S(2)}) collective-permute-start(bf16[96,576]{1,0:T(8,128)(2,1)S(1)} %get-tuple-element.38), channel_id=1, source_target_pairs={{0,29},{1,28},{2,31},{3,30},{4,1},{5,0},{6,3},{7,2},{8,5},{9,4},{1... | collective-permute-start | bytes 331784 | tf_op jit(solution)/shard_map/ppermute | solution.py:265
  11.9 2.6 %collective-permute-start.6 = (bf16[96,576]{1,0:T(8,128)(2,1)S(1)}, bf16[96,576]{1,0:T(8,128)(2,1)S(1)}, u32[]{:S(2)}, u32[]{:S(2)}) collective-permute-start(bf16[96,576]{1,0:T(8,128)(2,1)S(1)} %get-tuple-element.39), channel_id=1, source_target_pairs={{0,28},{1,29},{2,30},{3,31},{4,0},{5,1},{6,2},{7,3},{8,4},{9,5},{1... | collective-permute-start | bytes 331784 | tf_op jit(solution)/shard_map/ppermute | solution.py:265
  14.4 0.0 collective-permute-done.1.keys_ref.rest_1_
  14.5 1.5 %far_visit_1.1 = (bf16[192,1024]{1,0:T(8,128)(2,1)S(1)}, bf16[96,576]{1,0:T(8,128)(2,1)S(1)}, bf16[96,576]{1,0:T(8,128)(2,1)S(1)}, bf16[96,576]{1,0:T(8,128)(2,1)S(1)}) custom-call(bf16[192,576]{1,0:T(8,128)(2,1)S(1)} %collective-permute-done.1.keys_ref.rest_1_, bf16[8,576,128]{2,1,0:T(8,128)(2,1)S(1)} %bitcast.8, ...), custom_call_target="tpu_custom_call", output_to_operand_aliasing={{3}: (5, {})} | custom-call | bytes 3067904 | tf_op jit(solution)/shard_map/far_visit_1/pallas_call | solution.py:189
  15.9 0.2 collective-permute-start.2
  16.1 1.6 %collective-permute-start.3 = (bf16[96,576]{1,0:T(8,128)(2,1)S(1)}, bf16[96,576]{1,0:T(8,128)(2,1)S(1)}, u32[]{:S(2)}, u32[]{:S(2)}) collective-permute-start(bf16[96,576]{1,0:T(8,128)(2,1)S(1)} %get-tuple-element.34), channel_id=1, source_target_pairs={{0,28},{1,29},{2,30},{3,31},{4,0},{5,1},{6,2},{7,3},{8,4},{9,5},{1... | collective-permute-start | bytes 331784 | tf_op jit(solution)/shard_map/ppermute | solution.py:265
  17.7 0.0 collective-permute-done.7.rest_3_
  17.7 1.6 %collective-permute-start.4 = (bf16[96,576]{1,0:T(8,128)(2,1)S(1)}, bf16[96,576]{1,0:T(8,128)(2,1)S(1)}, u32[]{:S(2)}, u32[]{:S(2)}) collective-permute-start(bf16[96,576]{1,0:T(8,128)(2,1)S(1)} %get-tuple-element.36), channel_id=1, source_target_pairs={{0,1},{1,0},{2,3},{3,2},{4,5},{5,4},{6,7},{7,6},{8,9},{9,8},{10,11... | collective-permute-start | bytes 331784 | tf_op jit(solution)/shard_map/ppermute | solution.py:263
  19.3 0.0 collective-permute-done.5.rest_0_
  19.3 0.0 collective-permute-done.6.rest_1_
  19.3 0.1 combine_0.1
  19.4 2.7 %collective-permute-start.9 = (bf16[96,576]{1,0:T(8,128)(2,1)S(1)}, bf16[96,576]{1,0:T(8,128)(2,1)S(1)}, u32[]{:S(2)}, u32[]{:S(2)}) collective-permute-start(bf16[96,576]{1,0:T(8,128)(2,1)S(1)} %get-tuple-element.43), channel_id=1, source_target_pairs={{0,2},{1,3},{2,0},{3,1},{4,6},{5,7},{6,4},{7,5},{8,10},{9,11},{10,... | collective-permute-start | bytes 331784 | tf_op jit(solution)/shard_map/ppermute | solution.py:275
  22.1 0.0 collective-permute-done.2.rest_0_
  22.1 0.0 collective-permute-done.3.rest_1_
  22.1 4.8 %collective-permute-done.4.rest_3_ = bf16[96,576]{1,0:T(8,128)(2,1)S(1)} collective-permute-done((bf16[96,576]{1,0:T(8,128)(2,1)S(1)}, bf16[96,576]{1,0:T(8,128)(2,1)S(1)}, u32[]{:S(2)}, u32[]{:S(2)}) %collective-permute-start.4) | collective-permute-done | bytes 110624 | tf_op jit(solution)/shard_map/ppermute | solution.py:263
  26.9 0.1 combine_1.1
  27.0 0.1 collective-permute-start.8
  27.0 2.4 %query_grad.1 = bf16[8,576,128]{2,1,0:T(8,128)(2,1)} custom-call(s32[1,2]{1,0:T(1,128)S(1)} %copy-done.4, bf16[2,576,384]{2,1,0:T(8,128)(2,1)S(1)} %get-tuple-element.23.lat_ref, bf16[384,1024]{1,0:T(8,128)(2,1)S(1)} %get-tuple-element.24.own_ds_ref, bf16[192,576]{1,0:T(8,128)(2,1)S(1)} %collective-permute-done.keys_ref.rest_0_, ...), custom_call_target="tpu_custom_call" | custom-call | flops 905969664 | bytes 4079624 | tf_op jit(solution)/shard_map/query_grad/pallas_call | solution.py:189
  29.5 0.0 collective-permute-done.9.refs_3_
  29.5 5.4 %collective-permute-done.8.refs_2_ = bf16[96,576]{1,0:T(8,128)(2,1)S(1)} collective-permute-done((bf16[96,576]{1,0:T(8,128)(2,1)S(1)}, bf16[96,576]{1,0:T(8,128)(2,1)S(1)}, u32[]{:S(2)}, u32[]{:S(2)}) %collective-permute-start.8) | collective-permute-done | bytes 110624 | tf_op jit(solution)/shard_map/ppermute | solution.py:275
  34.9 0.7 %last_sum.1 = bf16[192,576]{1,0:T(8,128)(2,1)} custom-call(f32[96,576]{1,0:T(8,128)S(1)} %get-tuple-element.37.refs_0_, f32[96,576]{1,0:T(8,128)S(1)} %get-tuple-element.41.refs_1_, bf16[96,576]{1,0:T(8,128)(2,1)S(1)} %collective-permute-done.8.refs_2_, bf16[96,576]{1,0:T(8,128)(2,1)S(1)} %collective-permute-done.9.refs_3_), custom_call_target="tpu_custom_call" | custom-call | bytes 884736 | tf_op jit(solution)/shard_map/last_sum/pallas_call | solution.py:189
Async XLA Ops:
  0.6 4.5 %copy-start = (bf16[128,8,576]{0,2,1:T(8,128)(2,1)S(1)}, bf16[128,8,576]{0,2,1:T(8,128)(2,1)}, u32[]{:S(2)}) copy-start(bf16[128,8,576]{0,2,1:T(8,128)(2,1)} %param.6) | copy-start | bytes 3538948
  0.6 4.5 %copy-start.1 = (bf16[128,8,512]{2,1,0:T(8,128)(2,1)S(1)}, bf16[128,8,512]{2,1,0:T(8,128)(2,1)}, u32[]{:S(2)}) copy-start(bf16[128,8,512]{2,1,0:T(8,128)(2,1)} %param.7) | copy-start | bytes 3145732
  0.7 4.5 %copy-start.2 = (bf16[128,8]{0,1:T(8,128)(2,1)S(1)}, bf16[128,8]{0,1:T(8,128)(2,1)}, u32[]{:S(2)}) copy-start(bf16[128,8]{0,1:T(8,128)(2,1)} %param.9) | copy-start | bytes 6148
  0.7 4.5 %copy-start.3 = (bf16[128,8]{0,1:T(8,128)(2,1)S(1)}, bf16[128,8]{0,1:T(8,128)(2,1)}, u32[]{:S(2)}) copy-start(bf16[128,8]{0,1:T(8,128)(2,1)} %param.10) | copy-start | bytes 6148
  0.7 4.5 %copy-start.4 = (s32[1,2]{1,0:T(1,128)S(1)}, s32[1,2]{1,0:T(1,128)}, u32[]{:S(2)}) copy-start(s32[1,2]{1,0:T(1,128)} %plan_ref.3) | copy-start | bytes 28
  2.1 7.6 %collective-permute-start = (bf16[192,576]{1,0:T(8,128)(2,1)S(1)}, bf16[192,576]{1,0:T(8,128)(2,1)S(1)}, u32[]{:S(2)}, u32[]{:S(2)}) collective-permute-start(bf16[192,576]{1,0:T(8,128)(2,1)S(1)} %get-tuple-element.25), channel_id=1, source_target_pairs={{0,4},{4,8},{8,12},{12,16},{16,20},{20,24},{24,28},{28,0},{1,5},{5... | collective-permute-start | bytes 663560 | tf_op jit(solution)/shard_map/ppermute | solution.py:238
  2.6 11.9 %collective-permute-start.1 = (bf16[192,576]{1,0:T(8,128)(2,1)S(1)}, bf16[192,576]{1,0:T(8,128)(2,1)S(1)}, u32[]{:S(2)}, u32[]{:S(2)}) collective-permute-start(bf16[192,576]{1,0:T(8,128)(2,1)S(1)} %get-tuple-element.26), channel_id=1, source_target_pairs={{0,4},{4,8},{8,12},{12,16},{16,20},{20,24},{24,28},{28,0},{1,5},{5... | collective-permute-start | bytes 663560 | tf_op jit(solution)/shard_map/ppermute | solution.py:238
  8.1 9.6 %collective-permute-start.7 = (bf16[96,576]{1,0:T(8,128)(2,1)S(1)}, bf16[96,576]{1,0:T(8,128)(2,1)S(1)}, u32[]{:S(2)}, u32[]{:S(2)}) collective-permute-start(bf16[96,576]{1,0:T(8,128)(2,1)S(1)} %get-tuple-element.40), channel_id=1, source_target_pairs={{0,1},{1,0},{2,3},{3,2},{4,5},{5,4},{6,7},{7,6},{8,9},{9,8},{10,11... | collective-permute-start | bytes 331784 | tf_op jit(solution)/shard_map/ppermute | solution.py:263
  11.2 8.1 %collective-permute-start.5 = (bf16[96,576]{1,0:T(8,128)(2,1)S(1)}, bf16[96,576]{1,0:T(8,128)(2,1)S(1)}, u32[]{:S(2)}, u32[]{:S(2)}) collective-permute-start(bf16[96,576]{1,0:T(8,128)(2,1)S(1)} %get-tuple-element.38), channel_id=1, source_target_pairs={{0,29},{1,28},{2,31},{3,30},{4,1},{5,0},{6,3},{7,2},{8,5},{9,4},{1... | collective-permute-start | bytes 331784 | tf_op jit(solution)/shard_map/ppermute | solution.py:265
  11.9 7.4 %collective-permute-start.6 = (bf16[96,576]{1,0:T(8,128)(2,1)S(1)}, bf16[96,576]{1,0:T(8,128)(2,1)S(1)}, u32[]{:S(2)}, u32[]{:S(2)}) collective-permute-start(bf16[96,576]{1,0:T(8,128)(2,1)S(1)} %get-tuple-element.39), channel_id=1, source_target_pairs={{0,28},{1,29},{2,30},{3,31},{4,0},{5,1},{6,2},{7,3},{8,4},{9,5},{1... | collective-permute-start | bytes 331784 | tf_op jit(solution)/shard_map/ppermute | solution.py:265
  15.9 6.1 %collective-permute-start.2 = (bf16[96,576]{1,0:T(8,128)(2,1)S(1)}, bf16[96,576]{1,0:T(8,128)(2,1)S(1)}, u32[]{:S(2)}, u32[]{:S(2)}) collective-permute-start(bf16[96,576]{1,0:T(8,128)(2,1)S(1)} %get-tuple-element.33), channel_id=1, source_target_pairs={{0,29},{1,28},{2,31},{3,30},{4,1},{5,0},{6,3},{7,2},{8,5},{9,4},{1... | collective-permute-start | bytes 331784 | tf_op jit(solution)/shard_map/ppermute | solution.py:265
  16.1 5.9 %collective-permute-start.3 = (bf16[96,576]{1,0:T(8,128)(2,1)S(1)}, bf16[96,576]{1,0:T(8,128)(2,1)S(1)}, u32[]{:S(2)}, u32[]{:S(2)}) collective-permute-start(bf16[96,576]{1,0:T(8,128)(2,1)S(1)} %get-tuple-element.34), channel_id=1, source_target_pairs={{0,28},{1,29},{2,30},{3,31},{4,0},{5,1},{6,2},{7,3},{8,4},{9,5},{1... | collective-permute-start | bytes 331784 | tf_op jit(solution)/shard_map/ppermute | solution.py:265
  17.7 9.1 %collective-permute-start.4 = (bf16[96,576]{1,0:T(8,128)(2,1)S(1)}, bf16[96,576]{1,0:T(8,128)(2,1)S(1)}, u32[]{:S(2)}, u32[]{:S(2)}) collective-permute-start(bf16[96,576]{1,0:T(8,128)(2,1)S(1)} %get-tuple-element.36), channel_id=1, source_target_pairs={{0,1},{1,0},{2,3},{3,2},{4,5},{5,4},{6,7},{7,6},{8,9},{9,8},{10,11... | collective-permute-start | bytes 331784 | tf_op jit(solution)/shard_map/ppermute | solution.py:263
  19.4 10.1 %collective-permute-start.9 = (bf16[96,576]{1,0:T(8,128)(2,1)S(1)}, bf16[96,576]{1,0:T(8,128)(2,1)S(1)}, u32[]{:S(2)}, u32[]{:S(2)}) collective-permute-start(bf16[96,576]{1,0:T(8,128)(2,1)S(1)} %get-tuple-element.43), channel_id=1, source_target_pairs={{0,2},{1,3},{2,0},{3,1},{4,6},{5,7},{6,4},{7,5},{8,10},{9,11},{10,... | collective-permute-start | bytes 331784 | tf_op jit(solution)/shard_map/ppermute | solution.py:275
  27.0 7.9 %collective-permute-start.8 = (bf16[96,576]{1,0:T(8,128)(2,1)S(1)}, bf16[96,576]{1,0:T(8,128)(2,1)S(1)}, u32[]{:S(2)}, u32[]{:S(2)}) collective-permute-start(bf16[96,576]{1,0:T(8,128)(2,1)S(1)} %get-tuple-element.42), channel_id=1, source_target_pairs={{0,2},{1,3},{2,0},{3,1},{4,6},{5,7},{6,4},{7,5},{8,10},{9,11},{10,... | collective-permute-start | bytes 331784 | tf_op jit(solution)/shard_map/ppermute | solution.py:275
